TPU v7x, 256 devices: a whole 4x4x8 slice. The times are simulated.
256 devices in a mesh: dom: 32 (over z_lo, y, core), rep: 8 (over x, z_hi).
Axes of the slice: x: 4, y: 4, z: 8 (z_hi: 2, z_lo: 4; z = z_hi * 4 + z_lo), core: 2. Of those that a mesh axis runs over, the one named last changes fastest.
Arguments:
- entity: float32 [65536, 256], P(('dom', 'rep'))
- entity_accum: float32 [65536], P(('dom', 'rep')), may hold values from 0.5 to 50
- relation: float32 [4, 256, 256], replicated, may hold values from -0.375 to 0.375
- relation_accum: float32 [4, 256], replicated, may hold values from 0.01 to 1
- src_index: int32 [1024000], P(('dom', 'rep')), may hold values from 0 to 2047
- dst_index: int32 [1024000], P(('dom', 'rep')), may hold values from 0 to 2047
- neg_index: int32 [1024, 1000], P(('dom', 'rep')), may hold values from 0 to 2047
- rel_id: int32 [1024], P(('dom', 'rep')), may hold values from 0 to 3
- counts: int32 [256], P(('dom', 'rep')), may hold values from 1000 to 4000, as said below
Outputs:
- entity_new: float32 [65536, 256], P(('dom', 'rep'))
- entity_accum_new: float32 [65536], P(('dom', 'rep'))
- relation_new: float32 [4, 256, 256], replicated
- relation_accum_new: float32 [4, 256], replicated
Inputs may be any that keep to these rules, and one draw needn't show every extreme that they name: `counts`: one block of 4000 slots has all slots live in every draw.
All inputs are finite; a program needn't handle non-finite values.
Results may differ from a plain program's by a relative error of at most 0.0047.
Values may be sent and summed in bfloat16 or wider, within the bound.
No kernel may reach another device: no remote copies, remote signals or barrier semaphores. Data moves between devices by JAX's collectives and lax.ppermute only.
A program may use at most 128 MiB of HBM per device.

v0:
```python
import jax
import jax.numpy as jnp
from jax import lax
from jax.sharding import PartitionSpec as P

learn_rate = 0.1


def shifted_2(block, axis, distance):
    devices = range(lax.axis_size(axis))
    route = [((i - distance) % len(devices), i) for i in devices]
    return lax.ppermute(block, axis, route)


def make_queries(block, src_index, rel_id, rel_b):
    groups = rel_id.shape[0]
    width = block.shape[1]
    srcs = block[src_index].reshape(groups, -1, width)
    mats = rel_b[rel_id]
    queries = jnp.einsum("cnd,cde->cne", srcs, mats, preferred_element_type=jnp.float32).astype(
        jnp.bfloat16
    )
    return (srcs, mats, queries)


def score_side(queries, block, dst_index, neg_index, count):
    groups = neg_index.shape[0]
    width = block.shape[1]
    targets = block[dst_index].reshape(queries.shape)
    negatives = block[neg_index]
    qfloat = queries.astype(jnp.float32)
    pos = jnp.sum(qfloat * targets.astype(jnp.float32), -1)
    neg = jnp.einsum("cnd,cmd->cnm", queries, negatives, preferred_element_type=jnp.float32)
    top = jnp.maximum(pos, jnp.max(neg, -1))
    epos = jnp.exp(pos - top)
    eneg = jnp.exp(neg - top[..., None])
    total = epos + jnp.sum(eneg, -1)
    slot = jnp.arange(dst_index.shape[0], dtype=jnp.int32).reshape(groups, -1)
    live = (slot < count).astype(jnp.float32)
    gpos = (epos / total - 1.0) * live
    gneg = (eneg / total[..., None] * live[..., None]).astype(jnp.bfloat16)
    grad_q = gpos[..., None] * targets.astype(jnp.float32) + jnp.einsum(
        "cnm,cmd->cnd", gneg, negatives, preferred_element_type=jnp.float32
    )
    grad_q = grad_q.astype(jnp.bfloat16)
    grad_tgt = gpos[..., None] * qfloat
    grad_neg = jnp.einsum("cnm,cnd->cmd", gneg, queries, preferred_element_type=jnp.float32)
    dst_grad = (
        jnp.zeros((block.shape[0], width), jnp.float32)
        .at[dst_index]
        .add(grad_tgt.reshape(-1, width))
    )
    dst_grad = dst_grad.at[neg_index.reshape(-1)].add(grad_neg.reshape(-1, width))
    return (grad_q, dst_grad)


def source_side(srcs, mats, grad_q, src_index, rel_id, rows, kinds):
    width = srcs.shape[2]
    grad_src = jnp.einsum("cne,cde->cnd", grad_q, mats, preferred_element_type=jnp.float32)
    src_grad = jnp.zeros((rows, width), jnp.float32).at[src_index].add(grad_src.reshape(-1, width))
    per_group = jnp.einsum("cnd,cne->cde", srcs, grad_q, preferred_element_type=jnp.float32)
    rel_grad = jnp.zeros((kinds, width, width), jnp.float32).at[rel_id].add(per_group)
    return (src_grad, rel_grad)


def rowwise(param, accum, grad):
    fresh = accum + jnp.mean(grad * grad, -1)
    return (param - learn_rate * grad / jnp.sqrt(fresh)[..., None], fresh)


def on_device(
    entity, entity_accum, relation, relation_accum, src_index, dst_index, neg_index, rel_id, counts
):
    ent_b = entity.astype(jnp.bfloat16)
    rel_b = relation.astype(jnp.bfloat16)
    kinds = relation.shape[0]
    count = counts[0]
    shifted = shifted_2(ent_b, "dom", -1)
    own, nxt = (
        lax.all_gather(ent_b, "rep", axis=0, tiled=True),
        lax.all_gather(shifted, "rep", axis=0, tiled=True),
    )
    srcs, mats, queries = make_queries(own, src_index, rel_id, rel_b)
    grad_q, dst_grad = score_side(queries, nxt, dst_index, neg_index, count)
    src_grad, rel_grad = source_side(srcs, mats, grad_q, src_index, rel_id, own.shape[0], kinds)
    src_part, dst_part = (
        lax.psum_scatter(
            src_grad.astype(jnp.bfloat16), "rep", scatter_dimension=0, tiled=True
        ).astype(jnp.float32),
        lax.psum_scatter(
            dst_grad.astype(jnp.bfloat16), "rep", scatter_dimension=0, tiled=True
        ).astype(jnp.float32),
    )
    returned = shifted_2(dst_part.astype(jnp.bfloat16), "dom", 1).astype(dst_part.dtype)
    grads = src_part + returned
    rel_total = lax.psum(rel_grad, ("dom", "rep"))
    entity_new, entity_accum_new = rowwise(entity, entity_accum, grads)
    relation_new, relation_accum_new = rowwise(relation, relation_accum, rel_total)
    return (entity_new, entity_accum_new, relation_new, relation_accum_new)


def solution(mesh):
    placed = (
        P(("dom", "rep"), None),
        P(("dom", "rep")),
        P(),
        P(),
        P(("dom", "rep")),
        P(("dom", "rep")),
        P(("dom", "rep"), None),
        P(("dom", "rep")),
        P(("dom", "rep")),
    )
    return jax.shard_map(
        on_device,
        mesh=mesh,
        in_specs=placed,
        out_specs=(P(("dom", "rep"), None), P(("dom", "rep")), P(), P()),
        check_vma=False,
    )
```

profile of v0, /device:TPU:1, one launch (start us, length us, event | category | flops | bytes accessed | tf_op | source)
XLA Modules:
  0.0 675.1 jit_solution(14981122258321238077)
XLA Ops:
  7.2 0.0 all-gather.3.cloned.1.call-start
  7.2 1.6 convert_element_type.46
  8.9 0.0 all-gather.3.cloned.1.call-update
  8.9 0.0 all-gather.5.cloned.1.call-start
  8.9 3.3 collective-permute-start
  12.2 0.7 compare_select_fusion.1
  13.0 0.7 compare_select_fusion.4
  13.6 0.9 collective-permute-done
  14.6 0.7 copy-done.8
  15.2 0.0 all-reduce.2.cloned.1.call-start
  15.3 0.8 reshape.106
  16.1 1.3 convert_element_type.47
  17.4 0.1 reshape.135
  18.1 1.4 gather_fusion.1
  19.6 55.9 %all-gather.3.cloned.1.call-done = bf16[2048,256]{1,0:T(8,128)(2,1)} async-done(((bf16[256,256]{1,0:T(8,128)(2,1)}), bf16[2048,256]{1,0:T(8,128)(2,1)}) %all-gather.3.cloned.1.call-update) | async-done | bytes 1048592 | tf_op jit(solution)/shard_map/all_gather | solution.py:80
  75.5 14.7 %gather_fusion = bf16[4000,256]{1,0:T(8,128)(2,1)S(1)} fusion(bf16[2048,256]{1,0:T(8,128)(2,1)} %all-gather.3.cloned.1.call-done, s32[4096]{0:T(1024)S(1)} %pad_clamp_fusion.2), kind=kCustom, calls=%fused_computation | custom fusion | bytes 4112000 | tf_op jit(solution)/shard_map/gather | solution.py:18
  90.2 46.0 %all-gather.5.cloned.1.call-done = bf16[2048,256]{1,0:T(8,128)(2,1)} async-done(((bf16[256,256]{1,0:T(8,128)(2,1)}), bf16[2048,256]{1,0:T(8,128)(2,1)}) %all-gather.5.cloned.1.call-update) | async-done | bytes 1048592 | tf_op jit(solution)/shard_map/all_gather | solution.py:81
  136.2 17.3 %gather_fusion.2 = bf16[4000,256]{1,0:T(8,128)(2,1)} fusion(bf16[2048,256]{1,0:T(8,128)(2,1)} %all-gather.5.cloned.1.call-done, s32[4096]{0:T(1024)S(1)} %pad_clamp_fusion.1), kind=kCustom, calls=%fused_computation.2 | custom fusion | bytes 4112000 | tf_op jit(solution)/shard_map/gather | solution.py:29
  153.5 3.8 fusion.1
  157.3 14.9 %gather_fusion.3 = bf16[4000,256]{1,0:T(8,128)(2,1)S(1)} fusion(bf16[2048,256]{1,0:T(8,128)(2,1)S(1)} %copy-done, s32[4096]{0:T(1024)S(1)} %pad_clamp_fusion), kind=kCustom, calls=%fused_computation.3 | custom fusion | bytes 4112000 | tf_op jit(solution)/shard_map/gather | solution.py:30
  172.2 10.3 %fusion.12 = (f32[4,1000]{1,0:T(4,128)S(1)}, f32[4,1000,1000]{1,2,0:T(8,128)}) fusion(bf16[4,1000,256]{2,1,0:T(8,128)(2,1)} %get-tuple-element.13, bf16[4,1000,256]{2,1,0:T(8,128)(2,1)S(1)} %bitcast.23), kind=kOutput, calls=%fused_computation.45 | convolution fusion | flops 2051996032 | bytes 20112000 | tf_op jit(solution)/shard_map/cnd,cmd->cnm/dot_general | solution.py:33
  182.5 7.9 %fusion = f32[4,1000]{1,0:T(4,128)S(1)} fusion(f32[4,1000,1000]{1,2,0:T(8,128)} %get-tuple-element.15, f32[4,1000]{1,0:T(4,128)S(1)} %max.13), kind=kLoop, calls=%fused_computation.10 | loop fusion | flops 7996000 | bytes 16032000 | tf_op jit(solution)/shard_map/reduce_sum | solution.py:37
  190.5 7.4 %multiply_convert_fusion = bf16[4,1000,1000]{1,2,0:T(8,128)(2,1)S(1)} fusion(f32[4,1000,1000]{1,2,0:T(8,128)} %get-tuple-element.15, f32[4,1000]{1,0:T(4,128)S(1)} %fusion.8, f32[4,1000]{1,0:T(4,128)S(1)} %get-tuple-element.8, f32[4,1000]{1,0:T(4,128)S(1)} %max.13), kind=kLoop, calls=%fused_computation.8 | loop fusion | flops 16000000 | bytes 24048000 | tf_op jit(solution)/shard_map/convert_element_type | solution.py:41
  197.8 10.2 %fusion.3 = (bf16[4,1000,256]{2,1,0:T(8,128)(2,1)}, f32[4,1000,256]{2,1,0:T(8,128)}) fusion(bf16[4,1000,256]{2,1,0:T(8,128)(2,1)} %bitcast.28, f32[4,1000]{1,0:T(4,128)S(1)} %get-tuple-element.9, bf16[4,1000,256]{2,1,0:T(8,128)(2,1)} %get-tuple-element.13, bf16[4,1000,1000]{1,2,0:T(8,128)(2,1)S(1)} %multiply_convert_fusion, bf16[4,1000,256]{2,1,0:T(8,128)(2,1)} %bitcast.24), kind=kOutput, calls=%fused_computation.16 | convolution fusion | flops 2054144000 | bytes 20304000 | tf_op jit(solution)/shard_map/cnm,cmd->cnd/dot_general | solution.py:42
  208.0 4.0 fusion.15
  212.1 21.5 %scatter_custom_fusion.1 = f32[2048,256]{1,0:T(8,128)S(1)} fusion(s32[4000]{0:T(1024)S(1)} %compare_select_fusion.2, f32[4000,256]{1,0:T(8,128)} %bitcast.31, f32[]{:T(128)} %constant.9.clone.1), kind=kCustom, calls=%fused_computation.20 | custom fusion | flops 1024000 | bytes 2097664 | tf_op jit(solution)/shard_map/scatter-add | solution.py:51
  233.6 0.1 broadcast_in_dim.14
  233.6 2.3 scatter_fusion.1
  235.9 1.0 copy-done.3
  236.9 0.0 all-reduce.2.cloned.1.call-update
  236.9 0.0 reduce-scatter.5.cloned.1.call-start
  237.0 8.2 %fusion.14 = f32[4,1000,256]{2,1,0:T(8,128)} fusion(bf16[4,1000,1000]{1,2,0:T(8,128)(2,1)} %copy-done.1, bf16[4,1000,256]{2,1,0:T(8,128)(2,1)} %get-tuple-element.13), kind=kOutput, calls=%fused_computation.47 | convolution fusion | flops 2048000000 | bytes 14144000 | tf_op jit(solution)/shard_map/cnm,cnd->cmd/dot_general | solution.py:47
  245.1 23.6 %scatter_fusion = f32[2048,256]{1,0:T(8,128)S(1)} fusion(f32[2048,256]{1,0:T(8,128)S(1)} %scatter_custom_fusion.1, s32[4000]{0:T(1024)S(1)} %bitcast.32, f32[4000,256]{1,0:T(8,128)} %bitcast.29), kind=kCustom, calls=%fused_computation.6 | custom fusion | flops 1024000 | bytes 12304000 | tf_op jit(solution)/shard_map/scatter-add | solution.py:53
  268.8 1.1 convert_element_type.57
  269.9 0.0 reduce-scatter.3.cloned.1.call-start
  270.0 4.2 fusion.13
  274.2 21.5 %scatter_custom_fusion = f32[2048,256]{1,0:T(8,128)S(1)} fusion(s32[4000]{0:T(1024)S(1)} %compare_select_fusion.3, f32[4000,256]{1,0:T(8,128)} %bitcast.30, f32[]{:T(128)} %constant.9.clone.1), kind=kCustom, calls=%fused_computation.22 | custom fusion | flops 1024000 | bytes 2097664 | tf_op jit(solution)/shard_map/scatter-add | solution.py:60
  295.8 1.1 convert_element_type.55
  296.9 191.9 %all-reduce.2.cloned.1.call-done = f32[4,256,256]{2,1,0:T(8,128)} async-done(((f32[4,256,256]{2,1,0:T(8,128)}), f32[4,256,256]{2,1,0:T(8,128)}) %all-reduce.2.cloned.1.call-update) | async-done | bytes 1048592 | tf_op jit(solution)/shard_map/psum | solution.py:96
  488.8 1.4 multiply_reduce_fusion
  490.2 0.6 fusion.10
  490.8 88.0 %reduce-scatter.5.cloned.1.call-done = bf16[256,256]{1,0:T(8,128)(2,1)} async-done(((bf16[2048,256]{1,0:T(8,128)(2,1)}), bf16[256,256]{1,0:T(8,128)(2,1)}) %reduce-scatter.5.cloned.1.call-update) | async-done | bytes 131088 | tf_op jit(solution)/shard_map/reduce_scatter | solution.py:90
  578.8 3.3 collective-permute-start.1
  582.1 2.4 divide_subtract_fusion
  584.6 80.7 %reduce-scatter.3.cloned.1.call-done = bf16[256,256]{1,0:T(8,128)(2,1)} async-done(((bf16[2048,256]{1,0:T(8,128)(2,1)}), bf16[256,256]{1,0:T(8,128)(2,1)}) %reduce-scatter.3.cloned.1.call-update) | async-done | bytes 131088 | tf_op jit(solution)/shard_map/reduce_scatter | solution.py:87
  665.3 1.0 multiply_reduce_fusion.1
  666.3 0.6 fusion.11
  666.9 1.7 divide_subtract_fusion.1
  (38 shorter events, 0.2 us)
Async XLA Ops:
  7.2 12.4 %copy-start.9 = (s32[4000]{0:T(1024)S(1)}, s32[4000]{0:T(1024)}, u32[]{:S(2)}) copy-start(s32[4000]{0:T(1024)} %param.14) | copy-start | bytes 48004
  7.2 12.4 %copy-start.10 = (s32[4000]{0:T(1024)S(1)}, s32[4000]{0:T(1024)}, u32[]{:S(2)}) copy-start(s32[4000]{0:T(1024)} %param.13) | copy-start | bytes 48004
  7.2 68.3 %all-gather.3.cloned.1.call-start = ((), (), s32[]{:S(2)}) async-start(), calls=%async_computation.2 | async-start | bytes 1179648 | tf_op jit(solution)/shard_map/all_gather | solution.py:80
  8.9 127.3 %all-gather.5.cloned.1.call-start = ((), (), s32[]{:S(2)}) async-start(), calls=%async_computation.3 | async-start | bytes 1179648 | tf_op jit(solution)/shard_map/all_gather | solution.py:81
  8.9 5.6 collective-permute-start
  14.6 0.7 copy-start.8
  15.2 473.5 %all-reduce.2.cloned.1.call-start = ((), (), s32[]{:S(2)}) async-start(), calls=%async_computation.6 | async-start | bytes 2097152 | tf_op jit(solution)/shard_map/psum | solution.py:96
  90.2 63.3 %copy-start.4 = (bf16[4000,256]{1,0:T(8,128)(2,1)}, bf16[4000,256]{1,0:T(8,128)(2,1)S(1)}, u32[]{:S(2)}) copy-start(bf16[4000,256]{1,0:T(8,128)(2,1)S(1)} %gather_fusion) | copy-start | bytes 6144004
  153.5 3.8 copy-start
  172.2 10.3 %copy-start.2 = (bf16[4000,256]{1,0:T(8,128)(2,1)}, bf16[4000,256]{1,0:T(8,128)(2,1)S(1)}, u32[]{:S(2)}) copy-start(bf16[4000,256]{1,0:T(8,128)(2,1)S(1)} %gather_fusion.3) | copy-start | bytes 6144004
  197.8 10.2 %copy-start.1 = (bf16[4,1000,1000]{1,2,0:T(8,128)(2,1)}, bf16[4,1000,1000]{1,2,0:T(8,128)(2,1)S(1)}, u32[]{:S(2)}) copy-start(bf16[4,1000,1000]{1,2,0:T(8,128)(2,1)S(1)} %multiply_convert_fusion) | copy-start | bytes 24000004
  235.9 1.0 copy-start.3
  236.9 341.9 %reduce-scatter.5.cloned.1.call-start = ((), (), s32[]{:S(2)}) async-start(), calls=%async_computation.5 | async-start | bytes 1179648 | tf_op jit(solution)/shard_map/reduce_scatter | solution.py:90
  268.8 1.2 copy-start.6
  269.9 395.4 %reduce-scatter.3.cloned.1.call-start = ((), (), s32[]{:S(2)}) async-start(), calls=%async_computation.4 | async-start | bytes 1179648 | tf_op jit(solution)/shard_map/reduce_scatter | solution.py:87
  295.7 194.5 %copy-start.11 = (f32[4,256]{1,0:T(4,128)S(1)}, f32[4,256]{1,0:T(4,128)}, u32[]{:S(2)}) copy-start(f32[4,256]{1,0:T(4,128)} %param.12) | copy-start | bytes 12292
  295.8 286.4 %copy-start.5 = (f32[4,256,256]{2,1,0:T(8,128)S(1)}, f32[4,256,256]{2,1,0:T(8,128)}, u32[]{:S(2)}) copy-start(f32[4,256,256]{2,1,0:T(8,128)} %param.11) | copy-start | bytes 3145732
  296.9 369.4 %copy-start.12 = (f32[256]{0:T(256)S(1)}, f32[256]{0:T(256)}, u32[]{:S(2)}) copy-start(f32[256]{0:T(256)} %param.10) | copy-start | bytes 3076
  296.9 370.0 %copy-start.7 = (f32[256,256]{1,0:T(8,128)S(1)}, f32[256,256]{1,0:T(8,128)}, u32[]{:S(2)}) copy-start(f32[256,256]{1,0:T(8,128)} %param.9) | copy-start | bytes 786436
  578.8 86.5 %collective-permute-start.1 = (bf16[256,256]{1,0:T(8,128)(2,1)}, bf16[256,256]{1,0:T(8,128)(2,1)S(1)}, u32[]{:S(2)}, u32[]{:S(2)}) collective-permute-start(bf16[256,256]{1,0:T(8,128)(2,1)} %reduce-scatter.5.cloned.1.call-done), channel_id=1, source_target_pairs={{248,0},{0,8},{8,16},{16,24},{24,32},{32,40},{40,48},{48,56},{56,6... | collective-permute-start | bytes 393224 | tf_op jit(solution)/shard_map/ppermute | solution.py:12
Sparse Core Ops, SparseCore 0:
  11.2 64.2 all-gather.2
  78.7 57.4 all-gather.4
  237.0 251.6 all-reduce.1
  493.7 85.1 reduce-scatter.4
  582.6 82.6 reduce-scatter.2
where the time goes:
time: 676 us; the launch traced here: 675 us
  waiting for transfers between devices  464 us (69%)
  other arithmetic  98.5 us (15%)
  local copies, waits for them, and re-layouts  50.8 us (8%)
  matrix products  40.8 us (6%)
  between operations  14.7 us (2%)
  starting transfers between devices  6.84 us (1%)
    psum x1, waiting for transfers between devices, on_device(): rel_total = lax.psum(rel_grad, ('dom', 'rep'))  192 us
    reduce_scatter x1, waiting for transfers between devices, on_device(): lax.psum_scatter(dst_grad.astype(jnp.bfloat16), 'rep', scatter_dimension=...  88 us
    reduce_scatter x1, waiting for transfers between devices, on_device(): lax.psum_scatter(src_grad.astype(jnp.bfloat16), 'rep', scatter_dimension=...  80.7 us
    all_gather x1, waiting for transfers between devices, on_device(): lax.all_gather(ent_b, 'rep', axis=0, tiled=True)  55.9 us
    all_gather x1, waiting for transfers between devices, on_device(): lax.all_gather(shifted, 'rep', axis=0, tiled=True)  46 us
    scatter-add x1, other arithmetic, score_side(): dst_grad.at[neg_index.reshape(-1)].add(grad_neg.reshape(-1, width))  23.6 us
    scatter-add x1, other arithmetic, source_side(): jnp.zeros((rows, width), jnp.float32).at[src_index]  21.5 us
    scatter-add x1, other arithmetic, score_side(): dst_grad = jnp.zeros((block.shape[0], width), jnp.float32).at[dst_index]....  21.5 us
  transfers between devices with their start and end apart: 7, of which 6 were waited for; matrix products, arithmetic and copies ran while one was open for 12% of the time, Pallas kernels for 0%

commit v1 on v0

v1 whole, which is shorter than its diff:
```python
import functools
import jax
import jax.numpy as jnp
from jax import lax
from jax.experimental import pallas as pl
from jax.experimental.pallas import tpu as pltpu
from jax.sharding import PartitionSpec as P

learn_rate = 0.1
LOG2E = 1.4426950408889634
GROUPS = 4
SLOTS = 1000
PAD = 1024
ROWS = 2048
D = 256
BLK = 256
NBLK = ROWS // BLK
CH = 512
NCH = GROUPS * PAD // CH
PER = PAD // CH
bf16 = jnp.bfloat16
f32 = jnp.float32

NN = (((1,), (0,)), ((), ()))
NT = (((1,), (1,)), ((), ()))
MB = 1024 * 1024


def mm(a, b, dims=NN):
    return lax.dot_general(a, b, dims, preferred_element_type=f32)


def params():
    return pltpu.CompilerParams(
        dimension_semantics=("arbitrary",), vmem_limit_bytes=48 * MB
    )


def count_kernel(neg_ref, out_ref):
    rows = lax.broadcasted_iota(jnp.int32, (BLK, PAD), 0)

    def body(b, carry):
        hits = jnp.where(rows == neg_ref[0] - b * BLK, 1.0, 0.0)
        count = jnp.sum(hits, axis=1, keepdims=True)
        at = pl.ds(pl.multiple_of(b * BLK, BLK), BLK)
        out_ref[0, at, 0:1] = jnp.log2(count)
        out_ref[0, at, 1:2] = jnp.log2(count + 1.0)
        return carry

    lax.fori_loop(0, NBLK, body, 0)


def neg_weights(neg_pad):
    return pl.pallas_call(
        count_kernel,
        grid=(GROUPS,),
        in_specs=[pl.BlockSpec((1, 1, PAD), lambda g: (g, 0, 0))],
        out_specs=pl.BlockSpec((1, ROWS, 2), lambda g: (g, 0, 0)),
        out_shape=jax.ShapeDtypeStruct((GROUPS, ROWS, 2), f32),
        compiler_params=params(),
        name="neg_weights",
    )(neg_pad.reshape(GROUPS, 1, PAD))


def query_kernel(rel_ref, own_ref, idx_ref, mat_ref, s_ref, q_ref):
    cols = lax.broadcasted_iota(jnp.int32, (CH, BLK), 1)
    acc = jnp.zeros((CH, D), f32)
    for b in range(NBLK):
        hot = jnp.where(cols == idx_ref[...] - b * BLK, 1.0, 0.0).astype(bf16)
        acc = acc + mm(hot, own_ref[b * BLK : (b + 1) * BLK, :])
    rows = acc.astype(bf16)
    s_ref[...] = rows
    q_ref[...] = mm(mat_ref[0], rows, NT).astype(bf16)


def make_queries(own, src_col, rel_id, rel_t):
    return pl.pallas_call(
        query_kernel,
        grid_spec=pltpu.PrefetchScalarGridSpec(
            num_scalar_prefetch=1,
            grid=(NCH,),
            in_specs=[
                pl.BlockSpec((ROWS, D), lambda j, rel: (0, 0)),
                pl.BlockSpec((CH, 1), lambda j, rel: (j, 0)),
                pl.BlockSpec((1, D, D), lambda j, rel: (rel[j // PER], 0, 0)),
            ],
            out_specs=[
                pl.BlockSpec((CH, D), lambda j, rel: (j, 0)),
                pl.BlockSpec((D, CH), lambda j, rel: (0, j)),
            ],
        ),
        out_shape=[
            jax.ShapeDtypeStruct((GROUPS * PAD, D), bf16),
            jax.ShapeDtypeStruct((D, GROUPS * PAD), bf16),
        ],
        compiler_params=params(),
        name="queries",
    )(rel_id, own, src_col, rel_t)


def score_kernel(
    rel_ref, cnt_ref, nxt_ref, nxt_t_ref, q_ref, s_ref, dst_ref, wt_ref,
    gq_ref, dg_ref, rg_ref, sc, w, dacc,
):
    j = pl.program_id(0)
    kind = rel_ref[j // PER]

    @pl.when(j == 0)
    def _():
        dacc[...] = jnp.zeros_like(dacc)
        rg_ref[...] = jnp.zeros_like(rg_ref)

    dst = dst_ref[0]
    rows = lax.broadcasted_iota(jnp.int32, (BLK, CH), 0)
    top = jnp.full((8, CH), -jnp.inf, f32)
    hit = jnp.zeros((8, CH), f32)
    for b in range(NBLK):
        at = slice(b * BLK, (b + 1) * BLK)
        raw = mm(nxt_ref[at, :], q_ref[...])
        mask = rows == dst - b * BLK
        val = raw * LOG2E + jnp.where(mask, wt_ref[0, at, 1:2], wt_ref[0, at, 0:1])
        sc[at, :] = val
        top = jnp.maximum(top, jnp.max(val.reshape(BLK // 8, 8, CH), axis=0))
        hit = hit + jnp.sum(jnp.where(mask, val, 0.0).reshape(BLK // 8, 8, CH), axis=0)
    top = jnp.max(top, axis=0, keepdims=True)
    hit = jnp.sum(hit, axis=0, keepdims=True)
    tot = jnp.zeros((8, CH), f32)
    for b in range(NBLK):
        at = slice(b * BLK, (b + 1) * BLK)
        e = jnp.exp2(sc[at, :] - top)
        tot = tot + jnp.sum(e.reshape(BLK // 8, 8, CH), axis=0)
        w[at, :] = e.astype(bf16)
    tot = jnp.sum(tot, axis=0, keepdims=True)
    gain = (jnp.exp2(hit - top) - tot).astype(bf16)
    lane = lax.broadcasted_iota(jnp.int32, (1, CH), 1) + lax.rem(j, PER) * CH
    slot = (j // PER) * SLOTS + lane
    live = jnp.logical_and(lane < SLOTS, slot < cnt_ref[0])
    scale = jnp.where(live, 1.0 / tot, 0.0)
    for b in range(NBLK):
        at = slice(b * BLK, (b + 1) * BLK)
        mask = rows == dst - b * BLK
        w[at, :] = jnp.where(mask, gain.astype(f32), w[at, :].astype(f32)).astype(bf16)
    gq = (mm(nxt_t_ref[...], w[...]) * scale).astype(bf16)
    gq_ref[...] = gq
    rg_ref[kind] += mm(gq, s_ref[...])
    qs = (q_ref[...].astype(f32) * scale).astype(bf16)
    for b in range(NBLK):
        at = slice(b * BLK, (b + 1) * BLK)
        dacc[at, :] += mm(w[at, :], qs, NT)

    @pl.when(j == NCH - 1)
    def _():
        dg_ref[...] = dacc[...].astype(bf16)


def score_side(nxt, nxt_t, q, s, dst_rows, weights, rel_id, counts, kinds):
    return pl.pallas_call(
        score_kernel,
        grid_spec=pltpu.PrefetchScalarGridSpec(
            num_scalar_prefetch=2,
            grid=(NCH,),
            in_specs=[
                pl.BlockSpec((ROWS, D), lambda j, rel, cnt: (0, 0)),
                pl.BlockSpec((D, ROWS), lambda j, rel, cnt: (0, 0)),
                pl.BlockSpec((D, CH), lambda j, rel, cnt: (0, j)),
                pl.BlockSpec((CH, D), lambda j, rel, cnt: (j, 0)),
                pl.BlockSpec((1, 1, CH), lambda j, rel, cnt: (j, 0, 0)),
                pl.BlockSpec((1, ROWS, 2), lambda j, rel, cnt: (j // PER, 0, 0)),
            ],
            out_specs=[
                pl.BlockSpec((D, CH), lambda j, rel, cnt: (0, j)),
                pl.BlockSpec((ROWS, D), lambda j, rel, cnt: (0, 0)),
                pl.BlockSpec((kinds, D, D), lambda j, rel, cnt: (0, 0, 0)),
            ],
            scratch_shapes=[
                pltpu.VMEM((ROWS, CH), f32),
                pltpu.VMEM((ROWS, CH), bf16),
                pltpu.VMEM((ROWS, D), f32),
            ],
        ),
        out_shape=[
            jax.ShapeDtypeStruct((D, GROUPS * PAD), bf16),
            jax.ShapeDtypeStruct((ROWS, D), bf16),
            jax.ShapeDtypeStruct((kinds, D, D), f32),
        ],
        compiler_params=params(),
        name="scores",
    )(rel_id, counts, nxt, nxt_t, q, s, dst_rows, weights)


def source_kernel(rel_ref, gq_ref, src_ref, mat_ref, out_ref, acc):
    j = pl.program_id(0)

    @pl.when(j == 0)
    def _():
        acc[...] = jnp.zeros_like(acc)

    grad = mm(mat_ref[0], gq_ref[...]).astype(bf16)
    rows = lax.broadcasted_iota(jnp.int32, (BLK, CH), 0)
    for b in range(NBLK):
        at = slice(b * BLK, (b + 1) * BLK)
        hot = jnp.where(rows == src_ref[0] - b * BLK, 1.0, 0.0).astype(bf16)
        acc[at, :] += mm(hot, grad, NT)

    @pl.when(j == NCH - 1)
    def _():
        out_ref[...] = acc[...].astype(bf16)


def source_side(gq, src_rows, rel_id, rel_b):
    return pl.pallas_call(
        source_kernel,
        grid_spec=pltpu.PrefetchScalarGridSpec(
            num_scalar_prefetch=1,
            grid=(NCH,),
            in_specs=[
                pl.BlockSpec((D, CH), lambda j, rel: (0, j)),
                pl.BlockSpec((1, 1, CH), lambda j, rel: (j, 0, 0)),
                pl.BlockSpec((1, D, D), lambda j, rel: (rel[j // PER], 0, 0)),
            ],
            out_specs=pl.BlockSpec((ROWS, D), lambda j, rel: (0, 0)),
            scratch_shapes=[pltpu.VMEM((ROWS, D), f32)],
        ),
        out_shape=jax.ShapeDtypeStruct((ROWS, D), bf16),
        compiler_params=params(),
        name="source_grads",
    )(rel_id, gq, src_rows, rel_b)


def rowwise(param, accum, grad):
    fresh = accum + jnp.mean(grad * grad, -1)
    return (param - learn_rate * grad / jnp.sqrt(fresh)[..., None], fresh)


def shift_dom(block, by):
    size = lax.axis_size("dom")
    return lax.ppermute(block, "dom", [(i, (i + by) % size) for i in range(size)])


def swap_z(block):
    return lax.ppermute(block, "rep", [(i, i ^ 1) for i in range(8)])


def shift_x(block, by):
    return lax.ppermute(block, "rep", [(i, (i + 2 * by) % 8) for i in range(8)])


def gather_part(shard):
    rep = lax.axis_index("rep")
    z, x = rep % 2, rep // 2
    other = swap_z(shard)
    pair = jnp.where(z == 0, jnp.concatenate([shard, other]), jnp.concatenate([other, shard]))
    parts = jnp.stack([pair] + [shift_x(pair, -k) for k in (1, 2, 3)])
    order = (jnp.arange(4) - x) % 4
    return parts[order].reshape(-1, shard.shape[-1])


def reduce_part(grad):
    rep = lax.axis_index("rep")
    z = rep % 2
    pieces = grad.reshape(4, 512, D)
    got = lax.all_to_all(pieces, "rep", 0, 0, axis_index_groups=[[0, 2, 4, 6], [1, 3, 5, 7]])
    total = jnp.sum(got.astype(f32), 0).reshape(2, 256, D)
    mine = lax.dynamic_index_in_dim(total, z, 0, False)
    give = lax.dynamic_index_in_dim(total, 1 - z, 0, False)
    return mine + swap_z(give.astype(bf16)).astype(f32)


def reduce_relation(rel_t):
    kinds = rel_t.shape[0]
    part = rel_t.transpose(0, 2, 1).reshape(32, -1, D).astype(bf16)
    got = lax.all_to_all(part, "dom", 0, 0)
    mine = jnp.sum(got.astype(f32), 0)
    every = lax.all_to_all(jnp.broadcast_to(mine, (8,) + mine.shape), "rep", 0, 0)
    total = jnp.sum(every, 0)
    full = lax.all_to_all(jnp.broadcast_to(total, (32,) + total.shape), "dom", 0, 0)
    return full.reshape(kinds, D, D)


def pad_slots(index, fill):
    return jnp.pad(index.reshape(GROUPS, SLOTS), ((0, 0), (0, PAD - SLOTS)), constant_values=fill)


def on_device(
    entity, entity_accum, relation, relation_accum, src_index, dst_index, neg_index, rel_id, counts
):
    ent_b = entity.astype(bf16)
    rel_b = relation.astype(bf16)
    rel_t = rel_b.transpose(0, 2, 1)
    shifted = shift_dom(ent_b, -1)
    own = gather_part(ent_b)
    nxt = gather_part(shifted)
    src_pad = pad_slots(src_index, -1)
    dst_pad = pad_slots(dst_index, -1)
    weights = neg_weights(pad_slots(neg_index, -1))
    s, q = make_queries(own, src_pad.reshape(-1, 1), rel_id, rel_t)
    gq, dst_grad, rel_grad = score_side(
        nxt, nxt.T, q, s, dst_pad.reshape(NCH, 1, CH), weights, rel_id, counts, relation.shape[0]
    )
    moved = shift_dom(dst_grad, 1)
    src_grad = source_side(gq, src_pad.reshape(NCH, 1, CH), rel_id, rel_b)
    both = (src_grad.astype(f32) + moved.astype(f32)).astype(bf16)
    grads = reduce_part(both)
    rel_total = reduce_relation(rel_grad)
    entity_new, entity_accum_new = rowwise(entity, entity_accum, grads)
    relation_new, relation_accum_new = rowwise(relation, relation_accum, rel_total)
    return (entity_new, entity_accum_new, relation_new, relation_accum_new)


def solution(mesh):
    placed = (
        P(("dom", "rep"), None),
        P(("dom", "rep")),
        P(),
        P(),
        P(("dom", "rep")),
        P(("dom", "rep")),
        P(("dom", "rep"), None),
        P(("dom", "rep")),
        P(("dom", "rep")),
    )
    return jax.shard_map(
        on_device,
        mesh=mesh,
        in_specs=placed,
        out_specs=(P(("dom", "rep"), None), P(("dom", "rep")), P(), P()),
        check_vma=False,
    )
```

time: 676 us -> 221 us (0.33)
  waiting for transfers between devices: 464 us -> 63 us
  other arithmetic: 98.5 us -> 14.8 us
  starting transfers between devices: 6.84 us -> 66.3 us
  Pallas kernels: 0 us -> 58.9 us
  matrix products: 40.8 us -> 0 us
  local copies, waits for them, and re-layouts: 50.8 us -> 15.2 us
  between operations: 14.7 us -> 1.65 us
    psum x1 -> x0, waiting for transfers between devices: 192 us -> none  [on_device(): rel_total = lax.psum(rel_grad, ('dom', 'rep'))]
    reduce_scatter x2 -> x0, waiting for transfers between devices: 169 us -> none  [the longest x1 88 us: on_device(): lax.psum_scatter(dst_grad.astype(jnp.bfloat16), 'rep', scatter_dimension=...]
    all_gather x2 -> x0, waiting for transfers between devices: 102 us -> none  [the longest x1 55.9 us: on_device(): lax.all_gather(ent_b, 'rep', axis=0, tiled=True)]
    scatter-add x4 -> x0, other arithmetic: 68.9 us -> none  [the longest x1 23.6 us: score_side(): dst_grad.at[neg_index.reshape(-1)].add(grad_neg.reshape(-1, width))]
    pallas_call x0 -> x4, Pallas kernels: none -> 58.9 us  [the longest x1 34.3 us: score_side(): pl.pallas_call(score_kernel, grid_spec=pltpu.PrefetchScalarGridSpec(num_s...]
    gather x4 -> x2, local copies, waits for them, and re-layouts: 48.2 us -> 1.23 us  [gather_part(): return parts[order].reshape(-1, shard.shape[-1])]
    all_to_all x0 -> x4, starting transfers between devices: none -> 42.3 us  [the longest x1 22.9 us: reduce_relation(): lax.all_to_all(jnp.broadcast_to(total, (32,) + total.shape), 'dom', 0, 0)]
    dot_general x6 -> x0, matrix products: 40.8 us -> none  [the longest x1 10.3 us: score_side(): jnp.einsum('cnd,cmd->cnm', queries, negatives, preferred_element_type=jnp...]
  transfers between devices with their start and end apart: 7 -> 15, of which waited for: 6 -> 8; matrix products, arithmetic and copies ran while one was open for 12% -> 6% of each run, Pallas kernels for 0% -> 11%
where the time goes in v1:
time: 221 us; the launch traced here: 220 us
  starting transfers between devices  66.3 us (30%)
  waiting for transfers between devices  63 us (29%)
  Pallas kernels  58.9 us (27%)
  local copies, waits for them, and re-layouts  15.2 us (7%)
  other arithmetic  14.8 us (7%)
    pallas_call x1, Pallas kernels, score_side(): pl.pallas_call(score_kernel, grid_spec=pltpu.PrefetchScalarGridSpec(num_s...  34.3 us
    ppermute x3, waiting for transfers between devices, swap_z(): return lax.ppermute(block, 'rep', [(i, i ^ 1) for i in range(8)])  23.5 us
    all_to_all x1, starting transfers between devices, reduce_relation(): lax.all_to_all(jnp.broadcast_to(total, (32,) + total.shape), 'dom', 0, 0)  22.9 us
    ppermute x3, starting transfers between devices, swap_z(): return lax.ppermute(block, 'rep', [(i, i ^ 1) for i in range(8)])  13.7 us
    all_to_all x1, starting transfers between devices, reduce_relation(): got = lax.all_to_all(part, 'dom', 0, 0)  11.7 us
    all_to_all x1, waiting for transfers between devices, reduce_part(): lax.all_to_all(pieces, 'rep', 0, 0, axis_index_groups=[[0, 2, 4, 6], [1,...  10.7 us
    pallas_call x1, Pallas kernels, make_queries(): pl.pallas_call(query_kernel, grid_spec=pltpu.PrefetchScalarGridSpec(num_s...  10.1 us
    ppermute x6, waiting for transfers between devices, shift_x(): return lax.ppermute(block, 'rep', [(i, (i + 2 * by) % 8) for i in range(8)])  10.1 us
  transfers between devices with their start and end apart: 15, of which 8 were waited for; matrix products, arithmetic and copies ran while one was open for 6% of the time, Pallas kernels for 11%

profile of v1, /device:TPU:1, one launch (start us, length us, event | category | flops | bytes accessed | tf_op | source)
XLA Modules:
  0.0 219.9 jit_solution(17889893590552861826)
XLA Ops:
  0.7 1.0 convert_element_type.39
  1.7 7.8 %collective-permute-start.5 = (bf16[256,256]{1,0:T(8,128)(2,1)S(1)}, bf16[256,256]{1,0:T(8,128)(2,1)S(1)}, u32[]{:S(2)}, u32[]{:S(2)}) collective-permute-start(bf16[256,256]{1,0:T(8,128)(2,1)S(1)} %convert_element_type.39), channel_id=1, source_target_pairs={{0,1},{1,0},{2,3},{3,2},{4,5},{5,4},{6,7},{7,6},{8,9},{9,8},{10,11... | collective-permute-start | bytes 393224 | tf_op jit(solution)/shard_map/ppermute | solution.py:241
  9.5 1.0 collective-permute-start
  10.5 1.3 convert_bitcast_fusion.1
  12.3 3.1 %collective-permute-start.6 = (bf16[512,256]{1,0:T(8,128)(2,1)S(1)}, bf16[512,256]{1,0:T(8,128)(2,1)S(1)}, u32[]{:S(2)}, u32[]{:S(2)}) collective-permute-start(bf16[512,256]{1,0:T(8,128)(2,1)S(1)} %maximum_select_fusion.3), channel_id=1, source_target_pairs={{0,6},{1,7},{2,0},{3,1},{4,2},{5,3},{6,4},{7,5},{8,14},{9,15},{10,... | collective-permute-start | bytes 786440 | tf_op jit(solution)/shard_map/ppermute | solution.py:245
  15.4 5.0 %collective-permute-start.1 = (bf16[256,256]{1,0:T(8,128)(2,1)S(1)}, bf16[256,256]{1,0:T(8,128)(2,1)S(1)}, u32[]{:S(2)}, u32[]{:S(2)}) collective-permute-start(bf16[256,256]{1,0:T(8,128)(2,1)S(1)} %collective-permute-done), channel_id=1, source_target_pairs={{0,1},{1,0},{2,3},{3,2},{4,5},{5,4},{6,7},{7,6},{8,9},{9,8},{10,11... | collective-permute-start | bytes 393224 | tf_op jit(solution)/shard_map/ppermute | solution.py:241
  20.5 2.0 copy.28
  22.7 6.0 %neg_weights.1.wt_ref = f32[4,2048,2]{2,1,0:T(8,128)S(1)} custom-call(s32[4,1,1024]{2,1,0:T(1,128)S(1)} %reshape.214.neg_ref), custom_call_target="tpu_custom_call" | custom-call | tf_op jit(solution)/shard_map/neg_weights/pallas_call | solution.py:54
  28.8 1.9 copy-done
  31.5 0.6 collective-permute-start.7
  32.1 0.6 collective-permute-start.8
  32.7 0.8 maximum_select_fusion.1
  33.5 2.1 collective-permute-start.2
  35.6 1.2 collective-permute-start.3
  37.1 1.3 collective-permute-done.7
  38.4 8.8 %collective-permute-done.8 = bf16[512,256]{1,0:T(8,128)(2,1)S(1)} collective-permute-done((bf16[512,256]{1,0:T(8,128)(2,1)S(1)}, bf16[512,256]{1,0:T(8,128)(2,1)S(1)}, u32[]{:S(2)}, u32[]{:S(2)}) %collective-permute-start.8) | collective-permute-done | bytes 262176 | tf_op jit(solution)/shard_map/ppermute | solution.py:245
  47.2 1.1 pad_maximum_fusion.1
  48.3 0.6 gather_fusion.1
  48.9 10.1 %queries.1 = (bf16[4096,256]{1,0:T(8,128)(2,1)S(1)}, bf16[256,4096]{1,0:T(8,128)(2,1)S(1)}) custom-call(s32[4]{0:T(128)S(1)} %copy-done.5, bf16[2048,256]{1,0:T(8,128)(2,1)S(1)} %bitcast.43, s32[4096,1]{1,0:T(8,128)} %bitcast.45, bf16[4,256,256]{2,1,0:T(8,128)(2,1)S(1)} %copy.23.mat_ref), custom_call_target="tpu_custom_call" | custom-call | tf_op jit(solution)/shard_map/queries/pallas_call | solution.py:77
  59.1 1.4 copy-done.3
  60.5 1.4 copy-done.4
  61.9 1.2 pad_maximum_fusion
  63.1 0.6 gather_fusion
  63.8 0.6 copy.26
  64.4 34.3 %scores.1 = (bf16[256,4096]{1,0:T(8,128)(2,1)}, bf16[2048,256]{1,0:T(8,128)(2,1)S(1)}, f32[4,256,256]{2,1,0:T(8,128)S(1)}) custom-call(s32[4]{0:T(128)S(1)} %copy-done.5, s32[1]{0:T(128)S(6)} %copy.29.cnt_ref, bf16[2048,256]{1,0:T(8,128)(2,1)S(1)} %bitcast.42, bf16[256,2048]{1,0:T(8,128)(2,1)S(1)} %bitcast.44, bf16[256,4096]{1,0:T(8,128)(2,1)} %copy-done.4, ...), custom_call_target="tpu_custom_call" | custom-call | tf_op jit(solution)/shard_map/scores/pallas_call | solution.py:157
  98.7 1.0 copy-done.6
  99.7 0.9 convert_bitcast_fusion
  100.5 2.2 copy.25
  102.7 11.7 %all-to-all-start.1 = ((bf16[32,32,256]{2,1,0:T(8,128)(2,1)}), bf16[32,32,256]{2,1,0:T(8,128)(2,1)}, u32[]{:S(2)}, u32[]{:S(2)}) async-start(bf16[32,32,256]{2,1,0:T(8,128)(2,1)} %bitcast.50), calls=%async_computation.1 | async-start | bytes 1048576 | tf_op jit(solution)/shard_map/all_to_all | solution.py:272
  114.4 1.7 collective-permute-start.9
  116.1 0.9 convert_element_type.40.mat_ref
  117.0 1.0 copy-done.2
  118.1 8.5 %source_grads.1 = bf16[2048,256]{1,0:T(8,128)(2,1)S(1)} custom-call(s32[4]{0:T(128)S(1)} %copy-done.5, bf16[256,4096]{1,0:T(8,128)(2,1)S(1)} %copy-done.1, s32[8,1,512]{2,1,0:T(1,128)S(1)} %reshape.215.src_ref, bf16[4,256,256]{2,1,0:T(8,128)(2,1)S(1)} %copy-done.2), custom_call_target="tpu_custom_call" | custom-call | tf_op jit(solution)/shard_map/source_grads/pallas_call | solution.py:211
  126.5 4.6 %all-to-all-done.1 = bf16[32,32,256]{2,1,0:T(8,128)(2,1)} async-done(((bf16[32,32,256]{2,1,0:T(8,128)(2,1)}), bf16[32,32,256]{2,1,0:T(8,128)(2,1)}, u32[]{:S(2)}, u32[]{:S(2)}) %all-to-all-start.1) | async-done | bytes 524320 | tf_op jit(solution)/shard_map/all_to_all | solution.py:272
  131.1 1.1 convert_reduce_fusion.1
  132.3 0.7 broadcast_in_dim.4
  133.0 4.3 %all-to-all-start.2 = ((f32[8,32,256]{2,1,0:T(8,128)}), f32[8,32,256]{2,1,0:T(8,128)S(1)}, u32[]{:S(2)}, u32[]{:S(2)}) async-start(f32[8,32,256]{2,1,0:T(8,128)} %broadcast_in_dim.4), calls=%async_computation.2 | async-start | bytes 524288 | tf_op jit(solution)/shard_map/all_to_all | solution.py:274
  137.3 2.5 %add_convert_fusion = bf16[2048,256]{1,0:T(8,128)(2,1)} fusion(bf16[2048,256]{1,0:T(8,128)(2,1)} %collective-permute-done.9, bf16[2048,256]{1,0:T(8,128)(2,1)S(1)} %source_grads.1), kind=kLoop, calls=%fused_computation.3 | loop fusion | flops 2097152 | bytes 3145728 | tf_op jit(solution)/shard_map/convert_element_type | solution.py:302
  139.8 7.6 %all-to-all-done.2 = f32[8,32,256]{2,1,0:T(8,128)S(1)} async-done(((f32[8,32,256]{2,1,0:T(8,128)}), f32[8,32,256]{2,1,0:T(8,128)S(1)}, u32[]{:S(2)}, u32[]{:S(2)}) %all-to-all-start.2) | async-done | bytes 262176 | tf_op jit(solution)/shard_map/all_to_all | solution.py:274
  147.4 3.5 %all-to-all-start = ((bf16[4,512,256]{2,1,0:T(8,128)(2,1)}), bf16[4,512,256]{2,1,0:T(8,128)(2,1)S(1)}, u32[]{:S(2)}, u32[]{:S(2)}) async-start(bf16[4,512,256]{2,1,0:T(8,128)(2,1)} %bitcast.15), calls=%async_computation | async-start | bytes 2097152 | tf_op jit(solution)/shard_map/all_to_all | solution.py:262
  150.9 10.7 %all-to-all-done = bf16[4,512,256]{2,1,0:T(8,128)(2,1)S(1)} async-done(((bf16[4,512,256]{2,1,0:T(8,128)(2,1)}), bf16[4,512,256]{2,1,0:T(8,128)(2,1)S(1)}, u32[]{:S(2)}, u32[]{:S(2)}) %all-to-all-start) | async-done | bytes 1048608 | tf_op jit(solution)/shard_map/all_to_all | solution.py:262
  161.6 1.1 broadcast_in_dim.5
  162.7 22.9 %all-to-all-start.3 = ((f32[32,32,256]{2,1,0:T(8,128)}), f32[32,32,256]{2,1,0:T(8,128)S(1)}, u32[]{:S(2)}, u32[]{:S(2)}) async-start(f32[32,32,256]{2,1,0:T(8,128)} %broadcast_in_dim.5), calls=%async_computation.3 | async-start | bytes 2097152 | tf_op jit(solution)/shard_map/all_to_all | solution.py:276
  185.8 0.8 collective-permute-start.10
  186.6 23.3 %collective-permute-done.10 = bf16[256,256]{1,0:T(8,128)(2,1)S(1)} collective-permute-done((bf16[256,256]{1,0:T(8,128)(2,1)S(1)}, bf16[256,256]{1,0:T(8,128)(2,1)S(1)}, u32[]{:S(2)}, u32[]{:S(2)}) %collective-permute-start.10) | collective-permute-done | bytes 131104 | tf_op jit(solution)/shard_map/ppermute | solution.py:241
  210.6 0.8 divide_subtract_fusion
  211.4 6.4 %all-to-all-done.3 = f32[32,32,256]{2,1,0:T(8,128)S(1)} async-done(((f32[32,32,256]{2,1,0:T(8,128)}), f32[32,32,256]{2,1,0:T(8,128)S(1)}, u32[]{:S(2)}, u32[]{:S(2)}) %all-to-all-start.3) | async-done | bytes 1048608 | tf_op jit(solution)/shard_map/all_to_all | solution.py:276
  218.7 1.2 fusion
  (61 shorter events, 3.0 us)
Async XLA Ops:
  0.6 11.1 %copy-start.9 = (f32[256,256]{1,0:T(8,128)S(1)}, f32[256,256]{1,0:T(8,128)}, u32[]{:S(2)}) copy-start(f32[256,256]{1,0:T(8,128)} %param.9) | copy-start | bytes 786436
  0.6 11.1 %copy-start.11 = (s32[4000]{0:T(1024)S(1)}, s32[4000]{0:T(1024)}, u32[]{:S(2)}) copy-start(s32[4000]{0:T(1024)} %param.13) | copy-start | bytes 48004
  1.7 10.5 %collective-permute-start.5 = (bf16[256,256]{1,0:T(8,128)(2,1)S(1)}, bf16[256,256]{1,0:T(8,128)(2,1)S(1)}, u32[]{:S(2)}, u32[]{:S(2)}) collective-permute-start(bf16[256,256]{1,0:T(8,128)(2,1)S(1)} %convert_element_type.39), channel_id=1, source_target_pairs={{0,1},{1,0},{2,3},{3,2},{4,5},{5,4},{6,7},{7,6},{8,9},{9,8},{10,11... | collective-permute-start | bytes 393224 | tf_op jit(solution)/shard_map/ppermute | solution.py:241
  9.5 5.9 %collective-permute-start = (bf16[256,256]{1,0:T(8,128)(2,1)S(1)}, bf16[256,256]{1,0:T(8,128)(2,1)S(1)}, u32[]{:S(2)}, u32[]{:S(2)}) collective-permute-start(bf16[256,256]{1,0:T(8,128)(2,1)S(1)} %convert_element_type.39), channel_id=1, source_target_pairs={{0,248},{8,0},{16,8},{24,16},{32,24},{40,32},{48,40},{56,48},{64,5... | collective-permute-start | bytes 393224 | tf_op jit(solution)/shard_map/ppermute | solution.py:237
  11.7 10.9 %copy-start.12 = (s32[4,1000]{1,0:T(4,128)S(1)}, s32[4,1000]{1,0:T(4,128)}, u32[]{:S(2)}) copy-start(s32[4,1000]{1,0:T(4,128)} %param.15) | copy-start | bytes 48004
  12.3 24.6 %collective-permute-start.6 = (bf16[512,256]{1,0:T(8,128)(2,1)S(1)}, bf16[512,256]{1,0:T(8,128)(2,1)S(1)}, u32[]{:S(2)}, u32[]{:S(2)}) collective-permute-start(bf16[512,256]{1,0:T(8,128)(2,1)S(1)} %maximum_select_fusion.3), channel_id=1, source_target_pairs={{0,6},{1,7},{2,0},{3,1},{4,2},{5,3},{6,4},{7,5},{8,14},{9,15},{10,... | collective-permute-start | bytes 786440 | tf_op jit(solution)/shard_map/ppermute | solution.py:245
  15.4 17.3 %collective-permute-start.1 = (bf16[256,256]{1,0:T(8,128)(2,1)S(1)}, bf16[256,256]{1,0:T(8,128)(2,1)S(1)}, u32[]{:S(2)}, u32[]{:S(2)}) collective-permute-start(bf16[256,256]{1,0:T(8,128)(2,1)S(1)} %collective-permute-done), channel_id=1, source_target_pairs={{0,1},{1,0},{2,3},{3,2},{4,5},{5,4},{6,7},{7,6},{8,9},{9,8},{10,11... | collective-permute-start | bytes 393224 | tf_op jit(solution)/shard_map/ppermute | solution.py:241
  22.7 8.0 %copy-start.13 = (s32[4000]{0:T(1024)S(1)}, s32[4000]{0:T(1024)}, u32[]{:S(2)}) copy-start(s32[4000]{0:T(1024)} %param.14) | copy-start | bytes 48004
  28.8 1.9 copy-start
  31.5 6.9 %collective-permute-start.7 = (bf16[512,256]{1,0:T(8,128)(2,1)S(1)}, bf16[512,256]{1,0:T(8,128)(2,1)S(1)}, u32[]{:S(2)}, u32[]{:S(2)}) collective-permute-start(bf16[512,256]{1,0:T(8,128)(2,1)S(1)} %maximum_select_fusion.3), channel_id=1, source_target_pairs={{0,4},{1,5},{2,6},{3,7},{4,0},{5,1},{6,2},{7,3},{8,12},{9,13},{10,... | collective-permute-start | bytes 786440 | tf_op jit(solution)/shard_map/ppermute | solution.py:245
  32.1 15.1 %collective-permute-start.8 = (bf16[512,256]{1,0:T(8,128)(2,1)S(1)}, bf16[512,256]{1,0:T(8,128)(2,1)S(1)}, u32[]{:S(2)}, u32[]{:S(2)}) collective-permute-start(bf16[512,256]{1,0:T(8,128)(2,1)S(1)} %maximum_select_fusion.3), channel_id=1, source_target_pairs={{0,2},{1,3},{2,4},{3,5},{4,6},{5,7},{6,0},{7,1},{8,10},{9,11},{10,... | collective-permute-start | bytes 786440 | tf_op jit(solution)/shard_map/ppermute | solution.py:245
  33.5 28.4 %collective-permute-start.2 = (bf16[512,256]{1,0:T(8,128)(2,1)}, bf16[512,256]{1,0:T(8,128)(2,1)}, u32[]{:S(2)}, u32[]{:S(2)}) collective-permute-start(bf16[512,256]{1,0:T(8,128)(2,1)} %maximum_select_fusion.1), channel_id=1, source_target_pairs={{0,6},{1,7},{2,0},{3,1},{4,2},{5,3},{6,4},{7,5},{8,14},{9,15},{10,... | collective-permute-start | bytes 786440 | tf_op jit(solution)/shard_map/ppermute | solution.py:245
  35.6 26.3 %collective-permute-start.3 = (bf16[512,256]{1,0:T(8,128)(2,1)}, bf16[512,256]{1,0:T(8,128)(2,1)}, u32[]{:S(2)}, u32[]{:S(2)}) collective-permute-start(bf16[512,256]{1,0:T(8,128)(2,1)} %maximum_select_fusion.1), channel_id=1, source_target_pairs={{0,4},{1,5},{2,6},{3,7},{4,0},{5,1},{6,2},{7,3},{8,12},{9,13},{10,... | collective-permute-start | bytes 786440 | tf_op jit(solution)/shard_map/ppermute | solution.py:245
  36.8 10.4 %copy-start.10 = (bf16[512,256]{1,0:T(8,128)(2,1)}, bf16[512,256]{1,0:T(8,128)(2,1)S(1)}, u32[]{:S(2)}) copy-start(bf16[512,256]{1,0:T(8,128)(2,1)S(1)} %collective-permute-done.6) | copy-start | bytes 786436
  36.8 25.0 %collective-permute-start.4 = (bf16[512,256]{1,0:T(8,128)(2,1)}, bf16[512,256]{1,0:T(8,128)(2,1)}, u32[]{:S(2)}, u32[]{:S(2)}) collective-permute-start(bf16[512,256]{1,0:T(8,128)(2,1)} %maximum_select_fusion.1), channel_id=1, source_target_pairs={{0,2},{1,3},{2,4},{3,5},{4,6},{5,7},{6,0},{7,1},{8,10},{9,11},{10,... | collective-permute-start | bytes 786440 | tf_op jit(solution)/shard_map/ppermute | solution.py:245
  47.2 1.7 copy-start.5
  59.1 1.4 copy-start.3
  60.5 1.4 copy-start.4
  98.7 1.0 copy-start.6
  98.7 17.4 %copy-start.7 = (f32[4,256,256]{2,1,0:T(8,128)S(1)}, f32[4,256,256]{2,1,0:T(8,128)}, u32[]{:S(2)}) copy-start(f32[4,256,256]{2,1,0:T(8,128)} %param.11) | copy-start | bytes 3145732
  100.5 16.5 %copy-start.1 = (bf16[256,4096]{1,0:T(8,128)(2,1)S(1)}, bf16[256,4096]{1,0:T(8,128)(2,1)}, u32[]{:S(2)}) copy-start(bf16[256,4096]{1,0:T(8,128)(2,1)} %get-tuple-element.11.gq_ref) | copy-start | bytes 6291460
  102.7 28.4 %all-to-all-start.1 = ((bf16[32,32,256]{2,1,0:T(8,128)(2,1)}), bf16[32,32,256]{2,1,0:T(8,128)(2,1)}, u32[]{:S(2)}, u32[]{:S(2)}) async-start(bf16[32,32,256]{2,1,0:T(8,128)(2,1)} %bitcast.50), calls=%async_computation.1 | async-start | bytes 1048576 | tf_op jit(solution)/shard_map/all_to_all | solution.py:272
  114.4 22.9 %collective-permute-start.9 = (bf16[2048,256]{1,0:T(8,128)(2,1)}, bf16[2048,256]{1,0:T(8,128)(2,1)}, u32[]{:S(2)}, u32[]{:S(2)}) collective-permute-start(bf16[2048,256]{1,0:T(8,128)(2,1)} %copy-done.6), channel_id=1, source_target_pairs={{0,8},{8,16},{16,24},{24,32},{32,40},{40,48},{48,56},{56,64},{64,7... | collective-permute-start | bytes 3145736 | tf_op jit(solution)/shard_map/ppermute | solution.py:237
  117.0 1.0 copy-start.2
  133.0 14.4 %all-to-all-start.2 = ((f32[8,32,256]{2,1,0:T(8,128)}), f32[8,32,256]{2,1,0:T(8,128)S(1)}, u32[]{:S(2)}, u32[]{:S(2)}) async-start(f32[8,32,256]{2,1,0:T(8,128)} %broadcast_in_dim.4), calls=%async_computation.2 | async-start | bytes 524288 | tf_op jit(solution)/shard_map/all_to_all | solution.py:274
  147.4 14.2 %all-to-all-start = ((bf16[4,512,256]{2,1,0:T(8,128)(2,1)}), bf16[4,512,256]{2,1,0:T(8,128)(2,1)S(1)}, u32[]{:S(2)}, u32[]{:S(2)}) async-start(bf16[4,512,256]{2,1,0:T(8,128)(2,1)} %bitcast.15), calls=%async_computation | async-start | bytes 2097152 | tf_op jit(solution)/shard_map/all_to_all | solution.py:262
  162.7 47.3 %copy-start.15 = (f32[256]{0:T(256)S(1)}, f32[256]{0:T(256)}, u32[]{:S(2)}) copy-start(f32[256]{0:T(256)} %param.10) | copy-start | bytes 3076
  162.7 55.1 %all-to-all-start.3 = ((f32[32,32,256]{2,1,0:T(8,128)}), f32[32,32,256]{2,1,0:T(8,128)S(1)}, u32[]{:S(2)}, u32[]{:S(2)}) async-start(f32[32,32,256]{2,1,0:T(8,128)} %broadcast_in_dim.5), calls=%async_computation.3 | async-start | bytes 2097152 | tf_op jit(solution)/shard_map/all_to_all | solution.py:276
  185.8 32.4 %copy-start.14 = (f32[4,256]{1,0:T(4,128)S(1)}, f32[4,256]{1,0:T(4,128)}, u32[]{:S(2)}) copy-start(f32[4,256]{1,0:T(4,128)} %param.12) | copy-start | bytes 12292
  185.8 33.0 %copy-start.8 = (f32[4,256,256]{2,1,0:T(8,128)S(1)}, f32[4,256,256]{2,1,0:T(8,128)}, u32[]{:S(2)}) copy-start(f32[4,256,256]{2,1,0:T(8,128)} %param.11) | copy-start | bytes 3145732
  185.8 24.0 %collective-permute-start.10 = (bf16[256,256]{1,0:T(8,128)(2,1)S(1)}, bf16[256,256]{1,0:T(8,128)(2,1)S(1)}, u32[]{:S(2)}, u32[]{:S(2)}) collective-permute-start(bf16[256,256]{1,0:T(8,128)(2,1)S(1)} %fusion.1), channel_id=1, source_target_pairs={{0,1},{1,0},{2,3},{3,2},{4,5},{5,4},{6,7},{7,6},{8,9},{9,8},{10,11... | collective-permute-start | bytes 393224 | tf_op jit(solution)/shard_map/ppermute | solution.py:241

commit v2 on v1

v2 whole, which is shorter than its diff:
```python
import functools
import jax
import jax.numpy as jnp
from jax import lax
from jax.experimental import pallas as pl
from jax.experimental.pallas import tpu as pltpu
from jax.sharding import PartitionSpec as P

learn_rate = 0.1
LOG2E = 1.4426950408889634
GROUPS = 4
SLOTS = 1000
PAD = 1024
ROWS = 2048
D = 256
BLK = 256
NBLK = ROWS // BLK
CH = 512
NCH = GROUPS * PAD // CH
PER = PAD // CH
bf16 = jnp.bfloat16
f32 = jnp.float32

NN = (((1,), (0,)), ((), ()))
NT = (((1,), (1,)), ((), ()))
MB = 1024 * 1024


def mm(a, b, dims=NN):
    return lax.dot_general(a, b, dims, preferred_element_type=f32)


def params():
    return pltpu.CompilerParams(
        dimension_semantics=("arbitrary",), vmem_limit_bytes=48 * MB
    )


PARTS = 4
PART = ROWS // PARTS


def block_of(parts, b):
    first = b * BLK % PART
    return parts[b * BLK // PART][first : first + BLK, :]


def count_kernel(neg_ref, after_ref, out_ref):
    rows = lax.broadcasted_iota(jnp.int32, (BLK, PAD), 0)

    def body(b, carry):
        hits = jnp.where(rows == neg_ref[0] - b * BLK, 1.0, 0.0)
        count = jnp.sum(hits, axis=1, keepdims=True)
        at = pl.ds(pl.multiple_of(b * BLK, BLK), BLK)
        out_ref[0, at, 0:1] = jnp.log2(count)
        out_ref[0, at, 1:2] = jnp.log2(count + 1.0)
        return carry

    lax.fori_loop(0, NBLK, body, 0)


def neg_weights(neg_pad, after):
    return pl.pallas_call(
        count_kernel,
        grid=(GROUPS,),
        in_specs=[
            pl.BlockSpec((1, 1, PAD), lambda g: (g, 0, 0)),
            pl.BlockSpec(memory_space=pl.ANY),
        ],
        out_specs=pl.BlockSpec((1, ROWS, 2), lambda g: (g, 0, 0)),
        out_shape=jax.ShapeDtypeStruct((GROUPS, ROWS, 2), f32),
        compiler_params=params(),
        name="neg_weights",
    )(neg_pad.reshape(GROUPS, 1, PAD), after)


def one_hot(rows, index, first):
    return jnp.where(rows == (index - first).astype(jnp.int16), bf16(1), bf16(0))


def query_kernel(rel_ref, *refs):
    own = refs[:PARTS]
    idx_ref, mat_ref, s_ref, q_ref = refs[PARTS:]
    column = jnp.broadcast_to(idx_ref[0].astype(f32), (128, CH)).T
    column = column.astype(jnp.int32).astype(jnp.int16)
    cols = lax.broadcasted_iota(jnp.int32, (CH, 128), 1).astype(jnp.int16)
    acc = None
    for b in range(NBLK):
        hot = jnp.concatenate(
            [
                jnp.where(cols + jnp.int16(first) == column, bf16(1), bf16(0))
                for first in (b * BLK, b * BLK + 128)
            ],
            axis=1,
        )
        part = mm(hot, block_of(own, b))
        acc = part if acc is None else acc + part
    rows = acc.astype(bf16)
    s_ref[...] = rows
    q_ref[...] = mm(mat_ref[0], rows, NT).astype(bf16)


def make_queries(own, src_rows, rel_id, rel_t):
    return pl.pallas_call(
        query_kernel,
        grid_spec=pltpu.PrefetchScalarGridSpec(
            num_scalar_prefetch=1,
            grid=(NCH,),
            in_specs=[
                *[pl.BlockSpec((PART, D), lambda j, rel: (0, 0))] * PARTS,
                pl.BlockSpec((1, 1, CH), lambda j, rel: (j, 0, 0)),
                pl.BlockSpec((1, D, D), lambda j, rel: (rel[j // PER], 0, 0)),
            ],
            out_specs=[
                pl.BlockSpec((CH, D), lambda j, rel: (j, 0)),
                pl.BlockSpec((D, CH), lambda j, rel: (0, j)),
            ],
        ),
        out_shape=[
            jax.ShapeDtypeStruct((GROUPS * PAD, D), bf16),
            jax.ShapeDtypeStruct((D, GROUPS * PAD), bf16),
        ],
        compiler_params=params(),
        name="queries",
    )(rel_id, *own, src_rows, rel_t)


SUB = 32


def score_kernel(rel_ref, cnt_ref, *refs):
    nxt = refs[:PARTS]
    q_ref, s_ref, dst_ref, wt_ref, gq_ref = refs[PARTS : PARTS + 5]
    dg = refs[PARTS + 5 : 2 * PARTS + 5]
    rg_ref, sc, nxt_t_ref, w0, w1, qs0, qs1, sl0, sl1, dacc = refs[2 * PARTS + 5 :]
    g = pl.program_id(0)
    rows = lax.broadcasted_iota(jnp.int32, (SUB, CH), 0)
    rows16 = lax.broadcasted_iota(jnp.int32, (BLK, CH), 0).astype(jnp.int16)

    @pl.when(g == 0)
    def _():
        dacc[...] = jnp.zeros_like(dacc)
        rg_ref[...] = jnp.zeros_like(rg_ref)
        w1[...] = jnp.zeros_like(w1)
        for b in range(NBLK):
            nxt_t_ref[:, b * BLK : (b + 1) * BLK] = block_of(nxt, b).T
        qs1[...] = jnp.zeros_like(qs1)
        sl1[...] = jnp.zeros_like(sl1)

    def spread(b, w, qs):
        at = slice(b * BLK, (b + 1) * BLK)
        dacc[at, :] += mm(w[at, :], qs[...], NT)

    def finish(acc, sl, chunk, s_at):
        gq = (acc * sl[0:1, :]).astype(bf16)
        gq_ref[:, pl.ds(pl.multiple_of(chunk * CH, CH), CH)] = gq
        rg_ref[rel_ref[chunk // PER]] += mm(gq, s_ref[pl.ds(pl.multiple_of(s_at, CH), CH), :])

    def stage(half, w, qs, sl, w_old, qs_old, sl_old, chunk_old):
        here = slice(half * CH, (half + 1) * CH)
        q = q_ref[:, here]
        dst = dst_ref[0, 0:1, here]
        top = jnp.full((8, CH), -jnp.inf, f32)
        hit = jnp.zeros((8, CH), f32)
        for b in range(NBLK):
            raw = mm(block_of(nxt, b), q)
            for i in range(BLK // SUB):
                at = slice(b * BLK + i * SUB, b * BLK + (i + 1) * SUB)
                mask = rows == dst - (b * BLK + i * SUB)
                val = raw[i * SUB : (i + 1) * SUB] * LOG2E + jnp.where(
                    mask, wt_ref[0, at, 1:2], wt_ref[0, at, 0:1]
                )
                sc[at, :] = val
                top = jnp.maximum(top, jnp.max(val.reshape(SUB // 8, 8, CH), axis=0))
                hit = hit + jnp.sum(jnp.where(mask, val, 0.0).reshape(SUB // 8, 8, CH), axis=0)
            spread(b, w_old, qs_old)
        top = jnp.max(top, axis=0, keepdims=True)
        hit = jnp.sum(hit, axis=0, keepdims=True)
        tot = jnp.zeros((8, CH), f32)
        acc = None
        for b in range(NBLK):
            for i in range(BLK // SUB):
                at = slice(b * BLK + i * SUB, b * BLK + (i + 1) * SUB)
                e = jnp.exp2(sc[at, :] - top)
                tot = tot + jnp.sum(e.reshape(SUB // 8, 8, CH), axis=0)
                w[at, :] = e.astype(bf16)
            at = slice(b * BLK, (b + 1) * BLK)
            part = mm(nxt_t_ref[:, at], w_old[at, :])
            acc = part if acc is None else acc + part
        finish(acc, sl_old, chunk_old, chunk_old * CH)
        tot = jnp.sum(tot, axis=0, keepdims=True)
        gain = (jnp.exp2(hit - top) - tot).astype(bf16)
        lane = lax.broadcasted_iota(jnp.int32, (1, CH), 1) + half * CH
        live = jnp.logical_and(lane < SLOTS, g * SLOTS + lane < cnt_ref[0])
        scale = jnp.where(live, 1.0 / tot, 0.0)
        sl[...] = jnp.broadcast_to(scale, (8, CH))
        qs[...] = (q.astype(f32) * scale).astype(bf16)
        for b in range(NBLK):
            at = slice(b * BLK, (b + 1) * BLK)
            mask = rows16 == (dst - b * BLK).astype(jnp.int16)
            w[at, :] = jnp.where(mask, gain, w[at, :])

    stage(0, w0, qs0, sl0, w1, qs1, sl1, jnp.maximum(2 * g - 1, 0))
    stage(1, w1, qs1, sl1, w0, qs0, sl0, 2 * g)

    @pl.when(g == GROUPS - 1)
    def _():
        for b in range(NBLK):
            spread(b, w1, qs1)
        finish(mm(nxt_t_ref[...], w1[...]), sl1, 2 * g + 1, (2 * g + 1) * CH)
        for p in range(PARTS):
            dg[p][...] = dacc[p * PART : (p + 1) * PART, :].astype(bf16)


def score_side(nxt, q, s, dst_rows, weights, rel_id, counts, kinds):
    return pl.pallas_call(
        score_kernel,
        grid_spec=pltpu.PrefetchScalarGridSpec(
            num_scalar_prefetch=2,
            grid=(GROUPS,),
            in_specs=[
                *[pl.BlockSpec((PART, D), lambda j, rel, cnt: (0, 0))] * PARTS,
                pl.BlockSpec((D, PAD), lambda j, rel, cnt: (0, j)),
                pl.BlockSpec((GROUPS * PAD, D), lambda j, rel, cnt: (0, 0)),
                pl.BlockSpec((1, 1, PAD), lambda j, rel, cnt: (j, 0, 0)),
                pl.BlockSpec((1, ROWS, 2), lambda j, rel, cnt: (j, 0, 0)),
            ],
            out_specs=[
                pl.BlockSpec((D, GROUPS * PAD), lambda j, rel, cnt: (0, 0)),
                *[pl.BlockSpec((PART, D), lambda j, rel, cnt: (0, 0))] * PARTS,
                pl.BlockSpec((kinds, D, D), lambda j, rel, cnt: (0, 0, 0)),
            ],
            scratch_shapes=[
                pltpu.VMEM((ROWS, CH), f32),
                pltpu.VMEM((D, ROWS), bf16),
                pltpu.VMEM((ROWS, CH), bf16),
                pltpu.VMEM((ROWS, CH), bf16),
                pltpu.VMEM((D, CH), bf16),
                pltpu.VMEM((D, CH), bf16),
                pltpu.VMEM((8, CH), f32),
                pltpu.VMEM((8, CH), f32),
                pltpu.VMEM((ROWS, D), f32),
            ],
        ),
        out_shape=[
            jax.ShapeDtypeStruct((D, GROUPS * PAD), bf16),
            *[jax.ShapeDtypeStruct((PART, D), bf16)] * PARTS,
            jax.ShapeDtypeStruct((kinds, D, D), f32),
        ],
        compiler_params=params(),
        name="scores",
    )(rel_id, counts, *nxt, q, s, dst_rows, weights)


def source_kernel(rel_ref, gq_ref, src_ref, mat_ref, *refs):
    out, acc = refs[:PARTS], refs[PARTS]
    g = pl.program_id(0)

    @pl.when(g == 0)
    def _():
        acc[...] = jnp.zeros_like(acc)

    grad = mm(mat_ref[0], gq_ref[...]).astype(bf16)
    rows = lax.broadcasted_iota(jnp.int32, (BLK, PAD), 0).astype(jnp.int16)
    for b in range(NBLK):
        at = slice(b * BLK, (b + 1) * BLK)
        acc[at, :] += mm(one_hot(rows, src_ref[0], b * BLK), grad, NT)

    @pl.when(g == GROUPS - 1)
    def _():
        for p in range(PARTS):
            out[p][...] = acc[p * PART : (p + 1) * PART, :].astype(bf16)


def source_side(gq, src_rows, rel_id, rel_b):
    return pl.pallas_call(
        source_kernel,
        grid_spec=pltpu.PrefetchScalarGridSpec(
            num_scalar_prefetch=1,
            grid=(GROUPS,),
            in_specs=[
                pl.BlockSpec((D, PAD), lambda j, rel: (0, j)),
                pl.BlockSpec((1, 1, PAD), lambda j, rel: (j, 0, 0)),
                pl.BlockSpec((1, D, D), lambda j, rel: (rel[j], 0, 0)),
            ],
            out_specs=[pl.BlockSpec((PART, D), lambda j, rel: (0, 0))] * PARTS,
            scratch_shapes=[pltpu.VMEM((ROWS, D), f32)],
        ),
        out_shape=[jax.ShapeDtypeStruct((PART, D), bf16)] * PARTS,
        compiler_params=params(),
        name="source_grads",
    )(rel_id, gq, src_rows, rel_b)


def rowwise(param, accum, grad):
    fresh = accum + jnp.mean(grad * grad, -1)
    return (param - learn_rate * grad / jnp.sqrt(fresh)[..., None], fresh)


def shift_dom(block, by):
    size = lax.axis_size("dom")
    return lax.ppermute(block, "dom", [(i, (i + by) % size) for i in range(size)])


def swap_z(block):
    return lax.ppermute(block, "rep", [(i, i ^ 1) for i in range(8)])


def shift_x(block, by):
    return lax.ppermute(block, "rep", [(i, (i + 2 * by) % 8) for i in range(8)])


def spread_x(pair):
    return [pair] + [shift_x(pair, -k) for k in (1, 2, 3)]


def collect_x(blocks):
    got = [blocks[0]] + [shift_x(blocks[k], k) for k in (1, 2, 3)]
    return sum(block.astype(f32) for block in got)


def turned(index):
    rep = lax.axis_index("rep")
    return ((index - PART * (rep // 2)) % ROWS) ^ (256 * (rep % 2))


def reduce_relation(rel_t):
    kinds = rel_t.shape[0]
    part = rel_t.astype(bf16).transpose(0, 2, 1).reshape(32, -1, D)
    got = lax.all_to_all(part, "dom", 0, 0)
    mine = jnp.sum(got.astype(f32), 0)
    every = lax.all_to_all(jnp.broadcast_to(mine, (8,) + mine.shape), "rep", 0, 0)
    total = jnp.sum(every, 0).astype(bf16)
    full = lax.all_to_all(jnp.broadcast_to(total, (32,) + total.shape), "dom", 0, 0)
    return full.reshape(kinds, D, D).astype(f32)


def pad_slots(index, fill):
    return jnp.pad(index.reshape(GROUPS, SLOTS), ((0, 0), (0, PAD - SLOTS)), constant_values=fill)


def source_stage(own, src_pad, rel_id, rel_t):
    return make_queries(own, src_pad.reshape(NCH, 1, CH), rel_id, rel_t)


def target_stage(nxt, q, s, dst_pad, weights, rel_id, counts, kinds):
    out = score_side(nxt, q, s, dst_pad.reshape(GROUPS, 1, PAD), weights, rel_id, counts, kinds)
    return out[0], out[1 : PARTS + 1], out[PARTS + 1]


def local_grads(own, nxt, relation, src_index, dst_index, neg_index, rel_id, counts):
    own, nxt, rel_b = own.astype(bf16), nxt.astype(bf16), relation.astype(bf16)
    src_pad = pad_slots(src_index, -1)
    weights = neg_weights(pad_slots(neg_index, -1), own)
    own = [own[k * PART : (k + 1) * PART] for k in range(PARTS)]
    nxt = [nxt[k * PART : (k + 1) * PART] for k in range(PARTS)]
    s, q = source_stage(own, src_pad, rel_id, rel_b.transpose(0, 2, 1))
    gq, dst_grad, rel_grad = target_stage(
        nxt, q, s, pad_slots(dst_index, -1), weights, rel_id, counts, relation.shape[0]
    )
    src_grad = source_side(gq, src_pad.reshape(GROUPS, 1, PAD), rel_id, rel_b)
    return jnp.concatenate(src_grad), jnp.concatenate(dst_grad), rel_grad.transpose(0, 2, 1)


def on_device(
    entity, entity_accum, relation, relation_accum, src_index, dst_index, neg_index, rel_id, counts
):
    ent_b = entity.astype(bf16)
    rel_b = relation.astype(bf16)
    src_pad = pad_slots(turned(src_index), -1)
    dst_pad = pad_slots(turned(dst_index), -1)
    neg_pad = pad_slots(turned(neg_index), -1)
    other = swap_z(ent_b)
    shifted = shift_dom(ent_b, -1)
    own = spread_x(jnp.concatenate([ent_b, other]))
    nxt = spread_x(jnp.concatenate([shifted, swap_z(shifted)]))
    weights = neg_weights(neg_pad, other)
    s, q = source_stage(own, src_pad, rel_id, rel_b.transpose(0, 2, 1))
    gq, dst_grad, rel_grad = target_stage(
        nxt, q, s, dst_pad, weights, rel_id, counts, relation.shape[0]
    )
    rel_total = reduce_relation(rel_grad)
    moved = shift_dom(collect_x(dst_grad).astype(bf16), 1)
    src_grad = source_side(gq, src_pad.reshape(GROUPS, 1, PAD), rel_id, rel_b)
    total = collect_x(src_grad) + moved.astype(f32)
    grads = total[:256] + swap_z(total[256:].astype(bf16)).astype(f32)
    entity_new, entity_accum_new = rowwise(entity, entity_accum, grads)
    relation_new, relation_accum_new = rowwise(relation, relation_accum, rel_total)
    return (entity_new, entity_accum_new, relation_new, relation_accum_new)


def solution(mesh):
    placed = (
        P(("dom", "rep"), None),
        P(("dom", "rep")),
        P(),
        P(),
        P(("dom", "rep")),
        P(("dom", "rep")),
        P(("dom", "rep"), None),
        P(("dom", "rep")),
        P(("dom", "rep")),
    )
    return jax.shard_map(
        on_device,
        mesh=mesh,
        in_specs=placed,
        out_specs=(P(("dom", "rep"), None), P(("dom", "rep")), P(), P()),
        check_vma=False,
    )
```

time: 221 us -> 167 us (0.76)
  waiting for transfers between devices: 63 us -> 28.5 us
  starting transfers between devices: 66.3 us -> 60.6 us
  Pallas kernels: 58.9 us -> 53.5 us
  local copies, waits for them, and re-layouts: 15.2 us -> 11.1 us
  other arithmetic: 14.8 us -> 11.6 us
    all_to_all x1, starting transfers between devices: 22.9 us -> 8.3 us  [reduce_relation(): lax.all_to_all(jnp.broadcast_to(total, (32,) + total.shape), 'dom', 0, 0)]
    all_to_all x1 -> x0, waiting for transfers between devices: 10.7 us -> none  [reduce_part(): lax.all_to_all(pieces, 'rep', 0, 0, axis_index_groups=[[0, 2, 4, 6], [1,...]
    ppermute x3, waiting for transfers between devices: 23.5 us -> 13.1 us  [swap_z(): return lax.ppermute(block, 'rep', [(i, i ^ 1) for i in range(8)])]
    ppermute x6 -> x12, waiting for transfers between devices: 10.1 us -> 1.84 us  [shift_x(): return lax.ppermute(block, 'rep', [(i, (i + 2 * by) % 8) for i in range(8)])]
    ppermute x6 -> x12, starting transfers between devices: 7.62 us -> 15.9 us  [shift_x(): return lax.ppermute(block, 'rep', [(i, (i + 2 * by) % 8) for i in range(8)])]
    all_to_all x1, waiting for transfers between devices: 4.61 us -> 0.62 us  [reduce_relation(): got = lax.all_to_all(part, 'dom', 0, 0)]
    all_to_all x1, starting transfers between devices: 4.25 us -> 8.15 us  [reduce_relation(): lax.all_to_all(jnp.broadcast_to(mine, (8,) + mine.shape), 'rep', 0, 0)]
    all_to_all x1 -> x0, starting transfers between devices: 3.52 us -> none  [reduce_part(): lax.all_to_all(pieces, 'rep', 0, 0, axis_index_groups=[[0, 2, 4, 6], [1,...]
  transfers between devices with their start and end apart: 15 -> 20, of which waited for: 8 -> 7; matrix products, arithmetic and copies ran while one was open for 6% -> 6% of each run, Pallas kernels for 11% -> 14%
where the time goes in v2:
time: 167 us
  starting transfers between devices  60.6 us (36%)
  Pallas kernels  53.5 us (32%)
  waiting for transfers between devices  28.5 us (17%)
  other arithmetic  11.6 us (7%)
  local copies, waits for them, and re-layouts  11.1 us (7%)
    pallas_call x1, Pallas kernels, score_side(): pl.pallas_call(score_kernel, grid_spec=pltpu.PrefetchScalarGridSpec(num_s...  30.9 us
    ppermute x12, starting transfers between devices, shift_x(): return lax.ppermute(block, 'rep', [(i, (i + 2 * by) % 8) for i in range(8)])  15.9 us
    ppermute x3, starting transfers between devices, swap_z(): return lax.ppermute(block, 'rep', [(i, i ^ 1) for i in range(8)])  13.8 us
    ppermute x3, waiting for transfers between devices, swap_z(): return lax.ppermute(block, 'rep', [(i, i ^ 1) for i in range(8)])  13.1 us
    all_to_all x1, starting transfers between devices, reduce_relation(): got = lax.all_to_all(part, 'dom', 0, 0)  11.7 us
    pallas_call x1, Pallas kernels, make_queries(): pl.pallas_call(query_kernel, grid_spec=pltpu.PrefetchScalarGridSpec(num_s...  8.85 us
    all_to_all x1, starting transfers between devices, reduce_relation(): lax.all_to_all(jnp.broadcast_to(total, (32,) + total.shape), 'dom', 0, 0)  8.3 us
    all_to_all x1, starting transfers between devices, reduce_relation(): lax.all_to_all(jnp.broadcast_to(mine, (8,) + mine.shape), 'rep', 0, 0)  8.15 us
  transfers between devices with their start and end apart: 20, of which 7 were waited for; matrix products, arithmetic and copies ran while one was open for 6% of the time, Pallas kernels for 14%

profile of v2, /device:TPU:1, one launch (start us, length us, event | category | flops | bytes accessed | tf_op | source)
XLA Modules:
  0.0 166.9 jit_solution(17333486567092672012)
XLA Ops:
  0.7 1.0 convert_element_type.54
  1.6 7.8 %collective-permute-start.5 = (bf16[256,256]{1,0:T(8,128)(2,1)S(1)}, bf16[256,256]{1,0:T(8,128)(2,1)S(1)}, u32[]{:S(2)}, u32[]{:S(2)}) collective-permute-start(bf16[256,256]{1,0:T(8,128)(2,1)S(1)} %convert_element_type.54), channel_id=1, source_target_pairs={{0,1},{1,0},{2,3},{3,2},{4,5},{5,4},{6,7},{7,6},{8,9},{9,8},{10,11... | collective-permute-start | bytes 393224 | tf_op jit(solution)/shard_map/ppermute | solution.py:306
  9.5 1.0 collective-permute-start
  10.4 1.7 %collective-permute-done.5.after_ref = bf16[256,256]{1,0:T(8,128)(2,1)S(1)} collective-permute-done((bf16[256,256]{1,0:T(8,128)(2,1)S(1)}, bf16[256,256]{1,0:T(8,128)(2,1)S(1)}, u32[]{:S(2)}, u32[]{:S(2)}) %collective-permute-start.5) | collective-permute-done | bytes 131104 | tf_op jit(solution)/shard_map/ppermute | solution.py:306
  12.2 3.1 %collective-permute-start.6 = (bf16[512,256]{1,0:T(8,128)(2,1)S(1)}, bf16[512,256]{1,0:T(8,128)(2,1)S(1)}, u32[]{:S(2)}, u32[]{:S(2)}) collective-permute-start(bf16[512,256]{1,0:T(8,128)(2,1)S(1)} %pad_maximum_fusion.refs_0_), channel_id=1, source_target_pairs={{0,6},{1,7},{2,0},{3,1},{4,2},{5,3},{6,4},{7,5},{8,14},{9,15},{10,... | collective-permute-start | bytes 786440 | tf_op jit(solution)/shard_map/ppermute | solution.py:310
  15.3 5.0 %collective-permute-start.1 = (bf16[256,256]{1,0:T(8,128)(2,1)S(1)}, bf16[256,256]{1,0:T(8,128)(2,1)S(1)}, u32[]{:S(2)}, u32[]{:S(2)}) collective-permute-start(bf16[256,256]{1,0:T(8,128)(2,1)S(1)} %collective-permute-done), channel_id=1, source_target_pairs={{0,1},{1,0},{2,3},{3,2},{4,5},{5,4},{6,7},{7,6},{8,9},{9,8},{10,11... | collective-permute-start | bytes 393224 | tf_op jit(solution)/shard_map/ppermute | solution.py:306
  20.3 1.3 convert_bitcast_fusion.1
  21.6 0.6 collective-permute-start.7
  22.2 0.6 collective-permute-start.8
  23.0 2.0 %collective-permute-start.2 = (bf16[512,256]{1,0:T(8,128)(2,1)S(1)}, bf16[512,256]{1,0:T(8,128)(2,1)S(1)}, u32[]{:S(2)}, u32[]{:S(2)}) collective-permute-start(bf16[512,256]{1,0:T(8,128)(2,1)S(1)} %constant_dynamic-update-slice_fusion.refs_0_), channel_id=1, source_target_pairs={{0,6},{1,7},{2,0},{3,1},{4,2},{5,3},{6,4},{7,5},{8,14},{9,15},{10,... | collective-permute-start | bytes 786440 | tf_op jit(solution)/shard_map/ppermute | solution.py:310
  25.0 1.2 collective-permute-start.3
  27.5 6.0 %neg_weights.1.refs_7_ = f32[4,2048,2]{2,1,0:T(8,128)S(1)} custom-call(s32[4,1,1024]{2,1,0:T(1,128)S(1)} %reshape.42.neg_ref, bf16[256,256]{1,0:T(8,128)(2,1)S(1)} %collective-permute-done.5.after_ref), custom_call_target="tpu_custom_call" | custom-call | tf_op jit(solution)/shard_map/neg_weights/pallas_call | solution.py:63
  33.6 1.9 %copy-done = f32[4,2048,2]{2,1,0:T(8,128)} copy-done((f32[4,2048,2]{2,1,0:T(8,128)}, f32[4,2048,2]{2,1,0:T(8,128)S(1)}, u32[]{:S(2)}) %copy-start) | copy-done | bytes 65560
  35.5 1.8 %collective-permute-done.8.refs_3_ = bf16[512,256]{1,0:T(8,128)(2,1)S(1)} collective-permute-done((bf16[512,256]{1,0:T(8,128)(2,1)S(1)}, bf16[512,256]{1,0:T(8,128)(2,1)S(1)}, u32[]{:S(2)}, u32[]{:S(2)}) %collective-permute-start.8) | collective-permute-done | bytes 262176 | tf_op jit(solution)/shard_map/ppermute | solution.py:310
  37.3 8.8 %queries.1 = (bf16[4096,256]{1,0:T(8,128)(2,1)S(1)}, bf16[256,4096]{1,0:T(8,128)(2,1)S(1)}) custom-call(s32[4]{0:T(128)S(1)} %copy-done.3, bf16[512,256]{1,0:T(8,128)(2,1)S(1)} %pad_maximum_fusion.refs_0_, bf16[512,256]{1,0:T(8,128)(2,1)S(1)} %collective-permute-done.6.refs_1_, bf16[512,256]{1,0:T(8,128)(2,1)S(1)} %collective-permute-done.7.refs_2_, ...), custom_call_target="tpu_custom_call" | custom-call | tf_op jit(solution)/shard_map/queries/pallas_call | solution.py:104
  46.2 1.4 copy-done.1
  47.6 1.4 copy-done.2
  49.0 30.9 %scores.1 = (bf16[256,4096]{1,0:T(8,128)(2,1)S(1)}, bf16[512,256]{1,0:T(8,128)(2,1)S(1)}, bf16[512,256]{1,0:T(8,128)(2,1)}, bf16[512,256]{1,0:T(8,128)(2,1)S(1)}...) custom-call(s32[4]{0:T(128)S(1)} %copy-done.3, s32[1]{0:T(128)S(6)} %copy.22.cnt_ref, ...), custom_call_target="tpu_custom_call" | custom-call | tf_op jit(solution)/shard_map/scores/pallas_call | solution.py:216
  79.9 0.7 copy-done.4
  80.6 0.7 copy-done.6
  81.3 0.8 convert_bitcast_fusion
  82.2 2.0 %copy.20 = bf16[4,256,256]{2,1,0:T(8,128)(2,1)} copy(bf16[4,256,256]{1,2,0:T(8,128)(2,1)} %convert_bitcast_fusion) | data formatting | bytes 1048576 | tf_op jit(solution)/shard_map/transpose | solution.py:329
  84.2 11.7 %all-to-all-start = ((bf16[32,32,256]{2,1,0:T(8,128)(2,1)}), bf16[32,32,256]{2,1,0:T(8,128)(2,1)}, u32[]{:S(2)}, u32[]{:S(2)}) async-start(bf16[32,32,256]{2,1,0:T(8,128)(2,1)} %bitcast.11), calls=%async_computation | async-start | bytes 1048576 | tf_op jit(solution)/shard_map/all_to_all | solution.py:330
  95.9 1.1 collective-permute-start.12
  97.0 1.9 %collective-permute-start.13 = (bf16[512,256]{1,0:T(8,128)(2,1)S(1)}, bf16[512,256]{1,0:T(8,128)(2,1)}, u32[]{:S(2)}, u32[]{:S(2)}) collective-permute-start(bf16[512,256]{1,0:T(8,128)(2,1)S(1)} %copy-done.7), channel_id=1, source_target_pairs={{0,4},{1,5},{2,6},{3,7},{4,0},{5,1},{6,2},{7,3},{8,12},{9,13},{10,... | collective-permute-start | bytes 786440 | tf_op jit(solution)/shard_map/ppermute | solution.py:310
  98.9 2.0 %collective-permute-start.14 = (bf16[512,256]{1,0:T(8,128)(2,1)S(1)}, bf16[512,256]{1,0:T(8,128)(2,1)}, u32[]{:S(2)}, u32[]{:S(2)}) collective-permute-start(bf16[512,256]{1,0:T(8,128)(2,1)S(1)} %copy-done.5), channel_id=1, source_target_pairs={{0,6},{1,7},{2,0},{3,1},{4,2},{5,3},{6,4},{7,5},{8,14},{9,15},{10,... | collective-permute-start | bytes 786440 | tf_op jit(solution)/shard_map/ppermute | solution.py:310
  100.9 1.3 convert_element_type.55.mat_ref
  102.2 7.7 %source_grads.1 = (bf16[512,256]{1,0:T(8,128)(2,1)S(1)}, bf16[512,256]{1,0:T(8,128)(2,1)S(1)}, bf16[512,256]{1,0:T(8,128)(2,1)}, bf16[512,256]{1,0:T(8,128)(2,1)}) custom-call(s32[4]{0:T(128)S(1)} %copy-done.3, bf16[256,4096]{1,0:T(8,128)(2,1)S(1)} %get-tuple-element.18.gq_ref, s32[4,1,1024]{2,1,0:T(1,128)S(1)} %reshape.43.src_ref, ...), custom_call_target="tpu_custom_call" | custom-call | tf_op jit(solution)/shard_map/source_grads/pallas_call | solution.py:276
  110.0 1.7 %collective-permute-start.11 = (bf16[512,256]{1,0:T(8,128)(2,1)}, bf16[512,256]{1,0:T(8,128)(2,1)}, u32[]{:S(2)}, u32[]{:S(2)}) collective-permute-start(bf16[512,256]{1,0:T(8,128)(2,1)} %get-tuple-element.22), channel_id=1, source_target_pairs={{0,6},{1,7},{2,0},{3,1},{4,2},{5,3},{6,4},{7,5},{8,14},{9,15},{10,... | collective-permute-start | bytes 786440 | tf_op jit(solution)/shard_map/ppermute | solution.py:310
  111.7 0.6 all-to-all-done
  112.3 1.1 convert_reduce_fusion
  113.5 0.7 broadcast_in_dim.8
  114.2 8.2 %all-to-all-start.1 = ((f32[8,32,256]{2,1,0:T(8,128)}), f32[8,32,256]{2,1,0:T(8,128)S(1)}, u32[]{:S(2)}, u32[]{:S(2)}) async-start(f32[8,32,256]{2,1,0:T(8,128)} %broadcast_in_dim.8), calls=%async_computation.1 | async-start | bytes 524288 | tf_op jit(solution)/shard_map/all_to_all | solution.py:332
  122.4 1.5 collective-permute-start.9
  123.8 1.2 add_convert_fusion
  125.1 1.9 %collective-permute-start.15 = (bf16[512,256]{1,0:T(8,128)(2,1)S(1)}, bf16[512,256]{1,0:T(8,128)(2,1)S(1)}, u32[]{:S(2)}, u32[]{:S(2)}) collective-permute-start(bf16[512,256]{1,0:T(8,128)(2,1)S(1)} %add_convert_fusion), channel_id=1, source_target_pairs={{0,8},{8,16},{16,24},{24,32},{32,40},{40,48},{48,56},{56,64},{64,7... | collective-permute-start | bytes 786440 | tf_op jit(solution)/shard_map/ppermute | solution.py:302
  127.0 6.6 %all-to-all-done.1 = f32[8,32,256]{2,1,0:T(8,128)S(1)} async-done(((f32[8,32,256]{2,1,0:T(8,128)}), f32[8,32,256]{2,1,0:T(8,128)S(1)}, u32[]{:S(2)}, u32[]{:S(2)}) %all-to-all-start.1) | async-done | bytes 262176 | tf_op jit(solution)/shard_map/all_to_all | solution.py:332
  133.6 0.9 broadcast_in_dim.9
  134.4 8.3 %all-to-all-start.2 = ((bf16[32,32,256]{2,1,0:T(8,128)(2,1)}), bf16[32,32,256]{2,1,0:T(8,128)(2,1)S(1)}, u32[]{:S(2)}, u32[]{:S(2)}) async-start(bf16[32,32,256]{2,1,0:T(8,128)(2,1)} %broadcast_in_dim.9), calls=%async_computation.2 | async-start | bytes 1048576 | tf_op jit(solution)/shard_map/all_to_all | solution.py:334
  142.8 0.7 copy-done.10
  143.5 1.3 convert_add_fusion
  144.8 0.9 collective-permute-start.16
  145.7 11.2 %collective-permute-done.16 = bf16[256,256]{1,0:T(8,128)(2,1)S(1)} collective-permute-done((bf16[256,256]{1,0:T(8,128)(2,1)S(1)}, bf16[256,256]{1,0:T(8,128)(2,1)S(1)}, u32[]{:S(2)}, u32[]{:S(2)}) %collective-permute-start.16) | collective-permute-done | bytes 131104 | tf_op jit(solution)/shard_map/ppermute | solution.py:306
  157.0 0.6 fusion.9
  157.6 0.8 divide_subtract_fusion
  158.4 6.4 %all-to-all-done.2 = bf16[32,32,256]{2,1,0:T(8,128)(2,1)S(1)} async-done(((bf16[32,32,256]{2,1,0:T(8,128)(2,1)}), bf16[32,32,256]{2,1,0:T(8,128)(2,1)S(1)}, u32[]{:S(2)}, u32[]{:S(2)}) %all-to-all-start.2) | async-done | bytes 524320 | tf_op jit(solution)/shard_map/all_to_all | solution.py:334
  165.1 0.6 fusion.8
  165.7 1.2 fusion.1
  (63 shorter events, 1.4 us)
Async XLA Ops:
  0.6 25.6 %copy-start.12 = (s32[4000]{0:T(1024)S(1)}, s32[4000]{0:T(1024)}, u32[]{:S(2)}) copy-start(s32[4000]{0:T(1024)} %param.13) | copy-start | bytes 48004
  0.6 25.6 %copy-start.13 = (s32[4000]{0:T(1024)S(1)}, s32[4000]{0:T(1024)}, u32[]{:S(2)}) copy-start(s32[4000]{0:T(1024)} %param.14) | copy-start | bytes 48004
  0.7 26.0 %copy-start.11 = (s32[4,1000]{1,0:T(4,128)S(1)}, s32[4,1000]{1,0:T(4,128)}, u32[]{:S(2)}) copy-start(s32[4,1000]{1,0:T(4,128)} %param.15) | copy-start | bytes 48004
  1.6 10.5 %collective-permute-start.5 = (bf16[256,256]{1,0:T(8,128)(2,1)S(1)}, bf16[256,256]{1,0:T(8,128)(2,1)S(1)}, u32[]{:S(2)}, u32[]{:S(2)}) collective-permute-start(bf16[256,256]{1,0:T(8,128)(2,1)S(1)} %convert_element_type.54), channel_id=1, source_target_pairs={{0,1},{1,0},{2,3},{3,2},{4,5},{5,4},{6,7},{7,6},{8,9},{9,8},{10,11... | collective-permute-start | bytes 393224 | tf_op jit(solution)/shard_map/ppermute | solution.py:306
  9.5 5.8 %collective-permute-start = (bf16[256,256]{1,0:T(8,128)(2,1)S(1)}, bf16[256,256]{1,0:T(8,128)(2,1)S(1)}, u32[]{:S(2)}, u32[]{:S(2)}) collective-permute-start(bf16[256,256]{1,0:T(8,128)(2,1)S(1)} %convert_element_type.54), channel_id=1, source_target_pairs={{0,248},{8,0},{16,8},{24,16},{32,24},{40,32},{48,40},{56,48},{64,5... | collective-permute-start | bytes 393224 | tf_op jit(solution)/shard_map/ppermute | solution.py:302
  12.2 14.1 %collective-permute-start.6 = (bf16[512,256]{1,0:T(8,128)(2,1)S(1)}, bf16[512,256]{1,0:T(8,128)(2,1)S(1)}, u32[]{:S(2)}, u32[]{:S(2)}) collective-permute-start(bf16[512,256]{1,0:T(8,128)(2,1)S(1)} %pad_maximum_fusion.refs_0_), channel_id=1, source_target_pairs={{0,6},{1,7},{2,0},{3,1},{4,2},{5,3},{6,4},{7,5},{8,14},{9,15},{10,... | collective-permute-start | bytes 786440 | tf_op jit(solution)/shard_map/ppermute | solution.py:310
  15.3 7.7 %collective-permute-start.1 = (bf16[256,256]{1,0:T(8,128)(2,1)S(1)}, bf16[256,256]{1,0:T(8,128)(2,1)S(1)}, u32[]{:S(2)}, u32[]{:S(2)}) collective-permute-start(bf16[256,256]{1,0:T(8,128)(2,1)S(1)} %collective-permute-done), channel_id=1, source_target_pairs={{0,1},{1,0},{2,3},{3,2},{4,5},{5,4},{6,7},{7,6},{8,9},{9,8},{10,11... | collective-permute-start | bytes 393224 | tf_op jit(solution)/shard_map/ppermute | solution.py:306
  21.6 13.9 %collective-permute-start.7 = (bf16[512,256]{1,0:T(8,128)(2,1)S(1)}, bf16[512,256]{1,0:T(8,128)(2,1)S(1)}, u32[]{:S(2)}, u32[]{:S(2)}) collective-permute-start(bf16[512,256]{1,0:T(8,128)(2,1)S(1)} %pad_maximum_fusion.refs_0_), channel_id=1, source_target_pairs={{0,4},{1,5},{2,6},{3,7},{4,0},{5,1},{6,2},{7,3},{8,12},{9,13},{10,... | collective-permute-start | bytes 786440 | tf_op jit(solution)/shard_map/ppermute | solution.py:310
  22.2 15.1 %collective-permute-start.8 = (bf16[512,256]{1,0:T(8,128)(2,1)S(1)}, bf16[512,256]{1,0:T(8,128)(2,1)S(1)}, u32[]{:S(2)}, u32[]{:S(2)}) collective-permute-start(bf16[512,256]{1,0:T(8,128)(2,1)S(1)} %pad_maximum_fusion.refs_0_), channel_id=1, source_target_pairs={{0,2},{1,3},{2,4},{3,5},{4,6},{5,7},{6,0},{7,1},{8,10},{9,11},{10,... | collective-permute-start | bytes 786440 | tf_op jit(solution)/shard_map/ppermute | solution.py:310
  23.0 25.9 %collective-permute-start.2 = (bf16[512,256]{1,0:T(8,128)(2,1)S(1)}, bf16[512,256]{1,0:T(8,128)(2,1)S(1)}, u32[]{:S(2)}, u32[]{:S(2)}) collective-permute-start(bf16[512,256]{1,0:T(8,128)(2,1)S(1)} %constant_dynamic-update-slice_fusion.refs_0_), channel_id=1, source_target_pairs={{0,6},{1,7},{2,0},{3,1},{4,2},{5,3},{6,4},{7,5},{8,14},{9,15},{10,... | collective-permute-start | bytes 786440 | tf_op jit(solution)/shard_map/ppermute | solution.py:310
  25.0 23.9 %collective-permute-start.3 = (bf16[512,256]{1,0:T(8,128)(2,1)S(1)}, bf16[512,256]{1,0:T(8,128)(2,1)S(1)}, u32[]{:S(2)}, u32[]{:S(2)}) collective-permute-start(bf16[512,256]{1,0:T(8,128)(2,1)S(1)} %constant_dynamic-update-slice_fusion.refs_0_), channel_id=1, source_target_pairs={{0,4},{1,5},{2,6},{3,7},{4,0},{5,1},{6,2},{7,3},{8,12},{9,13},{10,... | collective-permute-start | bytes 786440 | tf_op jit(solution)/shard_map/ppermute | solution.py:310
  26.3 22.7 %collective-permute-start.4 = (bf16[512,256]{1,0:T(8,128)(2,1)S(1)}, bf16[512,256]{1,0:T(8,128)(2,1)S(1)}, u32[]{:S(2)}, u32[]{:S(2)}) collective-permute-start(bf16[512,256]{1,0:T(8,128)(2,1)S(1)} %constant_dynamic-update-slice_fusion.refs_0_), channel_id=1, source_target_pairs={{0,2},{1,3},{2,4},{3,5},{4,6},{5,7},{6,0},{7,1},{8,10},{9,11},{10,... | collective-permute-start | bytes 786440 | tf_op jit(solution)/shard_map/ppermute | solution.py:310
  27.5 9.8 %copy-start.3 = (s32[4]{0:T(128)S(1)}, s32[4]{0:T(128)}, u32[]{:S(2)}) copy-start(s32[4]{0:T(128)} %rel_ref.5) | copy-start | bytes 52
  33.6 2.0 %copy-start = (f32[4,2048,2]{2,1,0:T(8,128)}, f32[4,2048,2]{2,1,0:T(8,128)S(1)}, u32[]{:S(2)}) copy-start(f32[4,2048,2]{2,1,0:T(8,128)S(1)} %neg_weights.1.refs_7_) | copy-start | bytes 196612
  46.2 1.4 copy-start.1
  47.6 1.4 copy-start.2
  79.9 0.7 copy-start.4
  80.6 0.7 copy-start.6
  81.3 15.7 %copy-start.7 = (bf16[512,256]{1,0:T(8,128)(2,1)S(1)}, bf16[512,256]{1,0:T(8,128)(2,1)}, u32[]{:S(2)}) copy-start(bf16[512,256]{1,0:T(8,128)(2,1)} %copy-done.6) | copy-start | bytes 786436
  81.3 17.6 %copy-start.5 = (bf16[512,256]{1,0:T(8,128)(2,1)S(1)}, bf16[512,256]{1,0:T(8,128)(2,1)}, u32[]{:S(2)}) copy-start(bf16[512,256]{1,0:T(8,128)(2,1)} %copy-done.4) | copy-start | bytes 786436
  84.2 28.1 %all-to-all-start = ((bf16[32,32,256]{2,1,0:T(8,128)(2,1)}), bf16[32,32,256]{2,1,0:T(8,128)(2,1)}, u32[]{:S(2)}, u32[]{:S(2)}) async-start(bf16[32,32,256]{2,1,0:T(8,128)(2,1)} %bitcast.11), calls=%async_computation | async-start | bytes 1048576 | tf_op jit(solution)/shard_map/all_to_all | solution.py:330
  95.9 26.5 %collective-permute-start.12 = (bf16[512,256]{1,0:T(8,128)(2,1)}, bf16[512,256]{1,0:T(8,128)(2,1)}, u32[]{:S(2)}, u32[]{:S(2)}) collective-permute-start(bf16[512,256]{1,0:T(8,128)(2,1)} %get-tuple-element.24), channel_id=1, source_target_pairs={{0,2},{1,3},{2,4},{3,5},{4,6},{5,7},{6,0},{7,1},{8,10},{9,11},{10,... | collective-permute-start | bytes 786440 | tf_op jit(solution)/shard_map/ppermute | solution.py:310
  97.0 26.8 %collective-permute-start.13 = (bf16[512,256]{1,0:T(8,128)(2,1)S(1)}, bf16[512,256]{1,0:T(8,128)(2,1)}, u32[]{:S(2)}, u32[]{:S(2)}) collective-permute-start(bf16[512,256]{1,0:T(8,128)(2,1)S(1)} %copy-done.7), channel_id=1, source_target_pairs={{0,4},{1,5},{2,6},{3,7},{4,0},{5,1},{6,2},{7,3},{8,12},{9,13},{10,... | collective-permute-start | bytes 786440 | tf_op jit(solution)/shard_map/ppermute | solution.py:310
  98.9 24.9 %collective-permute-start.14 = (bf16[512,256]{1,0:T(8,128)(2,1)S(1)}, bf16[512,256]{1,0:T(8,128)(2,1)}, u32[]{:S(2)}, u32[]{:S(2)}) collective-permute-start(bf16[512,256]{1,0:T(8,128)(2,1)S(1)} %copy-done.5), channel_id=1, source_target_pairs={{0,6},{1,7},{2,0},{3,1},{4,2},{5,3},{6,4},{7,5},{8,14},{9,15},{10,... | collective-permute-start | bytes 786440 | tf_op jit(solution)/shard_map/ppermute | solution.py:310
  109.8 32.9 %collective-permute-start.10 = (bf16[512,256]{1,0:T(8,128)(2,1)}, bf16[512,256]{1,0:T(8,128)(2,1)S(1)}, u32[]{:S(2)}, u32[]{:S(2)}) collective-permute-start(bf16[512,256]{1,0:T(8,128)(2,1)} %get-tuple-element.21), channel_id=1, source_target_pairs={{0,4},{1,5},{2,6},{3,7},{4,0},{5,1},{6,2},{7,3},{8,12},{9,13},{10,... | collective-permute-start | bytes 786440 | tf_op jit(solution)/shard_map/ppermute | solution.py:310
  110.0 32.8 %collective-permute-start.11 = (bf16[512,256]{1,0:T(8,128)(2,1)}, bf16[512,256]{1,0:T(8,128)(2,1)}, u32[]{:S(2)}, u32[]{:S(2)}) collective-permute-start(bf16[512,256]{1,0:T(8,128)(2,1)} %get-tuple-element.22), channel_id=1, source_target_pairs={{0,6},{1,7},{2,0},{3,1},{4,2},{5,3},{6,4},{7,5},{8,14},{9,15},{10,... | collective-permute-start | bytes 786440 | tf_op jit(solution)/shard_map/ppermute | solution.py:310
  114.2 19.3 %all-to-all-start.1 = ((f32[8,32,256]{2,1,0:T(8,128)}), f32[8,32,256]{2,1,0:T(8,128)S(1)}, u32[]{:S(2)}, u32[]{:S(2)}) async-start(f32[8,32,256]{2,1,0:T(8,128)} %broadcast_in_dim.8), calls=%async_computation.1 | async-start | bytes 524288 | tf_op jit(solution)/shard_map/all_to_all | solution.py:332
  122.4 20.4 %collective-permute-start.9 = (bf16[512,256]{1,0:T(8,128)(2,1)S(1)}, bf16[512,256]{1,0:T(8,128)(2,1)S(1)}, u32[]{:S(2)}, u32[]{:S(2)}) collective-permute-start(bf16[512,256]{1,0:T(8,128)(2,1)S(1)} %get-tuple-element.20), channel_id=1, source_target_pairs={{0,2},{1,3},{2,4},{3,5},{4,6},{5,7},{6,0},{7,1},{8,10},{9,11},{10,... | collective-permute-start | bytes 786440 | tf_op jit(solution)/shard_map/ppermute | solution.py:310
  125.1 17.7 %collective-permute-start.15 = (bf16[512,256]{1,0:T(8,128)(2,1)S(1)}, bf16[512,256]{1,0:T(8,128)(2,1)S(1)}, u32[]{:S(2)}, u32[]{:S(2)}) collective-permute-start(bf16[512,256]{1,0:T(8,128)(2,1)S(1)} %add_convert_fusion), channel_id=1, source_target_pairs={{0,8},{8,16},{16,24},{24,32},{32,40},{40,48},{48,56},{56,64},{64,7... | collective-permute-start | bytes 786440 | tf_op jit(solution)/shard_map/ppermute | solution.py:302
  133.6 23.5 %copy-start.15 = (f32[256]{0:T(256)S(1)}, f32[256]{0:T(256)}, u32[]{:S(2)}) copy-start(f32[256]{0:T(256)} %param.10) | copy-start | bytes 3076
  133.6 24.0 %copy-start.9 = (f32[256,256]{1,0:T(8,128)S(1)}, f32[256,256]{1,0:T(8,128)}, u32[]{:S(2)}) copy-start(f32[256,256]{1,0:T(8,128)} %param.9) | copy-start | bytes 786436
  134.4 30.3 %all-to-all-start.2 = ((bf16[32,32,256]{2,1,0:T(8,128)(2,1)}), bf16[32,32,256]{2,1,0:T(8,128)(2,1)S(1)}, u32[]{:S(2)}, u32[]{:S(2)}) async-start(bf16[32,32,256]{2,1,0:T(8,128)(2,1)} %broadcast_in_dim.9), calls=%async_computation.2 | async-start | bytes 1048576 | tf_op jit(solution)/shard_map/all_to_all | solution.py:334
  142.8 0.7 copy-start.10
  143.5 21.6 %copy-start.14 = (f32[4,256]{1,0:T(4,128)S(1)}, f32[4,256]{1,0:T(4,128)}, u32[]{:S(2)}) copy-start(f32[4,256]{1,0:T(4,128)} %param.12) | copy-start | bytes 12292
  143.5 22.2 %copy-start.8 = (f32[4,256,256]{2,1,0:T(8,128)S(1)}, f32[4,256,256]{2,1,0:T(8,128)}, u32[]{:S(2)}) copy-start(f32[4,256,256]{2,1,0:T(8,128)} %param.11) | copy-start | bytes 3145732
  144.8 12.1 %collective-permute-start.16 = (bf16[256,256]{1,0:T(8,128)(2,1)S(1)}, bf16[256,256]{1,0:T(8,128)(2,1)S(1)}, u32[]{:S(2)}, u32[]{:S(2)}) collective-permute-start(bf16[256,256]{1,0:T(8,128)(2,1)S(1)} %slice.17), channel_id=1, source_target_pairs={{0,1},{1,0},{2,3},{3,2},{4,5},{5,4},{6,7},{7,6},{8,9},{9,8},{10,11... | collective-permute-start | bytes 393224 | tf_op jit(solution)/shard_map/ppermute | solution.py:306

commit v3 on v2

--- a/solution.py
+++ b/solution.py
@@ -36,6 +36,10 @@
     )
 
 
+def one_hot(rows, index, first):
+    return jnp.where(rows == (index - first).astype(jnp.int16), bf16(1), bf16(0))
+
+
 PARTS = 4
 PART = ROWS // PARTS
 
@@ -46,17 +50,16 @@
 
 
 def count_kernel(neg_ref, after_ref, out_ref):
-    rows = lax.broadcasted_iota(jnp.int32, (BLK, PAD), 0)
-
-    def body(b, carry):
-        hits = jnp.where(rows == neg_ref[0] - b * BLK, 1.0, 0.0)
-        count = jnp.sum(hits, axis=1, keepdims=True)
-        at = pl.ds(pl.multiple_of(b * BLK, BLK), BLK)
+    rows = lax.broadcasted_iota(jnp.int32, (BLK, 128), 0).astype(jnp.int16)
+    for b in range(NBLK):
+        hits = None
+        for c in range(0, PAD, 128):
+            hot = one_hot(rows, neg_ref[0, :, c : c + 128], b * BLK)
+            hits = hot if hits is None else hits + hot
+        count = jnp.sum(hits.astype(f32), axis=1, keepdims=True)
+        at = slice(b * BLK, (b + 1) * BLK)
         out_ref[0, at, 0:1] = jnp.log2(count)
         out_ref[0, at, 1:2] = jnp.log2(count + 1.0)
-        return carry
-
-    lax.fori_loop(0, NBLK, body, 0)
 
 
 def neg_weights(neg_pad, after):
@@ -74,10 +77,6 @@
     )(neg_pad.reshape(GROUPS, 1, PAD), after)
 
 
-def one_hot(rows, index, first):
-    return jnp.where(rows == (index - first).astype(jnp.int16), bf16(1), bf16(0))
-
-
 def query_kernel(rel_ref, *refs):
     own = refs[:PARTS]
     idx_ref, mat_ref, s_ref, q_ref = refs[PARTS:]
@@ -97,10 +96,10 @@
         acc = part if acc is None else acc + part
     rows = acc.astype(bf16)
     s_ref[...] = rows
-    q_ref[...] = mm(mat_ref[0], rows, NT).astype(bf16)
-
-
-def make_queries(own, src_rows, rel_id, rel_t):
+    q_ref[...] = mm(mat_ref[0].astype(bf16).T, rows, NT).astype(bf16)
+
+
+def make_queries(own, src_rows, rel_id, relation):
     return pl.pallas_call(
         query_kernel,
         grid_spec=pltpu.PrefetchScalarGridSpec(
@@ -122,17 +121,17 @@
         ],
         compiler_params=params(),
         name="queries",
-    )(rel_id, *own, src_rows, rel_t)
+    )(rel_id, *own, src_rows, relation)
 
 
 SUB = 32
 
 
-def score_kernel(rel_ref, cnt_ref, *refs):
+def score_kernel(cnt_ref, *refs):
     nxt = refs[:PARTS]
-    q_ref, s_ref, dst_ref, wt_ref, gq_ref = refs[PARTS : PARTS + 5]
-    dg = refs[PARTS + 5 : 2 * PARTS + 5]
-    rg_ref, sc, nxt_t_ref, w0, w1, qs0, qs1, sl0, sl1, dacc = refs[2 * PARTS + 5 :]
+    q_ref, dst_ref, wt_ref, gq_ref = refs[PARTS : PARTS + 4]
+    dg = refs[PARTS + 4 : 2 * PARTS + 4]
+    sc, nxt_t_ref, w0, w1, qs0, qs1, sl0, sl1, dacc = refs[2 * PARTS + 4 :]
     g = pl.program_id(0)
     rows = lax.broadcasted_iota(jnp.int32, (SUB, CH), 0)
     rows16 = lax.broadcasted_iota(jnp.int32, (BLK, CH), 0).astype(jnp.int16)
@@ -140,7 +139,6 @@
     @pl.when(g == 0)
     def _():
         dacc[...] = jnp.zeros_like(dacc)
-        rg_ref[...] = jnp.zeros_like(rg_ref)
         w1[...] = jnp.zeros_like(w1)
         for b in range(NBLK):
             nxt_t_ref[:, b * BLK : (b + 1) * BLK] = block_of(nxt, b).T
@@ -151,10 +149,9 @@
         at = slice(b * BLK, (b + 1) * BLK)
         dacc[at, :] += mm(w[at, :], qs[...], NT)
 
-    def finish(acc, sl, chunk, s_at):
+    def finish(acc, sl, chunk):
         gq = (acc * sl[0:1, :]).astype(bf16)
         gq_ref[:, pl.ds(pl.multiple_of(chunk * CH, CH), CH)] = gq
-        rg_ref[rel_ref[chunk // PER]] += mm(gq, s_ref[pl.ds(pl.multiple_of(s_at, CH), CH), :])
 
     def stage(half, w, qs, sl, w_old, qs_old, sl_old, chunk_old):
         here = slice(half * CH, (half + 1) * CH)
@@ -187,7 +184,7 @@
             at = slice(b * BLK, (b + 1) * BLK)
             part = mm(nxt_t_ref[:, at], w_old[at, :])
             acc = part if acc is None else acc + part
-        finish(acc, sl_old, chunk_old, chunk_old * CH)
+        finish(acc, sl_old, chunk_old)
         tot = jnp.sum(tot, axis=0, keepdims=True)
         gain = (jnp.exp2(hit - top) - tot).astype(bf16)
         lane = lax.broadcasted_iota(jnp.int32, (1, CH), 1) + half * CH
@@ -207,28 +204,26 @@
     def _():
         for b in range(NBLK):
             spread(b, w1, qs1)
-        finish(mm(nxt_t_ref[...], w1[...]), sl1, 2 * g + 1, (2 * g + 1) * CH)
+        finish(mm(nxt_t_ref[...], w1[...]), sl1, 2 * g + 1)
         for p in range(PARTS):
             dg[p][...] = dacc[p * PART : (p + 1) * PART, :].astype(bf16)
 
 
-def score_side(nxt, q, s, dst_rows, weights, rel_id, counts, kinds):
+def score_side(nxt, q, dst_rows, weights, counts):
     return pl.pallas_call(
         score_kernel,
         grid_spec=pltpu.PrefetchScalarGridSpec(
-            num_scalar_prefetch=2,
+            num_scalar_prefetch=1,
             grid=(GROUPS,),
             in_specs=[
-                *[pl.BlockSpec((PART, D), lambda j, rel, cnt: (0, 0))] * PARTS,
-                pl.BlockSpec((D, PAD), lambda j, rel, cnt: (0, j)),
-                pl.BlockSpec((GROUPS * PAD, D), lambda j, rel, cnt: (0, 0)),
-                pl.BlockSpec((1, 1, PAD), lambda j, rel, cnt: (j, 0, 0)),
-                pl.BlockSpec((1, ROWS, 2), lambda j, rel, cnt: (j, 0, 0)),
+                *[pl.BlockSpec((PART, D), lambda j, cnt: (0, 0))] * PARTS,
+                pl.BlockSpec((D, PAD), lambda j, cnt: (0, j)),
+                pl.BlockSpec((1, 1, PAD), lambda j, cnt: (j, 0, 0)),
+                pl.BlockSpec((1, ROWS, 2), lambda j, cnt: (j, 0, 0)),
             ],
             out_specs=[
-                pl.BlockSpec((D, GROUPS * PAD), lambda j, rel, cnt: (0, 0)),
-                *[pl.BlockSpec((PART, D), lambda j, rel, cnt: (0, 0))] * PARTS,
-                pl.BlockSpec((kinds, D, D), lambda j, rel, cnt: (0, 0, 0)),
+                pl.BlockSpec((D, GROUPS * PAD), lambda j, cnt: (0, 0)),
+                *[pl.BlockSpec((PART, D), lambda j, cnt: (0, 0))] * PARTS,
             ],
             scratch_shapes=[
                 pltpu.VMEM((ROWS, CH), f32),
@@ -245,22 +240,23 @@
         out_shape=[
             jax.ShapeDtypeStruct((D, GROUPS * PAD), bf16),
             *[jax.ShapeDtypeStruct((PART, D), bf16)] * PARTS,
-            jax.ShapeDtypeStruct((kinds, D, D), f32),
         ],
         compiler_params=params(),
         name="scores",
-    )(rel_id, counts, *nxt, q, s, dst_rows, weights)
-
-
-def source_kernel(rel_ref, gq_ref, src_ref, mat_ref, *refs):
-    out, acc = refs[:PARTS], refs[PARTS]
+    )(counts, *nxt, q, dst_rows, weights)
+
+
+def source_kernel(rel_ref, gq_ref, s_ref, src_ref, mat_ref, *refs):
+    out, rg_ref, acc, racc = refs[:PARTS], *refs[PARTS:]
     g = pl.program_id(0)
 
     @pl.when(g == 0)
     def _():
         acc[...] = jnp.zeros_like(acc)
-
-    grad = mm(mat_ref[0], gq_ref[...]).astype(bf16)
+        racc[...] = jnp.zeros_like(racc)
+
+    racc[rel_ref[g]] += mm(gq_ref[...], s_ref[...])
+    grad = mm(mat_ref[0].astype(bf16), gq_ref[...]).astype(bf16)
     rows = lax.broadcasted_iota(jnp.int32, (BLK, PAD), 0).astype(jnp.int16)
     for b in range(NBLK):
         at = slice(b * BLK, (b + 1) * BLK)
@@ -270,9 +266,12 @@
     def _():
         for p in range(PARTS):
             out[p][...] = acc[p * PART : (p + 1) * PART, :].astype(bf16)
-
-
-def source_side(gq, src_rows, rel_id, rel_b):
+        for k in range(racc.shape[0]):
+            rg_ref[k] = racc[k].T.astype(bf16)
+
+
+def source_side(gq, s, src_rows, rel_id, relation):
+    kinds = relation.shape[0]
     return pl.pallas_call(
         source_kernel,
         grid_spec=pltpu.PrefetchScalarGridSpec(
@@ -280,16 +279,23 @@
             grid=(GROUPS,),
             in_specs=[
                 pl.BlockSpec((D, PAD), lambda j, rel: (0, j)),
+                pl.BlockSpec((PAD, D), lambda j, rel: (j, 0)),
                 pl.BlockSpec((1, 1, PAD), lambda j, rel: (j, 0, 0)),
                 pl.BlockSpec((1, D, D), lambda j, rel: (rel[j], 0, 0)),
             ],
-            out_specs=[pl.BlockSpec((PART, D), lambda j, rel: (0, 0))] * PARTS,
-            scratch_shapes=[pltpu.VMEM((ROWS, D), f32)],
+            out_specs=[
+                *[pl.BlockSpec((PART, D), lambda j, rel: (0, 0))] * PARTS,
+                pl.BlockSpec((kinds, D, D), lambda j, rel: (0, 0, 0)),
+            ],
+            scratch_shapes=[pltpu.VMEM((ROWS, D), f32), pltpu.VMEM((kinds, D, D), f32)],
         ),
-        out_shape=[jax.ShapeDtypeStruct((PART, D), bf16)] * PARTS,
+        out_shape=[
+            *[jax.ShapeDtypeStruct((PART, D), bf16)] * PARTS,
+            jax.ShapeDtypeStruct((kinds, D, D), bf16),
+        ],
         compiler_params=params(),
         name="source_grads",
-    )(rel_id, gq, src_rows, rel_b)
+    )(rel_id, gq, s, src_rows, relation)
 
 
 def rowwise(param, accum, grad):
@@ -324,49 +330,64 @@
     return ((index - PART * (rep // 2)) % ROWS) ^ (256 * (rep % 2))
 
 
-def reduce_relation(rel_t):
-    kinds = rel_t.shape[0]
-    part = rel_t.astype(bf16).transpose(0, 2, 1).reshape(32, -1, D)
-    got = lax.all_to_all(part, "dom", 0, 0)
-    mine = jnp.sum(got.astype(f32), 0)
+def spread_dom(block, stride, count):
+    size = lax.axis_size("dom")
+
+    def route(k):
+        step = [((i // stride % count + k) % count - i // stride % count) * stride for i in range(size)]
+        return [(i + step[i], i) for i in range(size)]
+
+    return jnp.concatenate([block] + [lax.ppermute(block, "dom", route(k)) for k in range(1, count)])
+
+
+def reduce_relation(grad):
+    kinds = grad.shape[0]
+    got = lax.all_to_all(grad.reshape(32, -1, D), "dom", 0, 0)
+    mine = jnp.sum(got.astype(f32), 0).astype(bf16)
     every = lax.all_to_all(jnp.broadcast_to(mine, (8,) + mine.shape), "rep", 0, 0)
-    total = jnp.sum(every, 0).astype(bf16)
-    full = lax.all_to_all(jnp.broadcast_to(total, (32,) + total.shape), "dom", 0, 0)
-    return full.reshape(kinds, D, D).astype(f32)
+    total = jnp.sum(every.astype(f32), 0)
+    full = spread_dom(spread_dom(spread_dom(total, 8, 4), 2, 4), 1, 2)
+    me = lax.axis_index("dom")
+    i = jnp.arange(32)
+    z, y, core = (i // 8 - me // 8) % 4, (i // 2 - me // 2) % 4, (i - me) % 2
+    order = core * 16 + y * 4 + z
+    return full.reshape(32, -1, D)[order].reshape(kinds, D, D)
 
 
 def pad_slots(index, fill):
     return jnp.pad(index.reshape(GROUPS, SLOTS), ((0, 0), (0, PAD - SLOTS)), constant_values=fill)
 
 
-def source_stage(own, src_pad, rel_id, rel_t):
-    return make_queries(own, src_pad.reshape(NCH, 1, CH), rel_id, rel_t)
-
-
-def target_stage(nxt, q, s, dst_pad, weights, rel_id, counts, kinds):
-    out = score_side(nxt, q, s, dst_pad.reshape(GROUPS, 1, PAD), weights, rel_id, counts, kinds)
-    return out[0], out[1 : PARTS + 1], out[PARTS + 1]
+def source_stage(own, src_pad, rel_id, relation):
+    return make_queries(own, src_pad.reshape(NCH, 1, CH), rel_id, relation)
+
+
+def target_stage(nxt, q, dst_pad, weights, counts):
+    out = score_side(nxt, q, dst_pad.reshape(GROUPS, 1, PAD), weights, counts)
+    return out[0], out[1:]
+
+
+def back_stage(gq, s, src_pad, rel_id, relation):
+    out = source_side(gq, s, src_pad.reshape(GROUPS, 1, PAD), rel_id, relation)
+    return out[:PARTS], out[PARTS]
 
 
 def local_grads(own, nxt, relation, src_index, dst_index, neg_index, rel_id, counts):
-    own, nxt, rel_b = own.astype(bf16), nxt.astype(bf16), relation.astype(bf16)
+    own, nxt = own.astype(bf16), nxt.astype(bf16)
     src_pad = pad_slots(src_index, -1)
     weights = neg_weights(pad_slots(neg_index, -1), own)
     own = [own[k * PART : (k + 1) * PART] for k in range(PARTS)]
     nxt = [nxt[k * PART : (k + 1) * PART] for k in range(PARTS)]
-    s, q = source_stage(own, src_pad, rel_id, rel_b.transpose(0, 2, 1))
-    gq, dst_grad, rel_grad = target_stage(
-        nxt, q, s, pad_slots(dst_index, -1), weights, rel_id, counts, relation.shape[0]
-    )
-    src_grad = source_side(gq, src_pad.reshape(GROUPS, 1, PAD), rel_id, rel_b)
-    return jnp.concatenate(src_grad), jnp.concatenate(dst_grad), rel_grad.transpose(0, 2, 1)
+    s, q = source_stage(own, src_pad, rel_id, relation)
+    gq, dst_grad = target_stage(nxt, q, pad_slots(dst_index, -1), weights, counts)
+    src_grad, rel_grad = back_stage(gq, s, src_pad, rel_id, relation)
+    return jnp.concatenate(src_grad), jnp.concatenate(dst_grad), rel_grad
 
 
 def on_device(
     entity, entity_accum, relation, relation_accum, src_index, dst_index, neg_index, rel_id, counts
 ):
     ent_b = entity.astype(bf16)
-    rel_b = relation.astype(bf16)
     src_pad = pad_slots(turned(src_index), -1)
     dst_pad = pad_slots(turned(dst_index), -1)
     neg_pad = pad_slots(turned(neg_index), -1)
@@ -375,13 +396,11 @@
     own = spread_x(jnp.concatenate([ent_b, other]))
     nxt = spread_x(jnp.concatenate([shifted, swap_z(shifted)]))
     weights = neg_weights(neg_pad, other)
-    s, q = source_stage(own, src_pad, rel_id, rel_b.transpose(0, 2, 1))
-    gq, dst_grad, rel_grad = target_stage(
-        nxt, q, s, dst_pad, weights, rel_id, counts, relation.shape[0]
-    )
+    s, q = source_stage(own, src_pad, rel_id, relation)
+    gq, dst_grad = target_stage(nxt, q, dst_pad, weights, counts)
+    moved = shift_dom(collect_x(dst_grad).astype(bf16), 1)
+    src_grad, rel_grad = back_stage(gq, s, src_pad, rel_id, relation)
     rel_total = reduce_relation(rel_grad)
-    moved = shift_dom(collect_x(dst_grad).astype(bf16), 1)
-    src_grad = source_side(gq, src_pad.reshape(GROUPS, 1, PAD), rel_id, rel_b)
     total = collect_x(src_grad) + moved.astype(f32)
     grads = total[:256] + swap_z(total[256:].astype(bf16)).astype(f32)
     entity_new, entity_accum_new = rowwise(entity, entity_accum, grads)

time: 167 us -> 167 us (level)
  waiting for transfers between devices: 28.5 us -> 35.7 us
  Pallas kernels: 53.5 us -> 48.6 us
  starting transfers between devices: 60.6 us -> 65.3 us
  local copies, waits for them, and re-layouts: 11.1 us -> 6.55 us
  other arithmetic: 11.6 us -> 9.15 us
    ppermute x12, waiting for transfers between devices: 1.84 us -> 17.2 us  [shift_x(): return lax.ppermute(block, 'rep', [(i, (i + 2 * by) % 8) for i in range(8)])]
    ppermute x0 -> x7, waiting for transfers between devices: none -> 12.2 us  [spread_dom(): lax.ppermute(block, 'dom', route(k))]
    ppermute x0 -> x7, starting transfers between devices: none -> 12 us  [spread_dom(): lax.ppermute(block, 'dom', route(k))]
    ppermute x3, waiting for transfers between devices: 13.1 us -> 3.26 us  [swap_z(): return lax.ppermute(block, 'rep', [(i, i ^ 1) for i in range(8)])]
    all_to_all x2 -> x1, starting transfers between devices: 20 us -> 12.1 us  [reduce_relation(): got = lax.all_to_all(grad.reshape(32, -1, D), 'dom', 0, 0)]
    all_to_all x2 -> x1, waiting for transfers between devices: 6.98 us -> 0.01 us  [reduce_relation(): got = lax.all_to_all(grad.reshape(32, -1, D), 'dom', 0, 0)]
    ppermute x3, starting transfers between devices: 13.8 us -> 18.3 us  [swap_z(): return lax.ppermute(block, 'rep', [(i, i ^ 1) for i in range(8)])]
    all_to_all x1, waiting for transfers between devices: 6.58 us -> 3.02 us  [reduce_relation(): lax.all_to_all(jnp.broadcast_to(mine, (8,) + mine.shape), 'rep', 0, 0)]
  transfers between devices with their start and end apart: 20 -> 26, of which waited for: 7 -> 11; matrix products, arithmetic and copies ran while one was open for 6% -> 4% of each run, Pallas kernels for 14% -> 7%
where the time goes in v3:
time: 167 us
  starting transfers between devices  65.3 us (39%)
  Pallas kernels  48.6 us (29%)
  waiting for transfers between devices  35.7 us (21%)
  other arithmetic  9.15 us (5%)
  local copies, waits for them, and re-layouts  6.55 us (4%)
    pallas_call x1, Pallas kernels, score_side(): pl.pallas_call(score_kernel, grid_spec=pltpu.PrefetchScalarGridSpec(num_s...  27.4 us
    ppermute x3, starting transfers between devices, swap_z(): return lax.ppermute(block, 'rep', [(i, i ^ 1) for i in range(8)])  18.3 us
    ppermute x12, waiting for transfers between devices, shift_x(): return lax.ppermute(block, 'rep', [(i, (i + 2 * by) % 8) for i in range(8)])  17.2 us
    ppermute x12, starting transfers between devices, shift_x(): return lax.ppermute(block, 'rep', [(i, (i + 2 * by) % 8) for i in range(8)])  12.9 us
    ppermute x7, waiting for transfers between devices, spread_dom(): lax.ppermute(block, 'dom', route(k))  12.2 us
    all_to_all x1, starting transfers between devices, reduce_relation(): got = lax.all_to_all(grad.reshape(32, -1, D), 'dom', 0, 0)  12.1 us
    ppermute x7, starting transfers between devices, spread_dom(): lax.ppermute(block, 'dom', route(k))  12 us
    pallas_call x1, Pallas kernels, make_queries(): pl.pallas_call(query_kernel, grid_spec=pltpu.PrefetchScalarGridSpec(num_s...  9.51 us
  transfers between devices with their start and end apart: 26, of which 11 were waited for; matrix products, arithmetic and copies ran while one was open for 4% of the time, Pallas kernels for 7%

profile of v3, /device:TPU:1, one launch (start us, length us, event | category | flops | bytes accessed | tf_op | source)
XLA Modules:
  0.0 166.8 jit_solution(16356583694515756919)
XLA Ops:
  0.6 1.0 convert_element_type.42
  1.6 7.8 %collective-permute-start.5 = (bf16[256,256]{1,0:T(8,128)(2,1)S(1)}, bf16[256,256]{1,0:T(8,128)(2,1)S(1)}, u32[]{:S(2)}, u32[]{:S(2)}) collective-permute-start(bf16[256,256]{1,0:T(8,128)(2,1)S(1)} %convert_element_type.42), channel_id=1, source_target_pairs={{0,1},{1,0},{2,3},{3,2},{4,5},{5,4},{6,7},{7,6},{8,9},{9,8},{10,11... | collective-permute-start | bytes 393224 | tf_op jit(solution)/shard_map/ppermute | solution.py:312
  9.4 1.0 collective-permute-start
  10.4 1.7 %collective-permute-done.5.after_ref = bf16[256,256]{1,0:T(8,128)(2,1)S(1)} collective-permute-done((bf16[256,256]{1,0:T(8,128)(2,1)S(1)}, bf16[256,256]{1,0:T(8,128)(2,1)S(1)}, u32[]{:S(2)}, u32[]{:S(2)}) %collective-permute-start.5) | collective-permute-done | bytes 131104 | tf_op jit(solution)/shard_map/ppermute | solution.py:312
  12.1 3.1 %collective-permute-start.6 = (bf16[512,256]{1,0:T(8,128)(2,1)S(1)}, bf16[512,256]{1,0:T(8,128)(2,1)S(1)}, u32[]{:S(2)}, u32[]{:S(2)}) collective-permute-start(bf16[512,256]{1,0:T(8,128)(2,1)S(1)} %pad_maximum_fusion.refs_0_), channel_id=1, source_target_pairs={{0,6},{1,7},{2,0},{3,1},{4,2},{5,3},{6,4},{7,5},{8,14},{9,15},{10,... | collective-permute-start | bytes 786440 | tf_op jit(solution)/shard_map/ppermute | solution.py:316
  15.2 5.0 %collective-permute-start.1 = (bf16[256,256]{1,0:T(8,128)(2,1)S(1)}, bf16[256,256]{1,0:T(8,128)(2,1)S(1)}, u32[]{:S(2)}, u32[]{:S(2)}) collective-permute-start(bf16[256,256]{1,0:T(8,128)(2,1)S(1)} %collective-permute-done), channel_id=1, source_target_pairs={{0,1},{1,0},{2,3},{3,2},{4,5},{5,4},{6,7},{7,6},{8,9},{9,8},{10,11... | collective-permute-start | bytes 393224 | tf_op jit(solution)/shard_map/ppermute | solution.py:312
  20.8 0.6 collective-permute-start.8
  21.4 1.5 collective-permute-done.1
  23.0 1.5 collective-permute-start.2
  25.1 0.6 collective-permute-start.4
  25.7 0.8 fusion.2
  26.6 0.7 fusion.6
  28.1 2.6 %neg_weights.1.refs_6_ = f32[4,2048,2]{2,1,0:T(8,128)S(1)} custom-call(s32[4,1,1024]{2,1,0:T(1,128)S(1)} %reshape.234.neg_ref, bf16[256,256]{1,0:T(8,128)(2,1)S(1)} %collective-permute-done.5.after_ref), custom_call_target="tpu_custom_call" | custom-call | tf_op jit(solution)/shard_map/neg_weights/pallas_call | solution.py:66
  30.7 2.0 %copy-done = f32[4,2048,2]{2,1,0:T(8,128)} copy-done((f32[4,2048,2]{2,1,0:T(8,128)}, f32[4,2048,2]{2,1,0:T(8,128)S(1)}, u32[]{:S(2)}) %copy-start) | copy-done | bytes 65560
  32.7 3.2 %collective-permute-done.8.refs_3_ = bf16[512,256]{1,0:T(8,128)(2,1)S(1)} collective-permute-done((bf16[512,256]{1,0:T(8,128)(2,1)S(1)}, bf16[512,256]{1,0:T(8,128)(2,1)S(1)}, u32[]{:S(2)}, u32[]{:S(2)}) %collective-permute-start.8) | collective-permute-done | bytes 262176 | tf_op jit(solution)/shard_map/ppermute | solution.py:316
  35.9 9.5 %queries.1 = (bf16[4096,256]{1,0:T(8,128)(2,1)S(1)}, bf16[256,4096]{1,0:T(8,128)(2,1)}) custom-call(s32[4]{0:T(128)S(1)} %copy-done.3, bf16[512,256]{1,0:T(8,128)(2,1)S(1)} %pad_maximum_fusion.refs_0_, bf16[512,256]{1,0:T(8,128)(2,1)S(1)} %collective-permute-done.6.refs_1_, bf16[512,256]{1,0:T(8,128)(2,1)S(1)} %collective-permute-done.7.refs_2_, ...), custom_call_target="tpu_custom_call" | custom-call | tf_op jit(solution)/shard_map/queries/pallas_call | solution.py:103
  45.4 1.4 copy-done.2
  46.8 27.4 %scores.1 = (bf16[256,4096]{1,0:T(8,128)(2,1)S(1)}, bf16[512,256]{1,0:T(8,128)(2,1)S(1)}, bf16[512,256]{1,0:T(8,128)(2,1)S(1)}, bf16[512,256]{1,0:T(8,128)(2,1)S(1)}, bf16[512,256]{1,0:T(8,128)(2,1)S(1)}) custom-call(s32[1]{0:T(128)S(6)} %copy.29.cnt_ref, bf16[512,256]{1,0:T(8,128)(2,1)S(1)} %constant_dynamic-update-slice_fusion.refs_0_, ...), custom_call_target="tpu_custom_call" | custom-call | tf_op jit(solution)/shard_map/scores/pallas_call | solution.py:213
  74.2 0.7 copy-done.4
  74.9 0.7 copy-done.6
  75.6 9.1 %source_grads.1 = (bf16[512,256]{1,0:T(8,128)(2,1)S(1)}, bf16[512,256]{1,0:T(8,128)(2,1)S(1)}, bf16[512,256]{1,0:T(8,128)(2,1)S(1)}, bf16[512,256]{1,0:T(8,128)(2,1)S(1)}, bf16[4,256,256]{2,1,0:T(8,128)(2,1)}) custom-call(s32[4]{0:T(128)S(1)} %copy-done.3, bf16[256,4096]{1,0:T(8,128)(2,1)S(1)} %get-tuple-element.17.gq_ref, bf16[4096,256]{1,0:T(8,128)(2,1)} %copy-done.2, ...), custom_call_target="tpu_custom_call" | custom-call | tf_op jit(solution)/shard_map/source_grads/pallas_call | solution.py:275
  84.7 12.1 %all-to-all-start = ((bf16[32,32,256]{2,1,0:T(8,128)(2,1)}), bf16[32,32,256]{2,1,0:T(8,128)(2,1)}, u32[]{:S(2)}, u32[]{:S(2)}) async-start(bf16[32,32,256]{2,1,0:T(8,128)(2,1)} %bitcast), calls=%async_computation | async-start | bytes 1048576 | tf_op jit(solution)/shard_map/all_to_all | solution.py:345
  97.1 1.7 %collective-permute-start.13 = (bf16[512,256]{1,0:T(8,128)(2,1)S(1)}, bf16[512,256]{1,0:T(8,128)(2,1)S(1)}, u32[]{:S(2)}, u32[]{:S(2)}) collective-permute-start(bf16[512,256]{1,0:T(8,128)(2,1)S(1)} %copy-done.5), channel_id=1, source_target_pairs={{0,4},{1,5},{2,6},{3,7},{4,0},{5,1},{6,2},{7,3},{8,12},{9,13},{10,... | collective-permute-start | bytes 786440 | tf_op jit(solution)/shard_map/ppermute | solution.py:316
  98.8 2.0 %collective-permute-start.14 = (bf16[512,256]{1,0:T(8,128)(2,1)S(1)}, bf16[512,256]{1,0:T(8,128)(2,1)S(1)}, u32[]{:S(2)}, u32[]{:S(2)}) collective-permute-start(bf16[512,256]{1,0:T(8,128)(2,1)S(1)} %get-tuple-element.26), channel_id=1, source_target_pairs={{0,6},{1,7},{2,0},{3,1},{4,2},{5,3},{6,4},{7,5},{8,14},{9,15},{10,... | collective-permute-start | bytes 786440 | tf_op jit(solution)/shard_map/ppermute | solution.py:316
  100.8 1.4 collective-permute-start.10
  102.2 0.6 collective-permute-start.11
  102.8 14.0 %collective-permute-done.12 = bf16[512,256]{1,0:T(8,128)(2,1)S(1)} collective-permute-done((bf16[512,256]{1,0:T(8,128)(2,1)S(1)}, bf16[512,256]{1,0:T(8,128)(2,1)S(1)}, u32[]{:S(2)}, u32[]{:S(2)}) %collective-permute-start.12) | collective-permute-done | bytes 262176 | tf_op jit(solution)/shard_map/ppermute | solution.py:316
  116.8 0.8 add_convert_fusion
  117.6 2.8 %collective-permute-start.15 = (bf16[512,256]{1,0:T(8,128)(2,1)}, bf16[512,256]{1,0:T(8,128)(2,1)S(1)}, u32[]{:S(2)}, u32[]{:S(2)}) collective-permute-start(bf16[512,256]{1,0:T(8,128)(2,1)} %add_convert_fusion), channel_id=1, source_target_pairs={{0,8},{8,16},{16,24},{24,32},{32,40},{40,48},{48,56},{56,64},{64,7... | collective-permute-start | bytes 786440 | tf_op jit(solution)/shard_map/ppermute | solution.py:308
  120.5 1.1 reduce_sum.40
  121.6 0.7 broadcast_in_dim.2
  122.3 6.3 %all-to-all-start.1 = ((bf16[8,32,256]{2,1,0:T(8,128)(2,1)}), bf16[8,32,256]{2,1,0:T(8,128)(2,1)S(1)}, u32[]{:S(2)}, u32[]{:S(2)}) async-start(bf16[8,32,256]{2,1,0:T(8,128)(2,1)} %broadcast_in_dim.2), calls=%async_computation.1 | async-start | bytes 262144 | tf_op jit(solution)/shard_map/all_to_all | solution.py:347
  128.6 1.1 convert_add_fusion
  129.8 5.4 %collective-permute-start.16 = (bf16[256,256]{1,0:T(8,128)(2,1)S(1)}, bf16[256,256]{1,0:T(8,128)(2,1)S(1)}, u32[]{:S(2)}, u32[]{:S(2)}) collective-permute-start(bf16[256,256]{1,0:T(8,128)(2,1)S(1)} %slice.19), channel_id=1, source_target_pairs={{0,1},{1,0},{2,3},{3,2},{4,5},{5,4},{6,7},{7,6},{8,9},{9,8},{10,11... | collective-permute-start | bytes 393224 | tf_op jit(solution)/shard_map/ppermute | solution.py:312
  135.2 3.0 %all-to-all-done.1 = bf16[8,32,256]{2,1,0:T(8,128)(2,1)S(1)} async-done(((bf16[8,32,256]{2,1,0:T(8,128)(2,1)}), bf16[8,32,256]{2,1,0:T(8,128)(2,1)S(1)}, u32[]{:S(2)}, u32[]{:S(2)}) %all-to-all-start.1) | async-done | bytes 131104 | tf_op jit(solution)/shard_map/all_to_all | solution.py:347
  138.3 3.3 %collective-permute-start.17 = (f32[32,256]{1,0:T(8,128)S(1)}, f32[32,256]{1,0:T(8,128)S(1)}, u32[]{:S(2)}, u32[]{:S(2)}) collective-permute-start(f32[32,256]{1,0:T(8,128)S(1)} %convert_reduce_fusion), channel_id=1, source_target_pairs={{64,0},{72,8},{80,16},{88,24},{96,32},{104,40},{112,48},{120,56},{... | collective-permute-start | bytes 98312 | tf_op jit(solution)/shard_map/ppermute | solution.py:340
  142.1 1.4 collective-permute-start.19
  143.8 2.6 %collective-permute-done.18 = f32[32,256]{1,0:T(8,128)S(1)} collective-permute-done((f32[32,256]{1,0:T(8,128)S(1)}, f32[32,256]{1,0:T(8,128)S(1)}, u32[]{:S(2)}, u32[]{:S(2)}) %collective-permute-start.18) | collective-permute-done | bytes 32800 | tf_op jit(solution)/shard_map/ppermute | solution.py:340
  146.8 5.5 %collective-permute-start.20 = (f32[128,256]{1,0:T(8,128)S(1)}, f32[128,256]{1,0:T(8,128)S(1)}, u32[]{:S(2)}, u32[]{:S(2)}) collective-permute-start(f32[128,256]{1,0:T(8,128)S(1)} %pad_maximum_fusion.1), channel_id=1, source_target_pairs={{16,0},{24,8},{32,16},{40,24},{48,32},{56,40},{0,48},{8,56},{80,64... | collective-permute-start | bytes 393224 | tf_op jit(solution)/shard_map/ppermute | solution.py:340
  153.0 5.1 %collective-permute-done.20 = f32[128,256]{1,0:T(8,128)S(1)} collective-permute-done((f32[128,256]{1,0:T(8,128)S(1)}, f32[128,256]{1,0:T(8,128)S(1)}, u32[]{:S(2)}, u32[]{:S(2)}) %collective-permute-start.20) | collective-permute-done | bytes 131104 | tf_op jit(solution)/shard_map/ppermute | solution.py:340
  158.1 1.1 collective-permute-done.21
  159.2 2.7 %collective-permute-done.22 = f32[128,256]{1,0:T(8,128)S(1)} collective-permute-done((f32[128,256]{1,0:T(8,128)S(1)}, f32[128,256]{1,0:T(8,128)S(1)}, u32[]{:S(2)}, u32[]{:S(2)}) %collective-permute-start.22) | collective-permute-done | bytes 131104 | tf_op jit(solution)/shard_map/ppermute | solution.py:340
  161.9 0.6 collective-permute-start.23
  162.6 0.6 fusion.18
  163.2 0.8 divide_subtract_fusion
  164.1 0.6 gather_fusion
  165.0 0.6 fusion.17
  165.6 1.2 fusion
  (71 shorter events, 4.3 us)
Async XLA Ops:
  1.6 10.5 %collective-permute-start.5 = (bf16[256,256]{1,0:T(8,128)(2,1)S(1)}, bf16[256,256]{1,0:T(8,128)(2,1)S(1)}, u32[]{:S(2)}, u32[]{:S(2)}) collective-permute-start(bf16[256,256]{1,0:T(8,128)(2,1)S(1)} %convert_element_type.42), channel_id=1, source_target_pairs={{0,1},{1,0},{2,3},{3,2},{4,5},{5,4},{6,7},{7,6},{8,9},{9,8},{10,11... | collective-permute-start | bytes 393224 | tf_op jit(solution)/shard_map/ppermute | solution.py:312
  9.4 5.8 %collective-permute-start = (bf16[256,256]{1,0:T(8,128)(2,1)S(1)}, bf16[256,256]{1,0:T(8,128)(2,1)S(1)}, u32[]{:S(2)}, u32[]{:S(2)}) collective-permute-start(bf16[256,256]{1,0:T(8,128)(2,1)S(1)} %convert_element_type.42), channel_id=1, source_target_pairs={{0,248},{8,0},{16,8},{24,16},{32,24},{40,32},{48,40},{56,48},{64,5... | collective-permute-start | bytes 393224 | tf_op jit(solution)/shard_map/ppermute | solution.py:308
  12.1 12.9 %collective-permute-start.6 = (bf16[512,256]{1,0:T(8,128)(2,1)S(1)}, bf16[512,256]{1,0:T(8,128)(2,1)S(1)}, u32[]{:S(2)}, u32[]{:S(2)}) collective-permute-start(bf16[512,256]{1,0:T(8,128)(2,1)S(1)} %pad_maximum_fusion.refs_0_), channel_id=1, source_target_pairs={{0,6},{1,7},{2,0},{3,1},{4,2},{5,3},{6,4},{7,5},{8,14},{9,15},{10,... | collective-permute-start | bytes 786440 | tf_op jit(solution)/shard_map/ppermute | solution.py:316
  15.2 7.7 %collective-permute-start.1 = (bf16[256,256]{1,0:T(8,128)(2,1)S(1)}, bf16[256,256]{1,0:T(8,128)(2,1)S(1)}, u32[]{:S(2)}, u32[]{:S(2)}) collective-permute-start(bf16[256,256]{1,0:T(8,128)(2,1)S(1)} %collective-permute-done), channel_id=1, source_target_pairs={{0,1},{1,0},{2,3},{3,2},{4,5},{5,4},{6,7},{7,6},{8,9},{9,8},{10,11... | collective-permute-start | bytes 393224 | tf_op jit(solution)/shard_map/ppermute | solution.py:312
  20.3 12.4 %collective-permute-start.7 = (bf16[512,256]{1,0:T(8,128)(2,1)S(1)}, bf16[512,256]{1,0:T(8,128)(2,1)S(1)}, u32[]{:S(2)}, u32[]{:S(2)}) collective-permute-start(bf16[512,256]{1,0:T(8,128)(2,1)S(1)} %pad_maximum_fusion.refs_0_), channel_id=1, source_target_pairs={{0,4},{1,5},{2,6},{3,7},{4,0},{5,1},{6,2},{7,3},{8,12},{9,13},{10,... | collective-permute-start | bytes 786440 | tf_op jit(solution)/shard_map/ppermute | solution.py:316
  20.8 15.1 %collective-permute-start.8 = (bf16[512,256]{1,0:T(8,128)(2,1)S(1)}, bf16[512,256]{1,0:T(8,128)(2,1)S(1)}, u32[]{:S(2)}, u32[]{:S(2)}) collective-permute-start(bf16[512,256]{1,0:T(8,128)(2,1)S(1)} %pad_maximum_fusion.refs_0_), channel_id=1, source_target_pairs={{0,2},{1,3},{2,4},{3,5},{4,6},{5,7},{6,0},{7,1},{8,10},{9,11},{10,... | collective-permute-start | bytes 786440 | tf_op jit(solution)/shard_map/ppermute | solution.py:316
  23.0 23.8 %collective-permute-start.2 = (bf16[512,256]{1,0:T(8,128)(2,1)S(1)}, bf16[512,256]{1,0:T(8,128)(2,1)S(1)}, u32[]{:S(2)}, u32[]{:S(2)}) collective-permute-start(bf16[512,256]{1,0:T(8,128)(2,1)S(1)} %constant_dynamic-update-slice_fusion.refs_0_), channel_id=1, source_target_pairs={{0,6},{1,7},{2,0},{3,1},{4,2},{5,3},{6,4},{7,5},{8,14},{9,15},{10,... | collective-permute-start | bytes 786440 | tf_op jit(solution)/shard_map/ppermute | solution.py:316
  24.5 22.3 %collective-permute-start.3 = (bf16[512,256]{1,0:T(8,128)(2,1)S(1)}, bf16[512,256]{1,0:T(8,128)(2,1)S(1)}, u32[]{:S(2)}, u32[]{:S(2)}) collective-permute-start(bf16[512,256]{1,0:T(8,128)(2,1)S(1)} %constant_dynamic-update-slice_fusion.refs_0_), channel_id=1, source_target_pairs={{0,4},{1,5},{2,6},{3,7},{4,0},{5,1},{6,2},{7,3},{8,12},{9,13},{10,... | collective-permute-start | bytes 786440 | tf_op jit(solution)/shard_map/ppermute | solution.py:316
  25.1 21.7 %collective-permute-start.4 = (bf16[512,256]{1,0:T(8,128)(2,1)S(1)}, bf16[512,256]{1,0:T(8,128)(2,1)S(1)}, u32[]{:S(2)}, u32[]{:S(2)}) collective-permute-start(bf16[512,256]{1,0:T(8,128)(2,1)S(1)} %constant_dynamic-update-slice_fusion.refs_0_), channel_id=1, source_target_pairs={{0,2},{1,3},{2,4},{3,5},{4,6},{5,7},{6,0},{7,1},{8,10},{9,11},{10,... | collective-permute-start | bytes 786440 | tf_op jit(solution)/shard_map/ppermute | solution.py:316
  28.1 7.8 %copy-start.1 = (f32[4,256,256]{2,1,0:T(8,128)S(1)}, f32[4,256,256]{2,1,0:T(8,128)}, u32[]{:S(2)}) copy-start(f32[4,256,256]{2,1,0:T(8,128)} %mat_ref.1) | copy-start | bytes 3145732
  28.1 7.8 %copy-start.3 = (s32[4]{0:T(128)S(1)}, s32[4]{0:T(128)}, u32[]{:S(2)}) copy-start(s32[4]{0:T(128)} %rel_ref.3) | copy-start | bytes 52
  30.7 2.0 %copy-start = (f32[4,2048,2]{2,1,0:T(8,128)}, f32[4,2048,2]{2,1,0:T(8,128)S(1)}, u32[]{:S(2)}) copy-start(f32[4,2048,2]{2,1,0:T(8,128)S(1)} %neg_weights.1.refs_6_) | copy-start | bytes 196612
  45.4 1.4 copy-start.2
  74.2 0.7 copy-start.4
  74.9 0.7 copy-start.6
  75.6 21.2 %copy-start.7 = (bf16[512,256]{1,0:T(8,128)(2,1)S(1)}, bf16[512,256]{1,0:T(8,128)(2,1)}, u32[]{:S(2)}) copy-start(bf16[512,256]{1,0:T(8,128)(2,1)} %copy-done.6) | copy-start | bytes 786436
  75.6 21.5 %copy-start.5 = (bf16[512,256]{1,0:T(8,128)(2,1)S(1)}, bf16[512,256]{1,0:T(8,128)(2,1)}, u32[]{:S(2)}) copy-start(bf16[512,256]{1,0:T(8,128)(2,1)} %copy-done.4) | copy-start | bytes 786436
  84.7 35.7 %all-to-all-start = ((bf16[32,32,256]{2,1,0:T(8,128)(2,1)}), bf16[32,32,256]{2,1,0:T(8,128)(2,1)}, u32[]{:S(2)}, u32[]{:S(2)}) async-start(bf16[32,32,256]{2,1,0:T(8,128)(2,1)} %bitcast), calls=%async_computation | async-start | bytes 1048576 | tf_op jit(solution)/shard_map/all_to_all | solution.py:345
  96.8 19.9 %collective-permute-start.12 = (bf16[512,256]{1,0:T(8,128)(2,1)S(1)}, bf16[512,256]{1,0:T(8,128)(2,1)S(1)}, u32[]{:S(2)}, u32[]{:S(2)}) collective-permute-start(bf16[512,256]{1,0:T(8,128)(2,1)S(1)} %copy-done.7), channel_id=1, source_target_pairs={{0,2},{1,3},{2,4},{3,5},{4,6},{5,7},{6,0},{7,1},{8,10},{9,11},{10,... | collective-permute-start | bytes 786440 | tf_op jit(solution)/shard_map/ppermute | solution.py:316
  97.1 19.6 %collective-permute-start.13 = (bf16[512,256]{1,0:T(8,128)(2,1)S(1)}, bf16[512,256]{1,0:T(8,128)(2,1)S(1)}, u32[]{:S(2)}, u32[]{:S(2)}) collective-permute-start(bf16[512,256]{1,0:T(8,128)(2,1)S(1)} %copy-done.5), channel_id=1, source_target_pairs={{0,4},{1,5},{2,6},{3,7},{4,0},{5,1},{6,2},{7,3},{8,12},{9,13},{10,... | collective-permute-start | bytes 786440 | tf_op jit(solution)/shard_map/ppermute | solution.py:316
  98.8 18.0 %collective-permute-start.14 = (bf16[512,256]{1,0:T(8,128)(2,1)S(1)}, bf16[512,256]{1,0:T(8,128)(2,1)S(1)}, u32[]{:S(2)}, u32[]{:S(2)}) collective-permute-start(bf16[512,256]{1,0:T(8,128)(2,1)S(1)} %get-tuple-element.26), channel_id=1, source_target_pairs={{0,6},{1,7},{2,0},{3,1},{4,2},{5,3},{6,4},{7,5},{8,14},{9,15},{10,... | collective-permute-start | bytes 786440 | tf_op jit(solution)/shard_map/ppermute | solution.py:316
  100.8 27.8 %collective-permute-start.10 = (bf16[512,256]{1,0:T(8,128)(2,1)S(1)}, bf16[512,256]{1,0:T(8,128)(2,1)S(1)}, u32[]{:S(2)}, u32[]{:S(2)}) collective-permute-start(bf16[512,256]{1,0:T(8,128)(2,1)S(1)} %get-tuple-element.21), channel_id=1, source_target_pairs={{0,4},{1,5},{2,6},{3,7},{4,0},{5,1},{6,2},{7,3},{8,12},{9,13},{10,... | collective-permute-start | bytes 786440 | tf_op jit(solution)/shard_map/ppermute | solution.py:316
  102.2 26.4 %collective-permute-start.11 = (bf16[512,256]{1,0:T(8,128)(2,1)S(1)}, bf16[512,256]{1,0:T(8,128)(2,1)}, u32[]{:S(2)}, u32[]{:S(2)}) collective-permute-start(bf16[512,256]{1,0:T(8,128)(2,1)S(1)} %get-tuple-element.22), channel_id=1, source_target_pairs={{0,6},{1,7},{2,0},{3,1},{4,2},{5,3},{6,4},{7,5},{8,14},{9,15},{10,... | collective-permute-start | bytes 786440 | tf_op jit(solution)/shard_map/ppermute | solution.py:316
  116.8 11.8 %collective-permute-start.9 = (bf16[512,256]{1,0:T(8,128)(2,1)S(1)}, bf16[512,256]{1,0:T(8,128)(2,1)S(1)}, u32[]{:S(2)}, u32[]{:S(2)}) collective-permute-start(bf16[512,256]{1,0:T(8,128)(2,1)S(1)} %get-tuple-element.20), channel_id=1, source_target_pairs={{0,2},{1,3},{2,4},{3,5},{4,6},{5,7},{6,0},{7,1},{8,10},{9,11},{10,... | collective-permute-start | bytes 786440 | tf_op jit(solution)/shard_map/ppermute | solution.py:316
  117.6 11.0 %collective-permute-start.15 = (bf16[512,256]{1,0:T(8,128)(2,1)}, bf16[512,256]{1,0:T(8,128)(2,1)S(1)}, u32[]{:S(2)}, u32[]{:S(2)}) collective-permute-start(bf16[512,256]{1,0:T(8,128)(2,1)} %add_convert_fusion), channel_id=1, source_target_pairs={{0,8},{8,16},{16,24},{24,32},{32,40},{40,48},{48,56},{56,64},{64,7... | collective-permute-start | bytes 786440 | tf_op jit(solution)/shard_map/ppermute | solution.py:308
  122.3 16.0 %all-to-all-start.1 = ((bf16[8,32,256]{2,1,0:T(8,128)(2,1)}), bf16[8,32,256]{2,1,0:T(8,128)(2,1)S(1)}, u32[]{:S(2)}, u32[]{:S(2)}) async-start(bf16[8,32,256]{2,1,0:T(8,128)(2,1)} %broadcast_in_dim.2), calls=%async_computation.1 | async-start | bytes 262144 | tf_op jit(solution)/shard_map/all_to_all | solution.py:347
  128.6 34.0 %copy-start.10 = (f32[256]{0:T(256)S(1)}, f32[256]{0:T(256)}, u32[]{:S(2)}) copy-start(f32[256]{0:T(256)} %param.10) | copy-start | bytes 3076
  128.6 34.6 %copy-start.8 = (f32[256,256]{1,0:T(8,128)S(1)}, f32[256,256]{1,0:T(8,128)}, u32[]{:S(2)}) copy-start(f32[256,256]{1,0:T(8,128)} %param.9) | copy-start | bytes 786436
  129.8 32.7 %collective-permute-start.16 = (bf16[256,256]{1,0:T(8,128)(2,1)S(1)}, bf16[256,256]{1,0:T(8,128)(2,1)S(1)}, u32[]{:S(2)}, u32[]{:S(2)}) collective-permute-start(bf16[256,256]{1,0:T(8,128)(2,1)S(1)} %slice.19), channel_id=1, source_target_pairs={{0,1},{1,0},{2,3},{3,2},{4,5},{5,4},{6,7},{7,6},{8,9},{9,8},{10,11... | collective-permute-start | bytes 393224 | tf_op jit(solution)/shard_map/ppermute | solution.py:312
  138.3 5.5 %collective-permute-start.17 = (f32[32,256]{1,0:T(8,128)S(1)}, f32[32,256]{1,0:T(8,128)S(1)}, u32[]{:S(2)}, u32[]{:S(2)}) collective-permute-start(f32[32,256]{1,0:T(8,128)S(1)} %convert_reduce_fusion), channel_id=1, source_target_pairs={{64,0},{72,8},{80,16},{88,24},{96,32},{104,40},{112,48},{120,56},{... | collective-permute-start | bytes 98312 | tf_op jit(solution)/shard_map/ppermute | solution.py:340
  141.6 4.9 %collective-permute-start.18 = (f32[32,256]{1,0:T(8,128)S(1)}, f32[32,256]{1,0:T(8,128)S(1)}, u32[]{:S(2)}, u32[]{:S(2)}) collective-permute-start(f32[32,256]{1,0:T(8,128)S(1)} %convert_reduce_fusion), channel_id=1, source_target_pairs={{128,0},{136,8},{144,16},{152,24},{160,32},{168,40},{176,48},{184,... | collective-permute-start | bytes 98312 | tf_op jit(solution)/shard_map/ppermute | solution.py:340
  142.1 4.6 %collective-permute-start.19 = (f32[32,256]{1,0:T(8,128)S(1)}, f32[32,256]{1,0:T(8,128)S(1)}, u32[]{:S(2)}, u32[]{:S(2)}) collective-permute-start(f32[32,256]{1,0:T(8,128)S(1)} %convert_reduce_fusion), channel_id=1, source_target_pairs={{192,0},{200,8},{208,16},{216,24},{224,32},{232,40},{240,48},{248,... | collective-permute-start | bytes 98312 | tf_op jit(solution)/shard_map/ppermute | solution.py:340
  146.8 11.3 %collective-permute-start.20 = (f32[128,256]{1,0:T(8,128)S(1)}, f32[128,256]{1,0:T(8,128)S(1)}, u32[]{:S(2)}, u32[]{:S(2)}) collective-permute-start(f32[128,256]{1,0:T(8,128)S(1)} %pad_maximum_fusion.1), channel_id=1, source_target_pairs={{16,0},{24,8},{32,16},{40,24},{48,32},{56,40},{0,48},{8,56},{80,64... | collective-permute-start | bytes 393224 | tf_op jit(solution)/shard_map/ppermute | solution.py:340
  152.2 6.9 %collective-permute-start.21 = (f32[128,256]{1,0:T(8,128)S(1)}, f32[128,256]{1,0:T(8,128)S(1)}, u32[]{:S(2)}, u32[]{:S(2)}) collective-permute-start(f32[128,256]{1,0:T(8,128)S(1)} %pad_maximum_fusion.1), channel_id=1, source_target_pairs={{32,0},{40,8},{48,16},{56,24},{0,32},{8,40},{16,48},{24,56},{96,64... | collective-permute-start | bytes 393224 | tf_op jit(solution)/shard_map/ppermute | solution.py:340
  152.5 9.4 %collective-permute-start.22 = (f32[128,256]{1,0:T(8,128)S(1)}, f32[128,256]{1,0:T(8,128)S(1)}, u32[]{:S(2)}, u32[]{:S(2)}) collective-permute-start(f32[128,256]{1,0:T(8,128)S(1)} %pad_maximum_fusion.1), channel_id=1, source_target_pairs={{48,0},{56,8},{0,16},{8,24},{16,32},{24,40},{32,48},{40,56},{112,6... | collective-permute-start | bytes 393224 | tf_op jit(solution)/shard_map/ppermute | solution.py:340
  161.9 2.1 %collective-permute-start.23 = (f32[512,256]{1,0:T(8,128)S(1)}, f32[512,256]{1,0:T(8,128)S(1)}, u32[]{:S(2)}, u32[]{:S(2)}) collective-permute-start(f32[512,256]{1,0:T(8,128)S(1)} %get-tuple-element.34), channel_id=1, source_target_pairs={{8,0},{0,8},{24,16},{16,24},{40,32},{32,40},{56,48},{48,56},{72,64... | collective-permute-start | bytes 1572872 | tf_op jit(solution)/shard_map/ppermute | solution.py:340
  164.1 1.0 copy-start.9

commit v4 on v3

--- a/solution.py
+++ b/solution.py
@@ -30,6 +30,10 @@
     return lax.dot_general(a, b, dims, preferred_element_type=f32)
 
 
+def cost(us):
+    return pl.CostEstimate(flops=int(us * 5e8), bytes_accessed=int(us * 3.5e6), transcendentals=0)
+
+
 def params():
     return pltpu.CompilerParams(
         dimension_semantics=("arbitrary",), vmem_limit_bytes=48 * MB
@@ -73,6 +77,7 @@
         out_specs=pl.BlockSpec((1, ROWS, 2), lambda g: (g, 0, 0)),
         out_shape=jax.ShapeDtypeStruct((GROUPS, ROWS, 2), f32),
         compiler_params=params(),
+        cost_estimate=cost(3),
         name="neg_weights",
     )(neg_pad.reshape(GROUPS, 1, PAD), after)
 
@@ -120,6 +125,7 @@
             jax.ShapeDtypeStruct((D, GROUPS * PAD), bf16),
         ],
         compiler_params=params(),
+        cost_estimate=cost(9),
         name="queries",
     )(rel_id, *own, src_rows, relation)
 
@@ -242,20 +248,54 @@
             *[jax.ShapeDtypeStruct((PART, D), bf16)] * PARTS,
         ],
         compiler_params=params(),
+        cost_estimate=cost(28),
         name="scores",
     )(counts, *nxt, q, dst_rows, weights)
 
 
-def source_kernel(rel_ref, gq_ref, s_ref, src_ref, mat_ref, *refs):
-    out, rg_ref, acc, racc = refs[:PARTS], *refs[PARTS:]
+def operator_kernel(rel_ref, gq_ref, s_ref, out_ref, acc):
     g = pl.program_id(0)
 
     @pl.when(g == 0)
     def _():
         acc[...] = jnp.zeros_like(acc)
-        racc[...] = jnp.zeros_like(racc)
-
-    racc[rel_ref[g]] += mm(gq_ref[...], s_ref[...])
+
+    acc[rel_ref[g]] += mm(gq_ref[...], s_ref[...])
+
+    @pl.when(g == GROUPS - 1)
+    def _():
+        for k in range(acc.shape[0]):
+            out_ref[k] = acc[k].T.astype(bf16)
+
+
+def operator_side(gq, s, rel_id, kinds):
+    return pl.pallas_call(
+        operator_kernel,
+        grid_spec=pltpu.PrefetchScalarGridSpec(
+            num_scalar_prefetch=1,
+            grid=(GROUPS,),
+            in_specs=[
+                pl.BlockSpec((D, PAD), lambda j, rel: (0, j)),
+                pl.BlockSpec((PAD, D), lambda j, rel: (j, 0)),
+            ],
+            out_specs=pl.BlockSpec((kinds, D, D), lambda j, rel: (0, 0, 0)),
+            scratch_shapes=[pltpu.VMEM((kinds, D, D), f32)],
+        ),
+        out_shape=jax.ShapeDtypeStruct((kinds, D, D), bf16),
+        compiler_params=params(),
+        cost_estimate=cost(2),
+        name="operator_grads",
+    )(rel_id, gq, s)
+
+
+def source_kernel(rel_ref, gq_ref, src_ref, mat_ref, *refs):
+    out, acc = refs[:PARTS], refs[PARTS]
+    g = pl.program_id(0)
+
+    @pl.when(g == 0)
+    def _():
+        acc[...] = jnp.zeros_like(acc)
+
     grad = mm(mat_ref[0].astype(bf16), gq_ref[...]).astype(bf16)
     rows = lax.broadcasted_iota(jnp.int32, (BLK, PAD), 0).astype(jnp.int16)
     for b in range(NBLK):
@@ -266,12 +306,9 @@
     def _():
         for p in range(PARTS):
             out[p][...] = acc[p * PART : (p + 1) * PART, :].astype(bf16)
-        for k in range(racc.shape[0]):
-            rg_ref[k] = racc[k].T.astype(bf16)
-
-
-def source_side(gq, s, src_rows, rel_id, relation):
-    kinds = relation.shape[0]
+
+
+def source_side(gq, src_rows, rel_id, relation):
     return pl.pallas_call(
         source_kernel,
         grid_spec=pltpu.PrefetchScalarGridSpec(
@@ -279,23 +316,17 @@
             grid=(GROUPS,),
             in_specs=[
                 pl.BlockSpec((D, PAD), lambda j, rel: (0, j)),
-                pl.BlockSpec((PAD, D), lambda j, rel: (j, 0)),
                 pl.BlockSpec((1, 1, PAD), lambda j, rel: (j, 0, 0)),
                 pl.BlockSpec((1, D, D), lambda j, rel: (rel[j], 0, 0)),
             ],
-            out_specs=[
-                *[pl.BlockSpec((PART, D), lambda j, rel: (0, 0))] * PARTS,
-                pl.BlockSpec((kinds, D, D), lambda j, rel: (0, 0, 0)),
-            ],
-            scratch_shapes=[pltpu.VMEM((ROWS, D), f32), pltpu.VMEM((kinds, D, D), f32)],
+            out_specs=[pl.BlockSpec((PART, D), lambda j, rel: (0, 0))] * PARTS,
+            scratch_shapes=[pltpu.VMEM((ROWS, D), f32)],
         ),
-        out_shape=[
-            *[jax.ShapeDtypeStruct((PART, D), bf16)] * PARTS,
-            jax.ShapeDtypeStruct((kinds, D, D), bf16),
-        ],
+        out_shape=[jax.ShapeDtypeStruct((PART, D), bf16)] * PARTS,
         compiler_params=params(),
+        cost_estimate=cost(8),
         name="source_grads",
-    )(rel_id, gq, s, src_rows, relation)
+    )(rel_id, gq, src_rows, relation)
 
 
 def rowwise(param, accum, grad):
@@ -328,16 +359,6 @@
 def turned(index):
     rep = lax.axis_index("rep")
     return ((index - PART * (rep // 2)) % ROWS) ^ (256 * (rep % 2))
-
-
-def spread_dom(block, stride, count):
-    size = lax.axis_size("dom")
-
-    def route(k):
-        step = [((i // stride % count + k) % count - i // stride % count) * stride for i in range(size)]
-        return [(i + step[i], i) for i in range(size)]
-
-    return jnp.concatenate([block] + [lax.ppermute(block, "dom", route(k)) for k in range(1, count)])
 
 
 def reduce_relation(grad):
@@ -346,12 +367,14 @@
     mine = jnp.sum(got.astype(f32), 0).astype(bf16)
     every = lax.all_to_all(jnp.broadcast_to(mine, (8,) + mine.shape), "rep", 0, 0)
     total = jnp.sum(every.astype(f32), 0)
-    full = spread_dom(spread_dom(spread_dom(total, 8, 4), 2, 4), 1, 2)
-    me = lax.axis_index("dom")
-    i = jnp.arange(32)
-    z, y, core = (i // 8 - me // 8) % 4, (i // 2 - me // 2) % 4, (i - me) % 2
-    order = core * 16 + y * 4 + z
-    return full.reshape(32, -1, D)[order].reshape(kinds, D, D)
+    cores = [[2 * i + c for i in range(16)] for c in range(2)]
+    half = lax.all_to_all(
+        jnp.broadcast_to(total, (16,) + total.shape), "dom", 0, 0, axis_index_groups=cores
+    )
+    other = lax.ppermute(half, "dom", [(i, i ^ 1) for i in range(32)])
+    second = lax.axis_index("dom") % 2 == 1
+    pairs = [jnp.where(second, other, half), jnp.where(second, half, other)]
+    return jnp.stack(pairs, 1).reshape(kinds, D, D)
 
 
 def pad_slots(index, fill):
@@ -362,14 +385,13 @@
     return make_queries(own, src_pad.reshape(NCH, 1, CH), rel_id, relation)
 
 
-def target_stage(nxt, q, dst_pad, weights, counts):
+def target_stage(nxt, q, s, dst_pad, weights, rel_id, counts, kinds):
     out = score_side(nxt, q, dst_pad.reshape(GROUPS, 1, PAD), weights, counts)
-    return out[0], out[1:]
-
-
-def back_stage(gq, s, src_pad, rel_id, relation):
-    out = source_side(gq, s, src_pad.reshape(GROUPS, 1, PAD), rel_id, relation)
-    return out[:PARTS], out[PARTS]
+    return out[0], out[1:], operator_side(out[0], s, rel_id, kinds)
+
+
+def back_stage(gq, src_pad, rel_id, relation):
+    return source_side(gq, src_pad.reshape(GROUPS, 1, PAD), rel_id, relation)
 
 
 def local_grads(own, nxt, relation, src_index, dst_index, neg_index, rel_id, counts):
@@ -379,8 +401,10 @@
     own = [own[k * PART : (k + 1) * PART] for k in range(PARTS)]
     nxt = [nxt[k * PART : (k + 1) * PART] for k in range(PARTS)]
     s, q = source_stage(own, src_pad, rel_id, relation)
-    gq, dst_grad = target_stage(nxt, q, pad_slots(dst_index, -1), weights, counts)
-    src_grad, rel_grad = back_stage(gq, s, src_pad, rel_id, relation)
+    gq, dst_grad, rel_grad = target_stage(
+        nxt, q, s, pad_slots(dst_index, -1), weights, rel_id, counts, relation.shape[0]
+    )
+    src_grad = back_stage(gq, src_pad, rel_id, relation)
     return jnp.concatenate(src_grad), jnp.concatenate(dst_grad), rel_grad
 
 
@@ -392,15 +416,16 @@
     dst_pad = pad_slots(turned(dst_index), -1)
     neg_pad = pad_slots(turned(neg_index), -1)
     other = swap_z(ent_b)
-    shifted = shift_dom(ent_b, -1)
     own = spread_x(jnp.concatenate([ent_b, other]))
-    nxt = spread_x(jnp.concatenate([shifted, swap_z(shifted)]))
+    nxt = [shift_dom(block, -1) for block in own]
     weights = neg_weights(neg_pad, other)
     s, q = source_stage(own, src_pad, rel_id, relation)
-    gq, dst_grad = target_stage(nxt, q, dst_pad, weights, counts)
+    gq, dst_grad, rel_grad = target_stage(
+        nxt, q, s, dst_pad, weights, rel_id, counts, relation.shape[0]
+    )
+    rel_total = reduce_relation(rel_grad)
     moved = shift_dom(collect_x(dst_grad).astype(bf16), 1)
-    src_grad, rel_grad = back_stage(gq, s, src_pad, rel_id, relation)
-    rel_total = reduce_relation(rel_grad)
+    src_grad = back_stage(gq, src_pad, rel_id, relation)
     total = collect_x(src_grad) + moved.astype(f32)
     grads = total[:256] + swap_z(total[256:].astype(bf16)).astype(f32)
     entity_new, entity_accum_new = rowwise(entity, entity_accum, grads)

time: 167 us -> 160 us (0.958)
  the two profiles are of different devices: /device:TPU:1 before, /device:TPU:14 now
where the time goes in v4:
time: 160 us; the launch traced here: 159 us
  Pallas kernels  48.6 us (30%)
  waiting for transfers between devices  35.2 us (22%)
  starting transfers between devices  34.7 us (22%)
  blocking collectives  24 us (15%)
  other arithmetic  10.6 us (7%)
  local copies, waits for them, and re-layouts  4.33 us (3%)
    pallas_call x1, Pallas kernels, score_side(): pl.pallas_call(score_kernel, grid_spec=pltpu.PrefetchScalarGridSpec(num_s...  27.4 us
    all_to_all x1, blocking collectives, reduce_relation(): got = lax.all_to_all(grad.reshape(32, -1, D), 'dom', 0, 0)  24 us
    ppermute x9, waiting for transfers between devices, shift_x(): return lax.ppermute(block, 'rep', [(i, (i + 2 * by) % 8) for i in range(8)])  15.2 us
    ppermute x2, waiting for transfers between devices, swap_z(): return lax.ppermute(block, 'rep', [(i, i ^ 1) for i in range(8)])  13.9 us
    ppermute x9, starting transfers between devices, shift_x(): return lax.ppermute(block, 'rep', [(i, (i + 2 * by) % 8) for i in range(8)])  9.54 us
    pallas_call x1, Pallas kernels, make_queries(): pl.pallas_call(query_kernel, grid_spec=pltpu.PrefetchScalarGridSpec(num_s...  9.53 us
    all_to_all x1, starting transfers between devices, reduce_relation(): lax.all_to_all(jnp.broadcast_to(mine, (8,) + mine.shape), 'rep', 0, 0)  9.42 us
    ppermute x2, starting transfers between devices, swap_z(): return lax.ppermute(block, 'rep', [(i, i ^ 1) for i in range(8)])  7.7 us
  transfers between devices with their start and end apart: 19, of which 9 were waited for; matrix products, arithmetic and copies ran while one was open for 4% of the time, Pallas kernels for 12%

profile of v4, /device:TPU:14, one launch (start us, length us, event | category | flops | bytes accessed | tf_op | source)
XLA Modules:
  0.0 159.0 jit_solution(1933447085511591002)
XLA Ops:
  0.6 1.0 convert_element_type.42
  1.6 7.3 %collective-permute-start = (bf16[256,256]{1,0:T(8,128)(2,1)S(1)}, bf16[256,256]{1,0:T(8,128)(2,1)S(1)}, u32[]{:S(2)}, u32[]{:S(2)}) collective-permute-start(bf16[256,256]{1,0:T(8,128)(2,1)S(1)} %convert_element_type.42), channel_id=1, source_target_pairs={{0,1},{1,0},{2,3},{3,2},{4,5},{5,4},{6,7},{7,6},{8,9},{9,8},{10,11... | collective-permute-start | bytes 393224 | tf_op jit(solution)/shard_map/ppermute | solution.py:343
  9.5 0.7 fusion.6
  10.3 2.2 %collective-permute-done.after_ref = bf16[256,256]{1,0:T(8,128)(2,1)S(1)} collective-permute-done((bf16[256,256]{1,0:T(8,128)(2,1)S(1)}, bf16[256,256]{1,0:T(8,128)(2,1)S(1)}, u32[]{:S(2)}, u32[]{:S(2)}) %collective-permute-start) | collective-permute-done | bytes 131104 | tf_op jit(solution)/shard_map/ppermute | solution.py:343
  12.5 0.6 collective-permute-start.6
  13.1 2.4 %collective-permute-start.4 = (bf16[512,256]{1,0:T(8,128)(2,1)S(1)}, bf16[512,256]{1,0:T(8,128)(2,1)S(1)}, u32[]{:S(2)}, u32[]{:S(2)}) collective-permute-start(bf16[512,256]{1,0:T(8,128)(2,1)S(1)} %pad_maximum_fusion.1.refs_0_), channel_id=1, source_target_pairs={{0,4},{1,5},{2,6},{3,7},{4,0},{5,1},{6,2},{7,3},{8,12},{9,13},{10,... | collective-permute-start | bytes 786440 | tf_op jit(solution)/shard_map/ppermute | solution.py:347
  15.5 0.8 fusion.2
  16.5 0.5 copy-done.7
  17.1 2.6 %neg_weights.1.refs_6_ = f32[4,2048,2]{2,1,0:T(8,128)S(1)} custom-call(s32[4,1,1024]{2,1,0:T(1,128)S(1)} %reshape.41.neg_ref, bf16[256,256]{1,0:T(8,128)(2,1)S(1)} %collective-permute-done.after_ref), custom_call_target="tpu_custom_call" | custom-call | flops 1500000000 | bytes 10500000 | tf_op jit(solution)/shard_map/neg_weights/pallas_call | solution.py:70
  19.6 1.9 %copy-done.5 = f32[4,2048,2]{2,1,0:T(8,128)} copy-done((f32[4,2048,2]{2,1,0:T(8,128)}, f32[4,2048,2]{2,1,0:T(8,128)S(1)}, u32[]{:S(2)}) %copy-start.5) | copy-done | bytes 65560
  21.6 0.3 collective-permute-done.6.refs_3_
  21.8 0.3 collective-permute-start.7
  22.1 1.7 %collective-permute-done.4.refs_2_ = bf16[512,256]{1,0:T(8,128)(2,1)S(1)} collective-permute-done((bf16[512,256]{1,0:T(8,128)(2,1)S(1)}, bf16[512,256]{1,0:T(8,128)(2,1)S(1)}, u32[]{:S(2)}, u32[]{:S(2)}) %collective-permute-start.4) | collective-permute-done | bytes 262176 | tf_op jit(solution)/shard_map/ppermute | solution.py:347
  23.8 1.8 %collective-permute-start.5 = (bf16[512,256]{1,0:T(8,128)(2,1)S(1)}, bf16[512,256]{1,0:T(8,128)(2,1)S(1)}, u32[]{:S(2)}, u32[]{:S(2)}) collective-permute-start(bf16[512,256]{1,0:T(8,128)(2,1)S(1)} %collective-permute-done.4.refs_2_), channel_id=1, source_target_pairs={{0,248},{8,0},{16,8},{24,16},{32,24},{40,32},{48,40},{56,48},{64,5... | collective-permute-start | bytes 786440 | tf_op jit(solution)/shard_map/ppermute | solution.py:339
  25.6 1.7 %collective-permute-done.2.refs_1_ = bf16[512,256]{1,0:T(8,128)(2,1)S(1)} collective-permute-done((bf16[512,256]{1,0:T(8,128)(2,1)S(1)}, bf16[512,256]{1,0:T(8,128)(2,1)S(1)}, u32[]{:S(2)}, u32[]{:S(2)}) %collective-permute-start.2) | collective-permute-done | bytes 262176 | tf_op jit(solution)/shard_map/ppermute | solution.py:347
  27.3 0.5 collective-permute-start.3
  27.8 9.5 %queries.1 = (bf16[4096,256]{1,0:T(8,128)(2,1)S(1)}, bf16[256,4096]{1,0:T(8,128)(2,1)}) custom-call(s32[4]{0:T(128)S(1)} %copy-done.1, bf16[512,256]{1,0:T(8,128)(2,1)S(1)} %pad_maximum_fusion.1.refs_0_, bf16[512,256]{1,0:T(8,128)(2,1)S(1)} %collective-permute-done.2.refs_1_, bf16[512,256]{1,0:T(8,128)(2,1)S(1)} %collective-permute-done.4.refs_2_, ...), custom_call_target="tpu_custom_call" | custom-call | flops 4499999744 | bytes 31500000 | tf_op jit(solution)/shard_map/queries/pallas_call | solution.py:108
  37.3 27.4 %scores.1 = (bf16[256,4096]{1,0:T(8,128)(2,1)S(1)}, bf16[512,256]{1,0:T(8,128)(2,1)S(1)}, bf16[512,256]{1,0:T(8,128)(2,1)S(1)}, bf16[512,256]{1,0:T(8,128)(2,1)S(1)}, bf16[512,256]{1,0:T(8,128)(2,1)S(1)}) custom-call(s32[1]{0:T(128)S(6)} %copy.17.cnt_ref, bf16[512,256]{1,0:T(8,128)(2,1)S(1)} %collective-permute-done.1.refs_0_, ...), custom_call_target="tpu_custom_call" | custom-call | flops 14000000000 | bytes 98000000 | tf_op jit(solution)/shard_map/scores/pallas_call | solution.py:219
  64.8 2.3 %operator_grads.1 = bf16[4,256,256]{2,1,0:T(8,128)(2,1)S(1)} custom-call(s32[4]{0:T(128)S(1)} %copy-done.1, bf16[256,4096]{1,0:T(8,128)(2,1)S(1)} %get-tuple-element.16.gq_ref, bf16[4096,256]{1,0:T(8,128)(2,1)S(1)} %get-tuple-element.25.s_ref), custom_call_target="tpu_custom_call" | custom-call | flops 1000000000 | bytes 7000000 | tf_op jit(solution)/shard_map/operator_grads/pallas_call | solution.py:272
  67.1 24.0 %all_to_all.15 = bf16[32,32,256]{2,1,0:T(8,128)(2,1)} all-to-all(bf16[32,32,256]{2,1,0:T(8,128)(2,1)S(1)} %bitcast.8), channel_id=1, replica_groups=mesh['dom'=32,'rep'=8] {'dom'}, dimensions={0} | all-to-all | bytes 1048576 | tf_op jit(solution)/shard_map/all_to_all | solution.py:366
  91.0 1.1 reduce_sum.40
  92.1 0.7 broadcast_in_dim.8
  92.8 9.4 %all-to-all-start.1 = ((bf16[8,32,256]{2,1,0:T(8,128)(2,1)}), bf16[8,32,256]{2,1,0:T(8,128)(2,1)}, u32[]{:S(2)}, u32[]{:S(2)}) async-start(bf16[8,32,256]{2,1,0:T(8,128)(2,1)} %broadcast_in_dim.8), calls=%async_computation.1 | async-start | bytes 262144 | tf_op jit(solution)/shard_map/all_to_all | solution.py:368
  102.2 0.1 collective-permute-start.11
  102.3 2.9 %collective-permute-start.12 = (bf16[512,256]{1,0:T(8,128)(2,1)}, bf16[512,256]{1,0:T(8,128)(2,1)}, u32[]{:S(2)}, u32[]{:S(2)}) collective-permute-start(bf16[512,256]{1,0:T(8,128)(2,1)} %copy-done.3), channel_id=1, source_target_pairs={{0,4},{1,5},{2,6},{3,7},{4,0},{5,1},{6,2},{7,3},{8,12},{9,13},{10,... | collective-permute-start | bytes 786440 | tf_op jit(solution)/shard_map/ppermute | solution.py:347
  105.2 6.1 %all-to-all-done.1 = bf16[8,32,256]{2,1,0:T(8,128)(2,1)} async-done(((bf16[8,32,256]{2,1,0:T(8,128)(2,1)}), bf16[8,32,256]{2,1,0:T(8,128)(2,1)}, u32[]{:S(2)}, u32[]{:S(2)}) %all-to-all-start.1) | async-done | bytes 131104 | tf_op jit(solution)/shard_map/all_to_all | solution.py:368
  111.3 0.9 convert_reduce_fusion
  112.2 0.8 broadcast_in_dim.9
  113.1 5.4 %all-to-all-start.2 = ((f32[16,32,256]{2,1,0:T(8,128)}), f32[16,32,256]{2,1,0:T(8,128)}, u32[]{:S(2)}, u32[]{:S(2)}) async-start(f32[16,32,256]{2,1,0:T(8,128)} %broadcast_in_dim.9), calls=%async_computation.2 | async-start | bytes 1048576 | tf_op jit(solution)/shard_map/all_to_all | solution.py:371
  118.5 6.9 %source_grads.1 = (bf16[512,256]{1,0:T(8,128)(2,1)S(1)}, bf16[512,256]{1,0:T(8,128)(2,1)S(1)}, bf16[512,256]{1,0:T(8,128)(2,1)S(1)}, bf16[512,256]{1,0:T(8,128)(2,1)S(1)}) custom-call(s32[4]{0:T(128)S(1)} %copy-done.1, bf16[256,4096]{1,0:T(8,128)(2,1)S(1)} %get-tuple-element.16.gq_ref, s32[4,1,1024]{2,1,0:T(1,128)S(1)} %reshape.42.src_ref, ...), custom_call_target="tpu_custom_call" | custom-call | flops 4000000000 | bytes 28000000 | tf_op jit(solution)/shard_map/source_grads/pallas_call | solution.py:312
  125.4 2.2 %collective-permute-start.8 = (bf16[512,256]{1,0:T(8,128)(2,1)S(1)}, bf16[512,256]{1,0:T(8,128)(2,1)S(1)}, u32[]{:S(2)}, u32[]{:S(2)}) collective-permute-start(bf16[512,256]{1,0:T(8,128)(2,1)S(1)} %get-tuple-element.18), channel_id=1, source_target_pairs={{0,2},{1,3},{2,4},{3,5},{4,6},{5,7},{6,0},{7,1},{8,10},{9,11},{10,... | collective-permute-start | bytes 786440 | tf_op jit(solution)/shard_map/ppermute | solution.py:347
  127.6 0.6 collective-permute-start.9
  128.2 0.7 collective-permute-start.10
  128.9 1.3 add_convert_fusion
  130.3 7.9 %collective-permute-done.8 = bf16[512,256]{1,0:T(8,128)(2,1)S(1)} collective-permute-done((bf16[512,256]{1,0:T(8,128)(2,1)S(1)}, bf16[512,256]{1,0:T(8,128)(2,1)S(1)}, u32[]{:S(2)}, u32[]{:S(2)}) %collective-permute-start.8) | collective-permute-done | bytes 262176 | tf_op jit(solution)/shard_map/ppermute | solution.py:347
  138.2 0.1 collective-permute-done.9
  138.3 3.5 %collective-permute-done.10 = bf16[512,256]{1,0:T(8,128)(2,1)S(1)} collective-permute-done((bf16[512,256]{1,0:T(8,128)(2,1)S(1)}, bf16[512,256]{1,0:T(8,128)(2,1)S(1)}, u32[]{:S(2)}, u32[]{:S(2)}) %collective-permute-start.10) | collective-permute-done | bytes 262176 | tf_op jit(solution)/shard_map/ppermute | solution.py:347
  141.8 0.2 convert_add_fusion
  142.0 0.4 collective-permute-start.15
  142.4 11.7 %collective-permute-done.15 = bf16[256,256]{1,0:T(8,128)(2,1)S(1)} collective-permute-done((bf16[256,256]{1,0:T(8,128)(2,1)S(1)}, bf16[256,256]{1,0:T(8,128)(2,1)S(1)}, u32[]{:S(2)}, u32[]{:S(2)}) %collective-permute-start.15) | collective-permute-done | bytes 131104 | tf_op jit(solution)/shard_map/ppermute | solution.py:343
  154.2 0.1 multiply_reduce_fusion.1
  154.3 0.6 fusion.8
  154.9 0.8 divide_subtract_fusion.1
  155.7 1.1 select_bitcast_fusion.1
  156.8 0.2 multiply_reduce_fusion
  157.1 0.1 div.49
  157.2 0.6 fusion.7
  157.8 1.2 divide_subtract_fusion
  (47 shorter events, 0.6 us)
Async XLA Ops:
  1.6 10.9 %collective-permute-start = (bf16[256,256]{1,0:T(8,128)(2,1)S(1)}, bf16[256,256]{1,0:T(8,128)(2,1)S(1)}, u32[]{:S(2)}, u32[]{:S(2)}) collective-permute-start(bf16[256,256]{1,0:T(8,128)(2,1)S(1)} %convert_element_type.42), channel_id=1, source_target_pairs={{0,1},{1,0},{2,3},{3,2},{4,5},{5,4},{6,7},{7,6},{8,9},{9,8},{10,11... | collective-permute-start | bytes 393224 | tf_op jit(solution)/shard_map/ppermute | solution.py:343
  12.5 9.3 %collective-permute-start.6 = (bf16[512,256]{1,0:T(8,128)(2,1)S(1)}, bf16[512,256]{1,0:T(8,128)(2,1)S(1)}, u32[]{:S(2)}, u32[]{:S(2)}) collective-permute-start(bf16[512,256]{1,0:T(8,128)(2,1)S(1)} %pad_maximum_fusion.1.refs_0_), channel_id=1, source_target_pairs={{0,2},{1,3},{2,4},{3,5},{4,6},{5,7},{6,0},{7,1},{8,10},{9,11},{10,... | collective-permute-start | bytes 786440 | tf_op jit(solution)/shard_map/ppermute | solution.py:347
  13.1 10.8 %collective-permute-start.4 = (bf16[512,256]{1,0:T(8,128)(2,1)S(1)}, bf16[512,256]{1,0:T(8,128)(2,1)S(1)}, u32[]{:S(2)}, u32[]{:S(2)}) collective-permute-start(bf16[512,256]{1,0:T(8,128)(2,1)S(1)} %pad_maximum_fusion.1.refs_0_), channel_id=1, source_target_pairs={{0,4},{1,5},{2,6},{3,7},{4,0},{5,1},{6,2},{7,3},{8,12},{9,13},{10,... | collective-permute-start | bytes 786440 | tf_op jit(solution)/shard_map/ppermute | solution.py:347
  15.5 11.8 %collective-permute-start.2 = (bf16[512,256]{1,0:T(8,128)(2,1)S(1)}, bf16[512,256]{1,0:T(8,128)(2,1)S(1)}, u32[]{:S(2)}, u32[]{:S(2)}) collective-permute-start(bf16[512,256]{1,0:T(8,128)(2,1)S(1)} %pad_maximum_fusion.1.refs_0_), channel_id=1, source_target_pairs={{0,6},{1,7},{2,0},{3,1},{4,2},{5,3},{6,4},{7,5},{8,14},{9,15},{10,... | collective-permute-start | bytes 786440 | tf_op jit(solution)/shard_map/ppermute | solution.py:347
  16.3 0.6 copy-start.7
  16.9 10.8 %copy-start = (f32[4,256,256]{2,1,0:T(8,128)S(1)}, f32[4,256,256]{2,1,0:T(8,128)}, u32[]{:S(2)}) copy-start(f32[4,256,256]{2,1,0:T(8,128)} %mat_ref.1) | copy-start | bytes 3145732
  17.0 10.8 %copy-start.1 = (s32[4]{0:T(128)S(1)}, s32[4]{0:T(128)}, u32[]{:S(2)}) copy-start(s32[4]{0:T(128)} %rel_ref.5) | copy-start | bytes 52
  17.0 20.3 %collective-permute-start.1 = (bf16[512,256]{1,0:T(8,128)(2,1)S(1)}, bf16[512,256]{1,0:T(8,128)(2,1)S(1)}, u32[]{:S(2)}, u32[]{:S(2)}) collective-permute-start(bf16[512,256]{1,0:T(8,128)(2,1)S(1)} %pad_maximum_fusion.1.refs_0_), channel_id=1, source_target_pairs={{0,248},{8,0},{16,8},{24,16},{32,24},{40,32},{48,40},{56,48},{64,5... | collective-permute-start | bytes 786440 | tf_op jit(solution)/shard_map/ppermute | solution.py:339
  19.6 1.9 %copy-start.5 = (f32[4,2048,2]{2,1,0:T(8,128)}, f32[4,2048,2]{2,1,0:T(8,128)S(1)}, u32[]{:S(2)}) copy-start(f32[4,2048,2]{2,1,0:T(8,128)S(1)} %neg_weights.1.refs_6_) | copy-start | bytes 196612
  21.8 15.5 %collective-permute-start.7 = (bf16[512,256]{1,0:T(8,128)(2,1)S(1)}, bf16[512,256]{1,0:T(8,128)(2,1)S(1)}, u32[]{:S(2)}, u32[]{:S(2)}) collective-permute-start(bf16[512,256]{1,0:T(8,128)(2,1)S(1)} %collective-permute-done.6.refs_3_), channel_id=1, source_target_pairs={{0,248},{8,0},{16,8},{24,16},{32,24},{40,32},{48,40},{56,48},{64,5... | collective-permute-start | bytes 786440 | tf_op jit(solution)/shard_map/ppermute | solution.py:339
  23.8 13.5 %collective-permute-start.5 = (bf16[512,256]{1,0:T(8,128)(2,1)S(1)}, bf16[512,256]{1,0:T(8,128)(2,1)S(1)}, u32[]{:S(2)}, u32[]{:S(2)}) collective-permute-start(bf16[512,256]{1,0:T(8,128)(2,1)S(1)} %collective-permute-done.4.refs_2_), channel_id=1, source_target_pairs={{0,248},{8,0},{16,8},{24,16},{32,24},{40,32},{48,40},{56,48},{64,5... | collective-permute-start | bytes 786440 | tf_op jit(solution)/shard_map/ppermute | solution.py:339
  27.3 10.0 %collective-permute-start.3 = (bf16[512,256]{1,0:T(8,128)(2,1)S(1)}, bf16[512,256]{1,0:T(8,128)(2,1)S(1)}, u32[]{:S(2)}, u32[]{:S(2)}) collective-permute-start(bf16[512,256]{1,0:T(8,128)(2,1)S(1)} %collective-permute-done.2.refs_1_), channel_id=1, source_target_pairs={{0,248},{8,0},{16,8},{24,16},{32,24},{40,32},{48,40},{56,48},{64,5... | collective-permute-start | bytes 786440 | tf_op jit(solution)/shard_map/ppermute | solution.py:339
  64.7 2.3 %copy-start.2 = (bf16[512,256]{1,0:T(8,128)(2,1)}, bf16[512,256]{1,0:T(8,128)(2,1)S(1)}, u32[]{:S(2)}) copy-start(bf16[512,256]{1,0:T(8,128)(2,1)S(1)} %get-tuple-element.24) | copy-start | bytes 786436
  64.7 2.3 %copy-start.3 = (bf16[512,256]{1,0:T(8,128)(2,1)}, bf16[512,256]{1,0:T(8,128)(2,1)S(1)}, u32[]{:S(2)}) copy-start(bf16[512,256]{1,0:T(8,128)(2,1)S(1)} %get-tuple-element.23) | copy-start | bytes 786436
  64.7 2.3 %copy-start.4 = (bf16[512,256]{1,0:T(8,128)(2,1)}, bf16[512,256]{1,0:T(8,128)(2,1)S(1)}, u32[]{:S(2)}) copy-start(bf16[512,256]{1,0:T(8,128)(2,1)S(1)} %get-tuple-element.22) | copy-start | bytes 786436
  64.8 37.5 %copy-start.8 = (s32[4,1024]{1,0:T(4,128)S(1)}, s32[4,1024]{1,0:T(4,128)}, u32[]{:S(2)}) copy-start(s32[4,1024]{1,0:T(4,128)} %copy-done.7) | copy-start | bytes 49156
  92.8 18.5 %all-to-all-start.1 = ((bf16[8,32,256]{2,1,0:T(8,128)(2,1)}), bf16[8,32,256]{2,1,0:T(8,128)(2,1)}, u32[]{:S(2)}, u32[]{:S(2)}) async-start(bf16[8,32,256]{2,1,0:T(8,128)(2,1)} %broadcast_in_dim.8), calls=%async_computation.1 | async-start | bytes 262144 | tf_op jit(solution)/shard_map/all_to_all | solution.py:368
  102.2 26.0 %collective-permute-start.11 = (bf16[512,256]{1,0:T(8,128)(2,1)}, bf16[512,256]{1,0:T(8,128)(2,1)}, u32[]{:S(2)}, u32[]{:S(2)}) collective-permute-start(bf16[512,256]{1,0:T(8,128)(2,1)} %copy-done.4), channel_id=1, source_target_pairs={{0,2},{1,3},{2,4},{3,5},{4,6},{5,7},{6,0},{7,1},{8,10},{9,11},{10,... | collective-permute-start | bytes 786440 | tf_op jit(solution)/shard_map/ppermute | solution.py:347
  102.3 26.6 %collective-permute-start.12 = (bf16[512,256]{1,0:T(8,128)(2,1)}, bf16[512,256]{1,0:T(8,128)(2,1)}, u32[]{:S(2)}, u32[]{:S(2)}) collective-permute-start(bf16[512,256]{1,0:T(8,128)(2,1)} %copy-done.3), channel_id=1, source_target_pairs={{0,4},{1,5},{2,6},{3,7},{4,0},{5,1},{6,2},{7,3},{8,12},{9,13},{10,... | collective-permute-start | bytes 786440 | tf_op jit(solution)/shard_map/ppermute | solution.py:347
  105.2 23.7 %collective-permute-start.13 = (bf16[512,256]{1,0:T(8,128)(2,1)}, bf16[512,256]{1,0:T(8,128)(2,1)}, u32[]{:S(2)}, u32[]{:S(2)}) collective-permute-start(bf16[512,256]{1,0:T(8,128)(2,1)} %copy-done.2), channel_id=1, source_target_pairs={{0,6},{1,7},{2,0},{3,1},{4,2},{5,3},{6,4},{7,5},{8,14},{9,15},{10,... | collective-permute-start | bytes 786440 | tf_op jit(solution)/shard_map/ppermute | solution.py:347
  113.1 29.4 %all-to-all-start.2 = ((f32[16,32,256]{2,1,0:T(8,128)}), f32[16,32,256]{2,1,0:T(8,128)}, u32[]{:S(2)}, u32[]{:S(2)}) async-start(f32[16,32,256]{2,1,0:T(8,128)} %broadcast_in_dim.9), calls=%async_computation.2 | async-start | bytes 1048576 | tf_op jit(solution)/shard_map/all_to_all | solution.py:371
  125.3 29.0 %copy-start.10 = (f32[256]{0:T(256)S(1)}, f32[256]{0:T(256)}, u32[]{:S(2)}) copy-start(f32[256]{0:T(256)} %param.10) | copy-start | bytes 3076
  125.3 29.5 %copy-start.6 = (f32[256,256]{1,0:T(8,128)S(1)}, f32[256,256]{1,0:T(8,128)}, u32[]{:S(2)}) copy-start(f32[256,256]{1,0:T(8,128)} %param.9) | copy-start | bytes 786436
  125.4 12.8 %collective-permute-start.8 = (bf16[512,256]{1,0:T(8,128)(2,1)S(1)}, bf16[512,256]{1,0:T(8,128)(2,1)S(1)}, u32[]{:S(2)}, u32[]{:S(2)}) collective-permute-start(bf16[512,256]{1,0:T(8,128)(2,1)S(1)} %get-tuple-element.18), channel_id=1, source_target_pairs={{0,2},{1,3},{2,4},{3,5},{4,6},{5,7},{6,0},{7,1},{8,10},{9,11},{10,... | collective-permute-start | bytes 786440 | tf_op jit(solution)/shard_map/ppermute | solution.py:347
  127.6 10.7 %collective-permute-start.9 = (bf16[512,256]{1,0:T(8,128)(2,1)S(1)}, bf16[512,256]{1,0:T(8,128)(2,1)S(1)}, u32[]{:S(2)}, u32[]{:S(2)}) collective-permute-start(bf16[512,256]{1,0:T(8,128)(2,1)S(1)} %get-tuple-element.19), channel_id=1, source_target_pairs={{0,4},{1,5},{2,6},{3,7},{4,0},{5,1},{6,2},{7,3},{8,12},{9,13},{10,... | collective-permute-start | bytes 786440 | tf_op jit(solution)/shard_map/ppermute | solution.py:347
  128.2 13.6 %collective-permute-start.10 = (bf16[512,256]{1,0:T(8,128)(2,1)S(1)}, bf16[512,256]{1,0:T(8,128)(2,1)S(1)}, u32[]{:S(2)}, u32[]{:S(2)}) collective-permute-start(bf16[512,256]{1,0:T(8,128)(2,1)S(1)} %get-tuple-element.20), channel_id=1, source_target_pairs={{0,6},{1,7},{2,0},{3,1},{4,2},{5,3},{6,4},{7,5},{8,14},{9,15},{10,... | collective-permute-start | bytes 786440 | tf_op jit(solution)/shard_map/ppermute | solution.py:347
  130.2 11.6 %collective-permute-start.14 = (bf16[512,256]{1,0:T(8,128)(2,1)S(1)}, bf16[512,256]{1,0:T(8,128)(2,1)S(1)}, u32[]{:S(2)}, u32[]{:S(2)}) collective-permute-start(bf16[512,256]{1,0:T(8,128)(2,1)S(1)} %add_convert_fusion), channel_id=1, source_target_pairs={{0,8},{8,16},{16,24},{24,32},{32,40},{40,48},{48,56},{56,64},{64,7... | collective-permute-start | bytes 786440 | tf_op jit(solution)/shard_map/ppermute | solution.py:339
  142.0 12.2 %collective-permute-start.15 = (bf16[256,256]{1,0:T(8,128)(2,1)S(1)}, bf16[256,256]{1,0:T(8,128)(2,1)S(1)}, u32[]{:S(2)}, u32[]{:S(2)}) collective-permute-start(bf16[256,256]{1,0:T(8,128)(2,1)S(1)} %slice.17), channel_id=1, source_target_pairs={{0,1},{1,0},{2,3},{3,2},{4,5},{5,4},{6,7},{7,6},{8,9},{9,8},{10,11... | collective-permute-start | bytes 393224 | tf_op jit(solution)/shard_map/ppermute | solution.py:343
  142.4 13.2 %collective-permute-start.16 = (f32[16,32,256]{2,1,0:T(8,128)}, f32[16,32,256]{2,1,0:T(8,128)S(1)}, u32[]{:S(2)}, u32[]{:S(2)}) collective-permute-start(f32[16,32,256]{2,1,0:T(8,128)} %all-to-all-done.2), channel_id=1, source_target_pairs={{0,8},{8,0},{16,24},{24,16},{32,40},{40,32},{48,56},{56,48},{64,72... | collective-permute-start | bytes 1572872 | tf_op jit(solution)/shard_map/ppermute | solution.py:374
  155.7 1.5 copy-start.9

commit v5 on v4

--- a/solution.py
+++ b/solution.py
@@ -53,7 +53,7 @@
     return parts[b * BLK // PART][first : first + BLK, :]
 
 
-def count_kernel(neg_ref, after_ref, out_ref):
+def count_kernel(neg_ref, out_ref):
     rows = lax.broadcasted_iota(jnp.int32, (BLK, 128), 0).astype(jnp.int16)
     for b in range(NBLK):
         hits = None
@@ -66,20 +66,17 @@
         out_ref[0, at, 1:2] = jnp.log2(count + 1.0)
 
 
-def neg_weights(neg_pad, after):
+def neg_weights(neg_pad):
     return pl.pallas_call(
         count_kernel,
         grid=(GROUPS,),
-        in_specs=[
-            pl.BlockSpec((1, 1, PAD), lambda g: (g, 0, 0)),
-            pl.BlockSpec(memory_space=pl.ANY),
-        ],
+        in_specs=[pl.BlockSpec((1, 1, PAD), lambda g: (g, 0, 0))],
         out_specs=pl.BlockSpec((1, ROWS, 2), lambda g: (g, 0, 0)),
         out_shape=jax.ShapeDtypeStruct((GROUPS, ROWS, 2), f32),
         compiler_params=params(),
         cost_estimate=cost(3),
         name="neg_weights",
-    )(neg_pad.reshape(GROUPS, 1, PAD), after)
+    )(neg_pad.reshape(GROUPS, 1, PAD))
 
 
 def query_kernel(rel_ref, *refs):
@@ -351,9 +348,43 @@
     return [pair] + [shift_x(pair, -k) for k in (1, 2, 3)]
 
 
-def collect_x(blocks):
-    got = [blocks[0]] + [shift_x(blocks[k], k) for k in (1, 2, 3)]
-    return sum(block.astype(f32) for block in got)
+def send_x(blocks):
+    return [blocks[0]] + [shift_x(blocks[k], k) for k in (1, 2, 3)]
+
+
+def add_up(blocks, after, dtype, copies=None):
+    stacked = len(blocks) == 1
+    shape = blocks[0].shape[1:] if stacked else blocks[0].shape
+    whole = pl.BlockSpec(memory_space=pltpu.VMEM)
+
+    def kernel(*refs):
+        out = refs[-1]
+        total = None
+        if stacked:
+            for i in range(blocks[0].shape[0]):
+                part = refs[0][i].astype(f32)
+                total = part if total is None else total + part
+            total = total.astype(dtype)
+        else:
+            for ref in refs[: len(blocks)]:
+                part = ref[...].astype(f32)
+                total = part if total is None else total + part
+            total = total.astype(dtype)
+        if copies is None:
+            out[...] = total
+        else:
+            for i in range(copies):
+                out[i] = total
+
+    return pl.pallas_call(
+        kernel,
+        in_specs=[whole] * len(blocks) + [pl.BlockSpec(memory_space=pl.ANY)],
+        out_specs=whole,
+        out_shape=jax.ShapeDtypeStruct(shape if copies is None else (copies,) + shape, dtype),
+        compiler_params=pltpu.CompilerParams(vmem_limit_bytes=16 * MB),
+        cost_estimate=cost(1),
+        name="add_up",
+    )(*blocks, after)
 
 
 def turned(index):
@@ -361,16 +392,9 @@
     return ((index - PART * (rep // 2)) % ROWS) ^ (256 * (rep % 2))
 
 
-def reduce_relation(grad):
-    kinds = grad.shape[0]
-    got = lax.all_to_all(grad.reshape(32, -1, D), "dom", 0, 0)
-    mine = jnp.sum(got.astype(f32), 0).astype(bf16)
-    every = lax.all_to_all(jnp.broadcast_to(mine, (8,) + mine.shape), "rep", 0, 0)
-    total = jnp.sum(every.astype(f32), 0)
+def spread_total(shares, kinds):
     cores = [[2 * i + c for i in range(16)] for c in range(2)]
-    half = lax.all_to_all(
-        jnp.broadcast_to(total, (16,) + total.shape), "dom", 0, 0, axis_index_groups=cores
-    )
+    half = lax.all_to_all(shares, "dom", 0, 0, axis_index_groups=cores)
     other = lax.ppermute(half, "dom", [(i, i ^ 1) for i in range(32)])
     second = lax.axis_index("dom") % 2 == 1
     pairs = [jnp.where(second, other, half), jnp.where(second, half, other)]
@@ -397,7 +421,7 @@
 def local_grads(own, nxt, relation, src_index, dst_index, neg_index, rel_id, counts):
     own, nxt = own.astype(bf16), nxt.astype(bf16)
     src_pad = pad_slots(src_index, -1)
-    weights = neg_weights(pad_slots(neg_index, -1), own)
+    weights = neg_weights(pad_slots(neg_index, -1))
     own = [own[k * PART : (k + 1) * PART] for k in range(PARTS)]
     nxt = [nxt[k * PART : (k + 1) * PART] for k in range(PARTS)]
     s, q = source_stage(own, src_pad, rel_id, relation)
@@ -418,15 +442,23 @@
     other = swap_z(ent_b)
     own = spread_x(jnp.concatenate([ent_b, other]))
     nxt = [shift_dom(block, -1) for block in own]
-    weights = neg_weights(neg_pad, other)
+    weights = neg_weights(neg_pad)
     s, q = source_stage(own, src_pad, rel_id, relation)
     gq, dst_grad, rel_grad = target_stage(
         nxt, q, s, dst_pad, weights, rel_id, counts, relation.shape[0]
     )
-    rel_total = reduce_relation(rel_grad)
-    moved = shift_dom(collect_x(dst_grad).astype(bf16), 1)
+    kinds = relation.shape[0]
+    dst_blocks = send_x(dst_grad)
+    got = lax.all_to_all(rel_grad.reshape(32, -1, D), "dom", 0, 0)
     src_grad = back_stage(gq, src_pad, rel_id, relation)
-    total = collect_x(src_grad) + moved.astype(f32)
+    src_blocks = send_x(src_grad)
+    mine = add_up([got], src_grad[0], bf16, 8)
+    every = lax.all_to_all(mine, "rep", 0, 0)
+    dst_sum = add_up(dst_blocks, mine, bf16)
+    moved = shift_dom(dst_sum, 1)
+    shares = add_up([every], dst_sum, f32, 16)
+    rel_total = spread_total(shares, kinds)
+    total = sum(block.astype(f32) for block in src_blocks + [moved])
     grads = total[:256] + swap_z(total[256:].astype(bf16)).astype(f32)
     entity_new, entity_accum_new = rowwise(entity, entity_accum, grads)
     relation_new, relation_accum_new = rowwise(relation, relation_accum, rel_total)

time: 160 us -> 153 us (0.956)
  the two profiles are of different devices: /device:TPU:14 before, /device:TPU:6 now
where the time goes in v5:
time: 153 us; the launch traced here: 152 us
  Pallas kernels  54.2 us (35%)
  starting transfers between devices  48.5 us (32%)
  waiting for transfers between devices  36.8 us (24%)
  other arithmetic  6.2 us (4%)
  local copies, waits for them, and re-layouts  4.82 us (3%)
  between operations  1.57 us (1%)
    pallas_call x1, Pallas kernels, score_side(): pl.pallas_call(score_kernel, grid_spec=pltpu.PrefetchScalarGridSpec(num_s...  28.3 us
    ppermute x2, waiting for transfers between devices, swap_z(): return lax.ppermute(block, 'rep', [(i, i ^ 1) for i in range(8)])  12.4 us
    ppermute x9, waiting for transfers between devices, shift_x(): return lax.ppermute(block, 'rep', [(i, (i + 2 * by) % 8) for i in range(8)])  12.3 us
    ppermute x5, starting transfers between devices, shift_dom(): lax.ppermute(block, 'dom', [(i, (i + by) % size) for i in range(size)])  10.6 us
    all_to_all x1, starting transfers between devices, on_device(): every = lax.all_to_all(mine, 'rep', 0, 0)  10.1 us
    pallas_call x1, Pallas kernels, make_queries(): pl.pallas_call(query_kernel, grid_spec=pltpu.PrefetchScalarGridSpec(num_s...  9.53 us
    ppermute x9, starting transfers between devices, shift_x(): return lax.ppermute(block, 'rep', [(i, (i + 2 * by) % 8) for i in range(8)])  9.28 us
    ppermute x2, starting transfers between devices, swap_z(): return lax.ppermute(block, 'rep', [(i, i ^ 1) for i in range(8)])  8.28 us
  transfers between devices with their start and end apart: 20, of which 8 were waited for; matrix products, arithmetic and copies ran while one was open for 2% of the time, Pallas kernels for 14%

profile of v5, /device:TPU:6, one launch (start us, length us, event | category | flops | bytes accessed | tf_op | source)
XLA Modules:
  0.0 152.1 jit_solution(9947548739596938855)
XLA Ops:
  0.6 1.0 convert_element_type.22
  1.6 7.3 %collective-permute-start = (bf16[256,256]{1,0:T(8,128)(2,1)S(1)}, bf16[256,256]{1,0:T(8,128)(2,1)S(1)}, u32[]{:S(2)}, u32[]{:S(2)}) collective-permute-start(bf16[256,256]{1,0:T(8,128)(2,1)S(1)} %convert_element_type.22), channel_id=1, source_target_pairs={{0,1},{1,0},{2,3},{3,2},{4,5},{5,4},{6,7},{7,6},{8,9},{9,8},{10,11... | collective-permute-start | bytes 393224 | tf_op jit(solution)/shard_map/ppermute | solution.py:340
  9.5 0.7 fusion.6
  10.3 2.2 %collective-permute-done = bf16[256,256]{1,0:T(8,128)(2,1)S(1)} collective-permute-done((bf16[256,256]{1,0:T(8,128)(2,1)S(1)}, bf16[256,256]{1,0:T(8,128)(2,1)S(1)}, u32[]{:S(2)}, u32[]{:S(2)}) %collective-permute-start) | collective-permute-done | bytes 131104 | tf_op jit(solution)/shard_map/ppermute | solution.py:340
  12.5 0.6 collective-permute-start.6
  13.1 2.4 %collective-permute-start.4 = (bf16[512,256]{1,0:T(8,128)(2,1)S(1)}, bf16[512,256]{1,0:T(8,128)(2,1)S(1)}, u32[]{:S(2)}, u32[]{:S(2)}) collective-permute-start(bf16[512,256]{1,0:T(8,128)(2,1)S(1)} %pad_maximum_fusion.1.refs_0_), channel_id=1, source_target_pairs={{0,4},{1,5},{2,6},{3,7},{4,0},{5,1},{6,2},{7,3},{8,12},{9,13},{10,... | collective-permute-start | bytes 786440 | tf_op jit(solution)/shard_map/ppermute | solution.py:344
  15.5 0.8 fusion.2
  16.5 2.6 %neg_weights.1.refs_6_ = f32[4,2048,2]{2,1,0:T(8,128)S(1)} custom-call(s32[4,1,1024]{2,1,0:T(1,128)S(1)} %reshape.41.neg_ref), custom_call_target="tpu_custom_call" | custom-call | flops 1500000000 | bytes 10500000 | tf_op jit(solution)/shard_map/neg_weights/pallas_call | solution.py:70
  19.1 2.0 %copy-done.8 = f32[4,2048,2]{2,1,0:T(8,128)} copy-done((f32[4,2048,2]{2,1,0:T(8,128)}, f32[4,2048,2]{2,1,0:T(8,128)S(1)}, u32[]{:S(2)}) %copy-start.8) | copy-done | bytes 65560
  21.0 3.5 %collective-permute-start.1 = (bf16[512,256]{1,0:T(8,128)(2,1)S(1)}, bf16[512,256]{1,0:T(8,128)(2,1)S(1)}, u32[]{:S(2)}, u32[]{:S(2)}) collective-permute-start(bf16[512,256]{1,0:T(8,128)(2,1)S(1)} %pad_maximum_fusion.1.refs_0_), channel_id=1, source_target_pairs={{0,248},{8,0},{16,8},{24,16},{32,24},{40,32},{48,40},{56,48},{64,5... | collective-permute-start | bytes 786440 | tf_op jit(solution)/shard_map/ppermute | solution.py:336
  24.6 2.1 %collective-permute-start.7 = (bf16[512,256]{1,0:T(8,128)(2,1)S(1)}, bf16[512,256]{1,0:T(8,128)(2,1)S(1)}, u32[]{:S(2)}, u32[]{:S(2)}) collective-permute-start(bf16[512,256]{1,0:T(8,128)(2,1)S(1)} %collective-permute-done.6.refs_3_), channel_id=1, source_target_pairs={{0,248},{8,0},{16,8},{24,16},{32,24},{40,32},{48,40},{56,48},{64,5... | collective-permute-start | bytes 786440 | tf_op jit(solution)/shard_map/ppermute | solution.py:336
  26.7 0.8 collective-permute-start.5
  27.5 4.2 %collective-permute-start.3 = (bf16[512,256]{1,0:T(8,128)(2,1)S(1)}, bf16[512,256]{1,0:T(8,128)(2,1)S(1)}, u32[]{:S(2)}, u32[]{:S(2)}) collective-permute-start(bf16[512,256]{1,0:T(8,128)(2,1)S(1)} %collective-permute-done.2.refs_1_), channel_id=1, source_target_pairs={{0,248},{8,0},{16,8},{24,16},{32,24},{40,32},{48,40},{56,48},{64,5... | collective-permute-start | bytes 786440 | tf_op jit(solution)/shard_map/ppermute | solution.py:336
  31.6 9.5 %queries.1 = (bf16[4096,256]{1,0:T(8,128)(2,1)S(1)}, bf16[256,4096]{1,0:T(8,128)(2,1)}) custom-call(s32[4]{0:T(128)S(1)} %copy-done.1, bf16[512,256]{1,0:T(8,128)(2,1)S(1)} %pad_maximum_fusion.1.refs_0_, bf16[512,256]{1,0:T(8,128)(2,1)S(1)} %collective-permute-done.2.refs_1_, bf16[512,256]{1,0:T(8,128)(2,1)S(1)} %collective-permute-done.4.refs_2_, ...), custom_call_target="tpu_custom_call" | custom-call | flops 4499999744 | bytes 31500000 | tf_op jit(solution)/shard_map/queries/pallas_call | solution.py:105
  41.2 28.3 %scores.1 = (bf16[256,4096]{1,0:T(8,128)(2,1)S(1)}, bf16[512,256]{1,0:T(8,128)(2,1)S(1)}, bf16[512,256]{1,0:T(8,128)(2,1)}, bf16[512,256]{1,0:T(8,128)(2,1)}, bf16[512,256]{1,0:T(8,128)(2,1)}) custom-call(s32[1]{0:T(128)S(6)} %copy.21.cnt_ref, bf16[512,256]{1,0:T(8,128)(2,1)S(1)} %collective-permute-done.1.refs_0_, ...), custom_call_target="tpu_custom_call" | custom-call | flops 14000000000 | bytes 98000000 | tf_op jit(solution)/shard_map/scores/pallas_call | solution.py:216
  69.5 3.1 %operator_grads.1 = bf16[4,256,256]{2,1,0:T(8,128)(2,1)} custom-call(s32[4]{0:T(128)S(1)} %copy-done.1, bf16[256,4096]{1,0:T(8,128)(2,1)S(1)} %get-tuple-element.16.gq_ref, bf16[4096,256]{1,0:T(8,128)(2,1)S(1)} %get-tuple-element.25.s_ref), custom_call_target="tpu_custom_call" | custom-call | flops 1000000000 | bytes 7000000 | tf_op jit(solution)/shard_map/operator_grads/pallas_call | solution.py:269
  72.5 5.4 %all-to-all-start = ((bf16[32,32,256]{2,1,0:T(8,128)(2,1)}), bf16[32,32,256]{2,1,0:T(8,128)(2,1)}, u32[]{:S(2)}, u32[]{:S(2)}) async-start(bf16[32,32,256]{2,1,0:T(8,128)(2,1)} %bitcast), calls=%async_computation | async-start | bytes 1048576 | tf_op jit(solution)/shard_map/all_to_all | solution.py:452
  77.9 1.8 %collective-permute-start.11 = (bf16[512,256]{1,0:T(8,128)(2,1)}, bf16[512,256]{1,0:T(8,128)(2,1)}, u32[]{:S(2)}, u32[]{:S(2)}) collective-permute-start(bf16[512,256]{1,0:T(8,128)(2,1)} %get-tuple-element.22), channel_id=1, source_target_pairs={{0,2},{1,3},{2,4},{3,5},{4,6},{5,7},{6,0},{7,1},{8,10},{9,11},{10,... | collective-permute-start | bytes 786440 | tf_op jit(solution)/shard_map/ppermute | solution.py:344
  79.7 0.8 collective-permute-start.12
  80.5 0.2 collective-permute-start.13
  80.7 6.9 %source_grads.1 = (bf16[512,256]{1,0:T(8,128)(2,1)S(1)}, bf16[512,256]{1,0:T(8,128)(2,1)S(1)}, bf16[512,256]{1,0:T(8,128)(2,1)S(1)}, bf16[512,256]{1,0:T(8,128)(2,1)S(1)}) custom-call(s32[4]{0:T(128)S(1)} %copy-done.1, bf16[256,4096]{1,0:T(8,128)(2,1)S(1)} %get-tuple-element.16.gq_ref, s32[4,1,1024]{2,1,0:T(1,128)S(1)} %reshape.42.src_ref, ...), custom_call_target="tpu_custom_call" | custom-call | flops 4000000000 | bytes 28000000 | tf_op jit(solution)/shard_map/source_grads/pallas_call | solution.py:309
  87.6 0.7 copy-done.2
  88.2 0.7 copy-done.4
  89.0 0.7 copy-done.6
  89.7 4.1 %all-to-all-done.refs_0_ = bf16[32,32,256]{2,1,0:T(8,128)(2,1)} async-done(((bf16[32,32,256]{2,1,0:T(8,128)(2,1)}), bf16[32,32,256]{2,1,0:T(8,128)(2,1)}, u32[]{:S(2)}, u32[]{:S(2)}) %all-to-all-start) | async-done | bytes 524320 | tf_op jit(solution)/shard_map/all_to_all | solution.py:452
  93.8 1.8 %add_up.3.refs_4_ = bf16[8,32,256]{2,1,0:T(8,128)(2,1)} custom-call(bf16[32,32,256]{2,1,0:T(8,128)(2,1)} %all-to-all-done.refs_0_, bf16[512,256]{1,0:T(8,128)(2,1)S(1)} %get-tuple-element.17.refs_1_), custom_call_target="tpu_custom_call" | custom-call | flops 500000000 | bytes 3500000 | tf_op jit(solution)/shard_map/add_up/pallas_call | solution.py:379
  95.5 10.1 %all-to-all-start.1 = ((bf16[8,32,256]{2,1,0:T(8,128)(2,1)}), bf16[8,32,256]{2,1,0:T(8,128)(2,1)S(1)}, u32[]{:S(2)}, u32[]{:S(2)}) async-start(bf16[8,32,256]{2,1,0:T(8,128)(2,1)} %add_up.3.refs_4_), calls=%async_computation.1 | async-start | bytes 262144 | tf_op jit(solution)/shard_map/all_to_all | solution.py:456
  105.8 1.3 add_up.4.refs_1_
  107.1 7.3 %all-to-all-done.1.refs_0_ = bf16[8,32,256]{2,1,0:T(8,128)(2,1)S(1)} async-done(((bf16[8,32,256]{2,1,0:T(8,128)(2,1)}), bf16[8,32,256]{2,1,0:T(8,128)(2,1)S(1)}, u32[]{:S(2)}, u32[]{:S(2)}) %all-to-all-start.1) | async-done | bytes 131104 | tf_op jit(solution)/shard_map/all_to_all | solution.py:456
  114.4 0.9 add_up.5
  115.3 4.8 %all-to-all-start.2 = ((f32[16,32,256]{2,1,0:T(8,128)}), f32[16,32,256]{2,1,0:T(8,128)S(1)}, u32[]{:S(2)}, u32[]{:S(2)}) async-start(f32[16,32,256]{2,1,0:T(8,128)} %add_up.5), calls=%async_computation.2 | async-start | bytes 1048576 | tf_op jit(solution)/shard_map/all_to_all | solution.py:397
  120.1 2.4 %collective-permute-start.8 = (bf16[512,256]{1,0:T(8,128)(2,1)S(1)}, bf16[512,256]{1,0:T(8,128)(2,1)S(1)}, u32[]{:S(2)}, u32[]{:S(2)}) collective-permute-start(bf16[512,256]{1,0:T(8,128)(2,1)S(1)} %copy-done.7), channel_id=1, source_target_pairs={{0,2},{1,3},{2,4},{3,5},{4,6},{5,7},{6,0},{7,1},{8,10},{9,11},{10,... | collective-permute-start | bytes 786440 | tf_op jit(solution)/shard_map/ppermute | solution.py:344
  122.5 0.5 collective-permute-start.9
  123.0 0.7 collective-permute-start.10
  123.7 8.7 %collective-permute-done.8 = bf16[512,256]{1,0:T(8,128)(2,1)S(1)} collective-permute-done((bf16[512,256]{1,0:T(8,128)(2,1)S(1)}, bf16[512,256]{1,0:T(8,128)(2,1)S(1)}, u32[]{:S(2)}, u32[]{:S(2)}) %collective-permute-start.8) | collective-permute-done | bytes 262176 | tf_op jit(solution)/shard_map/ppermute | solution.py:344
  132.4 0.9 collective-permute-done.9
  133.2 2.7 %collective-permute-done.10 = bf16[512,256]{1,0:T(8,128)(2,1)S(1)} collective-permute-done((bf16[512,256]{1,0:T(8,128)(2,1)S(1)}, bf16[512,256]{1,0:T(8,128)(2,1)S(1)}, u32[]{:S(2)}, u32[]{:S(2)}) %collective-permute-start.10) | collective-permute-done | bytes 262176 | tf_op jit(solution)/shard_map/ppermute | solution.py:344
  136.0 0.6 collective-permute-done.14
  136.5 0.2 convert_add_fusion
  136.7 1.0 collective-permute-start.15
  137.7 10.3 %collective-permute-done.15 = bf16[256,256]{1,0:T(8,128)(2,1)S(1)} collective-permute-done((bf16[256,256]{1,0:T(8,128)(2,1)S(1)}, bf16[256,256]{1,0:T(8,128)(2,1)S(1)}, u32[]{:S(2)}, u32[]{:S(2)}) %collective-permute-start.15) | collective-permute-done | bytes 131104 | tf_op jit(solution)/shard_map/ppermute | solution.py:340
  148.0 0.1 multiply_reduce_fusion.1
  148.1 0.6 fusion.8
  148.7 0.8 divide_subtract_fusion.1
  149.6 0.2 multiply_reduce_fusion
  150.1 0.2 copy-done.12
  150.3 0.6 fusion.7
  150.9 1.2 divide_subtract_fusion
  (54 shorter events, 0.7 us)
Async XLA Ops:
  1.6 10.9 %collective-permute-start = (bf16[256,256]{1,0:T(8,128)(2,1)S(1)}, bf16[256,256]{1,0:T(8,128)(2,1)S(1)}, u32[]{:S(2)}, u32[]{:S(2)}) collective-permute-start(bf16[256,256]{1,0:T(8,128)(2,1)S(1)} %convert_element_type.22), channel_id=1, source_target_pairs={{0,1},{1,0},{2,3},{3,2},{4,5},{5,4},{6,7},{7,6},{8,9},{9,8},{10,11... | collective-permute-start | bytes 393224 | tf_op jit(solution)/shard_map/ppermute | solution.py:340
  12.5 12.1 %collective-permute-start.6 = (bf16[512,256]{1,0:T(8,128)(2,1)S(1)}, bf16[512,256]{1,0:T(8,128)(2,1)S(1)}, u32[]{:S(2)}, u32[]{:S(2)}) collective-permute-start(bf16[512,256]{1,0:T(8,128)(2,1)S(1)} %pad_maximum_fusion.1.refs_0_), channel_id=1, source_target_pairs={{0,2},{1,3},{2,4},{3,5},{4,6},{5,7},{6,0},{7,1},{8,10},{9,11},{10,... | collective-permute-start | bytes 786440 | tf_op jit(solution)/shard_map/ppermute | solution.py:344
  13.1 13.6 %collective-permute-start.4 = (bf16[512,256]{1,0:T(8,128)(2,1)S(1)}, bf16[512,256]{1,0:T(8,128)(2,1)S(1)}, u32[]{:S(2)}, u32[]{:S(2)}) collective-permute-start(bf16[512,256]{1,0:T(8,128)(2,1)S(1)} %pad_maximum_fusion.1.refs_0_), channel_id=1, source_target_pairs={{0,4},{1,5},{2,6},{3,7},{4,0},{5,1},{6,2},{7,3},{8,12},{9,13},{10,... | collective-permute-start | bytes 786440 | tf_op jit(solution)/shard_map/ppermute | solution.py:344
  15.5 12.0 %collective-permute-start.2 = (bf16[512,256]{1,0:T(8,128)(2,1)S(1)}, bf16[512,256]{1,0:T(8,128)(2,1)S(1)}, u32[]{:S(2)}, u32[]{:S(2)}) collective-permute-start(bf16[512,256]{1,0:T(8,128)(2,1)S(1)} %pad_maximum_fusion.1.refs_0_), channel_id=1, source_target_pairs={{0,6},{1,7},{2,0},{3,1},{4,2},{5,3},{6,4},{7,5},{8,14},{9,15},{10,... | collective-permute-start | bytes 786440 | tf_op jit(solution)/shard_map/ppermute | solution.py:344
  16.5 15.2 %copy-start = (f32[4,256,256]{2,1,0:T(8,128)S(1)}, f32[4,256,256]{2,1,0:T(8,128)}, u32[]{:S(2)}) copy-start(f32[4,256,256]{2,1,0:T(8,128)} %mat_ref.1) | copy-start | bytes 3145732
  16.5 15.2 %copy-start.1 = (s32[4]{0:T(128)S(1)}, s32[4]{0:T(128)}, u32[]{:S(2)}) copy-start(s32[4]{0:T(128)} %rel_ref.5) | copy-start | bytes 52
  19.1 2.0 %copy-start.8 = (f32[4,2048,2]{2,1,0:T(8,128)}, f32[4,2048,2]{2,1,0:T(8,128)S(1)}, u32[]{:S(2)}) copy-start(f32[4,2048,2]{2,1,0:T(8,128)S(1)} %neg_weights.1.refs_6_) | copy-start | bytes 196612
  21.0 20.1 %collective-permute-start.1 = (bf16[512,256]{1,0:T(8,128)(2,1)S(1)}, bf16[512,256]{1,0:T(8,128)(2,1)S(1)}, u32[]{:S(2)}, u32[]{:S(2)}) collective-permute-start(bf16[512,256]{1,0:T(8,128)(2,1)S(1)} %pad_maximum_fusion.1.refs_0_), channel_id=1, source_target_pairs={{0,248},{8,0},{16,8},{24,16},{32,24},{40,32},{48,40},{56,48},{64,5... | collective-permute-start | bytes 786440 | tf_op jit(solution)/shard_map/ppermute | solution.py:336
  24.6 16.6 %collective-permute-start.7 = (bf16[512,256]{1,0:T(8,128)(2,1)S(1)}, bf16[512,256]{1,0:T(8,128)(2,1)S(1)}, u32[]{:S(2)}, u32[]{:S(2)}) collective-permute-start(bf16[512,256]{1,0:T(8,128)(2,1)S(1)} %collective-permute-done.6.refs_3_), channel_id=1, source_target_pairs={{0,248},{8,0},{16,8},{24,16},{32,24},{40,32},{48,40},{56,48},{64,5... | collective-permute-start | bytes 786440 | tf_op jit(solution)/shard_map/ppermute | solution.py:336
  26.7 14.5 %collective-permute-start.5 = (bf16[512,256]{1,0:T(8,128)(2,1)S(1)}, bf16[512,256]{1,0:T(8,128)(2,1)S(1)}, u32[]{:S(2)}, u32[]{:S(2)}) collective-permute-start(bf16[512,256]{1,0:T(8,128)(2,1)S(1)} %collective-permute-done.4.refs_2_), channel_id=1, source_target_pairs={{0,248},{8,0},{16,8},{24,16},{32,24},{40,32},{48,40},{56,48},{64,5... | collective-permute-start | bytes 786440 | tf_op jit(solution)/shard_map/ppermute | solution.py:336
  27.5 13.7 %collective-permute-start.3 = (bf16[512,256]{1,0:T(8,128)(2,1)S(1)}, bf16[512,256]{1,0:T(8,128)(2,1)S(1)}, u32[]{:S(2)}, u32[]{:S(2)}) collective-permute-start(bf16[512,256]{1,0:T(8,128)(2,1)S(1)} %collective-permute-done.2.refs_1_), channel_id=1, source_target_pairs={{0,248},{8,0},{16,8},{24,16},{32,24},{40,32},{48,40},{56,48},{64,5... | collective-permute-start | bytes 786440 | tf_op jit(solution)/shard_map/ppermute | solution.py:336
  69.5 3.1 %copy-start.9 = (bf16[512,256]{1,0:T(8,128)(2,1)}, bf16[512,256]{1,0:T(8,128)(2,1)S(1)}, u32[]{:S(2)}) copy-start(bf16[512,256]{1,0:T(8,128)(2,1)S(1)} %get-tuple-element.21.refs_0_) | copy-start | bytes 786436
  72.5 21.2 %all-to-all-start = ((bf16[32,32,256]{2,1,0:T(8,128)(2,1)}), bf16[32,32,256]{2,1,0:T(8,128)(2,1)}, u32[]{:S(2)}, u32[]{:S(2)}) async-start(bf16[32,32,256]{2,1,0:T(8,128)(2,1)} %bitcast), calls=%async_computation | async-start | bytes 1048576 | tf_op jit(solution)/shard_map/all_to_all | solution.py:452
  77.9 27.8 %collective-permute-start.11 = (bf16[512,256]{1,0:T(8,128)(2,1)}, bf16[512,256]{1,0:T(8,128)(2,1)}, u32[]{:S(2)}, u32[]{:S(2)}) collective-permute-start(bf16[512,256]{1,0:T(8,128)(2,1)} %get-tuple-element.22), channel_id=1, source_target_pairs={{0,2},{1,3},{2,4},{3,5},{4,6},{5,7},{6,0},{7,1},{8,10},{9,11},{10,... | collective-permute-start | bytes 786440 | tf_op jit(solution)/shard_map/ppermute | solution.py:344
  79.7 26.0 %collective-permute-start.12 = (bf16[512,256]{1,0:T(8,128)(2,1)}, bf16[512,256]{1,0:T(8,128)(2,1)}, u32[]{:S(2)}, u32[]{:S(2)}) collective-permute-start(bf16[512,256]{1,0:T(8,128)(2,1)} %get-tuple-element.23), channel_id=1, source_target_pairs={{0,4},{1,5},{2,6},{3,7},{4,0},{5,1},{6,2},{7,3},{8,12},{9,13},{10,... | collective-permute-start | bytes 786440 | tf_op jit(solution)/shard_map/ppermute | solution.py:344
  80.5 25.2 %collective-permute-start.13 = (bf16[512,256]{1,0:T(8,128)(2,1)}, bf16[512,256]{1,0:T(8,128)(2,1)}, u32[]{:S(2)}, u32[]{:S(2)}) collective-permute-start(bf16[512,256]{1,0:T(8,128)(2,1)} %get-tuple-element.24), channel_id=1, source_target_pairs={{0,6},{1,7},{2,0},{3,1},{4,2},{5,3},{6,4},{7,5},{8,14},{9,15},{10,... | collective-permute-start | bytes 786440 | tf_op jit(solution)/shard_map/ppermute | solution.py:344
  87.5 0.7 copy-start.2
  88.2 0.7 copy-start.4
  89.0 0.7 copy-start.6
  89.7 16.1 %copy-start.10 = (bf16[512,256]{1,0:T(8,128)(2,1)S(1)}, bf16[512,256]{1,0:T(8,128)(2,1)}, u32[]{:S(2)}) copy-start(bf16[512,256]{1,0:T(8,128)(2,1)} %copy-done.9) | copy-start | bytes 786436
  95.5 18.9 %all-to-all-start.1 = ((bf16[8,32,256]{2,1,0:T(8,128)(2,1)}), bf16[8,32,256]{2,1,0:T(8,128)(2,1)S(1)}, u32[]{:S(2)}, u32[]{:S(2)}) async-start(bf16[8,32,256]{2,1,0:T(8,128)(2,1)} %add_up.3.refs_4_), calls=%async_computation.1 | async-start | bytes 262144 | tf_op jit(solution)/shard_map/all_to_all | solution.py:456
  105.7 14.4 %copy-start.7 = (bf16[512,256]{1,0:T(8,128)(2,1)S(1)}, bf16[512,256]{1,0:T(8,128)(2,1)}, u32[]{:S(2)}) copy-start(bf16[512,256]{1,0:T(8,128)(2,1)} %copy-done.6) | copy-start | bytes 786436
  105.7 16.8 %copy-start.5 = (bf16[512,256]{1,0:T(8,128)(2,1)S(1)}, bf16[512,256]{1,0:T(8,128)(2,1)}, u32[]{:S(2)}) copy-start(bf16[512,256]{1,0:T(8,128)(2,1)} %copy-done.4) | copy-start | bytes 786436
  105.7 17.3 %copy-start.3 = (bf16[512,256]{1,0:T(8,128)(2,1)S(1)}, bf16[512,256]{1,0:T(8,128)(2,1)}, u32[]{:S(2)}) copy-start(bf16[512,256]{1,0:T(8,128)(2,1)} %copy-done.2) | copy-start | bytes 786436
  115.3 32.9 %copy-start.13 = (f32[256]{0:T(256)S(1)}, f32[256]{0:T(256)}, u32[]{:S(2)}) copy-start(f32[256]{0:T(256)} %param.10) | copy-start | bytes 3076
  115.3 33.4 %copy-start.11 = (f32[256,256]{1,0:T(8,128)S(1)}, f32[256,256]{1,0:T(8,128)}, u32[]{:S(2)}) copy-start(f32[256,256]{1,0:T(8,128)} %param.9) | copy-start | bytes 786436
  115.3 22.5 %all-to-all-start.2 = ((f32[16,32,256]{2,1,0:T(8,128)}), f32[16,32,256]{2,1,0:T(8,128)S(1)}, u32[]{:S(2)}, u32[]{:S(2)}) async-start(f32[16,32,256]{2,1,0:T(8,128)} %add_up.5), calls=%async_computation.2 | async-start | bytes 1048576 | tf_op jit(solution)/shard_map/all_to_all | solution.py:397
  120.1 12.3 %collective-permute-start.8 = (bf16[512,256]{1,0:T(8,128)(2,1)S(1)}, bf16[512,256]{1,0:T(8,128)(2,1)S(1)}, u32[]{:S(2)}, u32[]{:S(2)}) collective-permute-start(bf16[512,256]{1,0:T(8,128)(2,1)S(1)} %copy-done.7), channel_id=1, source_target_pairs={{0,2},{1,3},{2,4},{3,5},{4,6},{5,7},{6,0},{7,1},{8,10},{9,11},{10,... | collective-permute-start | bytes 786440 | tf_op jit(solution)/shard_map/ppermute | solution.py:344
  122.5 10.7 %collective-permute-start.9 = (bf16[512,256]{1,0:T(8,128)(2,1)S(1)}, bf16[512,256]{1,0:T(8,128)(2,1)S(1)}, u32[]{:S(2)}, u32[]{:S(2)}) collective-permute-start(bf16[512,256]{1,0:T(8,128)(2,1)S(1)} %copy-done.5), channel_id=1, source_target_pairs={{0,4},{1,5},{2,6},{3,7},{4,0},{5,1},{6,2},{7,3},{8,12},{9,13},{10,... | collective-permute-start | bytes 786440 | tf_op jit(solution)/shard_map/ppermute | solution.py:344
  123.0 13.0 %collective-permute-start.10 = (bf16[512,256]{1,0:T(8,128)(2,1)S(1)}, bf16[512,256]{1,0:T(8,128)(2,1)S(1)}, u32[]{:S(2)}, u32[]{:S(2)}) collective-permute-start(bf16[512,256]{1,0:T(8,128)(2,1)S(1)} %copy-done.3), channel_id=1, source_target_pairs={{0,6},{1,7},{2,0},{3,1},{4,2},{5,3},{6,4},{7,5},{8,14},{9,15},{10,... | collective-permute-start | bytes 786440 | tf_op jit(solution)/shard_map/ppermute | solution.py:344
  123.7 12.9 %collective-permute-start.14 = (bf16[512,256]{1,0:T(8,128)(2,1)S(1)}, bf16[512,256]{1,0:T(8,128)(2,1)S(1)}, u32[]{:S(2)}, u32[]{:S(2)}) collective-permute-start(bf16[512,256]{1,0:T(8,128)(2,1)S(1)} %add_up.4.refs_1_), channel_id=1, source_target_pairs={{0,8},{8,16},{16,24},{24,32},{32,40},{40,48},{48,56},{56,64},{64,7... | collective-permute-start | bytes 786440 | tf_op jit(solution)/shard_map/ppermute | solution.py:336
  136.7 11.3 %collective-permute-start.15 = (bf16[256,256]{1,0:T(8,128)(2,1)S(1)}, bf16[256,256]{1,0:T(8,128)(2,1)S(1)}, u32[]{:S(2)}, u32[]{:S(2)}) collective-permute-start(bf16[256,256]{1,0:T(8,128)(2,1)S(1)} %slice.17), channel_id=1, source_target_pairs={{0,1},{1,0},{2,3},{3,2},{4,5},{5,4},{6,7},{7,6},{8,9},{9,8},{10,11... | collective-permute-start | bytes 393224 | tf_op jit(solution)/shard_map/ppermute | solution.py:340
  137.7 11.8 %collective-permute-start.16 = (f32[16,32,256]{2,1,0:T(8,128)S(1)}, f32[16,32,256]{2,1,0:T(8,128)S(1)}, u32[]{:S(2)}, u32[]{:S(2)}) collective-permute-start(f32[16,32,256]{2,1,0:T(8,128)S(1)} %all-to-all-done.2), channel_id=1, source_target_pairs={{0,8},{8,0},{16,24},{24,16},{32,40},{40,32},{48,56},{56,48},{64,72... | collective-permute-start | bytes 1572872 | tf_op jit(solution)/shard_map/ppermute | solution.py:398
  149.6 0.7 copy-start.12

commit v6 on v5

--- a/solution.py
+++ b/solution.py
@@ -61,9 +61,9 @@
             hot = one_hot(rows, neg_ref[0, :, c : c + 128], b * BLK)
             hits = hot if hits is None else hits + hot
         count = jnp.sum(hits.astype(f32), axis=1, keepdims=True)
-        at = slice(b * BLK, (b + 1) * BLK)
-        out_ref[0, at, 0:1] = jnp.log2(count)
-        out_ref[0, at, 1:2] = jnp.log2(count + 1.0)
+        lane = lax.broadcasted_iota(jnp.int32, (BLK, 8), 1)
+        out_ref[0, :, b * BLK : (b + 1) * BLK] = jnp.where(lane == 0, count, count + 1.0).T
+    out_ref[0] = jnp.log2(out_ref[0])
 
 
 def neg_weights(neg_pad):
@@ -71,8 +71,8 @@
         count_kernel,
         grid=(GROUPS,),
         in_specs=[pl.BlockSpec((1, 1, PAD), lambda g: (g, 0, 0))],
-        out_specs=pl.BlockSpec((1, ROWS, 2), lambda g: (g, 0, 0)),
-        out_shape=jax.ShapeDtypeStruct((GROUPS, ROWS, 2), f32),
+        out_specs=pl.BlockSpec((1, 8, ROWS), lambda g: (g, 0, 0)),
+        out_shape=jax.ShapeDtypeStruct((GROUPS, 8, ROWS), f32),
         compiler_params=params(),
         cost_estimate=cost(3),
         name="neg_weights",
@@ -81,7 +81,7 @@
 
 def query_kernel(rel_ref, *refs):
     own = refs[:PARTS]
-    idx_ref, mat_ref, s_ref, q_ref = refs[PARTS:]
+    idx_ref, mat_ref, _, s_ref, q_ref = refs[PARTS:]
     column = jnp.broadcast_to(idx_ref[0].astype(f32), (128, CH)).T
     column = column.astype(jnp.int32).astype(jnp.int16)
     cols = lax.broadcasted_iota(jnp.int32, (CH, 128), 1).astype(jnp.int16)
@@ -101,7 +101,7 @@
     q_ref[...] = mm(mat_ref[0].astype(bf16).T, rows, NT).astype(bf16)
 
 
-def make_queries(own, src_rows, rel_id, relation):
+def make_queries(own, src_rows, rel_id, relation, after):
     return pl.pallas_call(
         query_kernel,
         grid_spec=pltpu.PrefetchScalarGridSpec(
@@ -111,6 +111,7 @@
                 *[pl.BlockSpec((PART, D), lambda j, rel: (0, 0))] * PARTS,
                 pl.BlockSpec((1, 1, CH), lambda j, rel: (j, 0, 0)),
                 pl.BlockSpec((1, D, D), lambda j, rel: (rel[j // PER], 0, 0)),
+                pl.BlockSpec(memory_space=pl.ANY),
             ],
             out_specs=[
                 pl.BlockSpec((CH, D), lambda j, rel: (j, 0)),
@@ -124,7 +125,7 @@
         compiler_params=params(),
         cost_estimate=cost(9),
         name="queries",
-    )(rel_id, *own, src_rows, relation)
+    )(rel_id, *own, src_rows, relation, after)
 
 
 SUB = 32
@@ -134,7 +135,7 @@
     nxt = refs[:PARTS]
     q_ref, dst_ref, wt_ref, gq_ref = refs[PARTS : PARTS + 4]
     dg = refs[PARTS + 4 : 2 * PARTS + 4]
-    sc, nxt_t_ref, w0, w1, qs0, qs1, sl0, sl1, dacc = refs[2 * PARTS + 4 :]
+    sc, nxt_t_ref, w0, w1, qs0, qs1, sl0, sl1, dacc, wcol = refs[2 * PARTS + 4 :]
     g = pl.program_id(0)
     rows = lax.broadcasted_iota(jnp.int32, (SUB, CH), 0)
     rows16 = lax.broadcasted_iota(jnp.int32, (BLK, CH), 0).astype(jnp.int16)
@@ -147,6 +148,10 @@
             nxt_t_ref[:, b * BLK : (b + 1) * BLK] = block_of(nxt, b).T
         qs1[...] = jnp.zeros_like(qs1)
         sl1[...] = jnp.zeros_like(sl1)
+
+    for b in range(NBLK):
+        at = slice(b * BLK, (b + 1) * BLK)
+        wcol[at, :] = wt_ref[0, :, at].T
 
     def spread(b, w, qs):
         at = slice(b * BLK, (b + 1) * BLK)
@@ -168,7 +173,7 @@
                 at = slice(b * BLK + i * SUB, b * BLK + (i + 1) * SUB)
                 mask = rows == dst - (b * BLK + i * SUB)
                 val = raw[i * SUB : (i + 1) * SUB] * LOG2E + jnp.where(
-                    mask, wt_ref[0, at, 1:2], wt_ref[0, at, 0:1]
+                    mask, wcol[at, 1:2], wcol[at, 0:1]
                 )
                 sc[at, :] = val
                 top = jnp.maximum(top, jnp.max(val.reshape(SUB // 8, 8, CH), axis=0))
@@ -222,7 +227,7 @@
                 *[pl.BlockSpec((PART, D), lambda j, cnt: (0, 0))] * PARTS,
                 pl.BlockSpec((D, PAD), lambda j, cnt: (0, j)),
                 pl.BlockSpec((1, 1, PAD), lambda j, cnt: (j, 0, 0)),
-                pl.BlockSpec((1, ROWS, 2), lambda j, cnt: (j, 0, 0)),
+                pl.BlockSpec((1, 8, ROWS), lambda j, cnt: (j, 0, 0)),
             ],
             out_specs=[
                 pl.BlockSpec((D, GROUPS * PAD), lambda j, cnt: (0, 0)),
@@ -238,6 +243,7 @@
                 pltpu.VMEM((8, CH), f32),
                 pltpu.VMEM((8, CH), f32),
                 pltpu.VMEM((ROWS, D), f32),
+                pltpu.VMEM((ROWS, 8), f32),
             ],
         ),
         out_shape=[
@@ -387,6 +393,29 @@
     )(*blocks, after)
 
 
+def split_sum(blocks):
+    half = blocks[0].shape[0] // 2
+    whole = pl.BlockSpec(memory_space=pltpu.VMEM)
+
+    def kernel(*refs):
+        for out, at in ((refs[-2], slice(0, half)), (refs[-1], slice(half, 2 * half))):
+            total = None
+            for ref in refs[:-2]:
+                part = ref[at, :].astype(f32)
+                total = part if total is None else total + part
+            out[...] = total.astype(out.dtype)
+
+    return pl.pallas_call(
+        kernel,
+        in_specs=[whole] * len(blocks),
+        out_specs=[whole] * 2,
+        out_shape=[jax.ShapeDtypeStruct((half, D), f32), jax.ShapeDtypeStruct((half, D), bf16)],
+        compiler_params=pltpu.CompilerParams(vmem_limit_bytes=16 * MB),
+        cost_estimate=cost(1),
+        name="split_sum",
+    )(*blocks)
+
+
 def turned(index):
     rep = lax.axis_index("rep")
     return ((index - PART * (rep // 2)) % ROWS) ^ (256 * (rep % 2))
@@ -405,8 +434,8 @@
     return jnp.pad(index.reshape(GROUPS, SLOTS), ((0, 0), (0, PAD - SLOTS)), constant_values=fill)
 
 
-def source_stage(own, src_pad, rel_id, relation):
-    return make_queries(own, src_pad.reshape(NCH, 1, CH), rel_id, relation)
+def source_stage(own, src_pad, rel_id, relation, after):
+    return make_queries(own, src_pad.reshape(NCH, 1, CH), rel_id, relation, after)
 
 
 def target_stage(nxt, q, s, dst_pad, weights, rel_id, counts, kinds):
@@ -424,7 +453,7 @@
     weights = neg_weights(pad_slots(neg_index, -1))
     own = [own[k * PART : (k + 1) * PART] for k in range(PARTS)]
     nxt = [nxt[k * PART : (k + 1) * PART] for k in range(PARTS)]
-    s, q = source_stage(own, src_pad, rel_id, relation)
+    s, q = source_stage(own, src_pad, rel_id, relation, nxt[0])
     gq, dst_grad, rel_grad = target_stage(
         nxt, q, s, pad_slots(dst_index, -1), weights, rel_id, counts, relation.shape[0]
     )
@@ -443,7 +472,7 @@
     own = spread_x(jnp.concatenate([ent_b, other]))
     nxt = [shift_dom(block, -1) for block in own]
     weights = neg_weights(neg_pad)
-    s, q = source_stage(own, src_pad, rel_id, relation)
+    s, q = source_stage(own, src_pad, rel_id, relation, nxt[0])
     gq, dst_grad, rel_grad = target_stage(
         nxt, q, s, dst_pad, weights, rel_id, counts, relation.shape[0]
     )
@@ -452,14 +481,14 @@
     got = lax.all_to_all(rel_grad.reshape(32, -1, D), "dom", 0, 0)
     src_grad = back_stage(gq, src_pad, rel_id, relation)
     src_blocks = send_x(src_grad)
-    mine = add_up([got], src_grad[0], bf16, 8)
-    every = lax.all_to_all(mine, "rep", 0, 0)
+    mine = add_up([got], src_grad[0], f32)
+    zsum = mine + swap_z(mine)
     dst_sum = add_up(dst_blocks, mine, bf16)
     moved = shift_dom(dst_sum, 1)
-    shares = add_up([every], dst_sum, f32, 16)
+    keep, give = split_sum(src_blocks + [moved])
+    shares = add_up([zsum] + [shift_x(zsum, k) for k in (1, 2, 3)], give, f32, 16)
     rel_total = spread_total(shares, kinds)
-    total = sum(block.astype(f32) for block in src_blocks + [moved])
-    grads = total[:256] + swap_z(total[256:].astype(bf16)).astype(f32)
+    grads = keep + swap_z(give).astype(f32)
     entity_new, entity_accum_new = rowwise(entity, entity_accum, grads)
     relation_new, relation_accum_new = rowwise(relation, relation_accum, rel_total)
     return (entity_new, entity_accum_new, relation_new, relation_accum_new)

time: 153 us -> 153 us (level)
  the two profiles are of different devices: /device:TPU:6 before, /device:TPU:1 now
where the time goes in v6:
time: 153 us; the launch traced here: 152 us
  starting transfers between devices  57.1 us (37%)
  Pallas kernels  56.2 us (37%)
  waiting for transfers between devices  28 us (18%)
  other arithmetic  6.06 us (4%)
  local copies, waits for them, and re-layouts  3.32 us (2%)
    pallas_call x1, Pallas kernels, score_side(): pl.pallas_call(score_kernel, grid_spec=pltpu.PrefetchScalarGridSpec(num_s...  29.4 us
    all_to_all x1, waiting for transfers between devices, spread_total(): half = lax.all_to_all(shares, 'dom', 0, 0, axis_index_groups=cores)  17.9 us
    ppermute x3, starting transfers between devices, swap_z(): return lax.ppermute(block, 'rep', [(i, i ^ 1) for i in range(8)])  15.8 us
    ppermute x12, starting transfers between devices, shift_x(): return lax.ppermute(block, 'rep', [(i, (i + 2 * by) % 8) for i in range(8)])  13.4 us
    ppermute x5, starting transfers between devices, shift_dom(): lax.ppermute(block, 'dom', [(i, (i + by) % size) for i in range(size)])  11.6 us
    pallas_call x1, Pallas kernels, make_queries(): pl.pallas_call(query_kernel, grid_spec=pltpu.PrefetchScalarGridSpec(num_s...  9.54 us
    all_to_all x1, starting transfers between devices, spread_total(): half = lax.all_to_all(shares, 'dom', 0, 0, axis_index_groups=cores)  9.03 us
    pallas_call x1, Pallas kernels, source_side(): pl.pallas_call(source_kernel, grid_spec=pltpu.PrefetchScalarGridSpec(num_...  7.65 us
  transfers between devices with their start and end apart: 23, of which 8 were waited for; matrix products, arithmetic and copies ran while one was open for 2% of the time, Pallas kernels for 15%

profile of v6, /device:TPU:1, one launch (start us, length us, event | category | flops | bytes accessed | tf_op | source)
XLA Modules:
  0.0 152.3 jit_solution(1377476936094579865)
XLA Ops:
  0.6 1.0 convert_element_type.6
  1.6 7.8 %collective-permute-start = (bf16[256,256]{1,0:T(8,128)(2,1)S(1)}, bf16[256,256]{1,0:T(8,128)(2,1)S(1)}, u32[]{:S(2)}, u32[]{:S(2)}) collective-permute-start(bf16[256,256]{1,0:T(8,128)(2,1)S(1)} %convert_element_type.6), channel_id=1, source_target_pairs={{0,1},{1,0},{2,3},{3,2},{4,5},{5,4},{6,7},{7,6},{8,9},{9,8},{10,11... | collective-permute-start | bytes 393224 | tf_op jit(solution)/shard_map/ppermute | solution.py:346
  10.1 0.7 fusion.6
  10.9 1.2 collective-permute-done
  12.1 1.8 %collective-permute-start.6 = (bf16[512,256]{1,0:T(8,128)(2,1)S(1)}, bf16[512,256]{1,0:T(8,128)(2,1)S(1)}, u32[]{:S(2)}, u32[]{:S(2)}) collective-permute-start(bf16[512,256]{1,0:T(8,128)(2,1)S(1)} %pad_maximum_fusion.1.refs_0_), channel_id=1, source_target_pairs={{0,2},{1,3},{2,4},{3,5},{4,6},{5,7},{6,0},{7,1},{8,10},{9,11},{10,... | collective-permute-start | bytes 786440 | tf_op jit(solution)/shard_map/ppermute | solution.py:350
  14.0 2.5 %collective-permute-start.4 = (bf16[512,256]{1,0:T(8,128)(2,1)S(1)}, bf16[512,256]{1,0:T(8,128)(2,1)S(1)}, u32[]{:S(2)}, u32[]{:S(2)}) collective-permute-start(bf16[512,256]{1,0:T(8,128)(2,1)S(1)} %pad_maximum_fusion.1.refs_0_), channel_id=1, source_target_pairs={{0,4},{1,5},{2,6},{3,7},{4,0},{5,1},{6,2},{7,3},{8,12},{9,13},{10,... | collective-permute-start | bytes 786440 | tf_op jit(solution)/shard_map/ppermute | solution.py:350
  16.4 1.2 collective-permute-start.2
  17.6 2.2 %collective-permute-start.1 = (bf16[512,256]{1,0:T(8,128)(2,1)S(1)}, bf16[512,256]{1,0:T(8,128)(2,1)S(1)}, u32[]{:S(2)}, u32[]{:S(2)}) collective-permute-start(bf16[512,256]{1,0:T(8,128)(2,1)S(1)} %pad_maximum_fusion.1.refs_0_), channel_id=1, source_target_pairs={{0,248},{8,0},{16,8},{24,16},{32,24},{40,32},{48,40},{56,48},{64,5... | collective-permute-start | bytes 786440 | tf_op jit(solution)/shard_map/ppermute | solution.py:342
  19.7 0.8 fusion.2
  20.8 3.2 %neg_weights.1.refs_6_ = f32[4,8,2048]{2,1,0:T(8,128)S(1)} custom-call(s32[4,1,1024]{2,1,0:T(1,128)S(1)} %reshape.41.neg_ref), custom_call_target="tpu_custom_call" | custom-call | flops 1500000000 | bytes 10500000 | tf_op jit(solution)/shard_map/neg_weights/pallas_call | solution.py:70
  24.0 3.3 %collective-permute-start.7 = (bf16[512,256]{1,0:T(8,128)(2,1)S(1)}, bf16[512,256]{1,0:T(8,128)(2,1)S(1)}, u32[]{:S(2)}, u32[]{:S(2)}) collective-permute-start(bf16[512,256]{1,0:T(8,128)(2,1)S(1)} %collective-permute-done.6.refs_3_), channel_id=1, source_target_pairs={{0,248},{8,0},{16,8},{24,16},{32,24},{40,32},{48,40},{56,48},{64,5... | collective-permute-start | bytes 786440 | tf_op jit(solution)/shard_map/ppermute | solution.py:342
  27.3 2.4 %collective-permute-start.5 = (bf16[512,256]{1,0:T(8,128)(2,1)S(1)}, bf16[512,256]{1,0:T(8,128)(2,1)S(1)}, u32[]{:S(2)}, u32[]{:S(2)}) collective-permute-start(bf16[512,256]{1,0:T(8,128)(2,1)S(1)} %collective-permute-done.4.refs_2_), channel_id=1, source_target_pairs={{0,248},{8,0},{16,8},{24,16},{32,24},{40,32},{48,40},{56,48},{64,5... | collective-permute-start | bytes 786440 | tf_op jit(solution)/shard_map/ppermute | solution.py:342
  29.7 2.5 %collective-permute-start.3 = (bf16[512,256]{1,0:T(8,128)(2,1)S(1)}, bf16[512,256]{1,0:T(8,128)(2,1)S(1)}, u32[]{:S(2)}, u32[]{:S(2)}) collective-permute-start(bf16[512,256]{1,0:T(8,128)(2,1)S(1)} %collective-permute-done.2.refs_1_), channel_id=1, source_target_pairs={{0,248},{8,0},{16,8},{24,16},{32,24},{40,32},{48,40},{56,48},{64,5... | collective-permute-start | bytes 786440 | tf_op jit(solution)/shard_map/ppermute | solution.py:342
  32.2 9.5 %queries.1 = (bf16[4096,256]{1,0:T(8,128)(2,1)S(1)}, bf16[256,4096]{1,0:T(8,128)(2,1)}) custom-call(s32[4]{0:T(128)S(1)} %copy-done.1, bf16[512,256]{1,0:T(8,128)(2,1)S(1)} %pad_maximum_fusion.1.refs_0_, bf16[512,256]{1,0:T(8,128)(2,1)S(1)} %collective-permute-done.2.refs_1_, bf16[512,256]{1,0:T(8,128)(2,1)S(1)} %collective-permute-done.4.refs_2_, ...), custom_call_target="tpu_custom_call" | custom-call | flops 4499999744 | bytes 31500000 | tf_op jit(solution)/shard_map/queries/pallas_call | solution.py:105
  41.8 29.4 %scores.1 = (bf16[256,4096]{1,0:T(8,128)(2,1)S(1)}, bf16[512,256]{1,0:T(8,128)(2,1)S(1)}, bf16[512,256]{1,0:T(8,128)(2,1)S(1)}, bf16[512,256]{1,0:T(8,128)(2,1)}, bf16[512,256]{1,0:T(8,128)(2,1)S(1)}) custom-call(s32[1]{0:T(128)S(6)} %copy.21.cnt_ref, bf16[512,256]{1,0:T(8,128)(2,1)S(1)} %collective-permute-done.1.refs_6_.refs_0_, ...), custom_call_target="tpu_custom_call" | custom-call | flops 14000000000 | bytes 98000000 | tf_op jit(solution)/shard_map/scores/pallas_call | solution.py:221
  71.1 3.1 %operator_grads.1 = bf16[4,256,256]{2,1,0:T(8,128)(2,1)} custom-call(s32[4]{0:T(128)S(1)} %copy-done.1, bf16[256,4096]{1,0:T(8,128)(2,1)S(1)} %get-tuple-element.18.gq_ref, bf16[4096,256]{1,0:T(8,128)(2,1)S(1)} %get-tuple-element.27.s_ref), custom_call_target="tpu_custom_call" | custom-call | flops 1000000000 | bytes 7000000 | tf_op jit(solution)/shard_map/operator_grads/pallas_call | solution.py:275
  74.2 7.2 %all-to-all-start = ((bf16[32,32,256]{2,1,0:T(8,128)(2,1)}), bf16[32,32,256]{2,1,0:T(8,128)(2,1)}, u32[]{:S(2)}, u32[]{:S(2)}) async-start(bf16[32,32,256]{2,1,0:T(8,128)(2,1)} %bitcast), calls=%async_computation | async-start | bytes 1048576 | tf_op jit(solution)/shard_map/all_to_all | solution.py:481
  81.5 2.4 %collective-permute-start.12 = (bf16[512,256]{1,0:T(8,128)(2,1)}, bf16[512,256]{1,0:T(8,128)(2,1)}, u32[]{:S(2)}, u32[]{:S(2)}) collective-permute-start(bf16[512,256]{1,0:T(8,128)(2,1)} %get-tuple-element.25), channel_id=1, source_target_pairs={{0,4},{1,5},{2,6},{3,7},{4,0},{5,1},{6,2},{7,3},{8,12},{9,13},{10,... | collective-permute-start | bytes 786440 | tf_op jit(solution)/shard_map/ppermute | solution.py:350
  84.0 0.7 collective-permute-start.13
  84.7 7.7 %source_grads.1 = (bf16[512,256]{1,0:T(8,128)(2,1)S(1)}, bf16[512,256]{1,0:T(8,128)(2,1)}, bf16[512,256]{1,0:T(8,128)(2,1)}, bf16[512,256]{1,0:T(8,128)(2,1)S(1)}) custom-call(s32[4]{0:T(128)S(1)} %copy-done.1, bf16[256,4096]{1,0:T(8,128)(2,1)S(1)} %get-tuple-element.18.gq_ref, s32[4,1,1024]{2,1,0:T(1,128)S(1)} %reshape.42.src_ref, f32[4,256,256]{2,1,0:T(8,128)S(1)} %copy-done), custom_call_target="tpu_custom_call" | custom-call | flops 4000000000 | bytes 28000000 | tf_op jit(solution)/shard_map/source_grads/pallas_call | solution.py:315
  92.3 0.7 copy-done.6
  93.0 0.7 collective-permute-start.8
  93.8 1.2 collective-permute-start.9
  94.9 2.9 %all-to-all-done.refs_0_ = bf16[32,32,256]{2,1,0:T(8,128)(2,1)} async-done(((bf16[32,32,256]{2,1,0:T(8,128)(2,1)}), bf16[32,32,256]{2,1,0:T(8,128)(2,1)}, u32[]{:S(2)}, u32[]{:S(2)}) %all-to-all-start) | async-done | bytes 524320 | tf_op jit(solution)/shard_map/all_to_all | solution.py:481
  97.9 0.9 copy-done.7
  98.8 1.1 add_up.3.refs_4_
  100.0 1.3 collective-permute-start.10
  101.3 0.9 copy-done.5
  102.2 1.2 add_up.4
  103.5 1.2 collective-permute-start.14
  104.7 5.6 %collective-permute-start.16 = (f32[32,256]{1,0:T(8,128)S(1)}, f32[32,256]{1,0:T(8,128)S(1)}, u32[]{:S(2)}, u32[]{:S(2)}) collective-permute-start(f32[32,256]{1,0:T(8,128)S(1)} %add_up.3.refs_4_), channel_id=1, source_target_pairs={{0,1},{1,0},{2,3},{3,2},{4,5},{5,4},{6,7},{7,6},{8,9},{9,8},{10,11... | collective-permute-start | bytes 98312 | tf_op jit(solution)/shard_map/ppermute | solution.py:346
  110.3 1.8 %collective-permute-done.16 = f32[32,256]{1,0:T(8,128)S(1)} collective-permute-done((f32[32,256]{1,0:T(8,128)S(1)}, f32[32,256]{1,0:T(8,128)S(1)}, u32[]{:S(2)}, u32[]{:S(2)}) %collective-permute-start.16) | collective-permute-done | bytes 32800 | tf_op jit(solution)/shard_map/ppermute | solution.py:346
  112.2 0.8 collective-permute-start.18
  113.1 0.6 collective-permute-start.17
  113.9 1.0 collective-permute-done.19.refs_3_
  114.9 1.6 %collective-permute-done.18.refs_2_ = f32[32,256]{1,0:T(8,128)S(1)} collective-permute-done((f32[32,256]{1,0:T(8,128)S(1)}, f32[32,256]{1,0:T(8,128)S(1)}, u32[]{:S(2)}, u32[]{:S(2)}) %collective-permute-start.18) | collective-permute-done | bytes 32800 | tf_op jit(solution)/shard_map/ppermute | solution.py:350
  116.5 1.1 collective-permute-done.17.refs_1_
  117.7 0.9 add_up.5
  118.5 9.0 %all-to-all-start.1 = ((f32[16,32,256]{2,1,0:T(8,128)}), f32[16,32,256]{2,1,0:T(8,128)S(1)}, u32[]{:S(2)}, u32[]{:S(2)}) async-start(f32[16,32,256]{2,1,0:T(8,128)} %add_up.5), calls=%async_computation.1 | async-start | bytes 1048576 | tf_op jit(solution)/shard_map/all_to_all | solution.py:426
  127.5 2.4 %collective-permute-start.15 = (bf16[256,256]{1,0:T(8,128)(2,1)S(1)}, bf16[256,256]{1,0:T(8,128)(2,1)S(1)}, u32[]{:S(2)}, u32[]{:S(2)}) collective-permute-start(bf16[256,256]{1,0:T(8,128)(2,1)S(1)} %get-tuple-element.29.refs_4_), channel_id=1, source_target_pairs={{0,1},{1,0},{2,3},{3,2},{4,5},{5,4},{6,7},{7,6},{8,9},{9,8},{10,11... | collective-permute-start | bytes 393224 | tf_op jit(solution)/shard_map/ppermute | solution.py:346
  129.9 17.9 %all-to-all-done.1 = f32[16,32,256]{2,1,0:T(8,128)S(1)} async-done(((f32[16,32,256]{2,1,0:T(8,128)}), f32[16,32,256]{2,1,0:T(8,128)S(1)}, u32[]{:S(2)}, u32[]{:S(2)}) %all-to-all-start.1) | async-done | bytes 524320 | tf_op jit(solution)/shard_map/all_to_all | solution.py:426
  147.9 0.6 fusion.8
  148.5 0.8 divide_subtract_fusion.1
  149.3 0.4 collective-permute-done.20
  149.8 0.2 multiply_reduce_fusion
  150.3 0.2 copy-done.9
  150.5 0.6 fusion.7
  151.1 1.2 divide_subtract_fusion
  (54 shorter events, 1.1 us)
Async XLA Ops:
  1.6 10.5 %collective-permute-start = (bf16[256,256]{1,0:T(8,128)(2,1)S(1)}, bf16[256,256]{1,0:T(8,128)(2,1)S(1)}, u32[]{:S(2)}, u32[]{:S(2)}) collective-permute-start(bf16[256,256]{1,0:T(8,128)(2,1)S(1)} %convert_element_type.6), channel_id=1, source_target_pairs={{0,1},{1,0},{2,3},{3,2},{4,5},{5,4},{6,7},{7,6},{8,9},{9,8},{10,11... | collective-permute-start | bytes 393224 | tf_op jit(solution)/shard_map/ppermute | solution.py:346
  12.1 11.9 %collective-permute-start.6 = (bf16[512,256]{1,0:T(8,128)(2,1)S(1)}, bf16[512,256]{1,0:T(8,128)(2,1)S(1)}, u32[]{:S(2)}, u32[]{:S(2)}) collective-permute-start(bf16[512,256]{1,0:T(8,128)(2,1)S(1)} %pad_maximum_fusion.1.refs_0_), channel_id=1, source_target_pairs={{0,2},{1,3},{2,4},{3,5},{4,6},{5,7},{6,0},{7,1},{8,10},{9,11},{10,... | collective-permute-start | bytes 786440 | tf_op jit(solution)/shard_map/ppermute | solution.py:350
  14.0 13.3 %collective-permute-start.4 = (bf16[512,256]{1,0:T(8,128)(2,1)S(1)}, bf16[512,256]{1,0:T(8,128)(2,1)S(1)}, u32[]{:S(2)}, u32[]{:S(2)}) collective-permute-start(bf16[512,256]{1,0:T(8,128)(2,1)S(1)} %pad_maximum_fusion.1.refs_0_), channel_id=1, source_target_pairs={{0,4},{1,5},{2,6},{3,7},{4,0},{5,1},{6,2},{7,3},{8,12},{9,13},{10,... | collective-permute-start | bytes 786440 | tf_op jit(solution)/shard_map/ppermute | solution.py:350
  16.4 13.3 %collective-permute-start.2 = (bf16[512,256]{1,0:T(8,128)(2,1)S(1)}, bf16[512,256]{1,0:T(8,128)(2,1)S(1)}, u32[]{:S(2)}, u32[]{:S(2)}) collective-permute-start(bf16[512,256]{1,0:T(8,128)(2,1)S(1)} %pad_maximum_fusion.1.refs_0_), channel_id=1, source_target_pairs={{0,6},{1,7},{2,0},{3,1},{4,2},{5,3},{6,4},{7,5},{8,14},{9,15},{10,... | collective-permute-start | bytes 786440 | tf_op jit(solution)/shard_map/ppermute | solution.py:350
  17.6 14.6 %collective-permute-start.1 = (bf16[512,256]{1,0:T(8,128)(2,1)S(1)}, bf16[512,256]{1,0:T(8,128)(2,1)S(1)}, u32[]{:S(2)}, u32[]{:S(2)}) collective-permute-start(bf16[512,256]{1,0:T(8,128)(2,1)S(1)} %pad_maximum_fusion.1.refs_0_), channel_id=1, source_target_pairs={{0,248},{8,0},{16,8},{24,16},{32,24},{40,32},{48,40},{56,48},{64,5... | collective-permute-start | bytes 786440 | tf_op jit(solution)/shard_map/ppermute | solution.py:342
  20.7 11.5 %copy-start = (f32[4,256,256]{2,1,0:T(8,128)S(1)}, f32[4,256,256]{2,1,0:T(8,128)}, u32[]{:S(2)}) copy-start(f32[4,256,256]{2,1,0:T(8,128)} %mat_ref.1) | copy-start | bytes 3145732
  20.7 11.5 %copy-start.1 = (s32[4]{0:T(128)S(1)}, s32[4]{0:T(128)}, u32[]{:S(2)}) copy-start(s32[4]{0:T(128)} %rel_ref.5) | copy-start | bytes 52
  24.0 17.8 %collective-permute-start.7 = (bf16[512,256]{1,0:T(8,128)(2,1)S(1)}, bf16[512,256]{1,0:T(8,128)(2,1)S(1)}, u32[]{:S(2)}, u32[]{:S(2)}) collective-permute-start(bf16[512,256]{1,0:T(8,128)(2,1)S(1)} %collective-permute-done.6.refs_3_), channel_id=1, source_target_pairs={{0,248},{8,0},{16,8},{24,16},{32,24},{40,32},{48,40},{56,48},{64,5... | collective-permute-start | bytes 786440 | tf_op jit(solution)/shard_map/ppermute | solution.py:342
  27.3 14.4 %collective-permute-start.5 = (bf16[512,256]{1,0:T(8,128)(2,1)S(1)}, bf16[512,256]{1,0:T(8,128)(2,1)S(1)}, u32[]{:S(2)}, u32[]{:S(2)}) collective-permute-start(bf16[512,256]{1,0:T(8,128)(2,1)S(1)} %collective-permute-done.4.refs_2_), channel_id=1, source_target_pairs={{0,248},{8,0},{16,8},{24,16},{32,24},{40,32},{48,40},{56,48},{64,5... | collective-permute-start | bytes 786440 | tf_op jit(solution)/shard_map/ppermute | solution.py:342
  29.7 12.0 %collective-permute-start.3 = (bf16[512,256]{1,0:T(8,128)(2,1)S(1)}, bf16[512,256]{1,0:T(8,128)(2,1)S(1)}, u32[]{:S(2)}, u32[]{:S(2)}) collective-permute-start(bf16[512,256]{1,0:T(8,128)(2,1)S(1)} %collective-permute-done.2.refs_1_), channel_id=1, source_target_pairs={{0,248},{8,0},{16,8},{24,16},{32,24},{40,32},{48,40},{56,48},{64,5... | collective-permute-start | bytes 786440 | tf_op jit(solution)/shard_map/ppermute | solution.py:342
  71.1 3.1 %copy-start.2 = (bf16[512,256]{1,0:T(8,128)(2,1)}, bf16[512,256]{1,0:T(8,128)(2,1)S(1)}, u32[]{:S(2)}) copy-start(bf16[512,256]{1,0:T(8,128)(2,1)S(1)} %get-tuple-element.26) | copy-start | bytes 786436
  71.1 3.1 %copy-start.3 = (bf16[512,256]{1,0:T(8,128)(2,1)}, bf16[512,256]{1,0:T(8,128)(2,1)S(1)}, u32[]{:S(2)}) copy-start(bf16[512,256]{1,0:T(8,128)(2,1)S(1)} %get-tuple-element.24) | copy-start | bytes 786436
  71.1 3.1 %copy-start.4 = (bf16[512,256]{1,0:T(8,128)(2,1)}, bf16[512,256]{1,0:T(8,128)(2,1)S(1)}, u32[]{:S(2)}) copy-start(bf16[512,256]{1,0:T(8,128)(2,1)S(1)} %get-tuple-element.23.refs_0_) | copy-start | bytes 786436
  74.2 23.7 %all-to-all-start = ((bf16[32,32,256]{2,1,0:T(8,128)(2,1)}), bf16[32,32,256]{2,1,0:T(8,128)(2,1)}, u32[]{:S(2)}, u32[]{:S(2)}) async-start(bf16[32,32,256]{2,1,0:T(8,128)(2,1)} %bitcast), calls=%async_computation | async-start | bytes 1048576 | tf_op jit(solution)/shard_map/all_to_all | solution.py:481
  81.4 18.5 %collective-permute-start.11 = (bf16[512,256]{1,0:T(8,128)(2,1)}, bf16[512,256]{1,0:T(8,128)(2,1)}, u32[]{:S(2)}, u32[]{:S(2)}) collective-permute-start(bf16[512,256]{1,0:T(8,128)(2,1)} %copy-done.3), channel_id=1, source_target_pairs={{0,2},{1,3},{2,4},{3,5},{4,6},{5,7},{6,0},{7,1},{8,10},{9,11},{10,... | collective-permute-start | bytes 786440 | tf_op jit(solution)/shard_map/ppermute | solution.py:350
  81.5 19.8 %collective-permute-start.12 = (bf16[512,256]{1,0:T(8,128)(2,1)}, bf16[512,256]{1,0:T(8,128)(2,1)}, u32[]{:S(2)}, u32[]{:S(2)}) collective-permute-start(bf16[512,256]{1,0:T(8,128)(2,1)} %get-tuple-element.25), channel_id=1, source_target_pairs={{0,4},{1,5},{2,6},{3,7},{4,0},{5,1},{6,2},{7,3},{8,12},{9,13},{10,... | collective-permute-start | bytes 786440 | tf_op jit(solution)/shard_map/ppermute | solution.py:350
  84.0 17.3 %collective-permute-start.13 = (bf16[512,256]{1,0:T(8,128)(2,1)}, bf16[512,256]{1,0:T(8,128)(2,1)}, u32[]{:S(2)}, u32[]{:S(2)}) collective-permute-start(bf16[512,256]{1,0:T(8,128)(2,1)} %copy-done.2), channel_id=1, source_target_pairs={{0,6},{1,7},{2,0},{3,1},{4,2},{5,3},{6,4},{7,5},{8,14},{9,15},{10,... | collective-permute-start | bytes 786440 | tf_op jit(solution)/shard_map/ppermute | solution.py:350
  92.3 0.7 copy-start.6
  93.0 19.2 %collective-permute-start.8 = (bf16[512,256]{1,0:T(8,128)(2,1)}, bf16[512,256]{1,0:T(8,128)(2,1)S(1)}, u32[]{:S(2)}, u32[]{:S(2)}) collective-permute-start(bf16[512,256]{1,0:T(8,128)(2,1)} %get-tuple-element.20), channel_id=1, source_target_pairs={{0,2},{1,3},{2,4},{3,5},{4,6},{5,7},{6,0},{7,1},{8,10},{9,11},{10,... | collective-permute-start | bytes 786440 | tf_op jit(solution)/shard_map/ppermute | solution.py:350
  93.8 19.3 %collective-permute-start.9 = (bf16[512,256]{1,0:T(8,128)(2,1)}, bf16[512,256]{1,0:T(8,128)(2,1)S(1)}, u32[]{:S(2)}, u32[]{:S(2)}) collective-permute-start(bf16[512,256]{1,0:T(8,128)(2,1)} %get-tuple-element.21), channel_id=1, source_target_pairs={{0,4},{1,5},{2,6},{3,7},{4,0},{5,1},{6,2},{7,3},{8,12},{9,13},{10,... | collective-permute-start | bytes 786440 | tf_op jit(solution)/shard_map/ppermute | solution.py:350
  97.9 1.0 copy-start.7
  100.0 13.8 %collective-permute-start.10 = (bf16[512,256]{1,0:T(8,128)(2,1)S(1)}, bf16[512,256]{1,0:T(8,128)(2,1)S(1)}, u32[]{:S(2)}, u32[]{:S(2)}) collective-permute-start(bf16[512,256]{1,0:T(8,128)(2,1)S(1)} %get-tuple-element.22), channel_id=1, source_target_pairs={{0,6},{1,7},{2,0},{3,1},{4,2},{5,3},{6,4},{7,5},{8,14},{9,15},{10,... | collective-permute-start | bytes 786440 | tf_op jit(solution)/shard_map/ppermute | solution.py:350
  101.3 1.0 copy-start.5
  103.5 10.2 %collective-permute-start.14 = (bf16[512,256]{1,0:T(8,128)(2,1)S(1)}, bf16[512,256]{1,0:T(8,128)(2,1)S(1)}, u32[]{:S(2)}, u32[]{:S(2)}) collective-permute-start(bf16[512,256]{1,0:T(8,128)(2,1)S(1)} %add_up.4), channel_id=1, source_target_pairs={{0,8},{8,16},{16,24},{24,32},{32,40},{40,48},{48,56},{56,64},{64,7... | collective-permute-start | bytes 786440 | tf_op jit(solution)/shard_map/ppermute | solution.py:342
  104.7 7.4 %collective-permute-start.16 = (f32[32,256]{1,0:T(8,128)S(1)}, f32[32,256]{1,0:T(8,128)S(1)}, u32[]{:S(2)}, u32[]{:S(2)}) collective-permute-start(f32[32,256]{1,0:T(8,128)S(1)} %add_up.3.refs_4_), channel_id=1, source_target_pairs={{0,1},{1,0},{2,3},{3,2},{4,5},{5,4},{6,7},{7,6},{8,9},{9,8},{10,11... | collective-permute-start | bytes 98312 | tf_op jit(solution)/shard_map/ppermute | solution.py:346
  112.1 2.8 %collective-permute-start.19 = (f32[32,256]{1,0:T(8,128)S(1)}, f32[32,256]{1,0:T(8,128)S(1)}, u32[]{:S(2)}, u32[]{:S(2)}) collective-permute-start(f32[32,256]{1,0:T(8,128)S(1)} %add.51.refs_0_), channel_id=1, source_target_pairs={{0,6},{1,7},{2,0},{3,1},{4,2},{5,3},{6,4},{7,5},{8,14},{9,15},{10,... | collective-permute-start | bytes 98312 | tf_op jit(solution)/shard_map/ppermute | solution.py:350
  112.2 4.3 %collective-permute-start.18 = (f32[32,256]{1,0:T(8,128)S(1)}, f32[32,256]{1,0:T(8,128)S(1)}, u32[]{:S(2)}, u32[]{:S(2)}) collective-permute-start(f32[32,256]{1,0:T(8,128)S(1)} %add.51.refs_0_), channel_id=1, source_target_pairs={{0,4},{1,5},{2,6},{3,7},{4,0},{5,1},{6,2},{7,3},{8,12},{9,13},{10,... | collective-permute-start | bytes 98312 | tf_op jit(solution)/shard_map/ppermute | solution.py:350
  113.1 4.6 %collective-permute-start.17 = (f32[32,256]{1,0:T(8,128)S(1)}, f32[32,256]{1,0:T(8,128)S(1)}, u32[]{:S(2)}, u32[]{:S(2)}) collective-permute-start(f32[32,256]{1,0:T(8,128)S(1)} %add.51.refs_0_), channel_id=1, source_target_pairs={{0,2},{1,3},{2,4},{3,5},{4,6},{5,7},{6,0},{7,1},{8,10},{9,11},{10,... | collective-permute-start | bytes 98312 | tf_op jit(solution)/shard_map/ppermute | solution.py:350
  113.9 34.0 %copy-start.10 = (f32[256]{0:T(256)S(1)}, f32[256]{0:T(256)}, u32[]{:S(2)}) copy-start(f32[256]{0:T(256)} %param.10) | copy-start | bytes 3076
  113.9 34.6 %copy-start.8 = (f32[256,256]{1,0:T(8,128)S(1)}, f32[256,256]{1,0:T(8,128)}, u32[]{:S(2)}) copy-start(f32[256,256]{1,0:T(8,128)} %param.9) | copy-start | bytes 786436
  118.5 29.3 %all-to-all-start.1 = ((f32[16,32,256]{2,1,0:T(8,128)}), f32[16,32,256]{2,1,0:T(8,128)S(1)}, u32[]{:S(2)}, u32[]{:S(2)}) async-start(f32[16,32,256]{2,1,0:T(8,128)} %add_up.5), calls=%async_computation.1 | async-start | bytes 1048576 | tf_op jit(solution)/shard_map/all_to_all | solution.py:426
  127.5 20.2 %collective-permute-start.15 = (bf16[256,256]{1,0:T(8,128)(2,1)S(1)}, bf16[256,256]{1,0:T(8,128)(2,1)S(1)}, u32[]{:S(2)}, u32[]{:S(2)}) collective-permute-start(bf16[256,256]{1,0:T(8,128)(2,1)S(1)} %get-tuple-element.29.refs_4_), channel_id=1, source_target_pairs={{0,1},{1,0},{2,3},{3,2},{4,5},{5,4},{6,7},{7,6},{8,9},{9,8},{10,11... | collective-permute-start | bytes 393224 | tf_op jit(solution)/shard_map/ppermute | solution.py:346
  147.8 1.9 %collective-permute-start.20 = (f32[16,32,256]{2,1,0:T(8,128)S(1)}, f32[16,32,256]{2,1,0:T(8,128)S(1)}, u32[]{:S(2)}, u32[]{:S(2)}) collective-permute-start(f32[16,32,256]{2,1,0:T(8,128)S(1)} %all-to-all-done.1), channel_id=1, source_target_pairs={{0,8},{8,0},{16,24},{24,16},{32,40},{40,32},{48,56},{56,48},{64,72... | collective-permute-start | bytes 1572872 | tf_op jit(solution)/shard_map/ppermute | solution.py:427
  149.8 0.7 copy-start.9

commit v7 on v6

--- a/solution.py
+++ b/solution.py
@@ -82,9 +82,9 @@
 def query_kernel(rel_ref, *refs):
     own = refs[:PARTS]
     idx_ref, mat_ref, _, s_ref, q_ref = refs[PARTS:]
-    column = jnp.broadcast_to(idx_ref[0].astype(f32), (128, CH)).T
+    column = jnp.broadcast_to(idx_ref[0].astype(f32), (128, PAD)).T
     column = column.astype(jnp.int32).astype(jnp.int16)
-    cols = lax.broadcasted_iota(jnp.int32, (CH, 128), 1).astype(jnp.int16)
+    cols = lax.broadcasted_iota(jnp.int32, (PAD, 128), 1).astype(jnp.int16)
     acc = None
     for b in range(NBLK):
         hot = jnp.concatenate(
@@ -106,16 +106,16 @@
         query_kernel,
         grid_spec=pltpu.PrefetchScalarGridSpec(
             num_scalar_prefetch=1,
-            grid=(NCH,),
+            grid=(GROUPS,),
             in_specs=[
                 *[pl.BlockSpec((PART, D), lambda j, rel: (0, 0))] * PARTS,
-                pl.BlockSpec((1, 1, CH), lambda j, rel: (j, 0, 0)),
-                pl.BlockSpec((1, D, D), lambda j, rel: (rel[j // PER], 0, 0)),
+                pl.BlockSpec((1, 1, PAD), lambda j, rel: (j, 0, 0)),
+                pl.BlockSpec((1, D, D), lambda j, rel: (rel[j], 0, 0)),
                 pl.BlockSpec(memory_space=pl.ANY),
             ],
             out_specs=[
-                pl.BlockSpec((CH, D), lambda j, rel: (j, 0)),
-                pl.BlockSpec((D, CH), lambda j, rel: (0, j)),
+                pl.BlockSpec((PAD, D), lambda j, rel: (j, 0)),
+                pl.BlockSpec((D, PAD), lambda j, rel: (0, j)),
             ],
         ),
         out_shape=[
@@ -131,40 +131,52 @@
 SUB = 32
 
 
-def score_kernel(cnt_ref, *refs):
+def score_kernel(rel_ref, cnt_ref, *refs):
     nxt = refs[:PARTS]
-    q_ref, dst_ref, wt_ref, gq_ref = refs[PARTS : PARTS + 4]
-    dg = refs[PARTS + 4 : 2 * PARTS + 4]
-    sc, nxt_t_ref, w0, w1, qs0, qs1, sl0, sl1, dacc, wcol = refs[2 * PARTS + 4 :]
+    q_ref, s_hbm, dst_ref, wt_ref, gq_ref = refs[PARTS : PARTS + 5]
+    dg = refs[PARTS + 5 : 2 * PARTS + 5]
+    rg_ref, sc, nxt_t_ref, *halves, dacc, wcol, racc, s_ref, s_sem = refs[
+        2 * PARTS + 5 :
+    ]
+    old = halves[0::2], halves[1::2]
+    load_s = pltpu.make_async_copy(s_hbm, s_ref, s_sem)
     g = pl.program_id(0)
     rows = lax.broadcasted_iota(jnp.int32, (SUB, CH), 0)
     rows16 = lax.broadcasted_iota(jnp.int32, (BLK, CH), 0).astype(jnp.int16)
 
     @pl.when(g == 0)
     def _():
+        load_s.start()
         dacc[...] = jnp.zeros_like(dacc)
-        w1[...] = jnp.zeros_like(w1)
+        racc[...] = jnp.zeros_like(racc)
+        for ref in old[1]:
+            ref[...] = jnp.zeros_like(ref)
         for b in range(NBLK):
             nxt_t_ref[:, b * BLK : (b + 1) * BLK] = block_of(nxt, b).T
-        qs1[...] = jnp.zeros_like(qs1)
-        sl1[...] = jnp.zeros_like(sl1)
-
-    for b in range(NBLK):
+
+    def spread(b, w, qs, sl, gain, dst):
         at = slice(b * BLK, (b + 1) * BLK)
-        wcol[at, :] = wt_ref[0, :, at].T
-
-    def spread(b, w, qs):
-        at = slice(b * BLK, (b + 1) * BLK)
-        dacc[at, :] += mm(w[at, :], qs[...], NT)
+        mask = rows16 == (dst[0:1, :] - b * BLK).astype(jnp.int16)
+        full = jnp.where(mask, gain[0:1, :].astype(bf16), w[at, :])
+        dacc[at, :] += mm(full, qs[...], NT)
+        return mm(nxt_t_ref[:, at], full)
 
     def finish(acc, sl, chunk):
         gq = (acc * sl[0:1, :]).astype(bf16)
         gq_ref[:, pl.ds(pl.multiple_of(chunk * CH, CH), CH)] = gq
 
-    def stage(half, w, qs, sl, w_old, qs_old, sl_old, chunk_old):
+    def stage(half, chunk_old):
+        w, qs, sl, gain_ref, dst_keep = old[half]
+        before = old[1 - half]
         here = slice(half * CH, (half + 1) * CH)
+        chunk = 2 * g + half
+        group = chunk // PER
+        for b in range(NBLK):
+            at = slice(b * BLK, (b + 1) * BLK)
+            wcol[at, :] = wt_ref[group, :, at].T
         q = q_ref[:, here]
         dst = dst_ref[0, 0:1, here]
+        acc = None
         top = jnp.full((8, CH), -jnp.inf, f32)
         hit = jnp.zeros((8, CH), f32)
         for b in range(NBLK):
@@ -178,117 +190,88 @@
                 sc[at, :] = val
                 top = jnp.maximum(top, jnp.max(val.reshape(SUB // 8, 8, CH), axis=0))
                 hit = hit + jnp.sum(jnp.where(mask, val, 0.0).reshape(SUB // 8, 8, CH), axis=0)
-            spread(b, w_old, qs_old)
+            part = spread(b, *before)
+            acc = part if acc is None else acc + part
+        finish(acc, before[2], chunk_old)
         top = jnp.max(top, axis=0, keepdims=True)
         hit = jnp.sum(hit, axis=0, keepdims=True)
         tot = jnp.zeros((8, CH), f32)
-        acc = None
         for b in range(NBLK):
             for i in range(BLK // SUB):
                 at = slice(b * BLK + i * SUB, b * BLK + (i + 1) * SUB)
                 e = jnp.exp2(sc[at, :] - top)
                 tot = tot + jnp.sum(e.reshape(SUB // 8, 8, CH), axis=0)
                 w[at, :] = e.astype(bf16)
-            at = slice(b * BLK, (b + 1) * BLK)
-            part = mm(nxt_t_ref[:, at], w_old[at, :])
-            acc = part if acc is None else acc + part
-        finish(acc, sl_old, chunk_old)
         tot = jnp.sum(tot, axis=0, keepdims=True)
-        gain = (jnp.exp2(hit - top) - tot).astype(bf16)
-        lane = lax.broadcasted_iota(jnp.int32, (1, CH), 1) + half * CH
-        live = jnp.logical_and(lane < SLOTS, g * SLOTS + lane < cnt_ref[0])
+        gain_ref[...] = jnp.broadcast_to(jnp.exp2(hit - top) - tot, (8, CH))
+        dst_keep[...] = jnp.broadcast_to(dst, (8, CH))
+        lane = lax.broadcasted_iota(jnp.int32, (1, CH), 1) + lax.rem(chunk, PER) * CH
+        live = jnp.logical_and(lane < SLOTS, group * SLOTS + lane < cnt_ref[0])
         scale = jnp.where(live, 1.0 / tot, 0.0)
         sl[...] = jnp.broadcast_to(scale, (8, CH))
         qs[...] = (q.astype(f32) * scale).astype(bf16)
+
+    stage(0, jnp.maximum(2 * g - 1, 0))
+    stage(1, 2 * g)
+
+    @pl.when(g == NCH // 2 - 1)
+    def _():
+        acc = None
         for b in range(NBLK):
-            at = slice(b * BLK, (b + 1) * BLK)
-            mask = rows16 == (dst - b * BLK).astype(jnp.int16)
-            w[at, :] = jnp.where(mask, gain, w[at, :])
-
-    stage(0, w0, qs0, sl0, w1, qs1, sl1, jnp.maximum(2 * g - 1, 0))
-    stage(1, w1, qs1, sl1, w0, qs0, sl0, 2 * g)
-
-    @pl.when(g == GROUPS - 1)
-    def _():
-        for b in range(NBLK):
-            spread(b, w1, qs1)
-        finish(mm(nxt_t_ref[...], w1[...]), sl1, 2 * g + 1)
+            part = spread(b, *old[1])
+            acc = part if acc is None else acc + part
+        finish(acc, old[1][2], 2 * g + 1)
+        load_s.wait()
+        for k in range(GROUPS):
+            at = slice(k * PAD, (k + 1) * PAD)
+            racc[rel_ref[k]] += mm(gq_ref[:, at], s_ref[at, :])
+        for k in range(racc.shape[0]):
+            rg_ref[k] = racc[k].T.astype(bf16)
         for p in range(PARTS):
             dg[p][...] = dacc[p * PART : (p + 1) * PART, :].astype(bf16)
 
 
-def score_side(nxt, q, dst_rows, weights, counts):
+def score_side(nxt, q, s, dst_rows, weights, rel_id, counts, kinds):
     return pl.pallas_call(
         score_kernel,
         grid_spec=pltpu.PrefetchScalarGridSpec(
-            num_scalar_prefetch=1,
-            grid=(GROUPS,),
+            num_scalar_prefetch=2,
+            grid=(NCH // 2,),
             in_specs=[
-                *[pl.BlockSpec((PART, D), lambda j, cnt: (0, 0))] * PARTS,
-                pl.BlockSpec((D, PAD), lambda j, cnt: (0, j)),
-                pl.BlockSpec((1, 1, PAD), lambda j, cnt: (j, 0, 0)),
-                pl.BlockSpec((1, 8, ROWS), lambda j, cnt: (j, 0, 0)),
+                *[pl.BlockSpec((PART, D), lambda j, rel, cnt: (0, 0))] * PARTS,
+                pl.BlockSpec((D, 2 * CH), lambda j, rel, cnt: (0, j)),
+                pl.BlockSpec(memory_space=pl.ANY),
+                pl.BlockSpec((1, 1, 2 * CH), lambda j, rel, cnt: (j, 0, 0)),
+                pl.BlockSpec((GROUPS, 8, ROWS), lambda j, rel, cnt: (0, 0, 0)),
             ],
             out_specs=[
-                pl.BlockSpec((D, GROUPS * PAD), lambda j, cnt: (0, 0)),
-                *[pl.BlockSpec((PART, D), lambda j, cnt: (0, 0))] * PARTS,
+                pl.BlockSpec((D, GROUPS * PAD), lambda j, rel, cnt: (0, 0)),
+                *[pl.BlockSpec((PART, D), lambda j, rel, cnt: (0, 0))] * PARTS,
+                pl.BlockSpec((kinds, D, D), lambda j, rel, cnt: (0, 0, 0)),
             ],
             scratch_shapes=[
                 pltpu.VMEM((ROWS, CH), f32),
                 pltpu.VMEM((D, ROWS), bf16),
-                pltpu.VMEM((ROWS, CH), bf16),
-                pltpu.VMEM((ROWS, CH), bf16),
-                pltpu.VMEM((D, CH), bf16),
-                pltpu.VMEM((D, CH), bf16),
-                pltpu.VMEM((8, CH), f32),
-                pltpu.VMEM((8, CH), f32),
+                *[pltpu.VMEM((ROWS, CH), bf16)] * 2,
+                *[pltpu.VMEM((D, CH), bf16)] * 2,
+                *[pltpu.VMEM((8, CH), f32)] * 4,
+                *[pltpu.VMEM((8, CH), jnp.int32)] * 2,
                 pltpu.VMEM((ROWS, D), f32),
                 pltpu.VMEM((ROWS, 8), f32),
+                pltpu.VMEM((kinds, D, D), f32),
+                pltpu.VMEM((GROUPS * PAD, D), bf16),
+                pltpu.SemaphoreType.DMA,
             ],
         ),
         out_shape=[
             jax.ShapeDtypeStruct((D, GROUPS * PAD), bf16),
             *[jax.ShapeDtypeStruct((PART, D), bf16)] * PARTS,
+            jax.ShapeDtypeStruct((kinds, D, D), bf16),
         ],
         compiler_params=params(),
         cost_estimate=cost(28),
         name="scores",
-    )(counts, *nxt, q, dst_rows, weights)
-
-
-def operator_kernel(rel_ref, gq_ref, s_ref, out_ref, acc):
-    g = pl.program_id(0)
-
-    @pl.when(g == 0)
-    def _():
-        acc[...] = jnp.zeros_like(acc)
-
-    acc[rel_ref[g]] += mm(gq_ref[...], s_ref[...])
-
-    @pl.when(g == GROUPS - 1)
-    def _():
-        for k in range(acc.shape[0]):
-            out_ref[k] = acc[k].T.astype(bf16)
-
-
-def operator_side(gq, s, rel_id, kinds):
-    return pl.pallas_call(
-        operator_kernel,
-        grid_spec=pltpu.PrefetchScalarGridSpec(
-            num_scalar_prefetch=1,
-            grid=(GROUPS,),
-            in_specs=[
-                pl.BlockSpec((D, PAD), lambda j, rel: (0, j)),
-                pl.BlockSpec((PAD, D), lambda j, rel: (j, 0)),
-            ],
-            out_specs=pl.BlockSpec((kinds, D, D), lambda j, rel: (0, 0, 0)),
-            scratch_shapes=[pltpu.VMEM((kinds, D, D), f32)],
-        ),
-        out_shape=jax.ShapeDtypeStruct((kinds, D, D), bf16),
-        compiler_params=params(),
-        cost_estimate=cost(2),
-        name="operator_grads",
-    )(rel_id, gq, s)
+    )(rel_id, counts, *nxt, q, s, dst_rows, weights)
 
 
 def source_kernel(rel_ref, gq_ref, src_ref, mat_ref, *refs):
@@ -421,13 +404,26 @@
     return ((index - PART * (rep // 2)) % ROWS) ^ (256 * (rep % 2))
 
 
-def spread_total(shares, kinds):
+def operator_update(total, relation, accum):
+    rows, width = total.shape
+    mine = lax.dynamic_slice(accum.reshape(-1), (lax.axis_index("dom") * rows,), (rows,))
+    fresh = mine + jnp.mean(total * total, -1)
+    step = total / jnp.sqrt(fresh)[:, None]
+    power = jnp.floor(jnp.log2(fresh))
+    part = fresh * jnp.exp2(-power)
+    high = lax.reduce_precision(part, 5, 10)
+    code = jnp.pad(jnp.stack([power, high, part - high]), ((0, 5), (0, width - rows)))
+    send = jnp.concatenate([step, code]).astype(jnp.float16)
     cores = [[2 * i + c for i in range(16)] for c in range(2)]
+    shares = jnp.broadcast_to(send, (16,) + send.shape)
     half = lax.all_to_all(shares, "dom", 0, 0, axis_index_groups=cores)
     other = lax.ppermute(half, "dom", [(i, i ^ 1) for i in range(32)])
     second = lax.axis_index("dom") % 2 == 1
     pairs = [jnp.where(second, other, half), jnp.where(second, half, other)]
-    return jnp.stack(pairs, 1).reshape(kinds, D, D)
+    full = jnp.stack(pairs, 1).reshape(32, rows + 8, width).astype(f32)
+    steps = full[:, :rows].reshape(relation.shape)
+    power, high, low = (full[:, rows + i, :rows].reshape(accum.shape) for i in range(3))
+    return relation - learn_rate * steps, (high + low) * jnp.exp2(power)
 
 
 def pad_slots(index, fill):
@@ -435,12 +431,13 @@
 
 
 def source_stage(own, src_pad, rel_id, relation, after):
-    return make_queries(own, src_pad.reshape(NCH, 1, CH), rel_id, relation, after)
+    return make_queries(own, src_pad.reshape(GROUPS, 1, PAD), rel_id, relation, after)
 
 
 def target_stage(nxt, q, s, dst_pad, weights, rel_id, counts, kinds):
-    out = score_side(nxt, q, dst_pad.reshape(GROUPS, 1, PAD), weights, counts)
-    return out[0], out[1:], operator_side(out[0], s, rel_id, kinds)
+    rows = dst_pad.reshape(NCH // 2, 1, 2 * CH)
+    out = score_side(nxt, q, s, rows, weights, rel_id, counts, kinds)
+    return out[0], out[1 : PARTS + 1], out[PARTS + 1]
 
 
 def back_stage(gq, src_pad, rel_id, relation):
@@ -476,21 +473,19 @@
     gq, dst_grad, rel_grad = target_stage(
         nxt, q, s, dst_pad, weights, rel_id, counts, relation.shape[0]
     )
-    kinds = relation.shape[0]
     dst_blocks = send_x(dst_grad)
     got = lax.all_to_all(rel_grad.reshape(32, -1, D), "dom", 0, 0)
     src_grad = back_stage(gq, src_pad, rel_id, relation)
     src_blocks = send_x(src_grad)
     mine = add_up([got], src_grad[0], f32)
     zsum = mine + swap_z(mine)
-    dst_sum = add_up(dst_blocks, mine, bf16)
+    dst_sum = add_up(dst_blocks, zsum, bf16)
     moved = shift_dom(dst_sum, 1)
     keep, give = split_sum(src_blocks + [moved])
-    shares = add_up([zsum] + [shift_x(zsum, k) for k in (1, 2, 3)], give, f32, 16)
-    rel_total = spread_total(shares, kinds)
+    rel_total = add_up([zsum] + [shift_x(zsum, k) for k in (1, 2, 3)], give, f32)
+    relation_new, relation_accum_new = operator_update(rel_total, relation, relation_accum)
     grads = keep + swap_z(give).astype(f32)
     entity_new, entity_accum_new = rowwise(entity, entity_accum, grads)
-    relation_new, relation_accum_new = rowwise(relation, relation_accum, rel_total)
     return (entity_new, entity_accum_new, relation_new, relation_accum_new)
 
 

time: 153 us -> 152 us (level)
  starting transfers between devices: 57.1 us -> 66.7 us
  waiting for transfers between devices: 28 us -> 18.5 us
  Pallas kernels: 56.2 us -> 49.8 us
  local copies, waits for them, and re-layouts: 3.32 us -> 9.42 us
    all_to_all x1, waiting for transfers between devices: 17.9 us -> 0.01 us  [operator_update(): half = lax.all_to_all(shares, 'dom', 0, 0, axis_index_groups=cores)]
    ppermute x1, starting transfers between devices: 0.01 us -> 6.18 us  [operator_update(): other = lax.ppermute(half, 'dom', [(i, i ^ 1) for i in range(32)])]
    ppermute x3, waiting for transfers between devices: 3.04 us -> 8.54 us  [swap_z(): return lax.ppermute(block, 'rep', [(i, i ^ 1) for i in range(8)])]
    all_to_all x1, starting transfers between devices: 9.03 us -> 3.54 us  [operator_update(): half = lax.all_to_all(shares, 'dom', 0, 0, axis_index_groups=cores)]
    unnamed x22 -> x29, local copies, waits for them, and re-layouts: 2.86 us -> 7.62 us
    ppermute x12, starting transfers between devices: 13.4 us -> 16.7 us  [shift_x(): return lax.ppermute(block, 'rep', [(i, (i + 2 * by) % 8) for i in range(8)])]
    ppermute x5, starting transfers between devices: 11.6 us -> 14.8 us  [shift_dom(): lax.ppermute(block, 'dom', [(i, (i + by) % size) for i in range(size)])]
    pallas_call x1 -> x0, Pallas kernels: 3.05 us -> none  [operator_side(): pl.pallas_call(operator_kernel, grid_spec=pltpu.PrefetchScalarGridSpec(nu...]
  transfers between devices with their start and end apart: 23 -> 23, of which waited for: 8 -> 5; matrix products, arithmetic and copies ran while one was open for 2% -> 2% of each run, Pallas kernels for 15% -> 13%
where the time goes in v7:
time: 152 us
  starting transfers between devices  66.7 us (44%)
  Pallas kernels  49.8 us (33%)
  waiting for transfers between devices  18.5 us (12%)
  local copies, waits for them, and re-layouts  9.42 us (6%)
  other arithmetic  5.89 us (4%)
  between operations  1.59 us (1%)
    pallas_call x1, Pallas kernels, score_side(): pl.pallas_call(score_kernel, grid_spec=pltpu.PrefetchScalarGridSpec(num_s...  30.2 us
    ppermute x3, starting transfers between devices, swap_z(): return lax.ppermute(block, 'rep', [(i, i ^ 1) for i in range(8)])  17.9 us
    ppermute x12, starting transfers between devices, shift_x(): return lax.ppermute(block, 'rep', [(i, (i + 2 * by) % 8) for i in range(8)])  16.7 us
    ppermute x5, starting transfers between devices, shift_dom(): lax.ppermute(block, 'dom', [(i, (i + by) % size) for i in range(size)])  14.8 us
    ppermute x3, waiting for transfers between devices, swap_z(): return lax.ppermute(block, 'rep', [(i, i ^ 1) for i in range(8)])  8.54 us
    pallas_call x1, Pallas kernels, make_queries(): pl.pallas_call(query_kernel, grid_spec=pltpu.PrefetchScalarGridSpec(num_s...  7.95 us
    unnamed x29, local copies, waits for them, and re-layouts  7.62 us
    all_to_all x1, starting transfers between devices, on_device(): got = lax.all_to_all(rel_grad.reshape(32, -1, D), 'dom', 0, 0)  7.56 us
  transfers between devices with their start and end apart: 23, of which 5 were waited for; matrix products, arithmetic and copies ran while one was open for 2% of the time, Pallas kernels for 13%

profile of v7, /device:TPU:1, one launch (start us, length us, event | category | flops | bytes accessed | tf_op | source)
XLA Modules:
  0.0 151.9 jit_solution(1181503380325388298)
XLA Ops:
  0.6 1.0 convert_element_type.15
  1.6 7.8 %collective-permute-start = (bf16[256,256]{1,0:T(8,128)(2,1)S(1)}, bf16[256,256]{1,0:T(8,128)(2,1)S(1)}, u32[]{:S(2)}, u32[]{:S(2)}) collective-permute-start(bf16[256,256]{1,0:T(8,128)(2,1)S(1)} %convert_element_type.15), channel_id=1, source_target_pairs={{0,1},{1,0},{2,3},{3,2},{4,5},{5,4},{6,7},{7,6},{8,9},{9,8},{10,11... | collective-permute-start | bytes 393224 | tf_op jit(solution)/shard_map/ppermute | solution.py:329
  9.4 0.8 fusion.1
  10.3 1.8 %collective-permute-done = bf16[256,256]{1,0:T(8,128)(2,1)S(1)} collective-permute-done((bf16[256,256]{1,0:T(8,128)(2,1)S(1)}, bf16[256,256]{1,0:T(8,128)(2,1)S(1)}, u32[]{:S(2)}, u32[]{:S(2)}) %collective-permute-start) | collective-permute-done | bytes 131104 | tf_op jit(solution)/shard_map/ppermute | solution.py:329
  12.1 2.0 %collective-permute-start.1 = (bf16[512,256]{1,0:T(8,128)(2,1)S(1)}, bf16[512,256]{1,0:T(8,128)(2,1)S(1)}, u32[]{:S(2)}, u32[]{:S(2)}) collective-permute-start(bf16[512,256]{1,0:T(8,128)(2,1)S(1)} %pad_maximum_fusion.refs_0_), channel_id=1, source_target_pairs={{0,248},{8,0},{16,8},{24,16},{32,24},{40,32},{48,40},{56,48},{64,5... | collective-permute-start | bytes 786440 | tf_op jit(solution)/shard_map/ppermute | solution.py:325
  14.1 2.5 %collective-permute-start.2 = (bf16[512,256]{1,0:T(8,128)(2,1)S(1)}, bf16[512,256]{1,0:T(8,128)(2,1)S(1)}, u32[]{:S(2)}, u32[]{:S(2)}) collective-permute-start(bf16[512,256]{1,0:T(8,128)(2,1)S(1)} %pad_maximum_fusion.refs_0_), channel_id=1, source_target_pairs={{0,6},{1,7},{2,0},{3,1},{4,2},{5,3},{6,4},{7,5},{8,14},{9,15},{10,... | collective-permute-start | bytes 786440 | tf_op jit(solution)/shard_map/ppermute | solution.py:333
  16.6 0.5 collective-permute-start.4
  17.1 0.6 collective-permute-start.6
  17.7 0.7 fusion.5
  19.2 3.2 %neg_weights.1.refs_7_ = f32[4,8,2048]{2,1,0:T(8,128)S(1)} custom-call(s32[4,1,1024]{2,1,0:T(1,128)S(1)} %reshape.47.neg_ref), custom_call_target="tpu_custom_call" | custom-call | flops 1500000000 | bytes 10500000 | tf_op jit(solution)/shard_map/neg_weights/pallas_call | solution.py:70
  22.5 0.6 collective-permute-done.2.refs_1_
  23.1 5.6 %collective-permute-start.3 = (bf16[512,256]{1,0:T(8,128)(2,1)S(1)}, bf16[512,256]{1,0:T(8,128)(2,1)S(1)}, u32[]{:S(2)}, u32[]{:S(2)}) collective-permute-start(bf16[512,256]{1,0:T(8,128)(2,1)S(1)} %collective-permute-done.2.refs_1_), channel_id=1, source_target_pairs={{0,248},{8,0},{16,8},{24,16},{32,24},{40,32},{48,40},{56,48},{64,5... | collective-permute-start | bytes 786440 | tf_op jit(solution)/shard_map/ppermute | solution.py:325
  28.7 4.6 %collective-permute-start.5 = (bf16[512,256]{1,0:T(8,128)(2,1)S(1)}, bf16[512,256]{1,0:T(8,128)(2,1)S(1)}, u32[]{:S(2)}, u32[]{:S(2)}) collective-permute-start(bf16[512,256]{1,0:T(8,128)(2,1)S(1)} %collective-permute-done.4.refs_2_), channel_id=1, source_target_pairs={{0,248},{8,0},{16,8},{24,16},{32,24},{40,32},{48,40},{56,48},{64,5... | collective-permute-start | bytes 786440 | tf_op jit(solution)/shard_map/ppermute | solution.py:325
  33.4 1.0 collective-permute-start.7
  34.4 8.0 %queries.1 = (bf16[4096,256]{1,0:T(8,128)(2,1)S(1)}, bf16[256,4096]{1,0:T(8,128)(2,1)}) custom-call(s32[4]{0:T(128)S(1)} %copy-done.3, bf16[512,256]{1,0:T(8,128)(2,1)S(1)} %pad_maximum_fusion.refs_0_, bf16[512,256]{1,0:T(8,128)(2,1)S(1)} %collective-permute-done.2.refs_1_, bf16[512,256]{1,0:T(8,128)(2,1)S(1)} %collective-permute-done.4.refs_2_, ...), custom_call_target="tpu_custom_call" | custom-call | flops 4499999744 | bytes 31500000 | tf_op jit(solution)/shard_map/queries/pallas_call | solution.py:105
  42.4 1.3 copy-done.10
  43.7 30.2 %scores.1 = (bf16[256,4096]{1,0:T(8,128)(2,1)S(1)}, bf16[512,256]{1,0:T(8,128)(2,1)S(1)}, bf16[512,256]{1,0:T(8,128)(2,1)}, bf16[512,256]{1,0:T(8,128)(2,1)S(1)}...) custom-call(s32[4]{0:T(128)S(1)} %copy-done.3, s32[1]{0:T(128)S(6)} %copy.18.cnt_ref, ...), custom_call_target="tpu_custom_call" | custom-call | flops 14000000000 | bytes 98000000 | tf_op jit(solution)/shard_map/scores/pallas_call | solution.py:235
  73.9 0.7 copy-done.4
  74.6 1.4 copy-done.8
  76.0 7.6 %all-to-all-start = ((bf16[32,32,256]{2,1,0:T(8,128)(2,1)}), bf16[32,32,256]{2,1,0:T(8,128)(2,1)S(1)}, u32[]{:S(2)}, u32[]{:S(2)}) async-start(bf16[32,32,256]{2,1,0:T(8,128)(2,1)} %bitcast), calls=%async_computation | async-start | bytes 1048576 | tf_op jit(solution)/shard_map/all_to_all | solution.py:477
  83.7 3.6 %collective-permute-start.12 = (bf16[512,256]{1,0:T(8,128)(2,1)S(1)}, bf16[512,256]{1,0:T(8,128)(2,1)}, u32[]{:S(2)}, u32[]{:S(2)}) collective-permute-start(bf16[512,256]{1,0:T(8,128)(2,1)S(1)} %get-tuple-element.27), channel_id=1, source_target_pairs={{0,4},{1,5},{2,6},{3,7},{4,0},{5,1},{6,2},{7,3},{8,12},{9,13},{10,... | collective-permute-start | bytes 786440 | tf_op jit(solution)/shard_map/ppermute | solution.py:333
  87.2 1.6 %copy-done.9 = bf16[256,4096]{1,0:T(8,128)(2,1)S(1)} copy-done((bf16[256,4096]{1,0:T(8,128)(2,1)S(1)}, bf16[256,4096]{1,0:T(8,128)(2,1)}, u32[]{:S(2)}) %copy-start.9) | copy-done | bytes 2097176
  88.8 6.9 %source_grads.1 = (bf16[512,256]{1,0:T(8,128)(2,1)S(1)}, bf16[512,256]{1,0:T(8,128)(2,1)S(1)}, bf16[512,256]{1,0:T(8,128)(2,1)S(1)}, bf16[512,256]{1,0:T(8,128)(2,1)S(1)}) custom-call(s32[4]{0:T(128)S(1)} %copy-done.3, bf16[256,4096]{1,0:T(8,128)(2,1)S(1)} %copy-done.9, s32[4,1,1024]{2,1,0:T(1,128)S(1)} %reshape.44.refs_4_.src_ref, f32[4,256,256]{2,1,0:T(8,128)S(1)} %copy-done), custom_call_target="tpu_custom_call" | custom-call | flops 4000000000 | bytes 28000000 | tf_op jit(solution)/shard_map/source_grads/pallas_call | solution.py:298
  95.7 4.3 %all-to-all-done.refs_0_ = bf16[32,32,256]{2,1,0:T(8,128)(2,1)S(1)} async-done(((bf16[32,32,256]{2,1,0:T(8,128)(2,1)}), bf16[32,32,256]{2,1,0:T(8,128)(2,1)S(1)}, u32[]{:S(2)}, u32[]{:S(2)}) %all-to-all-start) | async-done | bytes 524320 | tf_op jit(solution)/shard_map/all_to_all | solution.py:477
  100.1 5.0 %collective-permute-start.14 = (f32[32,256]{1,0:T(8,128)S(1)}, f32[32,256]{1,0:T(8,128)S(1)}, u32[]{:S(2)}, u32[]{:S(2)}) collective-permute-start(f32[32,256]{1,0:T(8,128)S(1)} %add_up.3), channel_id=1, source_target_pairs={{0,1},{1,0},{2,3},{3,2},{4,5},{5,4},{6,7},{7,6},{8,9},{9,8},{10,11... | collective-permute-start | bytes 98312 | tf_op jit(solution)/shard_map/ppermute | solution.py:329
  105.1 2.5 %collective-permute-start.10 = (bf16[512,256]{1,0:T(8,128)(2,1)S(1)}, bf16[512,256]{1,0:T(8,128)(2,1)S(1)}, u32[]{:S(2)}, u32[]{:S(2)}) collective-permute-start(bf16[512,256]{1,0:T(8,128)(2,1)S(1)} %get-tuple-element.24), channel_id=1, source_target_pairs={{0,6},{1,7},{2,0},{3,1},{4,2},{5,3},{6,4},{7,5},{8,14},{9,15},{10,... | collective-permute-start | bytes 786440 | tf_op jit(solution)/shard_map/ppermute | solution.py:333
  107.6 3.4 %collective-permute-start.9 = (bf16[512,256]{1,0:T(8,128)(2,1)S(1)}, bf16[512,256]{1,0:T(8,128)(2,1)S(1)}, u32[]{:S(2)}, u32[]{:S(2)}) collective-permute-start(bf16[512,256]{1,0:T(8,128)(2,1)S(1)} %get-tuple-element.23), channel_id=1, source_target_pairs={{0,4},{1,5},{2,6},{3,7},{4,0},{5,1},{6,2},{7,3},{8,12},{9,13},{10,... | collective-permute-start | bytes 786440 | tf_op jit(solution)/shard_map/ppermute | solution.py:333
  111.0 1.2 add_up.4
  112.2 1.6 %collective-permute-start.15 = (bf16[512,256]{1,0:T(8,128)(2,1)S(1)}, bf16[512,256]{1,0:T(8,128)(2,1)S(1)}, u32[]{:S(2)}, u32[]{:S(2)}) collective-permute-start(bf16[512,256]{1,0:T(8,128)(2,1)S(1)} %add_up.4), channel_id=1, source_target_pairs={{0,8},{8,16},{16,24},{24,32},{32,40},{40,48},{48,56},{56,64},{64,7... | collective-permute-start | bytes 786440 | tf_op jit(solution)/shard_map/ppermute | solution.py:325
  113.8 5.0 %collective-permute-done.10.refs_3_ = bf16[512,256]{1,0:T(8,128)(2,1)S(1)} collective-permute-done((bf16[512,256]{1,0:T(8,128)(2,1)S(1)}, bf16[512,256]{1,0:T(8,128)(2,1)S(1)}, u32[]{:S(2)}, u32[]{:S(2)}) %collective-permute-start.10) | collective-permute-done | bytes 262176 | tf_op jit(solution)/shard_map/ppermute | solution.py:333
  118.8 3.6 %collective-permute-start.19 = (f32[32,256]{1,0:T(8,128)S(1)}, f32[32,256]{1,0:T(8,128)S(1)}, u32[]{:S(2)}, u32[]{:S(2)}) collective-permute-start(f32[32,256]{1,0:T(8,128)S(1)} %add.57.refs_4_.refs_0_), channel_id=1, source_target_pairs={{0,6},{1,7},{2,0},{3,1},{4,2},{5,3},{6,4},{7,5},{8,14},{9,15},{10,... | collective-permute-start | bytes 98312 | tf_op jit(solution)/shard_map/ppermute | solution.py:333
  122.4 0.7 copy-done.1
  123.1 0.9 copy-done.2
  124.0 0.9 copy-done.7
  125.0 0.2 split_sum.1
  125.6 0.8 broadcast_in_dim.2
  126.4 3.5 %all-to-all-start.1 = ((f16[16,40,256]{2,1,0:T(8,128)(2,1)}), f16[16,40,256]{2,1,0:T(8,128)(2,1)S(1)}, u32[]{:S(2)}, u32[]{:S(2)}) async-start(f16[16,40,256]{2,1,0:T(8,128)(2,1)} %broadcast_in_dim.2), calls=%async_computation.1 | async-start | bytes 655360 | tf_op jit(solution)/shard_map/all_to_all | solution.py:419
  129.9 5.1 %collective-permute-start.16 = (bf16[256,256]{1,0:T(8,128)(2,1)S(1)}, bf16[256,256]{1,0:T(8,128)(2,1)S(1)}, u32[]{:S(2)}, u32[]{:S(2)}) collective-permute-start(bf16[256,256]{1,0:T(8,128)(2,1)S(1)} %get-tuple-element.31.refs_4_), channel_id=1, source_target_pairs={{0,1},{1,0},{2,3},{3,2},{4,5},{5,4},{6,7},{7,6},{8,9},{9,8},{10,11... | collective-permute-start | bytes 393224 | tf_op jit(solution)/shard_map/ppermute | solution.py:329
  135.0 6.7 %collective-permute-done.16 = bf16[256,256]{1,0:T(8,128)(2,1)S(1)} collective-permute-done((bf16[256,256]{1,0:T(8,128)(2,1)S(1)}, bf16[256,256]{1,0:T(8,128)(2,1)S(1)}, u32[]{:S(2)}, u32[]{:S(2)}) %collective-permute-start.16) | collective-permute-done | bytes 131104 | tf_op jit(solution)/shard_map/ppermute | solution.py:329
  141.7 0.1 multiply_reduce_fusion
  141.9 6.2 %collective-permute-start.20 = (f16[16,40,256]{2,1,0:T(8,128)(2,1)S(1)}, f16[16,40,256]{2,1,0:T(8,128)(2,1)S(1)}, u32[]{:S(2)}, u32[]{:S(2)}) collective-permute-start(f16[16,40,256]{2,1,0:T(8,128)(2,1)S(1)} %all-to-all-done.1), channel_id=1, source_target_pairs={{0,8},{8,0},{16,24},{24,16},{32,40},{40,32},{48,56},{56,48},{64,72... | collective-permute-start | bytes 983048 | tf_op jit(solution)/shard_map/ppermute | solution.py:420
  148.1 0.6 fusion.22
  148.6 0.8 divide_subtract_fusion
  149.4 0.2 select_bitcast_fusion.1
  149.7 0.2 copy.16
  149.9 0.1 slice_multiply_fusion
  150.1 1.1 bitcast_subtract_fusion
  151.2 0.7 mul.55
  (66 shorter events, 1.1 us)
Async XLA Ops:
  1.6 10.5 %collective-permute-start = (bf16[256,256]{1,0:T(8,128)(2,1)S(1)}, bf16[256,256]{1,0:T(8,128)(2,1)S(1)}, u32[]{:S(2)}, u32[]{:S(2)}) collective-permute-start(bf16[256,256]{1,0:T(8,128)(2,1)S(1)} %convert_element_type.15), channel_id=1, source_target_pairs={{0,1},{1,0},{2,3},{3,2},{4,5},{5,4},{6,7},{7,6},{8,9},{9,8},{10,11... | collective-permute-start | bytes 393224 | tf_op jit(solution)/shard_map/ppermute | solution.py:329
  12.1 22.3 %collective-permute-start.1 = (bf16[512,256]{1,0:T(8,128)(2,1)S(1)}, bf16[512,256]{1,0:T(8,128)(2,1)S(1)}, u32[]{:S(2)}, u32[]{:S(2)}) collective-permute-start(bf16[512,256]{1,0:T(8,128)(2,1)S(1)} %pad_maximum_fusion.refs_0_), channel_id=1, source_target_pairs={{0,248},{8,0},{16,8},{24,16},{32,24},{40,32},{48,40},{56,48},{64,5... | collective-permute-start | bytes 786440 | tf_op jit(solution)/shard_map/ppermute | solution.py:325
  14.1 9.0 %collective-permute-start.2 = (bf16[512,256]{1,0:T(8,128)(2,1)S(1)}, bf16[512,256]{1,0:T(8,128)(2,1)S(1)}, u32[]{:S(2)}, u32[]{:S(2)}) collective-permute-start(bf16[512,256]{1,0:T(8,128)(2,1)S(1)} %pad_maximum_fusion.refs_0_), channel_id=1, source_target_pairs={{0,6},{1,7},{2,0},{3,1},{4,2},{5,3},{6,4},{7,5},{8,14},{9,15},{10,... | collective-permute-start | bytes 786440 | tf_op jit(solution)/shard_map/ppermute | solution.py:333
  16.6 12.2 %collective-permute-start.4 = (bf16[512,256]{1,0:T(8,128)(2,1)S(1)}, bf16[512,256]{1,0:T(8,128)(2,1)S(1)}, u32[]{:S(2)}, u32[]{:S(2)}) collective-permute-start(bf16[512,256]{1,0:T(8,128)(2,1)S(1)} %pad_maximum_fusion.refs_0_), channel_id=1, source_target_pairs={{0,4},{1,5},{2,6},{3,7},{4,0},{5,1},{6,2},{7,3},{8,12},{9,13},{10,... | collective-permute-start | bytes 786440 | tf_op jit(solution)/shard_map/ppermute | solution.py:333
  17.1 16.3 %collective-permute-start.6 = (bf16[512,256]{1,0:T(8,128)(2,1)S(1)}, bf16[512,256]{1,0:T(8,128)(2,1)S(1)}, u32[]{:S(2)}, u32[]{:S(2)}) collective-permute-start(bf16[512,256]{1,0:T(8,128)(2,1)S(1)} %pad_maximum_fusion.refs_0_), channel_id=1, source_target_pairs={{0,2},{1,3},{2,4},{3,5},{4,6},{5,7},{6,0},{7,1},{8,10},{9,11},{10,... | collective-permute-start | bytes 786440 | tf_op jit(solution)/shard_map/ppermute | solution.py:333
  19.2 15.2 %copy-start = (f32[4,256,256]{2,1,0:T(8,128)S(1)}, f32[4,256,256]{2,1,0:T(8,128)}, u32[]{:S(2)}) copy-start(f32[4,256,256]{2,1,0:T(8,128)} %mat_ref.1) | copy-start | bytes 3145732
  19.2 15.2 %copy-start.3 = (s32[4]{0:T(128)S(1)}, s32[4]{0:T(128)}, u32[]{:S(2)}) copy-start(s32[4]{0:T(128)} %rel_ref.5) | copy-start | bytes 52
  23.1 20.6 %collective-permute-start.3 = (bf16[512,256]{1,0:T(8,128)(2,1)S(1)}, bf16[512,256]{1,0:T(8,128)(2,1)S(1)}, u32[]{:S(2)}, u32[]{:S(2)}) collective-permute-start(bf16[512,256]{1,0:T(8,128)(2,1)S(1)} %collective-permute-done.2.refs_1_), channel_id=1, source_target_pairs={{0,248},{8,0},{16,8},{24,16},{32,24},{40,32},{48,40},{56,48},{64,5... | collective-permute-start | bytes 786440 | tf_op jit(solution)/shard_map/ppermute | solution.py:325
  28.7 15.0 %collective-permute-start.5 = (bf16[512,256]{1,0:T(8,128)(2,1)S(1)}, bf16[512,256]{1,0:T(8,128)(2,1)S(1)}, u32[]{:S(2)}, u32[]{:S(2)}) collective-permute-start(bf16[512,256]{1,0:T(8,128)(2,1)S(1)} %collective-permute-done.4.refs_2_), channel_id=1, source_target_pairs={{0,248},{8,0},{16,8},{24,16},{32,24},{40,32},{48,40},{56,48},{64,5... | collective-permute-start | bytes 786440 | tf_op jit(solution)/shard_map/ppermute | solution.py:325
  33.4 10.3 %collective-permute-start.7 = (bf16[512,256]{1,0:T(8,128)(2,1)S(1)}, bf16[512,256]{1,0:T(8,128)(2,1)S(1)}, u32[]{:S(2)}, u32[]{:S(2)}) collective-permute-start(bf16[512,256]{1,0:T(8,128)(2,1)S(1)} %collective-permute-done.6.refs_3_), channel_id=1, source_target_pairs={{0,248},{8,0},{16,8},{24,16},{32,24},{40,32},{48,40},{56,48},{64,5... | collective-permute-start | bytes 786440 | tf_op jit(solution)/shard_map/ppermute | solution.py:325
  42.4 1.3 copy-start.10
  73.9 0.7 copy-start.4
  74.6 1.4 copy-start.8
  76.0 24.0 %all-to-all-start = ((bf16[32,32,256]{2,1,0:T(8,128)(2,1)}), bf16[32,32,256]{2,1,0:T(8,128)(2,1)S(1)}, u32[]{:S(2)}, u32[]{:S(2)}) async-start(bf16[32,32,256]{2,1,0:T(8,128)(2,1)} %bitcast), calls=%async_computation | async-start | bytes 1048576 | tf_op jit(solution)/shard_map/all_to_all | solution.py:477
  83.6 24.0 %collective-permute-start.11 = (bf16[512,256]{1,0:T(8,128)(2,1)}, bf16[512,256]{1,0:T(8,128)(2,1)}, u32[]{:S(2)}, u32[]{:S(2)}) collective-permute-start(bf16[512,256]{1,0:T(8,128)(2,1)} %get-tuple-element.26), channel_id=1, source_target_pairs={{0,2},{1,3},{2,4},{3,5},{4,6},{5,7},{6,0},{7,1},{8,10},{9,11},{10,... | collective-permute-start | bytes 786440 | tf_op jit(solution)/shard_map/ppermute | solution.py:333
  83.7 27.3 %collective-permute-start.12 = (bf16[512,256]{1,0:T(8,128)(2,1)S(1)}, bf16[512,256]{1,0:T(8,128)(2,1)}, u32[]{:S(2)}, u32[]{:S(2)}) collective-permute-start(bf16[512,256]{1,0:T(8,128)(2,1)S(1)} %get-tuple-element.27), channel_id=1, source_target_pairs={{0,4},{1,5},{2,6},{3,7},{4,0},{5,1},{6,2},{7,3},{8,12},{9,13},{10,... | collective-permute-start | bytes 786440 | tf_op jit(solution)/shard_map/ppermute | solution.py:333
  87.2 23.8 %collective-permute-start.13 = (bf16[512,256]{1,0:T(8,128)(2,1)S(1)}, bf16[512,256]{1,0:T(8,128)(2,1)}, u32[]{:S(2)}, u32[]{:S(2)}) collective-permute-start(bf16[512,256]{1,0:T(8,128)(2,1)S(1)} %get-tuple-element.28), channel_id=1, source_target_pairs={{0,6},{1,7},{2,0},{3,1},{4,2},{5,3},{6,4},{7,5},{8,14},{9,15},{10,... | collective-permute-start | bytes 786440 | tf_op jit(solution)/shard_map/ppermute | solution.py:333
  87.2 1.6 %copy-start.9 = (bf16[256,4096]{1,0:T(8,128)(2,1)S(1)}, bf16[256,4096]{1,0:T(8,128)(2,1)}, u32[]{:S(2)}) copy-start(bf16[256,4096]{1,0:T(8,128)(2,1)} %copy-done.8) | copy-start | bytes 6291460
  95.7 9.4 %copy-start.6 = (bf16[512,256]{1,0:T(8,128)(2,1)}, bf16[512,256]{1,0:T(8,128)(2,1)S(1)}, u32[]{:S(2)}) copy-start(bf16[512,256]{1,0:T(8,128)(2,1)S(1)} %get-tuple-element.21.refs_1_.refs_0_) | copy-start | bytes 786436
  100.0 11.0 %copy-start.5 = (bf16[512,256]{1,0:T(8,128)(2,1)S(1)}, bf16[512,256]{1,0:T(8,128)(2,1)}, u32[]{:S(2)}) copy-start(bf16[512,256]{1,0:T(8,128)(2,1)} %copy-done.4) | copy-start | bytes 786436
  100.1 13.7 %copy-start.12 = (f32[4,256]{1,0:T(4,128)S(1)}, f32[4,256]{1,0:T(4,128)}, u32[]{:S(2)}) copy-start(f32[4,256]{1,0:T(4,128)} %param.12) | copy-start | bytes 12292
  100.1 7.5 %collective-permute-start.14 = (f32[32,256]{1,0:T(8,128)S(1)}, f32[32,256]{1,0:T(8,128)S(1)}, u32[]{:S(2)}, u32[]{:S(2)}) collective-permute-start(f32[32,256]{1,0:T(8,128)S(1)} %add_up.3), channel_id=1, source_target_pairs={{0,1},{1,0},{2,3},{3,2},{4,5},{5,4},{6,7},{7,6},{8,9},{9,8},{10,11... | collective-permute-start | bytes 98312 | tf_op jit(solution)/shard_map/ppermute | solution.py:329
  105.1 13.8 %collective-permute-start.10 = (bf16[512,256]{1,0:T(8,128)(2,1)S(1)}, bf16[512,256]{1,0:T(8,128)(2,1)S(1)}, u32[]{:S(2)}, u32[]{:S(2)}) collective-permute-start(bf16[512,256]{1,0:T(8,128)(2,1)S(1)} %get-tuple-element.24), channel_id=1, source_target_pairs={{0,6},{1,7},{2,0},{3,1},{4,2},{5,3},{6,4},{7,5},{8,14},{9,15},{10,... | collective-permute-start | bytes 786440 | tf_op jit(solution)/shard_map/ppermute | solution.py:333
  107.6 11.2 %collective-permute-start.8 = (bf16[512,256]{1,0:T(8,128)(2,1)S(1)}, bf16[512,256]{1,0:T(8,128)(2,1)S(1)}, u32[]{:S(2)}, u32[]{:S(2)}) collective-permute-start(bf16[512,256]{1,0:T(8,128)(2,1)S(1)} %get-tuple-element.22), channel_id=1, source_target_pairs={{0,2},{1,3},{2,4},{3,5},{4,6},{5,7},{6,0},{7,1},{8,10},{9,11},{10,... | collective-permute-start | bytes 786440 | tf_op jit(solution)/shard_map/ppermute | solution.py:333
  107.6 14.8 %collective-permute-start.9 = (bf16[512,256]{1,0:T(8,128)(2,1)S(1)}, bf16[512,256]{1,0:T(8,128)(2,1)S(1)}, u32[]{:S(2)}, u32[]{:S(2)}) collective-permute-start(bf16[512,256]{1,0:T(8,128)(2,1)S(1)} %get-tuple-element.23), channel_id=1, source_target_pairs={{0,4},{1,5},{2,6},{3,7},{4,0},{5,1},{6,2},{7,3},{8,12},{9,13},{10,... | collective-permute-start | bytes 786440 | tf_op jit(solution)/shard_map/ppermute | solution.py:333
  112.2 10.8 %collective-permute-start.15 = (bf16[512,256]{1,0:T(8,128)(2,1)S(1)}, bf16[512,256]{1,0:T(8,128)(2,1)S(1)}, u32[]{:S(2)}, u32[]{:S(2)}) collective-permute-start(bf16[512,256]{1,0:T(8,128)(2,1)S(1)} %add_up.4), channel_id=1, source_target_pairs={{0,8},{8,16},{16,24},{24,32},{32,40},{40,48},{48,56},{56,64},{64,7... | collective-permute-start | bytes 786440 | tf_op jit(solution)/shard_map/ppermute | solution.py:325
  113.8 11.3 %collective-permute-start.17 = (f32[32,256]{1,0:T(8,128)S(1)}, f32[32,256]{1,0:T(8,128)S(1)}, u32[]{:S(2)}, u32[]{:S(2)}) collective-permute-start(f32[32,256]{1,0:T(8,128)S(1)} %add.57.refs_4_.refs_0_), channel_id=1, source_target_pairs={{0,2},{1,3},{2,4},{3,5},{4,6},{5,7},{6,0},{7,1},{8,10},{9,11},{10,... | collective-permute-start | bytes 98312 | tf_op jit(solution)/shard_map/ppermute | solution.py:333
  118.8 6.3 %collective-permute-start.18 = (f32[32,256]{1,0:T(8,128)S(1)}, f32[32,256]{1,0:T(8,128)S(1)}, u32[]{:S(2)}, u32[]{:S(2)}) collective-permute-start(f32[32,256]{1,0:T(8,128)S(1)} %add.57.refs_4_.refs_0_), channel_id=1, source_target_pairs={{0,4},{1,5},{2,6},{3,7},{4,0},{5,1},{6,2},{7,3},{8,12},{9,13},{10,... | collective-permute-start | bytes 98312 | tf_op jit(solution)/shard_map/ppermute | solution.py:333
  118.8 6.4 %collective-permute-start.19 = (f32[32,256]{1,0:T(8,128)S(1)}, f32[32,256]{1,0:T(8,128)S(1)}, u32[]{:S(2)}, u32[]{:S(2)}) collective-permute-start(f32[32,256]{1,0:T(8,128)S(1)} %add.57.refs_4_.refs_0_), channel_id=1, source_target_pairs={{0,6},{1,7},{2,0},{3,1},{4,2},{5,3},{6,4},{7,5},{8,14},{9,15},{10,... | collective-permute-start | bytes 98312 | tf_op jit(solution)/shard_map/ppermute | solution.py:333
  122.4 0.7 copy-start.1
  123.1 1.0 copy-start.2
  124.0 0.9 copy-start.7
  125.2 22.9 %copy-start.13 = (f32[256]{0:T(256)S(1)}, f32[256]{0:T(256)}, u32[]{:S(2)}) copy-start(f32[256]{0:T(256)} %param.10) | copy-start | bytes 3076
  125.2 23.4 %copy-start.11 = (f32[256,256]{1,0:T(8,128)S(1)}, f32[256,256]{1,0:T(8,128)}, u32[]{:S(2)}) copy-start(f32[256,256]{1,0:T(8,128)} %param.9) | copy-start | bytes 786436
  126.4 15.5 %all-to-all-start.1 = ((f16[16,40,256]{2,1,0:T(8,128)(2,1)}), f16[16,40,256]{2,1,0:T(8,128)(2,1)S(1)}, u32[]{:S(2)}, u32[]{:S(2)}) async-start(f16[16,40,256]{2,1,0:T(8,128)(2,1)} %broadcast_in_dim.2), calls=%async_computation.1 | async-start | bytes 655360 | tf_op jit(solution)/shard_map/all_to_all | solution.py:419
  129.9 11.8 %collective-permute-start.16 = (bf16[256,256]{1,0:T(8,128)(2,1)S(1)}, bf16[256,256]{1,0:T(8,128)(2,1)S(1)}, u32[]{:S(2)}, u32[]{:S(2)}) collective-permute-start(bf16[256,256]{1,0:T(8,128)(2,1)S(1)} %get-tuple-element.31.refs_4_), channel_id=1, source_target_pairs={{0,1},{1,0},{2,3},{3,2},{4,5},{5,4},{6,7},{7,6},{8,9},{9,8},{10,11... | collective-permute-start | bytes 393224 | tf_op jit(solution)/shard_map/ppermute | solution.py:329
  141.9 7.6 %collective-permute-start.20 = (f16[16,40,256]{2,1,0:T(8,128)(2,1)S(1)}, f16[16,40,256]{2,1,0:T(8,128)(2,1)S(1)}, u32[]{:S(2)}, u32[]{:S(2)}) collective-permute-start(f16[16,40,256]{2,1,0:T(8,128)(2,1)S(1)} %all-to-all-done.1), channel_id=1, source_target_pairs={{0,8},{8,0},{16,24},{24,16},{32,40},{40,32},{48,56},{56,48},{64,72... | collective-permute-start | bytes 983048 | tf_op jit(solution)/shard_map/ppermute | solution.py:420

commit v8 on v7

--- a/solution.py
+++ b/solution.py
@@ -34,9 +34,9 @@
     return pl.CostEstimate(flops=int(us * 5e8), bytes_accessed=int(us * 3.5e6), transcendentals=0)
 
 
-def params():
+def params(size):
     return pltpu.CompilerParams(
-        dimension_semantics=("arbitrary",), vmem_limit_bytes=48 * MB
+        dimension_semantics=("arbitrary",), vmem_limit_bytes=size * MB
     )
 
 
@@ -46,6 +46,11 @@
 
 PARTS = 4
 PART = ROWS // PARTS
+
+
+def part_specs():
+    spots = (0, 0, 1, 2)
+    return [pl.BlockSpec((PART, D), functools.partial(lambda k, *_: (k, 0), k)) for k in spots]
 
 
 def block_of(parts, b):
@@ -73,7 +78,7 @@
         in_specs=[pl.BlockSpec((1, 1, PAD), lambda g: (g, 0, 0))],
         out_specs=pl.BlockSpec((1, 8, ROWS), lambda g: (g, 0, 0)),
         out_shape=jax.ShapeDtypeStruct((GROUPS, 8, ROWS), f32),
-        compiler_params=params(),
+        compiler_params=params(8),
         cost_estimate=cost(3),
         name="neg_weights",
     )(neg_pad.reshape(GROUPS, 1, PAD))
@@ -81,7 +86,7 @@
 
 def query_kernel(rel_ref, *refs):
     own = refs[:PARTS]
-    idx_ref, mat_ref, _, s_ref, q_ref = refs[PARTS:]
+    idx_ref, mat_ref, s_ref, q_ref = refs[PARTS:]
     column = jnp.broadcast_to(idx_ref[0].astype(f32), (128, PAD)).T
     column = column.astype(jnp.int32).astype(jnp.int16)
     cols = lax.broadcasted_iota(jnp.int32, (PAD, 128), 1).astype(jnp.int16)
@@ -101,17 +106,16 @@
     q_ref[...] = mm(mat_ref[0].astype(bf16).T, rows, NT).astype(bf16)
 
 
-def make_queries(own, src_rows, rel_id, relation, after):
+def make_queries(own, src_rows, rel_id, relation):
     return pl.pallas_call(
         query_kernel,
         grid_spec=pltpu.PrefetchScalarGridSpec(
             num_scalar_prefetch=1,
             grid=(GROUPS,),
             in_specs=[
-                *[pl.BlockSpec((PART, D), lambda j, rel: (0, 0))] * PARTS,
+                *part_specs(),
                 pl.BlockSpec((1, 1, PAD), lambda j, rel: (j, 0, 0)),
                 pl.BlockSpec((1, D, D), lambda j, rel: (rel[j], 0, 0)),
-                pl.BlockSpec(memory_space=pl.ANY),
             ],
             out_specs=[
                 pl.BlockSpec((PAD, D), lambda j, rel: (j, 0)),
@@ -122,10 +126,10 @@
             jax.ShapeDtypeStruct((GROUPS * PAD, D), bf16),
             jax.ShapeDtypeStruct((D, GROUPS * PAD), bf16),
         ],
-        compiler_params=params(),
+        compiler_params=params(20),
         cost_estimate=cost(9),
         name="queries",
-    )(rel_id, *own, src_rows, relation, after)
+    )(rel_id, own[0], *[own[1]] * 3, src_rows, relation)
 
 
 SUB = 32
@@ -133,20 +137,18 @@
 
 def score_kernel(rel_ref, cnt_ref, *refs):
     nxt = refs[:PARTS]
-    q_ref, s_hbm, dst_ref, wt_ref, gq_ref = refs[PARTS : PARTS + 5]
+    q_ref, s_ref, dst_ref, wt_ref, gq_ref = refs[PARTS : PARTS + 5]
     dg = refs[PARTS + 5 : 2 * PARTS + 5]
-    rg_ref, sc, nxt_t_ref, *halves, dacc, wcol, racc, s_ref, s_sem = refs[
+    rg_ref, sc, nxt_t_ref, *halves, dacc, wcol, racc = refs[
         2 * PARTS + 5 :
     ]
     old = halves[0::2], halves[1::2]
-    load_s = pltpu.make_async_copy(s_hbm, s_ref, s_sem)
     g = pl.program_id(0)
     rows = lax.broadcasted_iota(jnp.int32, (SUB, CH), 0)
     rows16 = lax.broadcasted_iota(jnp.int32, (BLK, CH), 0).astype(jnp.int16)
 
     @pl.when(g == 0)
     def _():
-        load_s.start()
         dacc[...] = jnp.zeros_like(dacc)
         racc[...] = jnp.zeros_like(racc)
         for ref in old[1]:
@@ -221,7 +223,6 @@
             part = spread(b, *old[1])
             acc = part if acc is None else acc + part
         finish(acc, old[1][2], 2 * g + 1)
-        load_s.wait()
         for k in range(GROUPS):
             at = slice(k * PAD, (k + 1) * PAD)
             racc[rel_ref[k]] += mm(gq_ref[:, at], s_ref[at, :])
@@ -238,9 +239,9 @@
             num_scalar_prefetch=2,
             grid=(NCH // 2,),
             in_specs=[
-                *[pl.BlockSpec((PART, D), lambda j, rel, cnt: (0, 0))] * PARTS,
+                *part_specs(),
                 pl.BlockSpec((D, 2 * CH), lambda j, rel, cnt: (0, j)),
-                pl.BlockSpec(memory_space=pl.ANY),
+                pl.BlockSpec((GROUPS * PAD, D), lambda j, rel, cnt: (0, 0)),
                 pl.BlockSpec((1, 1, 2 * CH), lambda j, rel, cnt: (j, 0, 0)),
                 pl.BlockSpec((GROUPS, 8, ROWS), lambda j, rel, cnt: (0, 0, 0)),
             ],
@@ -259,8 +260,6 @@
                 pltpu.VMEM((ROWS, D), f32),
                 pltpu.VMEM((ROWS, 8), f32),
                 pltpu.VMEM((kinds, D, D), f32),
-                pltpu.VMEM((GROUPS * PAD, D), bf16),
-                pltpu.SemaphoreType.DMA,
             ],
         ),
         out_shape=[
@@ -268,10 +267,10 @@
             *[jax.ShapeDtypeStruct((PART, D), bf16)] * PARTS,
             jax.ShapeDtypeStruct((kinds, D, D), bf16),
         ],
-        compiler_params=params(),
+        compiler_params=params(34),
         cost_estimate=cost(28),
         name="scores",
-    )(rel_id, counts, *nxt, q, s, dst_rows, weights)
+    )(rel_id, counts, nxt[0], *[nxt[1]] * 3, q, s, dst_rows, weights)
 
 
 def source_kernel(rel_ref, gq_ref, src_ref, mat_ref, *refs):
@@ -309,7 +308,7 @@
             scratch_shapes=[pltpu.VMEM((ROWS, D), f32)],
         ),
         out_shape=[jax.ShapeDtypeStruct((PART, D), bf16)] * PARTS,
-        compiler_params=params(),
+        compiler_params=params(16),
         cost_estimate=cost(8),
         name="source_grads",
     )(rel_id, gq, src_rows, relation)
@@ -430,8 +429,8 @@
     return jnp.pad(index.reshape(GROUPS, SLOTS), ((0, 0), (0, PAD - SLOTS)), constant_values=fill)
 
 
-def source_stage(own, src_pad, rel_id, relation, after):
-    return make_queries(own, src_pad.reshape(GROUPS, 1, PAD), rel_id, relation, after)
+def source_stage(own, src_pad, rel_id, relation):
+    return make_queries(own, src_pad.reshape(GROUPS, 1, PAD), rel_id, relation)
 
 
 def target_stage(nxt, q, s, dst_pad, weights, rel_id, counts, kinds):
@@ -448,9 +447,8 @@
     own, nxt = own.astype(bf16), nxt.astype(bf16)
     src_pad = pad_slots(src_index, -1)
     weights = neg_weights(pad_slots(neg_index, -1))
-    own = [own[k * PART : (k + 1) * PART] for k in range(PARTS)]
-    nxt = [nxt[k * PART : (k + 1) * PART] for k in range(PARTS)]
-    s, q = source_stage(own, src_pad, rel_id, relation, nxt[0])
+    own, nxt = ([rows[:PART], rows[PART:]] for rows in (own, nxt))
+    s, q = source_stage(own, src_pad, rel_id, relation)
     gq, dst_grad, rel_grad = target_stage(
         nxt, q, s, pad_slots(dst_index, -1), weights, rel_id, counts, relation.shape[0]
     )
@@ -466,10 +464,11 @@
     dst_pad = pad_slots(turned(dst_index), -1)
     neg_pad = pad_slots(turned(neg_index), -1)
     other = swap_z(ent_b)
-    own = spread_x(jnp.concatenate([ent_b, other]))
+    pair = jnp.concatenate([ent_b, other])
+    own = [pair, jnp.concatenate(spread_x(pair)[1:])]
     nxt = [shift_dom(block, -1) for block in own]
     weights = neg_weights(neg_pad)
-    s, q = source_stage(own, src_pad, rel_id, relation, nxt[0])
+    s, q = source_stage(own, src_pad, rel_id, relation)
     gq, dst_grad, rel_grad = target_stage(
         nxt, q, s, dst_pad, weights, rel_id, counts, relation.shape[0]
     )

time: 152 us -> 155 us (1.020)
  waiting for transfers between devices: 18.5 us -> 43.9 us
  starting transfers between devices: 66.7 us -> 50.2 us
  local copies, waits for them, and re-layouts: 9.42 us -> 6.48 us
  Pallas kernels: 49.8 us -> 47.6 us
    ppermute x12, waiting for transfers between devices: 5.68 us -> 25.1 us  [shift_x(): return lax.ppermute(block, 'rep', [(i, (i + 2 * by) % 8) for i in range(8)])]
    ppermute x12, starting transfers between devices: 16.7 us -> 8.4 us  [shift_x(): return lax.ppermute(block, 'rep', [(i, (i + 2 * by) % 8) for i in range(8)])]
    ppermute x5 -> x3, starting transfers between devices: 14.8 us -> 6.77 us  [shift_dom(): lax.ppermute(block, 'dom', [(i, (i + by) % size) for i in range(size)])]
    ppermute x3, waiting for transfers between devices: 8.54 us -> 12.9 us  [swap_z(): return lax.ppermute(block, 'rep', [(i, i ^ 1) for i in range(8)])]
    unnamed x29 -> x27, local copies, waits for them, and re-layouts: 7.62 us -> 4.66 us
    ppermute x3, starting transfers between devices: 17.9 us -> 15.5 us  [swap_z(): return lax.ppermute(block, 'rep', [(i, i ^ 1) for i in range(8)])]
    ppermute x1, starting transfers between devices: 6.18 us -> 8.03 us  [operator_update(): other = lax.ppermute(half, 'dom', [(i, i ^ 1) for i in range(32)])]
    all_to_all x1, waiting for transfers between devices: 4.28 us -> 5.88 us  [on_device(): got = lax.all_to_all(rel_grad.reshape(32, -1, D), 'dom', 0, 0)]
  transfers between devices with their start and end apart: 23 -> 21, of which waited for: 5 -> 10; matrix products, arithmetic and copies ran while one was open for 2% -> 2% of each run, Pallas kernels for 13% -> 12%
where the time goes in v8:
time: 155 us
  starting transfers between devices  50.2 us (32%)
  Pallas kernels  47.6 us (31%)
  waiting for transfers between devices  43.9 us (28%)
  local copies, waits for them, and re-layouts  6.48 us (4%)
  other arithmetic  5.18 us (3%)
  between operations  1.56 us (1%)
    pallas_call x1, Pallas kernels, score_side(): pl.pallas_call(score_kernel, grid_spec=pltpu.PrefetchScalarGridSpec(num_s...  28.9 us
    ppermute x12, waiting for transfers between devices, shift_x(): return lax.ppermute(block, 'rep', [(i, (i + 2 * by) % 8) for i in range(8)])  25.1 us
    ppermute x3, starting transfers between devices, swap_z(): return lax.ppermute(block, 'rep', [(i, i ^ 1) for i in range(8)])  15.5 us
    ppermute x3, waiting for transfers between devices, swap_z(): return lax.ppermute(block, 'rep', [(i, i ^ 1) for i in range(8)])  12.9 us
    ppermute x12, starting transfers between devices, shift_x(): return lax.ppermute(block, 'rep', [(i, (i + 2 * by) % 8) for i in range(8)])  8.4 us
    ppermute x1, starting transfers between devices, operator_update(): other = lax.ppermute(half, 'dom', [(i, i ^ 1) for i in range(32)])  8.03 us
    all_to_all x1, starting transfers between devices, on_device(): got = lax.all_to_all(rel_grad.reshape(32, -1, D), 'dom', 0, 0)  8.01 us
    pallas_call x1, Pallas kernels, make_queries(): pl.pallas_call(query_kernel, grid_spec=pltpu.PrefetchScalarGridSpec(num_s...  7.18 us
  transfers between devices with their start and end apart: 21, of which 10 were waited for; matrix products, arithmetic and copies ran while one was open for 2% of the time, Pallas kernels for 12%

profile of v8, /device:TPU:1, one launch (start us, length us, event | category | flops | bytes accessed | tf_op | source)
XLA Modules:
  0.0 155.0 jit_solution(9057411629480852449)
XLA Ops:
  0.6 1.0 convert_element_type.15
  1.6 7.8 %collective-permute-start = (bf16[256,256]{1,0:T(8,128)(2,1)S(1)}, bf16[256,256]{1,0:T(8,128)(2,1)S(1)}, u32[]{:S(2)}, u32[]{:S(2)}) collective-permute-start(bf16[256,256]{1,0:T(8,128)(2,1)S(1)} %convert_element_type.15), channel_id=1, source_target_pairs={{0,1},{1,0},{2,3},{3,2},{4,5},{5,4},{6,7},{7,6},{8,9},{9,8},{10,11... | collective-permute-start | bytes 393224 | tf_op jit(solution)/shard_map/ppermute | solution.py:328
  9.4 2.7 %collective-permute-done = bf16[256,256]{1,0:T(8,128)(2,1)S(1)} collective-permute-done((bf16[256,256]{1,0:T(8,128)(2,1)S(1)}, bf16[256,256]{1,0:T(8,128)(2,1)S(1)}, u32[]{:S(2)}, u32[]{:S(2)}) %collective-permute-start) | collective-permute-done | bytes 131104 | tf_op jit(solution)/shard_map/ppermute | solution.py:328
  12.1 3.1 %collective-permute-start.2 = (bf16[512,256]{1,0:T(8,128)(2,1)S(1)}, bf16[512,256]{1,0:T(8,128)(2,1)S(1)}, u32[]{:S(2)}, u32[]{:S(2)}) collective-permute-start(bf16[512,256]{1,0:T(8,128)(2,1)S(1)} %pad_maximum_fusion.refs_0_), channel_id=1, source_target_pairs={{0,6},{1,7},{2,0},{3,1},{4,2},{5,3},{6,4},{7,5},{8,14},{9,15},{10,... | collective-permute-start | bytes 786440 | tf_op jit(solution)/shard_map/ppermute | solution.py:332
  15.2 0.5 collective-permute-start.3
  15.8 0.6 collective-permute-start.4
  16.4 0.8 fusion.1
  17.2 3.6 %collective-permute-done.2 = bf16[512,256]{1,0:T(8,128)(2,1)S(1)} collective-permute-done((bf16[512,256]{1,0:T(8,128)(2,1)S(1)}, bf16[512,256]{1,0:T(8,128)(2,1)S(1)}, u32[]{:S(2)}, u32[]{:S(2)}) %collective-permute-start.2) | collective-permute-done | bytes 262176 | tf_op jit(solution)/shard_map/ppermute | solution.py:332
  20.8 2.2 %collective-permute-done.3 = bf16[512,256]{1,0:T(8,128)(2,1)S(1)} collective-permute-done((bf16[512,256]{1,0:T(8,128)(2,1)S(1)}, bf16[512,256]{1,0:T(8,128)(2,1)S(1)}, u32[]{:S(2)}, u32[]{:S(2)}) %collective-permute-start.3) | collective-permute-done | bytes 262176 | tf_op jit(solution)/shard_map/ppermute | solution.py:332
  23.0 7.6 %collective-permute-done.4 = bf16[512,256]{1,0:T(8,128)(2,1)S(1)} collective-permute-done((bf16[512,256]{1,0:T(8,128)(2,1)S(1)}, bf16[512,256]{1,0:T(8,128)(2,1)S(1)}, u32[]{:S(2)}, u32[]{:S(2)}) %collective-permute-start.4) | collective-permute-done | bytes 262176 | tf_op jit(solution)/shard_map/ppermute | solution.py:332
  30.6 0.6 collective-permute-start.5
  32.0 3.2 %neg_weights.1.refs_7_ = f32[4,8,2048]{2,1,0:T(8,128)S(1)} custom-call(s32[4,1,1024]{2,1,0:T(1,128)S(1)} %reshape.47.neg_ref), custom_call_target="tpu_custom_call" | custom-call | flops 1500000000 | bytes 10500000 | tf_op jit(solution)/shard_map/neg_weights/pallas_call | solution.py:75
  35.2 5.2 %collective-permute-start.1 = (bf16[512,256]{1,0:T(8,128)(2,1)S(1)}, bf16[512,256]{1,0:T(8,128)(2,1)S(1)}, u32[]{:S(2)}, u32[]{:S(2)}) collective-permute-start(bf16[512,256]{1,0:T(8,128)(2,1)S(1)} %pad_maximum_fusion.refs_0_), channel_id=1, source_target_pairs={{0,248},{8,0},{16,8},{24,16},{32,24},{40,32},{48,40},{56,48},{64,5... | collective-permute-start | bytes 786440 | tf_op jit(solution)/shard_map/ppermute | solution.py:324
  40.4 7.2 %queries.1 = (bf16[4096,256]{1,0:T(8,128)(2,1)S(1)}, bf16[256,4096]{1,0:T(8,128)(2,1)S(1)}) custom-call(s32[4]{0:T(128)S(1)} %copy-done.1, bf16[512,256]{1,0:T(8,128)(2,1)S(1)} %pad_maximum_fusion.refs_0_, bf16[1536,256]{1,0:T(8,128)(2,1)S(1)} %constant_dynamic-update-slice_fusion.refs_1_.refs_2_.refs_3_, ...), custom_call_target="tpu_custom_call" | custom-call | flops 4499999744 | bytes 31500000 | tf_op jit(solution)/shard_map/queries/pallas_call | solution.py:110
  47.6 28.9 %scores.1 = (bf16[256,4096]{1,0:T(8,128)(2,1)S(1)}, bf16[512,256]{1,0:T(8,128)(2,1)S(1)}, bf16[512,256]{1,0:T(8,128)(2,1)S(1)}, bf16[512,256]{1,0:T(8,128)(2,1)S...) custom-call(s32[4]{0:T(128)S(1)} %copy-done.1, s32[1]{0:T(128)S(6)} %copy.20.cnt_ref, ...), custom_call_target="tpu_custom_call" | custom-call | flops 14000000000 | bytes 98000000 | tf_op jit(solution)/shard_map/scores/pallas_call | solution.py:236
  76.5 0.7 copy-done.2
  77.2 1.3 copy-done.6
  78.6 8.0 %all-to-all-start = ((bf16[32,32,256]{2,1,0:T(8,128)(2,1)}), bf16[32,32,256]{2,1,0:T(8,128)(2,1)S(1)}, u32[]{:S(2)}, u32[]{:S(2)}) async-start(bf16[32,32,256]{2,1,0:T(8,128)(2,1)} %bitcast), calls=%async_computation | async-start | bytes 1048576 | tf_op jit(solution)/shard_map/all_to_all | solution.py:476
  86.6 0.6 collective-permute-start.10
  87.2 1.5 collective-permute-start.9
  88.6 1.6 %copy-done.7 = bf16[256,4096]{1,0:T(8,128)(2,1)S(1)} copy-done((bf16[256,4096]{1,0:T(8,128)(2,1)S(1)}, bf16[256,4096]{1,0:T(8,128)(2,1)}, u32[]{:S(2)}) %copy-start.7) | copy-done | bytes 2097176
  90.2 6.9 %source_grads.1 = (bf16[512,256]{1,0:T(8,128)(2,1)S(1)}, bf16[512,256]{1,0:T(8,128)(2,1)S(1)}, bf16[512,256]{1,0:T(8,128)(2,1)S(1)}, bf16[512,256]{1,0:T(8,128)(2,1)S(1)}) custom-call(s32[4]{0:T(128)S(1)} %copy-done.1, bf16[256,4096]{1,0:T(8,128)(2,1)S(1)} %copy-done.7, s32[4,1,1024]{2,1,0:T(1,128)S(1)} %reshape.44.refs_4_.src_ref, f32[4,256,256]{2,1,0:T(8,128)S(1)} %copy-done), custom_call_target="tpu_custom_call" | custom-call | flops 4000000000 | bytes 28000000 | tf_op jit(solution)/shard_map/source_grads/pallas_call | solution.py:297
  97.1 5.9 %all-to-all-done.refs_0_ = bf16[32,32,256]{2,1,0:T(8,128)(2,1)S(1)} async-done(((bf16[32,32,256]{2,1,0:T(8,128)(2,1)}), bf16[32,32,256]{2,1,0:T(8,128)(2,1)S(1)}, u32[]{:S(2)}, u32[]{:S(2)}) %all-to-all-start) | async-done | bytes 524320 | tf_op jit(solution)/shard_map/all_to_all | solution.py:476
  103.1 6.2 %collective-permute-start.12 = (f32[32,256]{1,0:T(8,128)S(1)}, f32[32,256]{1,0:T(8,128)S(1)}, u32[]{:S(2)}, u32[]{:S(2)}) collective-permute-start(f32[32,256]{1,0:T(8,128)S(1)} %add_up.3), channel_id=1, source_target_pairs={{0,1},{1,0},{2,3},{3,2},{4,5},{5,4},{6,7},{7,6},{8,9},{9,8},{10,11... | collective-permute-start | bytes 98312 | tf_op jit(solution)/shard_map/ppermute | solution.py:328
  109.3 1.7 %collective-permute-done.12 = f32[32,256]{1,0:T(8,128)S(1)} collective-permute-done((f32[32,256]{1,0:T(8,128)S(1)}, f32[32,256]{1,0:T(8,128)S(1)}, u32[]{:S(2)}, u32[]{:S(2)}) %collective-permute-start.12) | collective-permute-done | bytes 32800 | tf_op jit(solution)/shard_map/ppermute | solution.py:328
  111.0 0.5 collective-permute-start.7
  111.5 0.5 collective-permute-start.8
  112.1 1.2 add_up.4
  113.3 1.0 collective-permute-start.13
  114.4 1.1 collective-permute-start.15
  115.4 8.6 %collective-permute-done.6.refs_1_ = bf16[512,256]{1,0:T(8,128)(2,1)S(1)} collective-permute-done((bf16[512,256]{1,0:T(8,128)(2,1)S(1)}, bf16[512,256]{1,0:T(8,128)(2,1)S(1)}, u32[]{:S(2)}, u32[]{:S(2)}) %collective-permute-start.6) | collective-permute-done | bytes 262176 | tf_op jit(solution)/shard_map/ppermute | solution.py:332
  124.1 0.3 collective-permute-done.8.refs_3_
  124.4 0.9 copy-done.5
  125.3 0.2 split_sum.1
  125.5 2.8 %collective-permute-done.16.refs_2_ = f32[32,256]{1,0:T(8,128)S(1)} collective-permute-done((f32[32,256]{1,0:T(8,128)S(1)}, f32[32,256]{1,0:T(8,128)S(1)}, u32[]{:S(2)}, u32[]{:S(2)}) %collective-permute-start.16) | collective-permute-done | bytes 32800 | tf_op jit(solution)/shard_map/ppermute | solution.py:332
  128.7 0.8 broadcast_in_dim.2
  129.5 3.5 %all-to-all-start.1 = ((f16[16,40,256]{2,1,0:T(8,128)(2,1)}), f16[16,40,256]{2,1,0:T(8,128)(2,1)S(1)}, u32[]{:S(2)}, u32[]{:S(2)}) async-start(f16[16,40,256]{2,1,0:T(8,128)(2,1)} %broadcast_in_dim.2), calls=%async_computation.1 | async-start | bytes 655360 | tf_op jit(solution)/shard_map/all_to_all | solution.py:418
  133.0 1.4 collective-permute-start.14
  134.5 8.5 %collective-permute-done.14 = bf16[256,256]{1,0:T(8,128)(2,1)S(1)} collective-permute-done((bf16[256,256]{1,0:T(8,128)(2,1)S(1)}, bf16[256,256]{1,0:T(8,128)(2,1)S(1)}, u32[]{:S(2)}, u32[]{:S(2)}) %collective-permute-start.14) | collective-permute-done | bytes 131104 | tf_op jit(solution)/shard_map/ppermute | solution.py:328
  143.0 0.1 multiply_reduce_fusion
  143.1 8.0 %collective-permute-start.18 = (f16[16,40,256]{2,1,0:T(8,128)(2,1)S(1)}, f16[16,40,256]{2,1,0:T(8,128)(2,1)S(1)}, u32[]{:S(2)}, u32[]{:S(2)}) collective-permute-start(f16[16,40,256]{2,1,0:T(8,128)(2,1)S(1)} %all-to-all-done.1), channel_id=1, source_target_pairs={{0,8},{8,0},{16,24},{24,16},{32,40},{40,32},{48,56},{56,48},{64,72... | collective-permute-start | bytes 983048 | tf_op jit(solution)/shard_map/ppermute | solution.py:419
  151.2 0.6 fusion.22
  151.7 0.8 divide_subtract_fusion
  152.6 0.2 select_bitcast_fusion.1
  152.8 0.2 copy.16
  153.0 0.1 slice_multiply_fusion
  153.2 1.1 bitcast_subtract_fusion
  154.3 0.7 mul.55
  (61 shorter events, 1.0 us)
Async XLA Ops:
  0.6 30.6 %copy-start.9 = (s32[4,1000]{1,0:T(4,128)S(1)}, s32[4,1000]{1,0:T(4,128)}, u32[]{:S(2)}) copy-start(s32[4,1000]{1,0:T(4,128)} %param.15) | copy-start | bytes 48004
  1.6 10.5 %collective-permute-start = (bf16[256,256]{1,0:T(8,128)(2,1)S(1)}, bf16[256,256]{1,0:T(8,128)(2,1)S(1)}, u32[]{:S(2)}, u32[]{:S(2)}) collective-permute-start(bf16[256,256]{1,0:T(8,128)(2,1)S(1)} %convert_element_type.15), channel_id=1, source_target_pairs={{0,1},{1,0},{2,3},{3,2},{4,5},{5,4},{6,7},{7,6},{8,9},{9,8},{10,11... | collective-permute-start | bytes 393224 | tf_op jit(solution)/shard_map/ppermute | solution.py:328
  12.1 8.7 %collective-permute-start.2 = (bf16[512,256]{1,0:T(8,128)(2,1)S(1)}, bf16[512,256]{1,0:T(8,128)(2,1)S(1)}, u32[]{:S(2)}, u32[]{:S(2)}) collective-permute-start(bf16[512,256]{1,0:T(8,128)(2,1)S(1)} %pad_maximum_fusion.refs_0_), channel_id=1, source_target_pairs={{0,6},{1,7},{2,0},{3,1},{4,2},{5,3},{6,4},{7,5},{8,14},{9,15},{10,... | collective-permute-start | bytes 786440 | tf_op jit(solution)/shard_map/ppermute | solution.py:332
  15.2 7.8 %collective-permute-start.3 = (bf16[512,256]{1,0:T(8,128)(2,1)S(1)}, bf16[512,256]{1,0:T(8,128)(2,1)S(1)}, u32[]{:S(2)}, u32[]{:S(2)}) collective-permute-start(bf16[512,256]{1,0:T(8,128)(2,1)S(1)} %pad_maximum_fusion.refs_0_), channel_id=1, source_target_pairs={{0,4},{1,5},{2,6},{3,7},{4,0},{5,1},{6,2},{7,3},{8,12},{9,13},{10,... | collective-permute-start | bytes 786440 | tf_op jit(solution)/shard_map/ppermute | solution.py:332
  15.8 14.8 %collective-permute-start.4 = (bf16[512,256]{1,0:T(8,128)(2,1)S(1)}, bf16[512,256]{1,0:T(8,128)(2,1)S(1)}, u32[]{:S(2)}, u32[]{:S(2)}) collective-permute-start(bf16[512,256]{1,0:T(8,128)(2,1)S(1)} %pad_maximum_fusion.refs_0_), channel_id=1, source_target_pairs={{0,2},{1,3},{2,4},{3,5},{4,6},{5,7},{6,0},{7,1},{8,10},{9,11},{10,... | collective-permute-start | bytes 786440 | tf_op jit(solution)/shard_map/ppermute | solution.py:332
  30.6 17.0 %collective-permute-start.5 = (bf16[1536,256]{1,0:T(8,128)(2,1)S(1)}, bf16[1536,256]{1,0:T(8,128)(2,1)S(1)}, u32[]{:S(2)}, u32[]{:S(2)}) collective-permute-start(bf16[1536,256]{1,0:T(8,128)(2,1)S(1)} %constant_dynamic-update-slice_fusion.refs_1_.refs_2_.refs_3_), channel_id=1, source_target_pairs={{0,248},{8,0},{16,8},{24,16},{32,24},{40,32},{48,40},{56,48},{64,5... | collective-permute-start | bytes 2359304 | tf_op jit(solution)/shard_map/ppermute | solution.py:324
  32.0 8.4 %copy-start = (f32[4,256,256]{2,1,0:T(8,128)S(1)}, f32[4,256,256]{2,1,0:T(8,128)}, u32[]{:S(2)}) copy-start(f32[4,256,256]{2,1,0:T(8,128)} %mat_ref.1) | copy-start | bytes 3145732
  32.0 8.4 %copy-start.1 = (s32[4]{0:T(128)S(1)}, s32[4]{0:T(128)}, u32[]{:S(2)}) copy-start(s32[4]{0:T(128)} %rel_ref.5) | copy-start | bytes 52
  35.2 12.4 %collective-permute-start.1 = (bf16[512,256]{1,0:T(8,128)(2,1)S(1)}, bf16[512,256]{1,0:T(8,128)(2,1)S(1)}, u32[]{:S(2)}, u32[]{:S(2)}) collective-permute-start(bf16[512,256]{1,0:T(8,128)(2,1)S(1)} %pad_maximum_fusion.refs_0_), channel_id=1, source_target_pairs={{0,248},{8,0},{16,8},{24,16},{32,24},{40,32},{48,40},{56,48},{64,5... | collective-permute-start | bytes 786440 | tf_op jit(solution)/shard_map/ppermute | solution.py:324
  76.5 0.7 copy-start.2
  77.2 1.3 copy-start.6
  78.6 24.4 %all-to-all-start = ((bf16[32,32,256]{2,1,0:T(8,128)(2,1)}), bf16[32,32,256]{2,1,0:T(8,128)(2,1)S(1)}, u32[]{:S(2)}, u32[]{:S(2)}) async-start(bf16[32,32,256]{2,1,0:T(8,128)(2,1)} %bitcast), calls=%async_computation | async-start | bytes 1048576 | tf_op jit(solution)/shard_map/all_to_all | solution.py:476
  86.6 25.0 %collective-permute-start.10 = (bf16[512,256]{1,0:T(8,128)(2,1)S(1)}, bf16[512,256]{1,0:T(8,128)(2,1)}, u32[]{:S(2)}, u32[]{:S(2)}) collective-permute-start(bf16[512,256]{1,0:T(8,128)(2,1)S(1)} %get-tuple-element.27), channel_id=1, source_target_pairs={{0,4},{1,5},{2,6},{3,7},{4,0},{5,1},{6,2},{7,3},{8,12},{9,13},{10,... | collective-permute-start | bytes 786440 | tf_op jit(solution)/shard_map/ppermute | solution.py:332
  87.2 24.9 %collective-permute-start.11 = (bf16[512,256]{1,0:T(8,128)(2,1)}, bf16[512,256]{1,0:T(8,128)(2,1)}, u32[]{:S(2)}, u32[]{:S(2)}) collective-permute-start(bf16[512,256]{1,0:T(8,128)(2,1)} %get-tuple-element.28), channel_id=1, source_target_pairs={{0,6},{1,7},{2,0},{3,1},{4,2},{5,3},{6,4},{7,5},{8,14},{9,15},{10,... | collective-permute-start | bytes 786440 | tf_op jit(solution)/shard_map/ppermute | solution.py:332
  87.2 24.9 %collective-permute-start.9 = (bf16[512,256]{1,0:T(8,128)(2,1)S(1)}, bf16[512,256]{1,0:T(8,128)(2,1)}, u32[]{:S(2)}, u32[]{:S(2)}) collective-permute-start(bf16[512,256]{1,0:T(8,128)(2,1)S(1)} %get-tuple-element.26), channel_id=1, source_target_pairs={{0,2},{1,3},{2,4},{3,5},{4,6},{5,7},{6,0},{7,1},{8,10},{9,11},{10,... | collective-permute-start | bytes 786440 | tf_op jit(solution)/shard_map/ppermute | solution.py:332
  88.6 1.6 %copy-start.7 = (bf16[256,4096]{1,0:T(8,128)(2,1)S(1)}, bf16[256,4096]{1,0:T(8,128)(2,1)}, u32[]{:S(2)}) copy-start(bf16[256,4096]{1,0:T(8,128)(2,1)} %copy-done.6) | copy-start | bytes 6291460
  97.1 12.2 %copy-start.4 = (bf16[512,256]{1,0:T(8,128)(2,1)}, bf16[512,256]{1,0:T(8,128)(2,1)S(1)}, u32[]{:S(2)}) copy-start(bf16[512,256]{1,0:T(8,128)(2,1)S(1)} %get-tuple-element.21.refs_1_.refs_0_) | copy-start | bytes 786436
  103.0 9.1 %copy-start.3 = (bf16[512,256]{1,0:T(8,128)(2,1)S(1)}, bf16[512,256]{1,0:T(8,128)(2,1)}, u32[]{:S(2)}) copy-start(bf16[512,256]{1,0:T(8,128)(2,1)} %copy-done.2) | copy-start | bytes 786436
  103.1 11.3 %copy-start.10 = (f32[4,256]{1,0:T(4,128)S(1)}, f32[4,256]{1,0:T(4,128)}, u32[]{:S(2)}) copy-start(f32[4,256]{1,0:T(4,128)} %param.12) | copy-start | bytes 12292
  103.1 7.9 %collective-permute-start.12 = (f32[32,256]{1,0:T(8,128)S(1)}, f32[32,256]{1,0:T(8,128)S(1)}, u32[]{:S(2)}, u32[]{:S(2)}) collective-permute-start(f32[32,256]{1,0:T(8,128)S(1)} %add_up.3), channel_id=1, source_target_pairs={{0,1},{1,0},{2,3},{3,2},{4,5},{5,4},{6,7},{7,6},{8,9},{9,8},{10,11... | collective-permute-start | bytes 98312 | tf_op jit(solution)/shard_map/ppermute | solution.py:328
  109.3 14.8 %collective-permute-start.6 = (bf16[512,256]{1,0:T(8,128)(2,1)S(1)}, bf16[512,256]{1,0:T(8,128)(2,1)S(1)}, u32[]{:S(2)}, u32[]{:S(2)}) collective-permute-start(bf16[512,256]{1,0:T(8,128)(2,1)S(1)} %get-tuple-element.22), channel_id=1, source_target_pairs={{0,2},{1,3},{2,4},{3,5},{4,6},{5,7},{6,0},{7,1},{8,10},{9,11},{10,... | collective-permute-start | bytes 786440 | tf_op jit(solution)/shard_map/ppermute | solution.py:332
  111.0 13.1 %collective-permute-start.7 = (bf16[512,256]{1,0:T(8,128)(2,1)S(1)}, bf16[512,256]{1,0:T(8,128)(2,1)S(1)}, u32[]{:S(2)}, u32[]{:S(2)}) collective-permute-start(bf16[512,256]{1,0:T(8,128)(2,1)S(1)} %get-tuple-element.23), channel_id=1, source_target_pairs={{0,4},{1,5},{2,6},{3,7},{4,0},{5,1},{6,2},{7,3},{8,12},{9,13},{10,... | collective-permute-start | bytes 786440 | tf_op jit(solution)/shard_map/ppermute | solution.py:332
  111.5 12.8 %collective-permute-start.8 = (bf16[512,256]{1,0:T(8,128)(2,1)S(1)}, bf16[512,256]{1,0:T(8,128)(2,1)S(1)}, u32[]{:S(2)}, u32[]{:S(2)}) collective-permute-start(bf16[512,256]{1,0:T(8,128)(2,1)S(1)} %get-tuple-element.24), channel_id=1, source_target_pairs={{0,6},{1,7},{2,0},{3,1},{4,2},{5,3},{6,4},{7,5},{8,14},{9,15},{10,... | collective-permute-start | bytes 786440 | tf_op jit(solution)/shard_map/ppermute | solution.py:332
  113.3 11.1 %collective-permute-start.13 = (bf16[512,256]{1,0:T(8,128)(2,1)S(1)}, bf16[512,256]{1,0:T(8,128)(2,1)S(1)}, u32[]{:S(2)}, u32[]{:S(2)}) collective-permute-start(bf16[512,256]{1,0:T(8,128)(2,1)S(1)} %add_up.4), channel_id=1, source_target_pairs={{0,8},{8,16},{16,24},{24,32},{32,40},{40,48},{48,56},{56,64},{64,7... | collective-permute-start | bytes 786440 | tf_op jit(solution)/shard_map/ppermute | solution.py:324
  114.4 11.1 %collective-permute-start.15 = (f32[32,256]{1,0:T(8,128)S(1)}, f32[32,256]{1,0:T(8,128)S(1)}, u32[]{:S(2)}, u32[]{:S(2)}) collective-permute-start(f32[32,256]{1,0:T(8,128)S(1)} %add.57.refs_4_.refs_0_), channel_id=1, source_target_pairs={{0,2},{1,3},{2,4},{3,5},{4,6},{5,7},{6,0},{7,1},{8,10},{9,11},{10,... | collective-permute-start | bytes 98312 | tf_op jit(solution)/shard_map/ppermute | solution.py:332
  124.1 4.3 %collective-permute-start.16 = (f32[32,256]{1,0:T(8,128)S(1)}, f32[32,256]{1,0:T(8,128)S(1)}, u32[]{:S(2)}, u32[]{:S(2)}) collective-permute-start(f32[32,256]{1,0:T(8,128)S(1)} %add.57.refs_4_.refs_0_), channel_id=1, source_target_pairs={{0,4},{1,5},{2,6},{3,7},{4,0},{5,1},{6,2},{7,3},{8,12},{9,13},{10,... | collective-permute-start | bytes 98312 | tf_op jit(solution)/shard_map/ppermute | solution.py:332
  124.1 4.3 %collective-permute-start.17 = (f32[32,256]{1,0:T(8,128)S(1)}, f32[32,256]{1,0:T(8,128)S(1)}, u32[]{:S(2)}, u32[]{:S(2)}) collective-permute-start(f32[32,256]{1,0:T(8,128)S(1)} %add.57.refs_4_.refs_0_), channel_id=1, source_target_pairs={{0,6},{1,7},{2,0},{3,1},{4,2},{5,3},{6,4},{7,5},{8,14},{9,15},{10,... | collective-permute-start | bytes 98312 | tf_op jit(solution)/shard_map/ppermute | solution.py:332
  124.4 1.0 copy-start.5
  128.3 22.8 %copy-start.11 = (f32[256]{0:T(256)S(1)}, f32[256]{0:T(256)}, u32[]{:S(2)}) copy-start(f32[256]{0:T(256)} %param.10) | copy-start | bytes 3076
  128.3 23.4 %copy-start.8 = (f32[256,256]{1,0:T(8,128)S(1)}, f32[256,256]{1,0:T(8,128)}, u32[]{:S(2)}) copy-start(f32[256,256]{1,0:T(8,128)} %param.9) | copy-start | bytes 786436
  129.5 13.7 %all-to-all-start.1 = ((f16[16,40,256]{2,1,0:T(8,128)(2,1)}), f16[16,40,256]{2,1,0:T(8,128)(2,1)S(1)}, u32[]{:S(2)}, u32[]{:S(2)}) async-start(f16[16,40,256]{2,1,0:T(8,128)(2,1)} %broadcast_in_dim.2), calls=%async_computation.1 | async-start | bytes 655360 | tf_op jit(solution)/shard_map/all_to_all | solution.py:418
  133.0 10.0 %collective-permute-start.14 = (bf16[256,256]{1,0:T(8,128)(2,1)S(1)}, bf16[256,256]{1,0:T(8,128)(2,1)S(1)}, u32[]{:S(2)}, u32[]{:S(2)}) collective-permute-start(bf16[256,256]{1,0:T(8,128)(2,1)S(1)} %get-tuple-element.31.refs_4_), channel_id=1, source_target_pairs={{0,1},{1,0},{2,3},{3,2},{4,5},{5,4},{6,7},{7,6},{8,9},{9,8},{10,11... | collective-permute-start | bytes 393224 | tf_op jit(solution)/shard_map/ppermute | solution.py:328
  143.1 9.4 %collective-permute-start.18 = (f16[16,40,256]{2,1,0:T(8,128)(2,1)S(1)}, f16[16,40,256]{2,1,0:T(8,128)(2,1)S(1)}, u32[]{:S(2)}, u32[]{:S(2)}) collective-permute-start(f16[16,40,256]{2,1,0:T(8,128)(2,1)S(1)} %all-to-all-done.1), channel_id=1, source_target_pairs={{0,8},{8,0},{16,24},{24,16},{32,40},{40,32},{48,56},{56,48},{64,72... | collective-permute-start | bytes 983048 | tf_op jit(solution)/shard_map/ppermute | solution.py:419

commit v9 on v8

--- a/solution.py
+++ b/solution.py
@@ -49,8 +49,7 @@
 
 
 def part_specs():
-    spots = (0, 0, 1, 2)
-    return [pl.BlockSpec((PART, D), functools.partial(lambda k, *_: (k, 0), k)) for k in spots]
+    return [pl.BlockSpec((PART, D), lambda *_: (0, 0))] * PARTS
 
 
 def block_of(parts, b):
@@ -129,7 +128,7 @@
         compiler_params=params(20),
         cost_estimate=cost(9),
         name="queries",
-    )(rel_id, own[0], *[own[1]] * 3, src_rows, relation)
+    )(rel_id, *own, src_rows, relation)
 
 
 SUB = 32
@@ -270,7 +269,7 @@
         compiler_params=params(34),
         cost_estimate=cost(28),
         name="scores",
-    )(rel_id, counts, nxt[0], *[nxt[1]] * 3, q, s, dst_rows, weights)
+    )(rel_id, counts, *nxt, q, s, dst_rows, weights)
 
 
 def source_kernel(rel_ref, gq_ref, src_ref, mat_ref, *refs):
@@ -375,27 +374,45 @@
     )(*blocks, after)
 
 
-def split_sum(blocks):
+def split_sum(blocks, after):
     half = blocks[0].shape[0] // 2
     whole = pl.BlockSpec(memory_space=pltpu.VMEM)
 
     def kernel(*refs):
         for out, at in ((refs[-2], slice(0, half)), (refs[-1], slice(half, 2 * half))):
             total = None
-            for ref in refs[:-2]:
+            for ref in refs[: len(blocks)]:
                 part = ref[at, :].astype(f32)
                 total = part if total is None else total + part
             out[...] = total.astype(out.dtype)
 
     return pl.pallas_call(
         kernel,
-        in_specs=[whole] * len(blocks),
+        in_specs=[whole] * len(blocks) + [pl.BlockSpec(memory_space=pl.ANY)],
         out_specs=[whole] * 2,
         out_shape=[jax.ShapeDtypeStruct((half, D), f32), jax.ShapeDtypeStruct((half, D), bf16)],
         compiler_params=pltpu.CompilerParams(vmem_limit_bytes=16 * MB),
         cost_estimate=cost(1),
         name="split_sum",
-    )(*blocks)
+    )(*blocks, after)
+
+
+def relay(blocks, after):
+    whole = pl.BlockSpec(memory_space=pltpu.VMEM)
+
+    def kernel(*refs):
+        for i in range(len(blocks)):
+            refs[len(blocks) + 1 + i][...] = refs[i][...]
+
+    return pl.pallas_call(
+        kernel,
+        in_specs=[whole] * len(blocks) + [pl.BlockSpec(memory_space=pl.ANY)],
+        out_specs=[whole] * len(blocks),
+        out_shape=[jax.ShapeDtypeStruct(block.shape, block.dtype) for block in blocks],
+        compiler_params=pltpu.CompilerParams(vmem_limit_bytes=16 * MB),
+        cost_estimate=cost(1),
+        name="relay",
+    )(*blocks, after)
 
 
 def turned(index):
@@ -403,7 +420,7 @@
     return ((index - PART * (rep // 2)) % ROWS) ^ (256 * (rep % 2))
 
 
-def operator_update(total, relation, accum):
+def operator_step(total, accum):
     rows, width = total.shape
     mine = lax.dynamic_slice(accum.reshape(-1), (lax.axis_index("dom") * rows,), (rows,))
     fresh = mine + jnp.mean(total * total, -1)
@@ -413,8 +430,12 @@
     high = lax.reduce_precision(part, 5, 10)
     code = jnp.pad(jnp.stack([power, high, part - high]), ((0, 5), (0, width - rows)))
     send = jnp.concatenate([step, code]).astype(jnp.float16)
+    return jnp.broadcast_to(send, (16,) + send.shape)
+
+
+def operator_update(shares, relation, accum):
+    rows, width = shares.shape[1] - 8, shares.shape[2]
     cores = [[2 * i + c for i in range(16)] for c in range(2)]
-    shares = jnp.broadcast_to(send, (16,) + send.shape)
     half = lax.all_to_all(shares, "dom", 0, 0, axis_index_groups=cores)
     other = lax.ppermute(half, "dom", [(i, i ^ 1) for i in range(32)])
     second = lax.axis_index("dom") % 2 == 1
@@ -447,7 +468,7 @@
     own, nxt = own.astype(bf16), nxt.astype(bf16)
     src_pad = pad_slots(src_index, -1)
     weights = neg_weights(pad_slots(neg_index, -1))
-    own, nxt = ([rows[:PART], rows[PART:]] for rows in (own, nxt))
+    own, nxt = (jnp.split(rows, PARTS) for rows in (own, nxt))
     s, q = source_stage(own, src_pad, rel_id, relation)
     gq, dst_grad, rel_grad = target_stage(
         nxt, q, s, pad_slots(dst_index, -1), weights, rel_id, counts, relation.shape[0]
@@ -464,8 +485,7 @@
     dst_pad = pad_slots(turned(dst_index), -1)
     neg_pad = pad_slots(turned(neg_index), -1)
     other = swap_z(ent_b)
-    pair = jnp.concatenate([ent_b, other])
-    own = [pair, jnp.concatenate(spread_x(pair)[1:])]
+    own = spread_x(jnp.concatenate([ent_b, other]))
     nxt = [shift_dom(block, -1) for block in own]
     weights = neg_weights(neg_pad)
     s, q = source_stage(own, src_pad, rel_id, relation)
@@ -475,14 +495,15 @@
     dst_blocks = send_x(dst_grad)
     got = lax.all_to_all(rel_grad.reshape(32, -1, D), "dom", 0, 0)
     src_grad = back_stage(gq, src_pad, rel_id, relation)
-    src_blocks = send_x(src_grad)
     mine = add_up([got], src_grad[0], f32)
-    zsum = mine + swap_z(mine)
-    dst_sum = add_up(dst_blocks, zsum, bf16)
+    dst_sum = add_up(dst_blocks, mine, bf16)
+    xsum = add_up([mine] + [shift_x(mine, k) for k in (1, 2, 3)], dst_sum, f32)
+    zsum = xsum + swap_z(xsum)
+    src_blocks = send_x([src_grad[0]] + list(relay(src_grad[1:], xsum)))
     moved = shift_dom(dst_sum, 1)
-    keep, give = split_sum(src_blocks + [moved])
-    rel_total = add_up([zsum] + [shift_x(zsum, k) for k in (1, 2, 3)], give, f32)
-    relation_new, relation_accum_new = operator_update(rel_total, relation, relation_accum)
+    shares = operator_step(zsum, relation_accum)
+    relation_new, relation_accum_new = operator_update(shares, relation, relation_accum)
+    keep, give = split_sum(src_blocks + [moved], zsum)
     grads = keep + swap_z(give).astype(f32)
     entity_new, entity_accum_new = rowwise(entity, entity_accum, grads)
     return (entity_new, entity_accum_new, relation_new, relation_accum_new)

time: 155 us -> 153 us (0.987)
  waiting for transfers between devices: 43.9 us -> 30.8 us
  starting transfers between devices: 50.2 us -> 59.7 us
    ppermute x12, waiting for transfers between devices: 25.1 us -> 16.8 us  [shift_x(): return lax.ppermute(block, 'rep', [(i, (i + 2 * by) % 8) for i in range(8)])]
    ppermute x12, starting transfers between devices: 8.4 us -> 15.2 us  [shift_x(): return lax.ppermute(block, 'rep', [(i, (i + 2 * by) % 8) for i in range(8)])]
    ppermute x3 -> x5, starting transfers between devices: 6.77 us -> 12.2 us  [shift_dom(): lax.ppermute(block, 'dom', [(i, (i + by) % size) for i in range(size)])]
    ppermute x1, starting transfers between devices: 8.03 us -> 2.88 us  [operator_update(): other = lax.ppermute(half, 'dom', [(i, i ^ 1) for i in range(32)])]
    all_to_all x1, waiting for transfers between devices: 5.88 us -> 2.35 us  [on_device(): got = lax.all_to_all(rel_grad.reshape(32, -1, D), 'dom', 0, 0)]
    all_to_all x1, starting transfers between devices: 3.54 us -> 6.23 us  [operator_update(): half = lax.all_to_all(shares, 'dom', 0, 0, axis_index_groups=cores)]
    unnamed x27 -> x31, local copies, waits for them, and re-layouts: 4.66 us -> 5.79 us
  transfers between devices with their start and end apart: 21 -> 23, of which waited for: 10 -> 8; matrix products, arithmetic and copies ran while one was open for 2% -> 3% of each run, Pallas kernels for 12% -> 12%
where the time goes in v9:
time: 153 us; the launch traced here: 152 us
  starting transfers between devices  59.7 us (39%)
  Pallas kernels  46.8 us (31%)
  waiting for transfers between devices  30.8 us (20%)
  local copies, waits for them, and re-layouts  7.59 us (5%)
  other arithmetic  5.88 us (4%)
  between operations  1.66 us (1%)
    pallas_call x1, Pallas kernels, score_side(): pl.pallas_call(score_kernel, grid_spec=pltpu.PrefetchScalarGridSpec(num_s...  29.1 us
    ppermute x12, waiting for transfers between devices, shift_x(): return lax.ppermute(block, 'rep', [(i, (i + 2 * by) % 8) for i in range(8)])  16.8 us
    ppermute x3, starting transfers between devices, swap_z(): return lax.ppermute(block, 'rep', [(i, i ^ 1) for i in range(8)])  15.4 us
    ppermute x12, starting transfers between devices, shift_x(): return lax.ppermute(block, 'rep', [(i, (i + 2 * by) % 8) for i in range(8)])  15.2 us
    ppermute x5, starting transfers between devices, shift_dom(): lax.ppermute(block, 'dom', [(i, (i + by) % size) for i in range(size)])  12.2 us
    ppermute x3, waiting for transfers between devices, swap_z(): return lax.ppermute(block, 'rep', [(i, i ^ 1) for i in range(8)])  11.6 us
    all_to_all x1, starting transfers between devices, on_device(): got = lax.all_to_all(rel_grad.reshape(32, -1, D), 'dom', 0, 0)  7.84 us
    pallas_call x1, Pallas kernels, make_queries(): pl.pallas_call(query_kernel, grid_spec=pltpu.PrefetchScalarGridSpec(num_s...  7.18 us
  transfers between devices with their start and end apart: 23, of which 8 were waited for; matrix products, arithmetic and copies ran while one was open for 3% of the time, Pallas kernels for 12%

profile of v9, /device:TPU:1, one launch (start us, length us, event | category | flops | bytes accessed | tf_op | source)
XLA Modules:
  0.0 152.4 jit_solution(14571861913433369954)
XLA Ops:
  0.6 1.0 convert_element_type.15
  1.6 7.8 %collective-permute-start = (bf16[256,256]{1,0:T(8,128)(2,1)S(1)}, bf16[256,256]{1,0:T(8,128)(2,1)S(1)}, u32[]{:S(2)}, u32[]{:S(2)}) collective-permute-start(bf16[256,256]{1,0:T(8,128)(2,1)S(1)} %convert_element_type.15), channel_id=1, source_target_pairs={{0,1},{1,0},{2,3},{3,2},{4,5},{5,4},{6,7},{7,6},{8,9},{9,8},{10,11... | collective-permute-start | bytes 393224 | tf_op jit(solution)/shard_map/ppermute | solution.py:327
  9.4 0.8 fusion.1
  10.3 1.8 %collective-permute-done = bf16[256,256]{1,0:T(8,128)(2,1)S(1)} collective-permute-done((bf16[256,256]{1,0:T(8,128)(2,1)S(1)}, bf16[256,256]{1,0:T(8,128)(2,1)S(1)}, u32[]{:S(2)}, u32[]{:S(2)}) %collective-permute-start) | collective-permute-done | bytes 131104 | tf_op jit(solution)/shard_map/ppermute | solution.py:327
  12.1 3.1 %collective-permute-start.2 = (bf16[512,256]{1,0:T(8,128)(2,1)S(1)}, bf16[512,256]{1,0:T(8,128)(2,1)S(1)}, u32[]{:S(2)}, u32[]{:S(2)}) collective-permute-start(bf16[512,256]{1,0:T(8,128)(2,1)S(1)} %pad_maximum_fusion.refs_0_), channel_id=1, source_target_pairs={{0,6},{1,7},{2,0},{3,1},{4,2},{5,3},{6,4},{7,5},{8,14},{9,15},{10,... | collective-permute-start | bytes 786440 | tf_op jit(solution)/shard_map/ppermute | solution.py:331
  15.2 0.5 collective-permute-start.4
  15.7 0.6 collective-permute-start.6
  16.4 0.7 fusion.5
  17.9 3.2 %neg_weights.1.refs_7_ = f32[4,8,2048]{2,1,0:T(8,128)S(1)} custom-call(s32[4,1,1024]{2,1,0:T(1,128)S(1)} %reshape.47.neg_ref), custom_call_target="tpu_custom_call" | custom-call | flops 1500000000 | bytes 10500000 | tf_op jit(solution)/shard_map/neg_weights/pallas_call | solution.py:74
  21.1 2.2 %collective-permute-start.1 = (bf16[512,256]{1,0:T(8,128)(2,1)S(1)}, bf16[512,256]{1,0:T(8,128)(2,1)S(1)}, u32[]{:S(2)}, u32[]{:S(2)}) collective-permute-start(bf16[512,256]{1,0:T(8,128)(2,1)S(1)} %pad_maximum_fusion.refs_0_), channel_id=1, source_target_pairs={{0,248},{8,0},{16,8},{24,16},{32,24},{40,32},{48,40},{56,48},{64,5... | collective-permute-start | bytes 786440 | tf_op jit(solution)/shard_map/ppermute | solution.py:323
  23.4 4.0 %collective-permute-start.3 = (bf16[512,256]{1,0:T(8,128)(2,1)S(1)}, bf16[512,256]{1,0:T(8,128)(2,1)S(1)}, u32[]{:S(2)}, u32[]{:S(2)}) collective-permute-start(bf16[512,256]{1,0:T(8,128)(2,1)S(1)} %collective-permute-done.2.refs_1_), channel_id=1, source_target_pairs={{0,248},{8,0},{16,8},{24,16},{32,24},{40,32},{48,40},{56,48},{64,5... | collective-permute-start | bytes 786440 | tf_op jit(solution)/shard_map/ppermute | solution.py:323
  27.4 1.7 %collective-permute-start.5 = (bf16[512,256]{1,0:T(8,128)(2,1)S(1)}, bf16[512,256]{1,0:T(8,128)(2,1)S(1)}, u32[]{:S(2)}, u32[]{:S(2)}) collective-permute-start(bf16[512,256]{1,0:T(8,128)(2,1)S(1)} %collective-permute-done.4.refs_2_), channel_id=1, source_target_pairs={{0,248},{8,0},{16,8},{24,16},{32,24},{40,32},{48,40},{56,48},{64,5... | collective-permute-start | bytes 786440 | tf_op jit(solution)/shard_map/ppermute | solution.py:323
  29.0 1.5 %collective-permute-done.6.refs_3_ = bf16[512,256]{1,0:T(8,128)(2,1)S(1)} collective-permute-done((bf16[512,256]{1,0:T(8,128)(2,1)S(1)}, bf16[512,256]{1,0:T(8,128)(2,1)S(1)}, u32[]{:S(2)}, u32[]{:S(2)}) %collective-permute-start.6) | collective-permute-done | bytes 262176 | tf_op jit(solution)/shard_map/ppermute | solution.py:331
  30.6 2.2 %collective-permute-start.7 = (bf16[512,256]{1,0:T(8,128)(2,1)S(1)}, bf16[512,256]{1,0:T(8,128)(2,1)S(1)}, u32[]{:S(2)}, u32[]{:S(2)}) collective-permute-start(bf16[512,256]{1,0:T(8,128)(2,1)S(1)} %collective-permute-done.6.refs_3_), channel_id=1, source_target_pairs={{0,248},{8,0},{16,8},{24,16},{32,24},{40,32},{48,40},{56,48},{64,5... | collective-permute-start | bytes 786440 | tf_op jit(solution)/shard_map/ppermute | solution.py:323
  32.8 7.2 %queries.1 = (bf16[4096,256]{1,0:T(8,128)(2,1)S(1)}, bf16[256,4096]{1,0:T(8,128)(2,1)S(1)}) custom-call(s32[4]{0:T(128)S(1)} %copy-done.1, bf16[512,256]{1,0:T(8,128)(2,1)S(1)} %pad_maximum_fusion.refs_0_, bf16[512,256]{1,0:T(8,128)(2,1)S(1)} %collective-permute-done.2.refs_1_, bf16[512,256]{1,0:T(8,128)(2,1)S(1)} %collective-permute-done.4.refs_2_, ...), custom_call_target="tpu_custom_call" | custom-call | flops 4499999744 | bytes 31500000 | tf_op jit(solution)/shard_map/queries/pallas_call | solution.py:109
  40.1 29.1 %scores.1 = (bf16[256,4096]{1,0:T(8,128)(2,1)S(1)}, bf16[512,256]{1,0:T(8,128)(2,1)S(1)}, bf16[512,256]{1,0:T(8,128)(2,1)S(1)}, bf16[512,256]{1,0:T(8,128)(2,1)S...) custom-call(s32[4]{0:T(128)S(1)} %copy-done.1, s32[1]{0:T(128)S(6)} %copy.18.cnt_ref, ...), custom_call_target="tpu_custom_call" | custom-call | flops 14000000000 | bytes 98000000 | tf_op jit(solution)/shard_map/scores/pallas_call | solution.py:235
  69.1 0.7 copy-done.2
  69.8 1.4 copy-done.10
  71.2 7.8 %all-to-all-start = ((bf16[32,32,256]{2,1,0:T(8,128)(2,1)}), bf16[32,32,256]{2,1,0:T(8,128)(2,1)S(1)}, u32[]{:S(2)}, u32[]{:S(2)}) async-start(bf16[32,32,256]{2,1,0:T(8,128)(2,1)} %bitcast), calls=%async_computation | async-start | bytes 1048576 | tf_op jit(solution)/shard_map/all_to_all | solution.py:496
  79.1 3.4 %collective-permute-start.12 = (bf16[512,256]{1,0:T(8,128)(2,1)S(1)}, bf16[512,256]{1,0:T(8,128)(2,1)S(1)}, u32[]{:S(2)}, u32[]{:S(2)}) collective-permute-start(bf16[512,256]{1,0:T(8,128)(2,1)S(1)} %get-tuple-element.31), channel_id=1, source_target_pairs={{0,4},{1,5},{2,6},{3,7},{4,0},{5,1},{6,2},{7,3},{8,12},{9,13},{10,... | collective-permute-start | bytes 786440 | tf_op jit(solution)/shard_map/ppermute | solution.py:331
  82.5 1.6 %copy-done.11 = bf16[256,4096]{1,0:T(8,128)(2,1)S(1)} copy-done((bf16[256,4096]{1,0:T(8,128)(2,1)S(1)}, bf16[256,4096]{1,0:T(8,128)(2,1)}, u32[]{:S(2)}) %copy-start.11) | copy-done | bytes 2097176
  84.1 6.9 %source_grads.1 = (bf16[512,256]{1,0:T(8,128)(2,1)S(1)}, bf16[512,256]{1,0:T(8,128)(2,1)S(1)}, bf16[512,256]{1,0:T(8,128)(2,1)S(1)}, bf16[512,256]{1,0:T(8,128)(2,1)S(1)}) custom-call(s32[4]{0:T(128)S(1)} %copy-done.1, bf16[256,4096]{1,0:T(8,128)(2,1)S(1)} %copy-done.11, s32[4,1,1024]{2,1,0:T(1,128)S(1)} %reshape.44.refs_4_.src_ref, f32[4,256,256]{2,1,0:T(8,128)S(1)} %copy-done), custom_call_target="tpu_custom_call" | custom-call | flops 4000000000 | bytes 28000000 | tf_op jit(solution)/shard_map/source_grads/pallas_call | solution.py:296
  91.0 0.7 copy-done.4
  91.7 0.7 copy-done.6
  92.4 0.7 copy-done.8
  93.1 2.4 %all-to-all-done.refs_0_ = bf16[32,32,256]{2,1,0:T(8,128)(2,1)S(1)} async-done(((bf16[32,32,256]{2,1,0:T(8,128)(2,1)}), bf16[32,32,256]{2,1,0:T(8,128)(2,1)S(1)}, u32[]{:S(2)}, u32[]{:S(2)}) %all-to-all-start) | async-done | bytes 524320 | tf_op jit(solution)/shard_map/all_to_all | solution.py:496
  95.5 2.3 %collective-permute-start.10 = (f32[32,256]{1,0:T(8,128)S(1)}, f32[32,256]{1,0:T(8,128)S(1)}, u32[]{:S(2)}, u32[]{:S(2)}) collective-permute-start(f32[32,256]{1,0:T(8,128)S(1)} %add_up.3.refs_4_.refs_0_), channel_id=1, source_target_pairs={{0,6},{1,7},{2,0},{3,1},{4,2},{5,3},{6,4},{7,5},{8,14},{9,15},{10,... | collective-permute-start | bytes 98312 | tf_op jit(solution)/shard_map/ppermute | solution.py:331
  97.8 1.3 collective-permute-start.9
  99.3 2.5 %collective-permute-done.8.refs_1_ = f32[32,256]{1,0:T(8,128)S(1)} collective-permute-done((f32[32,256]{1,0:T(8,128)S(1)}, f32[32,256]{1,0:T(8,128)S(1)}, u32[]{:S(2)}, u32[]{:S(2)}) %collective-permute-start.8) | collective-permute-done | bytes 32800 | tf_op jit(solution)/shard_map/ppermute | solution.py:331
  101.8 0.4 collective-permute-done.9.refs_2_
  102.2 7.5 %collective-permute-start.18 = (f32[32,256]{1,0:T(8,128)S(1)}, f32[32,256]{1,0:T(8,128)S(1)}, u32[]{:S(2)}, u32[]{:S(2)}) collective-permute-start(f32[32,256]{1,0:T(8,128)S(1)} %add_up.5.refs_3_), channel_id=1, source_target_pairs={{0,1},{1,0},{2,3},{3,2},{4,5},{5,4},{6,7},{7,6},{8,9},{9,8},{10,11... | collective-permute-start | bytes 98312 | tf_op jit(solution)/shard_map/ppermute | solution.py:327
  109.7 2.1 %collective-permute-start.17 = (bf16[512,256]{1,0:T(8,128)(2,1)S(1)}, bf16[512,256]{1,0:T(8,128)(2,1)S(1)}, u32[]{:S(2)}, u32[]{:S(2)}) collective-permute-start(bf16[512,256]{1,0:T(8,128)(2,1)S(1)} %add_up.4.refs_4_), channel_id=1, source_target_pairs={{0,8},{8,16},{16,24},{24,32},{32,40},{40,48},{48,56},{56,64},{64,7... | collective-permute-start | bytes 786440 | tf_op jit(solution)/shard_map/ppermute | solution.py:323
  112.1 0.8 broadcast_in_dim.2
  112.9 6.2 %all-to-all-start.1 = ((f16[16,40,256]{2,1,0:T(8,128)(2,1)}), f16[16,40,256]{2,1,0:T(8,128)(2,1)S(1)}, u32[]{:S(2)}, u32[]{:S(2)}) async-start(f16[16,40,256]{2,1,0:T(8,128)(2,1)} %broadcast_in_dim.2), calls=%async_computation.1 | async-start | bytes 655360 | tf_op jit(solution)/shard_map/all_to_all | solution.py:439
  119.2 1.1 collective-permute-start.14
  120.3 2.8 %collective-permute-start.15 = (bf16[512,256]{1,0:T(8,128)(2,1)S(1)}, bf16[512,256]{1,0:T(8,128)(2,1)S(1)}, u32[]{:S(2)}, u32[]{:S(2)}) collective-permute-start(bf16[512,256]{1,0:T(8,128)(2,1)S(1)} %get-tuple-element.34), channel_id=1, source_target_pairs={{0,4},{1,5},{2,6},{3,7},{4,0},{5,1},{6,2},{7,3},{8,12},{9,13},{10,... | collective-permute-start | bytes 786440 | tf_op jit(solution)/shard_map/ppermute | solution.py:331
  123.1 4.5 %collective-permute-done.14.refs_1_ = bf16[512,256]{1,0:T(8,128)(2,1)S(1)} collective-permute-done((bf16[512,256]{1,0:T(8,128)(2,1)S(1)}, bf16[512,256]{1,0:T(8,128)(2,1)S(1)}, u32[]{:S(2)}, u32[]{:S(2)}) %collective-permute-start.14) | collective-permute-done | bytes 262176 | tf_op jit(solution)/shard_map/ppermute | solution.py:331
  127.6 7.9 %collective-permute-done.15.refs_2_ = bf16[512,256]{1,0:T(8,128)(2,1)S(1)} collective-permute-done((bf16[512,256]{1,0:T(8,128)(2,1)S(1)}, bf16[512,256]{1,0:T(8,128)(2,1)S(1)}, u32[]{:S(2)}, u32[]{:S(2)}) %collective-permute-start.15) | collective-permute-done | bytes 262176 | tf_op jit(solution)/shard_map/ppermute | solution.py:331
  135.5 0.2 split_sum.1
  135.8 9.8 %collective-permute-done.19 = bf16[256,256]{1,0:T(8,128)(2,1)S(1)} collective-permute-done((bf16[256,256]{1,0:T(8,128)(2,1)S(1)}, bf16[256,256]{1,0:T(8,128)(2,1)S(1)}, u32[]{:S(2)}, u32[]{:S(2)}) %collective-permute-start.19) | collective-permute-done | bytes 131104 | tf_op jit(solution)/shard_map/ppermute | solution.py:327
  145.7 2.9 %collective-permute-start.20 = (f16[16,40,256]{2,1,0:T(8,128)(2,1)S(1)}, f16[16,40,256]{2,1,0:T(8,128)(2,1)S(1)}, u32[]{:S(2)}, u32[]{:S(2)}) collective-permute-start(f16[16,40,256]{2,1,0:T(8,128)(2,1)S(1)} %all-to-all-done.1), channel_id=1, source_target_pairs={{0,8},{8,0},{16,24},{24,16},{32,40},{40,32},{48,56},{56,48},{64,72... | collective-permute-start | bytes 983048 | tf_op jit(solution)/shard_map/ppermute | solution.py:440
  148.6 0.6 fusion.22
  149.2 0.8 divide_subtract_fusion
  150.0 0.2 select_bitcast_fusion.1
  150.2 0.2 copy.16
  150.4 0.1 slice_multiply_fusion
  150.6 1.1 bitcast_subtract_fusion
  151.7 0.7 mul.55
  (68 shorter events, 1.5 us)
Async XLA Ops:
  1.6 10.5 %collective-permute-start = (bf16[256,256]{1,0:T(8,128)(2,1)S(1)}, bf16[256,256]{1,0:T(8,128)(2,1)S(1)}, u32[]{:S(2)}, u32[]{:S(2)}) collective-permute-start(bf16[256,256]{1,0:T(8,128)(2,1)S(1)} %convert_element_type.15), channel_id=1, source_target_pairs={{0,1},{1,0},{2,3},{3,2},{4,5},{5,4},{6,7},{7,6},{8,9},{9,8},{10,11... | collective-permute-start | bytes 393224 | tf_op jit(solution)/shard_map/ppermute | solution.py:327
  12.1 11.3 %collective-permute-start.2 = (bf16[512,256]{1,0:T(8,128)(2,1)S(1)}, bf16[512,256]{1,0:T(8,128)(2,1)S(1)}, u32[]{:S(2)}, u32[]{:S(2)}) collective-permute-start(bf16[512,256]{1,0:T(8,128)(2,1)S(1)} %pad_maximum_fusion.refs_0_), channel_id=1, source_target_pairs={{0,6},{1,7},{2,0},{3,1},{4,2},{5,3},{6,4},{7,5},{8,14},{9,15},{10,... | collective-permute-start | bytes 786440 | tf_op jit(solution)/shard_map/ppermute | solution.py:331
  15.2 12.1 %collective-permute-start.4 = (bf16[512,256]{1,0:T(8,128)(2,1)S(1)}, bf16[512,256]{1,0:T(8,128)(2,1)S(1)}, u32[]{:S(2)}, u32[]{:S(2)}) collective-permute-start(bf16[512,256]{1,0:T(8,128)(2,1)S(1)} %pad_maximum_fusion.refs_0_), channel_id=1, source_target_pairs={{0,4},{1,5},{2,6},{3,7},{4,0},{5,1},{6,2},{7,3},{8,12},{9,13},{10,... | collective-permute-start | bytes 786440 | tf_op jit(solution)/shard_map/ppermute | solution.py:331
  15.7 14.8 %collective-permute-start.6 = (bf16[512,256]{1,0:T(8,128)(2,1)S(1)}, bf16[512,256]{1,0:T(8,128)(2,1)S(1)}, u32[]{:S(2)}, u32[]{:S(2)}) collective-permute-start(bf16[512,256]{1,0:T(8,128)(2,1)S(1)} %pad_maximum_fusion.refs_0_), channel_id=1, source_target_pairs={{0,2},{1,3},{2,4},{3,5},{4,6},{5,7},{6,0},{7,1},{8,10},{9,11},{10,... | collective-permute-start | bytes 786440 | tf_op jit(solution)/shard_map/ppermute | solution.py:331
  17.9 14.9 %copy-start = (f32[4,256,256]{2,1,0:T(8,128)S(1)}, f32[4,256,256]{2,1,0:T(8,128)}, u32[]{:S(2)}) copy-start(f32[4,256,256]{2,1,0:T(8,128)} %mat_ref.1) | copy-start | bytes 3145732
  17.9 14.9 %copy-start.1 = (s32[4]{0:T(128)S(1)}, s32[4]{0:T(128)}, u32[]{:S(2)}) copy-start(s32[4]{0:T(128)} %rel_ref.5) | copy-start | bytes 52
  21.1 18.9 %collective-permute-start.1 = (bf16[512,256]{1,0:T(8,128)(2,1)S(1)}, bf16[512,256]{1,0:T(8,128)(2,1)S(1)}, u32[]{:S(2)}, u32[]{:S(2)}) collective-permute-start(bf16[512,256]{1,0:T(8,128)(2,1)S(1)} %pad_maximum_fusion.refs_0_), channel_id=1, source_target_pairs={{0,248},{8,0},{16,8},{24,16},{32,24},{40,32},{48,40},{56,48},{64,5... | collective-permute-start | bytes 786440 | tf_op jit(solution)/shard_map/ppermute | solution.py:323
  23.4 16.6 %collective-permute-start.3 = (bf16[512,256]{1,0:T(8,128)(2,1)S(1)}, bf16[512,256]{1,0:T(8,128)(2,1)S(1)}, u32[]{:S(2)}, u32[]{:S(2)}) collective-permute-start(bf16[512,256]{1,0:T(8,128)(2,1)S(1)} %collective-permute-done.2.refs_1_), channel_id=1, source_target_pairs={{0,248},{8,0},{16,8},{24,16},{32,24},{40,32},{48,40},{56,48},{64,5... | collective-permute-start | bytes 786440 | tf_op jit(solution)/shard_map/ppermute | solution.py:323
  27.4 12.7 %collective-permute-start.5 = (bf16[512,256]{1,0:T(8,128)(2,1)S(1)}, bf16[512,256]{1,0:T(8,128)(2,1)S(1)}, u32[]{:S(2)}, u32[]{:S(2)}) collective-permute-start(bf16[512,256]{1,0:T(8,128)(2,1)S(1)} %collective-permute-done.4.refs_2_), channel_id=1, source_target_pairs={{0,248},{8,0},{16,8},{24,16},{32,24},{40,32},{48,40},{56,48},{64,5... | collective-permute-start | bytes 786440 | tf_op jit(solution)/shard_map/ppermute | solution.py:323
  30.6 9.5 %collective-permute-start.7 = (bf16[512,256]{1,0:T(8,128)(2,1)S(1)}, bf16[512,256]{1,0:T(8,128)(2,1)S(1)}, u32[]{:S(2)}, u32[]{:S(2)}) collective-permute-start(bf16[512,256]{1,0:T(8,128)(2,1)S(1)} %collective-permute-done.6.refs_3_), channel_id=1, source_target_pairs={{0,248},{8,0},{16,8},{24,16},{32,24},{40,32},{48,40},{56,48},{64,5... | collective-permute-start | bytes 786440 | tf_op jit(solution)/shard_map/ppermute | solution.py:323
  69.1 0.7 copy-start.2
  69.8 1.4 copy-start.10
  71.2 24.3 %all-to-all-start = ((bf16[32,32,256]{2,1,0:T(8,128)(2,1)}), bf16[32,32,256]{2,1,0:T(8,128)(2,1)S(1)}, u32[]{:S(2)}, u32[]{:S(2)}) async-start(bf16[32,32,256]{2,1,0:T(8,128)(2,1)} %bitcast), calls=%async_computation | async-start | bytes 1048576 | tf_op jit(solution)/shard_map/all_to_all | solution.py:496
  79.0 18.8 %collective-permute-start.11 = (bf16[512,256]{1,0:T(8,128)(2,1)S(1)}, bf16[512,256]{1,0:T(8,128)(2,1)S(1)}, u32[]{:S(2)}, u32[]{:S(2)}) collective-permute-start(bf16[512,256]{1,0:T(8,128)(2,1)S(1)} %get-tuple-element.30), channel_id=1, source_target_pairs={{0,2},{1,3},{2,4},{3,5},{4,6},{5,7},{6,0},{7,1},{8,10},{9,11},{10,... | collective-permute-start | bytes 786440 | tf_op jit(solution)/shard_map/ppermute | solution.py:331
  79.1 20.0 %collective-permute-start.12 = (bf16[512,256]{1,0:T(8,128)(2,1)S(1)}, bf16[512,256]{1,0:T(8,128)(2,1)S(1)}, u32[]{:S(2)}, u32[]{:S(2)}) collective-permute-start(bf16[512,256]{1,0:T(8,128)(2,1)S(1)} %get-tuple-element.31), channel_id=1, source_target_pairs={{0,4},{1,5},{2,6},{3,7},{4,0},{5,1},{6,2},{7,3},{8,12},{9,13},{10,... | collective-permute-start | bytes 786440 | tf_op jit(solution)/shard_map/ppermute | solution.py:331
  82.5 16.6 %collective-permute-start.13 = (bf16[512,256]{1,0:T(8,128)(2,1)S(1)}, bf16[512,256]{1,0:T(8,128)(2,1)S(1)}, u32[]{:S(2)}, u32[]{:S(2)}) collective-permute-start(bf16[512,256]{1,0:T(8,128)(2,1)S(1)} %get-tuple-element.32), channel_id=1, source_target_pairs={{0,6},{1,7},{2,0},{3,1},{4,2},{5,3},{6,4},{7,5},{8,14},{9,15},{10,... | collective-permute-start | bytes 786440 | tf_op jit(solution)/shard_map/ppermute | solution.py:331
  82.5 1.6 %copy-start.11 = (bf16[256,4096]{1,0:T(8,128)(2,1)S(1)}, bf16[256,4096]{1,0:T(8,128)(2,1)}, u32[]{:S(2)}) copy-start(bf16[256,4096]{1,0:T(8,128)(2,1)} %copy-done.10) | copy-start | bytes 6291460
  91.0 0.7 copy-start.4
  91.7 0.7 copy-start.6
  92.4 0.7 copy-start.8
  95.4 3.7 %copy-start.3 = (bf16[512,256]{1,0:T(8,128)(2,1)S(1)}, bf16[512,256]{1,0:T(8,128)(2,1)}, u32[]{:S(2)}) copy-start(bf16[512,256]{1,0:T(8,128)(2,1)} %copy-done.2) | copy-start | bytes 786436
  95.5 3.8 %collective-permute-start.10 = (f32[32,256]{1,0:T(8,128)S(1)}, f32[32,256]{1,0:T(8,128)S(1)}, u32[]{:S(2)}, u32[]{:S(2)}) collective-permute-start(f32[32,256]{1,0:T(8,128)S(1)} %add_up.3.refs_4_.refs_0_), channel_id=1, source_target_pairs={{0,6},{1,7},{2,0},{3,1},{4,2},{5,3},{6,4},{7,5},{8,14},{9,15},{10,... | collective-permute-start | bytes 98312 | tf_op jit(solution)/shard_map/ppermute | solution.py:331
  97.8 4.0 %collective-permute-start.8 = (f32[32,256]{1,0:T(8,128)S(1)}, f32[32,256]{1,0:T(8,128)S(1)}, u32[]{:S(2)}, u32[]{:S(2)}) collective-permute-start(f32[32,256]{1,0:T(8,128)S(1)} %add_up.3.refs_4_.refs_0_), channel_id=1, source_target_pairs={{0,2},{1,3},{2,4},{3,5},{4,6},{5,7},{6,0},{7,1},{8,10},{9,11},{10,... | collective-permute-start | bytes 98312 | tf_op jit(solution)/shard_map/ppermute | solution.py:331
  97.8 4.3 %collective-permute-start.9 = (f32[32,256]{1,0:T(8,128)S(1)}, f32[32,256]{1,0:T(8,128)S(1)}, u32[]{:S(2)}, u32[]{:S(2)}) collective-permute-start(f32[32,256]{1,0:T(8,128)S(1)} %add_up.3.refs_4_.refs_0_), channel_id=1, source_target_pairs={{0,4},{1,5},{2,6},{3,7},{4,0},{5,1},{6,2},{7,3},{8,12},{9,13},{10,... | collective-permute-start | bytes 98312 | tf_op jit(solution)/shard_map/ppermute | solution.py:331
  99.3 10.4 %copy-start.13 = (f32[4,256]{1,0:T(4,128)S(1)}, f32[4,256]{1,0:T(4,128)}, u32[]{:S(2)}) copy-start(f32[4,256]{1,0:T(4,128)} %param.12) | copy-start | bytes 12292
  99.3 19.8 %copy-start.5 = (bf16[512,256]{1,0:T(8,128)(2,1)S(1)}, bf16[512,256]{1,0:T(8,128)(2,1)}, u32[]{:S(2)}) copy-start(bf16[512,256]{1,0:T(8,128)(2,1)} %copy-done.4) | copy-start | bytes 786436
  99.3 19.8 %copy-start.7 = (bf16[512,256]{1,0:T(8,128)(2,1)S(1)}, bf16[512,256]{1,0:T(8,128)(2,1)}, u32[]{:S(2)}) copy-start(bf16[512,256]{1,0:T(8,128)(2,1)} %copy-done.6) | copy-start | bytes 786436
  99.3 19.8 %copy-start.9 = (bf16[512,256]{1,0:T(8,128)(2,1)S(1)}, bf16[512,256]{1,0:T(8,128)(2,1)}, u32[]{:S(2)}) copy-start(bf16[512,256]{1,0:T(8,128)(2,1)} %copy-done.8) | copy-start | bytes 786436
  102.2 9.5 %collective-permute-start.18 = (f32[32,256]{1,0:T(8,128)S(1)}, f32[32,256]{1,0:T(8,128)S(1)}, u32[]{:S(2)}, u32[]{:S(2)}) collective-permute-start(f32[32,256]{1,0:T(8,128)S(1)} %add_up.5.refs_3_), channel_id=1, source_target_pairs={{0,1},{1,0},{2,3},{3,2},{4,5},{5,4},{6,7},{7,6},{8,9},{9,8},{10,11... | collective-permute-start | bytes 98312 | tf_op jit(solution)/shard_map/ppermute | solution.py:327
  109.7 13.4 %collective-permute-start.17 = (bf16[512,256]{1,0:T(8,128)(2,1)S(1)}, bf16[512,256]{1,0:T(8,128)(2,1)S(1)}, u32[]{:S(2)}, u32[]{:S(2)}) collective-permute-start(bf16[512,256]{1,0:T(8,128)(2,1)S(1)} %add_up.4.refs_4_), channel_id=1, source_target_pairs={{0,8},{8,16},{16,24},{24,32},{32,40},{40,48},{48,56},{56,64},{64,7... | collective-permute-start | bytes 786440 | tf_op jit(solution)/shard_map/ppermute | solution.py:323
  112.9 32.8 %all-to-all-start.1 = ((f16[16,40,256]{2,1,0:T(8,128)(2,1)}), f16[16,40,256]{2,1,0:T(8,128)(2,1)S(1)}, u32[]{:S(2)}, u32[]{:S(2)}) async-start(f16[16,40,256]{2,1,0:T(8,128)(2,1)} %broadcast_in_dim.2), calls=%async_computation.1 | async-start | bytes 655360 | tf_op jit(solution)/shard_map/all_to_all | solution.py:439
  119.2 29.4 %copy-start.14 = (f32[256]{0:T(256)S(1)}, f32[256]{0:T(256)}, u32[]{:S(2)}) copy-start(f32[256]{0:T(256)} %param.10) | copy-start | bytes 3076
  119.2 30.0 %copy-start.12 = (f32[256,256]{1,0:T(8,128)S(1)}, f32[256,256]{1,0:T(8,128)}, u32[]{:S(2)}) copy-start(f32[256,256]{1,0:T(8,128)} %param.9) | copy-start | bytes 786436
  119.2 8.4 %collective-permute-start.14 = (bf16[512,256]{1,0:T(8,128)(2,1)S(1)}, bf16[512,256]{1,0:T(8,128)(2,1)S(1)}, u32[]{:S(2)}, u32[]{:S(2)}) collective-permute-start(bf16[512,256]{1,0:T(8,128)(2,1)S(1)} %get-tuple-element.33), channel_id=1, source_target_pairs={{0,2},{1,3},{2,4},{3,5},{4,6},{5,7},{6,0},{7,1},{8,10},{9,11},{10,... | collective-permute-start | bytes 786440 | tf_op jit(solution)/shard_map/ppermute | solution.py:331
  120.3 15.2 %collective-permute-start.15 = (bf16[512,256]{1,0:T(8,128)(2,1)S(1)}, bf16[512,256]{1,0:T(8,128)(2,1)S(1)}, u32[]{:S(2)}, u32[]{:S(2)}) collective-permute-start(bf16[512,256]{1,0:T(8,128)(2,1)S(1)} %get-tuple-element.34), channel_id=1, source_target_pairs={{0,4},{1,5},{2,6},{3,7},{4,0},{5,1},{6,2},{7,3},{8,12},{9,13},{10,... | collective-permute-start | bytes 786440 | tf_op jit(solution)/shard_map/ppermute | solution.py:331
  123.1 12.4 %collective-permute-start.16 = (bf16[512,256]{1,0:T(8,128)(2,1)S(1)}, bf16[512,256]{1,0:T(8,128)(2,1)S(1)}, u32[]{:S(2)}, u32[]{:S(2)}) collective-permute-start(bf16[512,256]{1,0:T(8,128)(2,1)S(1)} %get-tuple-element.35), channel_id=1, source_target_pairs={{0,6},{1,7},{2,0},{3,1},{4,2},{5,3},{6,4},{7,5},{8,14},{9,15},{10,... | collective-permute-start | bytes 786440 | tf_op jit(solution)/shard_map/ppermute | solution.py:331
  135.7 9.9 %collective-permute-start.19 = (bf16[256,256]{1,0:T(8,128)(2,1)S(1)}, bf16[256,256]{1,0:T(8,128)(2,1)S(1)}, u32[]{:S(2)}, u32[]{:S(2)}) collective-permute-start(bf16[256,256]{1,0:T(8,128)(2,1)S(1)} %get-tuple-element.37), channel_id=1, source_target_pairs={{0,1},{1,0},{2,3},{3,2},{4,5},{5,4},{6,7},{7,6},{8,9},{9,8},{10,11... | collective-permute-start | bytes 393224 | tf_op jit(solution)/shard_map/ppermute | solution.py:327
  145.7 4.3 %collective-permute-start.20 = (f16[16,40,256]{2,1,0:T(8,128)(2,1)S(1)}, f16[16,40,256]{2,1,0:T(8,128)(2,1)S(1)}, u32[]{:S(2)}, u32[]{:S(2)}) collective-permute-start(f16[16,40,256]{2,1,0:T(8,128)(2,1)S(1)} %all-to-all-done.1), channel_id=1, source_target_pairs={{0,8},{8,0},{16,24},{24,16},{32,40},{40,32},{48,56},{56,48},{64,72... | collective-permute-start | bytes 983048 | tf_op jit(solution)/shard_map/ppermute | solution.py:440

commit v10 on v9

--- a/solution.py
+++ b/solution.py
@@ -50,6 +50,10 @@
 
 def part_specs():
     return [pl.BlockSpec((PART, D), lambda *_: (0, 0))] * PARTS
+
+
+def send_shapes():
+    return [jax.ShapeDtypeStruct((PART, D), bf16)] + [pltpu.HBM((PART, D), bf16)] * (PARTS - 1)
 
 
 def block_of(parts, b):
@@ -262,8 +266,8 @@
             ],
         ),
         out_shape=[
-            jax.ShapeDtypeStruct((D, GROUPS * PAD), bf16),
-            *[jax.ShapeDtypeStruct((PART, D), bf16)] * PARTS,
+            pltpu.HBM((D, GROUPS * PAD), bf16),
+            *send_shapes(),
             jax.ShapeDtypeStruct((kinds, D, D), bf16),
         ],
         compiler_params=params(34),
@@ -306,7 +310,7 @@
             out_specs=[pl.BlockSpec((PART, D), lambda j, rel: (0, 0))] * PARTS,
             scratch_shapes=[pltpu.VMEM((ROWS, D), f32)],
         ),
-        out_shape=[jax.ShapeDtypeStruct((PART, D), bf16)] * PARTS,
+        out_shape=send_shapes(),
         compiler_params=params(16),
         cost_estimate=cost(8),
         name="source_grads",
@@ -397,24 +401,6 @@
     )(*blocks, after)
 
 
-def relay(blocks, after):
-    whole = pl.BlockSpec(memory_space=pltpu.VMEM)
-
-    def kernel(*refs):
-        for i in range(len(blocks)):
-            refs[len(blocks) + 1 + i][...] = refs[i][...]
-
-    return pl.pallas_call(
-        kernel,
-        in_specs=[whole] * len(blocks) + [pl.BlockSpec(memory_space=pl.ANY)],
-        out_specs=[whole] * len(blocks),
-        out_shape=[jax.ShapeDtypeStruct(block.shape, block.dtype) for block in blocks],
-        compiler_params=pltpu.CompilerParams(vmem_limit_bytes=16 * MB),
-        cost_estimate=cost(1),
-        name="relay",
-    )(*blocks, after)
-
-
 def turned(index):
     rep = lax.axis_index("rep")
     return ((index - PART * (rep // 2)) % ROWS) ^ (256 * (rep % 2))
@@ -495,15 +481,16 @@
     dst_blocks = send_x(dst_grad)
     got = lax.all_to_all(rel_grad.reshape(32, -1, D), "dom", 0, 0)
     src_grad = back_stage(gq, src_pad, rel_id, relation)
+    src_blocks = send_x(src_grad)
     mine = add_up([got], src_grad[0], f32)
+    zsum = mine + swap_z(mine)
     dst_sum = add_up(dst_blocks, mine, bf16)
-    xsum = add_up([mine] + [shift_x(mine, k) for k in (1, 2, 3)], dst_sum, f32)
-    zsum = xsum + swap_z(xsum)
-    src_blocks = send_x([src_grad[0]] + list(relay(src_grad[1:], xsum)))
     moved = shift_dom(dst_sum, 1)
-    shares = operator_step(zsum, relation_accum)
+    src_sum = add_up(src_blocks, dst_sum, f32)
+    total = add_up([zsum] + [shift_x(zsum, k) for k in (1, 2, 3)], src_sum, f32)
+    shares = operator_step(total, relation_accum)
     relation_new, relation_accum_new = operator_update(shares, relation, relation_accum)
-    keep, give = split_sum(src_blocks + [moved], zsum)
+    keep, give = split_sum([src_sum, moved], total)
     grads = keep + swap_z(give).astype(f32)
     entity_new, entity_accum_new = rowwise(entity, entity_accum, grads)
     return (entity_new, entity_accum_new, relation_new, relation_accum_new)

time: 153 us -> 150 us (0.980)
  waiting for transfers between devices: 30.8 us -> 14.8 us
  starting transfers between devices: 59.7 us -> 74.2 us
  local copies, waits for them, and re-layouts: 7.59 us -> 4.12 us
  Pallas kernels: 46.8 us -> 48.6 us
    ppermute x12, waiting for transfers between devices: 16.8 us -> 4.47 us  [shift_x(): return lax.ppermute(block, 'rep', [(i, (i + 2 * by) % 8) for i in range(8)])]
    ppermute x3, waiting for transfers between devices: 11.6 us -> 5.45 us  [swap_z(): return lax.ppermute(block, 'rep', [(i, i ^ 1) for i in range(8)])]
    ppermute x3, starting transfers between devices: 15.4 us -> 20.8 us  [swap_z(): return lax.ppermute(block, 'rep', [(i, i ^ 1) for i in range(8)])]
    ppermute x1, starting transfers between devices: 2.88 us -> 7.91 us  [operator_update(): other = lax.ppermute(half, 'dom', [(i, i ^ 1) for i in range(32)])]
    ppermute x5, waiting for transfers between devices: 0.01 us -> 4.64 us  [shift_dom(): lax.ppermute(block, 'dom', [(i, (i + by) % size) for i in range(size)])]
    ppermute x5, starting transfers between devices: 12.2 us -> 16.6 us  [shift_dom(): lax.ppermute(block, 'dom', [(i, (i + by) % size) for i in range(size)])]
    unnamed x31 -> x17, local copies, waits for them, and re-layouts: 5.79 us -> 2.32 us
    all_to_all x1, waiting for transfers between devices: 2.35 us -> 0.27 us  [on_device(): got = lax.all_to_all(rel_grad.reshape(32, -1, D), 'dom', 0, 0)]
  transfers between devices with their start and end apart: 23 -> 23, of which waited for: 8 -> 9; matrix products, arithmetic and copies ran while one was open for 3% -> 2% of each run, Pallas kernels for 12% -> 12%
where the time goes in v10:
time: 150 us; the launch traced here: 149 us
  starting transfers between devices  74.2 us (49%)
  Pallas kernels  48.6 us (32%)
  waiting for transfers between devices  14.8 us (10%)
  other arithmetic  5.89 us (4%)
  local copies, waits for them, and re-layouts  4.12 us (3%)
  between operations  1.55 us (1%)
    pallas_call x1, Pallas kernels, score_side(): pl.pallas_call(score_kernel, grid_spec=pltpu.PrefetchScalarGridSpec(num_s...  30.1 us
    ppermute x3, starting transfers between devices, swap_z(): return lax.ppermute(block, 'rep', [(i, i ^ 1) for i in range(8)])  20.8 us
    ppermute x5, starting transfers between devices, shift_dom(): lax.ppermute(block, 'dom', [(i, (i + by) % size) for i in range(size)])  16.6 us
    ppermute x12, starting transfers between devices, shift_x(): return lax.ppermute(block, 'rep', [(i, (i + 2 * by) % 8) for i in range(8)])  14.7 us
    ppermute x1, starting transfers between devices, operator_update(): other = lax.ppermute(half, 'dom', [(i, i ^ 1) for i in range(32)])  7.91 us
    all_to_all x1, starting transfers between devices, on_device(): got = lax.all_to_all(rel_grad.reshape(32, -1, D), 'dom', 0, 0)  7.84 us
    pallas_call x1, Pallas kernels, source_side(): pl.pallas_call(source_kernel, grid_spec=pltpu.PrefetchScalarGridSpec(num_...  7.77 us
    pallas_call x1, Pallas kernels, make_queries(): pl.pallas_call(query_kernel, grid_spec=pltpu.PrefetchScalarGridSpec(num_s...  7.18 us
  transfers between devices with their start and end apart: 23, of which 9 were waited for; matrix products, arithmetic and copies ran while one was open for 2% of the time, Pallas kernels for 12%

profile of v10, /device:TPU:1, one launch (start us, length us, event | category | flops | bytes accessed | tf_op | source)
XLA Modules:
  0.0 149.2 jit_solution(11657594231646296607)
XLA Ops:
  0.6 1.0 convert_element_type.15
  1.6 7.8 %collective-permute-start = (bf16[256,256]{1,0:T(8,128)(2,1)S(1)}, bf16[256,256]{1,0:T(8,128)(2,1)S(1)}, u32[]{:S(2)}, u32[]{:S(2)}) collective-permute-start(bf16[256,256]{1,0:T(8,128)(2,1)S(1)} %convert_element_type.15), channel_id=1, source_target_pairs={{0,1},{1,0},{2,3},{3,2},{4,5},{5,4},{6,7},{7,6},{8,9},{9,8},{10,11... | collective-permute-start | bytes 393224 | tf_op jit(solution)/shard_map/ppermute | solution.py:331
  9.4 0.8 fusion.1
  10.3 1.8 %collective-permute-done = bf16[256,256]{1,0:T(8,128)(2,1)S(1)} collective-permute-done((bf16[256,256]{1,0:T(8,128)(2,1)S(1)}, bf16[256,256]{1,0:T(8,128)(2,1)S(1)}, u32[]{:S(2)}, u32[]{:S(2)}) %collective-permute-start) | collective-permute-done | bytes 131104 | tf_op jit(solution)/shard_map/ppermute | solution.py:331
  12.1 3.1 %collective-permute-start.2 = (bf16[512,256]{1,0:T(8,128)(2,1)S(1)}, bf16[512,256]{1,0:T(8,128)(2,1)S(1)}, u32[]{:S(2)}, u32[]{:S(2)}) collective-permute-start(bf16[512,256]{1,0:T(8,128)(2,1)S(1)} %pad_maximum_fusion.refs_0_), channel_id=1, source_target_pairs={{0,6},{1,7},{2,0},{3,1},{4,2},{5,3},{6,4},{7,5},{8,14},{9,15},{10,... | collective-permute-start | bytes 786440 | tf_op jit(solution)/shard_map/ppermute | solution.py:335
  15.2 0.5 collective-permute-start.4
  15.7 0.6 collective-permute-start.6
  16.4 0.7 fusion.5
  17.9 3.2 %neg_weights.1.refs_7_ = f32[4,8,2048]{2,1,0:T(8,128)S(1)} custom-call(s32[4,1,1024]{2,1,0:T(1,128)S(1)} %reshape.47.neg_ref), custom_call_target="tpu_custom_call" | custom-call | flops 1500000000 | bytes 10500000 | tf_op jit(solution)/shard_map/neg_weights/pallas_call | solution.py:78
  21.1 2.2 %collective-permute-start.1 = (bf16[512,256]{1,0:T(8,128)(2,1)S(1)}, bf16[512,256]{1,0:T(8,128)(2,1)S(1)}, u32[]{:S(2)}, u32[]{:S(2)}) collective-permute-start(bf16[512,256]{1,0:T(8,128)(2,1)S(1)} %pad_maximum_fusion.refs_0_), channel_id=1, source_target_pairs={{0,248},{8,0},{16,8},{24,16},{32,24},{40,32},{48,40},{56,48},{64,5... | collective-permute-start | bytes 786440 | tf_op jit(solution)/shard_map/ppermute | solution.py:327
  23.4 4.0 %collective-permute-start.3 = (bf16[512,256]{1,0:T(8,128)(2,1)S(1)}, bf16[512,256]{1,0:T(8,128)(2,1)S(1)}, u32[]{:S(2)}, u32[]{:S(2)}) collective-permute-start(bf16[512,256]{1,0:T(8,128)(2,1)S(1)} %collective-permute-done.2.refs_1_), channel_id=1, source_target_pairs={{0,248},{8,0},{16,8},{24,16},{32,24},{40,32},{48,40},{56,48},{64,5... | collective-permute-start | bytes 786440 | tf_op jit(solution)/shard_map/ppermute | solution.py:327
  27.4 1.7 %collective-permute-start.5 = (bf16[512,256]{1,0:T(8,128)(2,1)S(1)}, bf16[512,256]{1,0:T(8,128)(2,1)S(1)}, u32[]{:S(2)}, u32[]{:S(2)}) collective-permute-start(bf16[512,256]{1,0:T(8,128)(2,1)S(1)} %collective-permute-done.4.refs_2_), channel_id=1, source_target_pairs={{0,248},{8,0},{16,8},{24,16},{32,24},{40,32},{48,40},{56,48},{64,5... | collective-permute-start | bytes 786440 | tf_op jit(solution)/shard_map/ppermute | solution.py:327
  29.0 1.5 %collective-permute-done.6.refs_3_ = bf16[512,256]{1,0:T(8,128)(2,1)S(1)} collective-permute-done((bf16[512,256]{1,0:T(8,128)(2,1)S(1)}, bf16[512,256]{1,0:T(8,128)(2,1)S(1)}, u32[]{:S(2)}, u32[]{:S(2)}) %collective-permute-start.6) | collective-permute-done | bytes 262176 | tf_op jit(solution)/shard_map/ppermute | solution.py:335
  30.6 2.2 %collective-permute-start.7 = (bf16[512,256]{1,0:T(8,128)(2,1)S(1)}, bf16[512,256]{1,0:T(8,128)(2,1)S(1)}, u32[]{:S(2)}, u32[]{:S(2)}) collective-permute-start(bf16[512,256]{1,0:T(8,128)(2,1)S(1)} %collective-permute-done.6.refs_3_), channel_id=1, source_target_pairs={{0,248},{8,0},{16,8},{24,16},{32,24},{40,32},{48,40},{56,48},{64,5... | collective-permute-start | bytes 786440 | tf_op jit(solution)/shard_map/ppermute | solution.py:327
  32.8 7.2 %queries.1 = (bf16[4096,256]{1,0:T(8,128)(2,1)S(1)}, bf16[256,4096]{1,0:T(8,128)(2,1)S(1)}) custom-call(s32[4]{0:T(128)S(1)} %copy-done.1, bf16[512,256]{1,0:T(8,128)(2,1)S(1)} %pad_maximum_fusion.refs_0_, bf16[512,256]{1,0:T(8,128)(2,1)S(1)} %collective-permute-done.2.refs_1_, bf16[512,256]{1,0:T(8,128)(2,1)S(1)} %collective-permute-done.4.refs_2_, ...), custom_call_target="tpu_custom_call" | custom-call | flops 4499999744 | bytes 31500000 | tf_op jit(solution)/shard_map/queries/pallas_call | solution.py:113
  40.1 30.1 %scores.1 = (bf16[256,4096]{1,0:T(8,128)(2,1)}, bf16[512,256]{1,0:T(8,128)(2,1)S(1)}, bf16[512,256]{1,0:T(8,128)(2,1)}, bf16[512,256]{1,0:T(8,128)(2,1)}, bf16[5...) custom-call(s32[4]{0:T(128)S(1)} %copy-done.1, s32[1]{0:T(128)S(6)} %copy.18.cnt_ref, ...), custom_call_target="tpu_custom_call" | custom-call | flops 14000000000 | bytes 98000000 | tf_op jit(solution)/shard_map/scores/pallas_call | solution.py:239
  70.1 0.7 copy-done.2
  70.8 7.8 %all-to-all-start = ((bf16[32,32,256]{2,1,0:T(8,128)(2,1)}), bf16[32,32,256]{2,1,0:T(8,128)(2,1)S(1)}, u32[]{:S(2)}, u32[]{:S(2)}) async-start(bf16[32,32,256]{2,1,0:T(8,128)(2,1)} %bitcast), calls=%async_computation | async-start | bytes 1048576 | tf_op jit(solution)/shard_map/all_to_all | solution.py:482
  78.7 3.4 %collective-permute-start.12 = (bf16[512,256]{1,0:T(8,128)(2,1)}, bf16[512,256]{1,0:T(8,128)(2,1)S(1)}, u32[]{:S(2)}, u32[]{:S(2)}) collective-permute-start(bf16[512,256]{1,0:T(8,128)(2,1)} %get-tuple-element.27), channel_id=1, source_target_pairs={{0,4},{1,5},{2,6},{3,7},{4,0},{5,1},{6,2},{7,3},{8,12},{9,13},{10,... | collective-permute-start | bytes 786440 | tf_op jit(solution)/shard_map/ppermute | solution.py:335
  82.2 1.6 %copy-done.4 = bf16[256,4096]{1,0:T(8,128)(2,1)S(1)} copy-done((bf16[256,4096]{1,0:T(8,128)(2,1)S(1)}, bf16[256,4096]{1,0:T(8,128)(2,1)}, u32[]{:S(2)}) %copy-start.4) | copy-done | bytes 2097176
  83.7 7.8 %source_grads.1 = (bf16[512,256]{1,0:T(8,128)(2,1)S(1)}, bf16[512,256]{1,0:T(8,128)(2,1)}, bf16[512,256]{1,0:T(8,128)(2,1)}, bf16[512,256]{1,0:T(8,128)(2,1)}) custom-call(s32[4]{0:T(128)S(1)} %copy-done.1, bf16[256,4096]{1,0:T(8,128)(2,1)S(1)} %copy-done.4, s32[4,1,1024]{2,1,0:T(1,128)S(1)} %reshape.44.refs_4_.src_ref, f32[4,256,256]{2,1,0:T(8,128)S(1)} %copy-done), custom_call_target="tpu_custom_call" | custom-call | flops 4000000000 | bytes 28000000 | tf_op jit(solution)/shard_map/source_grads/pallas_call | solution.py:300
  91.5 0.3 collective-permute-start.10
  91.8 1.2 collective-permute-start.8
  93.0 1.8 %collective-permute-start.9 = (bf16[512,256]{1,0:T(8,128)(2,1)}, bf16[512,256]{1,0:T(8,128)(2,1)S(1)}, u32[]{:S(2)}, u32[]{:S(2)}) collective-permute-start(bf16[512,256]{1,0:T(8,128)(2,1)} %get-tuple-element.23), channel_id=1, source_target_pairs={{0,4},{1,5},{2,6},{3,7},{4,0},{5,1},{6,2},{7,3},{8,12},{9,13},{10,... | collective-permute-start | bytes 786440 | tf_op jit(solution)/shard_map/ppermute | solution.py:335
  94.8 0.3 all-to-all-done.refs_0_
  95.2 7.2 %collective-permute-start.15 = (f32[32,256]{1,0:T(8,128)S(1)}, f32[32,256]{1,0:T(8,128)S(1)}, u32[]{:S(2)}, u32[]{:S(2)}) collective-permute-start(f32[32,256]{1,0:T(8,128)S(1)} %add_up.4.refs_4_), channel_id=1, source_target_pairs={{0,1},{1,0},{2,3},{3,2},{4,5},{5,4},{6,7},{7,6},{8,9},{9,8},{10,11... | collective-permute-start | bytes 98312 | tf_op jit(solution)/shard_map/ppermute | solution.py:331
  102.4 0.1 add_up.5.refs_4_
  102.5 1.2 collective-permute-done.15
  103.7 0.3 collective-permute-start.16
  104.0 3.5 %collective-permute-start.17 = (f32[32,256]{1,0:T(8,128)S(1)}, f32[32,256]{1,0:T(8,128)S(1)}, u32[]{:S(2)}, u32[]{:S(2)}) collective-permute-start(f32[32,256]{1,0:T(8,128)S(1)} %add.57.refs_0_), channel_id=1, source_target_pairs={{0,4},{1,5},{2,6},{3,7},{4,0},{5,1},{6,2},{7,3},{8,12},{9,13},{10,... | collective-permute-start | bytes 98312 | tf_op jit(solution)/shard_map/ppermute | solution.py:335
  107.5 0.1 add_up.6.refs_4_.refs_0_
  107.7 1.4 collective-permute-done.17.refs_2_
  109.1 1.4 collective-permute-done.18.refs_3_
  110.9 0.8 broadcast_in_dim.2
  111.7 6.4 %all-to-all-start.1 = ((f16[16,40,256]{2,1,0:T(8,128)(2,1)}), f16[16,40,256]{2,1,0:T(8,128)(2,1)S(1)}, u32[]{:S(2)}, u32[]{:S(2)}) async-start(f16[16,40,256]{2,1,0:T(8,128)(2,1)} %broadcast_in_dim.2), calls=%async_computation.1 | async-start | bytes 655360 | tf_op jit(solution)/shard_map/all_to_all | solution.py:425
  118.0 6.4 %collective-permute-start.14 = (bf16[512,256]{1,0:T(8,128)(2,1)S(1)}, bf16[512,256]{1,0:T(8,128)(2,1)S(1)}, u32[]{:S(2)}, u32[]{:S(2)}) collective-permute-start(bf16[512,256]{1,0:T(8,128)(2,1)S(1)} %add_up.5.refs_4_), channel_id=1, source_target_pairs={{0,8},{8,16},{16,24},{24,32},{32,40},{40,48},{48,56},{56,64},{64,7... | collective-permute-start | bytes 786440 | tf_op jit(solution)/shard_map/ppermute | solution.py:327
  124.4 4.6 %collective-permute-done.14.refs_1_ = bf16[512,256]{1,0:T(8,128)(2,1)S(1)} collective-permute-done((bf16[512,256]{1,0:T(8,128)(2,1)S(1)}, bf16[512,256]{1,0:T(8,128)(2,1)S(1)}, u32[]{:S(2)}, u32[]{:S(2)}) %collective-permute-start.14) | collective-permute-done | bytes 262176 | tf_op jit(solution)/shard_map/ppermute | solution.py:327
  129.1 5.7 %collective-permute-start.19 = (bf16[256,256]{1,0:T(8,128)(2,1)S(1)}, bf16[256,256]{1,0:T(8,128)(2,1)S(1)}, u32[]{:S(2)}, u32[]{:S(2)}) collective-permute-start(bf16[256,256]{1,0:T(8,128)(2,1)S(1)} %get-tuple-element.31), channel_id=1, source_target_pairs={{0,1},{1,0},{2,3},{3,2},{4,5},{5,4},{6,7},{7,6},{8,9},{9,8},{10,11... | collective-permute-start | bytes 393224 | tf_op jit(solution)/shard_map/ppermute | solution.py:331
  134.9 2.5 %collective-permute-done.19 = bf16[256,256]{1,0:T(8,128)(2,1)S(1)} collective-permute-done((bf16[256,256]{1,0:T(8,128)(2,1)S(1)}, bf16[256,256]{1,0:T(8,128)(2,1)S(1)}, u32[]{:S(2)}, u32[]{:S(2)}) %collective-permute-start.19) | collective-permute-done | bytes 131104 | tf_op jit(solution)/shard_map/ppermute | solution.py:331
  137.3 0.1 multiply_reduce_fusion
  137.5 7.9 %collective-permute-start.20 = (f16[16,40,256]{2,1,0:T(8,128)(2,1)S(1)}, f16[16,40,256]{2,1,0:T(8,128)(2,1)S(1)}, u32[]{:S(2)}, u32[]{:S(2)}) collective-permute-start(f16[16,40,256]{2,1,0:T(8,128)(2,1)S(1)} %all-to-all-done.1), channel_id=1, source_target_pairs={{0,8},{8,0},{16,24},{24,16},{32,40},{40,32},{48,56},{56,48},{64,72... | collective-permute-start | bytes 983048 | tf_op jit(solution)/shard_map/ppermute | solution.py:426
  145.4 0.6 fusion.22
  145.9 0.8 divide_subtract_fusion
  146.8 0.2 select_bitcast_fusion.1
  147.0 0.2 copy.16
  147.2 0.1 slice_multiply_fusion
  147.4 1.1 bitcast_subtract_fusion
  148.5 0.7 mul.55
  (55 shorter events, 1.1 us)
Async XLA Ops:
  1.6 10.5 %collective-permute-start = (bf16[256,256]{1,0:T(8,128)(2,1)S(1)}, bf16[256,256]{1,0:T(8,128)(2,1)S(1)}, u32[]{:S(2)}, u32[]{:S(2)}) collective-permute-start(bf16[256,256]{1,0:T(8,128)(2,1)S(1)} %convert_element_type.15), channel_id=1, source_target_pairs={{0,1},{1,0},{2,3},{3,2},{4,5},{5,4},{6,7},{7,6},{8,9},{9,8},{10,11... | collective-permute-start | bytes 393224 | tf_op jit(solution)/shard_map/ppermute | solution.py:331
  12.1 11.3 %collective-permute-start.2 = (bf16[512,256]{1,0:T(8,128)(2,1)S(1)}, bf16[512,256]{1,0:T(8,128)(2,1)S(1)}, u32[]{:S(2)}, u32[]{:S(2)}) collective-permute-start(bf16[512,256]{1,0:T(8,128)(2,1)S(1)} %pad_maximum_fusion.refs_0_), channel_id=1, source_target_pairs={{0,6},{1,7},{2,0},{3,1},{4,2},{5,3},{6,4},{7,5},{8,14},{9,15},{10,... | collective-permute-start | bytes 786440 | tf_op jit(solution)/shard_map/ppermute | solution.py:335
  15.2 12.1 %collective-permute-start.4 = (bf16[512,256]{1,0:T(8,128)(2,1)S(1)}, bf16[512,256]{1,0:T(8,128)(2,1)S(1)}, u32[]{:S(2)}, u32[]{:S(2)}) collective-permute-start(bf16[512,256]{1,0:T(8,128)(2,1)S(1)} %pad_maximum_fusion.refs_0_), channel_id=1, source_target_pairs={{0,4},{1,5},{2,6},{3,7},{4,0},{5,1},{6,2},{7,3},{8,12},{9,13},{10,... | collective-permute-start | bytes 786440 | tf_op jit(solution)/shard_map/ppermute | solution.py:335
  15.7 14.8 %collective-permute-start.6 = (bf16[512,256]{1,0:T(8,128)(2,1)S(1)}, bf16[512,256]{1,0:T(8,128)(2,1)S(1)}, u32[]{:S(2)}, u32[]{:S(2)}) collective-permute-start(bf16[512,256]{1,0:T(8,128)(2,1)S(1)} %pad_maximum_fusion.refs_0_), channel_id=1, source_target_pairs={{0,2},{1,3},{2,4},{3,5},{4,6},{5,7},{6,0},{7,1},{8,10},{9,11},{10,... | collective-permute-start | bytes 786440 | tf_op jit(solution)/shard_map/ppermute | solution.py:335
  17.9 14.9 %copy-start = (f32[4,256,256]{2,1,0:T(8,128)S(1)}, f32[4,256,256]{2,1,0:T(8,128)}, u32[]{:S(2)}) copy-start(f32[4,256,256]{2,1,0:T(8,128)} %mat_ref.1) | copy-start | bytes 3145732
  17.9 14.9 %copy-start.1 = (s32[4]{0:T(128)S(1)}, s32[4]{0:T(128)}, u32[]{:S(2)}) copy-start(s32[4]{0:T(128)} %rel_ref.5) | copy-start | bytes 52
  21.1 18.9 %collective-permute-start.1 = (bf16[512,256]{1,0:T(8,128)(2,1)S(1)}, bf16[512,256]{1,0:T(8,128)(2,1)S(1)}, u32[]{:S(2)}, u32[]{:S(2)}) collective-permute-start(bf16[512,256]{1,0:T(8,128)(2,1)S(1)} %pad_maximum_fusion.refs_0_), channel_id=1, source_target_pairs={{0,248},{8,0},{16,8},{24,16},{32,24},{40,32},{48,40},{56,48},{64,5... | collective-permute-start | bytes 786440 | tf_op jit(solution)/shard_map/ppermute | solution.py:327
  23.4 16.6 %collective-permute-start.3 = (bf16[512,256]{1,0:T(8,128)(2,1)S(1)}, bf16[512,256]{1,0:T(8,128)(2,1)S(1)}, u32[]{:S(2)}, u32[]{:S(2)}) collective-permute-start(bf16[512,256]{1,0:T(8,128)(2,1)S(1)} %collective-permute-done.2.refs_1_), channel_id=1, source_target_pairs={{0,248},{8,0},{16,8},{24,16},{32,24},{40,32},{48,40},{56,48},{64,5... | collective-permute-start | bytes 786440 | tf_op jit(solution)/shard_map/ppermute | solution.py:327
  27.4 12.7 %collective-permute-start.5 = (bf16[512,256]{1,0:T(8,128)(2,1)S(1)}, bf16[512,256]{1,0:T(8,128)(2,1)S(1)}, u32[]{:S(2)}, u32[]{:S(2)}) collective-permute-start(bf16[512,256]{1,0:T(8,128)(2,1)S(1)} %collective-permute-done.4.refs_2_), channel_id=1, source_target_pairs={{0,248},{8,0},{16,8},{24,16},{32,24},{40,32},{48,40},{56,48},{64,5... | collective-permute-start | bytes 786440 | tf_op jit(solution)/shard_map/ppermute | solution.py:327
  30.6 9.5 %collective-permute-start.7 = (bf16[512,256]{1,0:T(8,128)(2,1)S(1)}, bf16[512,256]{1,0:T(8,128)(2,1)S(1)}, u32[]{:S(2)}, u32[]{:S(2)}) collective-permute-start(bf16[512,256]{1,0:T(8,128)(2,1)S(1)} %collective-permute-done.6.refs_3_), channel_id=1, source_target_pairs={{0,248},{8,0},{16,8},{24,16},{32,24},{40,32},{48,40},{56,48},{64,5... | collective-permute-start | bytes 786440 | tf_op jit(solution)/shard_map/ppermute | solution.py:327
  70.1 0.7 copy-start.2
  70.8 24.2 %all-to-all-start = ((bf16[32,32,256]{2,1,0:T(8,128)(2,1)}), bf16[32,32,256]{2,1,0:T(8,128)(2,1)S(1)}, u32[]{:S(2)}, u32[]{:S(2)}) async-start(bf16[32,32,256]{2,1,0:T(8,128)(2,1)} %bitcast), calls=%async_computation | async-start | bytes 1048576 | tf_op jit(solution)/shard_map/all_to_all | solution.py:482
  78.7 14.3 %collective-permute-start.11 = (bf16[512,256]{1,0:T(8,128)(2,1)}, bf16[512,256]{1,0:T(8,128)(2,1)S(1)}, u32[]{:S(2)}, u32[]{:S(2)}) collective-permute-start(bf16[512,256]{1,0:T(8,128)(2,1)} %get-tuple-element.26), channel_id=1, source_target_pairs={{0,2},{1,3},{2,4},{3,5},{4,6},{5,7},{6,0},{7,1},{8,10},{9,11},{10,... | collective-permute-start | bytes 786440 | tf_op jit(solution)/shard_map/ppermute | solution.py:335
  78.7 16.4 %collective-permute-start.12 = (bf16[512,256]{1,0:T(8,128)(2,1)}, bf16[512,256]{1,0:T(8,128)(2,1)S(1)}, u32[]{:S(2)}, u32[]{:S(2)}) collective-permute-start(bf16[512,256]{1,0:T(8,128)(2,1)} %get-tuple-element.27), channel_id=1, source_target_pairs={{0,4},{1,5},{2,6},{3,7},{4,0},{5,1},{6,2},{7,3},{8,12},{9,13},{10,... | collective-permute-start | bytes 786440 | tf_op jit(solution)/shard_map/ppermute | solution.py:335
  82.1 20.2 %collective-permute-start.13 = (bf16[512,256]{1,0:T(8,128)(2,1)}, bf16[512,256]{1,0:T(8,128)(2,1)S(1)}, u32[]{:S(2)}, u32[]{:S(2)}) collective-permute-start(bf16[512,256]{1,0:T(8,128)(2,1)} %get-tuple-element.28), channel_id=1, source_target_pairs={{0,6},{1,7},{2,0},{3,1},{4,2},{5,3},{6,4},{7,5},{8,14},{9,15},{10,... | collective-permute-start | bytes 786440 | tf_op jit(solution)/shard_map/ppermute | solution.py:335
  82.2 1.6 %copy-start.4 = (bf16[256,4096]{1,0:T(8,128)(2,1)S(1)}, bf16[256,4096]{1,0:T(8,128)(2,1)}, u32[]{:S(2)}) copy-start(bf16[256,4096]{1,0:T(8,128)(2,1)} %get-tuple-element.20.gq_ref) | copy-start | bytes 6291460
  83.7 11.0 %copy-start.6 = (f32[4,256]{1,0:T(4,128)S(1)}, f32[4,256]{1,0:T(4,128)}, u32[]{:S(2)}) copy-start(f32[4,256]{1,0:T(4,128)} %param.12) | copy-start | bytes 12292
  91.5 15.9 %collective-permute-start.10 = (bf16[512,256]{1,0:T(8,128)(2,1)}, bf16[512,256]{1,0:T(8,128)(2,1)S(1)}, u32[]{:S(2)}, u32[]{:S(2)}) collective-permute-start(bf16[512,256]{1,0:T(8,128)(2,1)} %get-tuple-element.24), channel_id=1, source_target_pairs={{0,6},{1,7},{2,0},{3,1},{4,2},{5,3},{6,4},{7,5},{8,14},{9,15},{10,... | collective-permute-start | bytes 786440 | tf_op jit(solution)/shard_map/ppermute | solution.py:335
  91.8 15.7 %collective-permute-start.8 = (bf16[512,256]{1,0:T(8,128)(2,1)}, bf16[512,256]{1,0:T(8,128)(2,1)S(1)}, u32[]{:S(2)}, u32[]{:S(2)}) collective-permute-start(bf16[512,256]{1,0:T(8,128)(2,1)} %get-tuple-element.22), channel_id=1, source_target_pairs={{0,2},{1,3},{2,4},{3,5},{4,6},{5,7},{6,0},{7,1},{8,10},{9,11},{10,... | collective-permute-start | bytes 786440 | tf_op jit(solution)/shard_map/ppermute | solution.py:335
  93.0 14.5 %collective-permute-start.9 = (bf16[512,256]{1,0:T(8,128)(2,1)}, bf16[512,256]{1,0:T(8,128)(2,1)S(1)}, u32[]{:S(2)}, u32[]{:S(2)}) collective-permute-start(bf16[512,256]{1,0:T(8,128)(2,1)} %get-tuple-element.23), channel_id=1, source_target_pairs={{0,4},{1,5},{2,6},{3,7},{4,0},{5,1},{6,2},{7,3},{8,12},{9,13},{10,... | collective-permute-start | bytes 786440 | tf_op jit(solution)/shard_map/ppermute | solution.py:335
  95.1 7.3 %copy-start.3 = (bf16[512,256]{1,0:T(8,128)(2,1)S(1)}, bf16[512,256]{1,0:T(8,128)(2,1)}, u32[]{:S(2)}) copy-start(bf16[512,256]{1,0:T(8,128)(2,1)} %copy-done.2) | copy-start | bytes 786436
  95.2 8.5 %collective-permute-start.15 = (f32[32,256]{1,0:T(8,128)S(1)}, f32[32,256]{1,0:T(8,128)S(1)}, u32[]{:S(2)}, u32[]{:S(2)}) collective-permute-start(f32[32,256]{1,0:T(8,128)S(1)} %add_up.4.refs_4_), channel_id=1, source_target_pairs={{0,1},{1,0},{2,3},{3,2},{4,5},{5,4},{6,7},{7,6},{8,9},{9,8},{10,11... | collective-permute-start | bytes 98312 | tf_op jit(solution)/shard_map/ppermute | solution.py:331
  103.7 4.0 %collective-permute-start.16 = (f32[32,256]{1,0:T(8,128)S(1)}, f32[32,256]{1,0:T(8,128)S(1)}, u32[]{:S(2)}, u32[]{:S(2)}) collective-permute-start(f32[32,256]{1,0:T(8,128)S(1)} %add.57.refs_0_), channel_id=1, source_target_pairs={{0,2},{1,3},{2,4},{3,5},{4,6},{5,7},{6,0},{7,1},{8,10},{9,11},{10,... | collective-permute-start | bytes 98312 | tf_op jit(solution)/shard_map/ppermute | solution.py:335
  104.0 5.1 %collective-permute-start.17 = (f32[32,256]{1,0:T(8,128)S(1)}, f32[32,256]{1,0:T(8,128)S(1)}, u32[]{:S(2)}, u32[]{:S(2)}) collective-permute-start(f32[32,256]{1,0:T(8,128)S(1)} %add.57.refs_0_), channel_id=1, source_target_pairs={{0,4},{1,5},{2,6},{3,7},{4,0},{5,1},{6,2},{7,3},{8,12},{9,13},{10,... | collective-permute-start | bytes 98312 | tf_op jit(solution)/shard_map/ppermute | solution.py:335
  107.5 3.1 %collective-permute-start.18 = (f32[32,256]{1,0:T(8,128)S(1)}, f32[32,256]{1,0:T(8,128)S(1)}, u32[]{:S(2)}, u32[]{:S(2)}) collective-permute-start(f32[32,256]{1,0:T(8,128)S(1)} %add.57.refs_0_), channel_id=1, source_target_pairs={{0,6},{1,7},{2,0},{3,1},{4,2},{5,3},{6,4},{7,5},{8,14},{9,15},{10,... | collective-permute-start | bytes 98312 | tf_op jit(solution)/shard_map/ppermute | solution.py:335
  111.6 33.7 %copy-start.7 = (f32[256]{0:T(256)S(1)}, f32[256]{0:T(256)}, u32[]{:S(2)}) copy-start(f32[256]{0:T(256)} %param.10) | copy-start | bytes 3076
  111.6 34.3 %copy-start.5 = (f32[256,256]{1,0:T(8,128)S(1)}, f32[256,256]{1,0:T(8,128)}, u32[]{:S(2)}) copy-start(f32[256,256]{1,0:T(8,128)} %param.9) | copy-start | bytes 786436
  111.7 25.8 %all-to-all-start.1 = ((f16[16,40,256]{2,1,0:T(8,128)(2,1)}), f16[16,40,256]{2,1,0:T(8,128)(2,1)S(1)}, u32[]{:S(2)}, u32[]{:S(2)}) async-start(f16[16,40,256]{2,1,0:T(8,128)(2,1)} %broadcast_in_dim.2), calls=%async_computation.1 | async-start | bytes 655360 | tf_op jit(solution)/shard_map/all_to_all | solution.py:425
  118.0 11.1 %collective-permute-start.14 = (bf16[512,256]{1,0:T(8,128)(2,1)S(1)}, bf16[512,256]{1,0:T(8,128)(2,1)S(1)}, u32[]{:S(2)}, u32[]{:S(2)}) collective-permute-start(bf16[512,256]{1,0:T(8,128)(2,1)S(1)} %add_up.5.refs_4_), channel_id=1, source_target_pairs={{0,8},{8,16},{16,24},{24,32},{32,40},{40,48},{48,56},{56,64},{64,7... | collective-permute-start | bytes 786440 | tf_op jit(solution)/shard_map/ppermute | solution.py:327
  129.1 8.2 %collective-permute-start.19 = (bf16[256,256]{1,0:T(8,128)(2,1)S(1)}, bf16[256,256]{1,0:T(8,128)(2,1)S(1)}, u32[]{:S(2)}, u32[]{:S(2)}) collective-permute-start(bf16[256,256]{1,0:T(8,128)(2,1)S(1)} %get-tuple-element.31), channel_id=1, source_target_pairs={{0,1},{1,0},{2,3},{3,2},{4,5},{5,4},{6,7},{7,6},{8,9},{9,8},{10,11... | collective-permute-start | bytes 393224 | tf_op jit(solution)/shard_map/ppermute | solution.py:331
  137.5 9.3 %collective-permute-start.20 = (f16[16,40,256]{2,1,0:T(8,128)(2,1)S(1)}, f16[16,40,256]{2,1,0:T(8,128)(2,1)S(1)}, u32[]{:S(2)}, u32[]{:S(2)}) collective-permute-start(f16[16,40,256]{2,1,0:T(8,128)(2,1)S(1)} %all-to-all-done.1), channel_id=1, source_target_pairs={{0,8},{8,0},{16,24},{24,16},{32,40},{40,32},{48,56},{56,48},{64,72... | collective-permute-start | bytes 983048 | tf_op jit(solution)/shard_map/ppermute | solution.py:426

commit v11 on v10

--- a/solution.py
+++ b/solution.py
@@ -486,11 +486,11 @@
     zsum = mine + swap_z(mine)
     dst_sum = add_up(dst_blocks, mine, bf16)
     moved = shift_dom(dst_sum, 1)
-    src_sum = add_up(src_blocks, dst_sum, f32)
+    src_sum = add_up(src_blocks + [moved], dst_sum, f32)
     total = add_up([zsum] + [shift_x(zsum, k) for k in (1, 2, 3)], src_sum, f32)
     shares = operator_step(total, relation_accum)
     relation_new, relation_accum_new = operator_update(shares, relation, relation_accum)
-    keep, give = split_sum([src_sum, moved], total)
+    keep, give = split_sum([src_sum], total)
     grads = keep + swap_z(give).astype(f32)
     entity_new, entity_accum_new = rowwise(entity, entity_accum, grads)
     return (entity_new, entity_accum_new, relation_new, relation_accum_new)

time: 150 us -> 147 us (0.980); the launches traced: 149 us -> 144 us
  starting transfers between devices: 74.2 us -> 63 us
  waiting for transfers between devices: 14.8 us -> 18.6 us
  local copies, waits for them, and re-layouts: 4.12 us -> 6.71 us
    ppermute x1, starting transfers between devices: 7.91 us -> 2.17 us  [operator_update(): other = lax.ppermute(half, 'dom', [(i, i ^ 1) for i in range(32)])]
    ppermute x3, waiting for transfers between devices: 5.45 us -> 10.4 us  [swap_z(): return lax.ppermute(block, 'rep', [(i, i ^ 1) for i in range(8)])]
    ppermute x5, waiting for transfers between devices: 4.64 us -> 0.01 us  [shift_dom(): lax.ppermute(block, 'dom', [(i, (i + by) % size) for i in range(size)])]
    ppermute x5, starting transfers between devices: 16.6 us -> 12.5 us  [shift_dom(): lax.ppermute(block, 'dom', [(i, (i + by) % size) for i in range(size)])]
    unnamed x17 -> x21, local copies, waits for them, and re-layouts: 2.32 us -> 4.91 us
    ppermute x3, starting transfers between devices: 20.8 us -> 18.5 us  [swap_z(): return lax.ppermute(block, 'rep', [(i, i ^ 1) for i in range(8)])]
    all_to_all x1, starting transfers between devices: 6.35 us -> 8.56 us  [operator_update(): half = lax.all_to_all(shares, 'dom', 0, 0, axis_index_groups=cores)]
    all_to_all x1, waiting for transfers between devices: 0.27 us -> 2.08 us  [on_device(): got = lax.all_to_all(rel_grad.reshape(32, -1, D), 'dom', 0, 0)]
  transfers between devices with their start and end apart: 23 -> 23, of which waited for: 9 -> 9; matrix products, arithmetic and copies ran while one was open for 2% -> 2% of each run, Pallas kernels for 12% -> 13%
where the time goes in v11:
time: 147 us; the launch traced here: 144 us
  starting transfers between devices  63 us (43%)
  Pallas kernels  48.6 us (33%)
  waiting for transfers between devices  18.6 us (13%)
  local copies, waits for them, and re-layouts  6.71 us (5%)
  other arithmetic  5.9 us (4%)
  between operations  1.55 us (1%)
    pallas_call x1, Pallas kernels, score_side(): pl.pallas_call(score_kernel, grid_spec=pltpu.PrefetchScalarGridSpec(num_s...  30.1 us
    ppermute x3, starting transfers between devices, swap_z(): return lax.ppermute(block, 'rep', [(i, i ^ 1) for i in range(8)])  18.5 us
    ppermute x12, starting transfers between devices, shift_x(): return lax.ppermute(block, 'rep', [(i, (i + 2 * by) % 8) for i in range(8)])  13.3 us
    ppermute x5, starting transfers between devices, shift_dom(): lax.ppermute(block, 'dom', [(i, (i + by) % size) for i in range(size)])  12.5 us
    ppermute x3, waiting for transfers between devices, swap_z(): return lax.ppermute(block, 'rep', [(i, i ^ 1) for i in range(8)])  10.4 us
    all_to_all x1, starting transfers between devices, operator_update(): half = lax.all_to_all(shares, 'dom', 0, 0, axis_index_groups=cores)  8.56 us
    all_to_all x1, starting transfers between devices, on_device(): got = lax.all_to_all(rel_grad.reshape(32, -1, D), 'dom', 0, 0)  7.84 us
    pallas_call x1, Pallas kernels, source_side(): pl.pallas_call(source_kernel, grid_spec=pltpu.PrefetchScalarGridSpec(num_...  7.76 us
  transfers between devices with their start and end apart: 23, of which 9 were waited for; matrix products, arithmetic and copies ran while one was open for 2% of the time, Pallas kernels for 13%

profile of v11, /device:TPU:1, one launch (start us, length us, event | category | flops | bytes accessed | tf_op | source)
XLA Modules:
  0.0 144.3 jit_solution(11933571303503148325)
XLA Ops:
  0.6 1.0 convert_element_type.15
  1.6 7.8 %collective-permute-start = (bf16[256,256]{1,0:T(8,128)(2,1)S(1)}, bf16[256,256]{1,0:T(8,128)(2,1)S(1)}, u32[]{:S(2)}, u32[]{:S(2)}) collective-permute-start(bf16[256,256]{1,0:T(8,128)(2,1)S(1)} %convert_element_type.15), channel_id=1, source_target_pairs={{0,1},{1,0},{2,3},{3,2},{4,5},{5,4},{6,7},{7,6},{8,9},{9,8},{10,11... | collective-permute-start | bytes 393224 | tf_op jit(solution)/shard_map/ppermute | solution.py:331
  9.4 0.8 fusion.1
  10.3 1.8 %collective-permute-done = bf16[256,256]{1,0:T(8,128)(2,1)S(1)} collective-permute-done((bf16[256,256]{1,0:T(8,128)(2,1)S(1)}, bf16[256,256]{1,0:T(8,128)(2,1)S(1)}, u32[]{:S(2)}, u32[]{:S(2)}) %collective-permute-start) | collective-permute-done | bytes 131104 | tf_op jit(solution)/shard_map/ppermute | solution.py:331
  12.1 3.1 %collective-permute-start.2 = (bf16[512,256]{1,0:T(8,128)(2,1)S(1)}, bf16[512,256]{1,0:T(8,128)(2,1)S(1)}, u32[]{:S(2)}, u32[]{:S(2)}) collective-permute-start(bf16[512,256]{1,0:T(8,128)(2,1)S(1)} %pad_maximum_fusion.refs_0_), channel_id=1, source_target_pairs={{0,6},{1,7},{2,0},{3,1},{4,2},{5,3},{6,4},{7,5},{8,14},{9,15},{10,... | collective-permute-start | bytes 786440 | tf_op jit(solution)/shard_map/ppermute | solution.py:335
  15.2 0.5 collective-permute-start.4
  15.7 0.6 collective-permute-start.6
  16.4 0.7 fusion.5
  17.9 3.2 %neg_weights.1.refs_7_ = f32[4,8,2048]{2,1,0:T(8,128)S(1)} custom-call(s32[4,1,1024]{2,1,0:T(1,128)S(1)} %reshape.47.neg_ref), custom_call_target="tpu_custom_call" | custom-call | flops 1500000000 | bytes 10500000 | tf_op jit(solution)/shard_map/neg_weights/pallas_call | solution.py:78
  21.1 2.2 %collective-permute-start.1 = (bf16[512,256]{1,0:T(8,128)(2,1)S(1)}, bf16[512,256]{1,0:T(8,128)(2,1)S(1)}, u32[]{:S(2)}, u32[]{:S(2)}) collective-permute-start(bf16[512,256]{1,0:T(8,128)(2,1)S(1)} %pad_maximum_fusion.refs_0_), channel_id=1, source_target_pairs={{0,248},{8,0},{16,8},{24,16},{32,24},{40,32},{48,40},{56,48},{64,5... | collective-permute-start | bytes 786440 | tf_op jit(solution)/shard_map/ppermute | solution.py:327
  23.4 4.0 %collective-permute-start.3 = (bf16[512,256]{1,0:T(8,128)(2,1)S(1)}, bf16[512,256]{1,0:T(8,128)(2,1)S(1)}, u32[]{:S(2)}, u32[]{:S(2)}) collective-permute-start(bf16[512,256]{1,0:T(8,128)(2,1)S(1)} %collective-permute-done.2.refs_1_), channel_id=1, source_target_pairs={{0,248},{8,0},{16,8},{24,16},{32,24},{40,32},{48,40},{56,48},{64,5... | collective-permute-start | bytes 786440 | tf_op jit(solution)/shard_map/ppermute | solution.py:327
  27.4 1.7 %collective-permute-start.5 = (bf16[512,256]{1,0:T(8,128)(2,1)S(1)}, bf16[512,256]{1,0:T(8,128)(2,1)S(1)}, u32[]{:S(2)}, u32[]{:S(2)}) collective-permute-start(bf16[512,256]{1,0:T(8,128)(2,1)S(1)} %collective-permute-done.4.refs_2_), channel_id=1, source_target_pairs={{0,248},{8,0},{16,8},{24,16},{32,24},{40,32},{48,40},{56,48},{64,5... | collective-permute-start | bytes 786440 | tf_op jit(solution)/shard_map/ppermute | solution.py:327
  29.0 1.5 %collective-permute-done.6.refs_3_ = bf16[512,256]{1,0:T(8,128)(2,1)S(1)} collective-permute-done((bf16[512,256]{1,0:T(8,128)(2,1)S(1)}, bf16[512,256]{1,0:T(8,128)(2,1)S(1)}, u32[]{:S(2)}, u32[]{:S(2)}) %collective-permute-start.6) | collective-permute-done | bytes 262176 | tf_op jit(solution)/shard_map/ppermute | solution.py:335
  30.6 2.2 %collective-permute-start.7 = (bf16[512,256]{1,0:T(8,128)(2,1)S(1)}, bf16[512,256]{1,0:T(8,128)(2,1)S(1)}, u32[]{:S(2)}, u32[]{:S(2)}) collective-permute-start(bf16[512,256]{1,0:T(8,128)(2,1)S(1)} %collective-permute-done.6.refs_3_), channel_id=1, source_target_pairs={{0,248},{8,0},{16,8},{24,16},{32,24},{40,32},{48,40},{56,48},{64,5... | collective-permute-start | bytes 786440 | tf_op jit(solution)/shard_map/ppermute | solution.py:327
  32.8 7.2 %queries.1 = (bf16[4096,256]{1,0:T(8,128)(2,1)S(1)}, bf16[256,4096]{1,0:T(8,128)(2,1)S(1)}) custom-call(s32[4]{0:T(128)S(1)} %copy-done.3, bf16[512,256]{1,0:T(8,128)(2,1)S(1)} %pad_maximum_fusion.refs_0_, bf16[512,256]{1,0:T(8,128)(2,1)S(1)} %collective-permute-done.2.refs_1_, bf16[512,256]{1,0:T(8,128)(2,1)S(1)} %collective-permute-done.4.refs_2_, ...), custom_call_target="tpu_custom_call" | custom-call | flops 4499999744 | bytes 31500000 | tf_op jit(solution)/shard_map/queries/pallas_call | solution.py:113
  40.1 30.1 %scores.1 = (bf16[256,4096]{1,0:T(8,128)(2,1)}, bf16[512,256]{1,0:T(8,128)(2,1)S(1)}, bf16[512,256]{1,0:T(8,128)(2,1)}, bf16[512,256]{1,0:T(8,128)(2,1)}, bf16[5...) custom-call(s32[4]{0:T(128)S(1)} %copy-done.3, s32[1]{0:T(128)S(6)} %copy.18.cnt_ref, ...), custom_call_target="tpu_custom_call" | custom-call | flops 14000000000 | bytes 98000000 | tf_op jit(solution)/shard_map/scores/pallas_call | solution.py:239
  70.1 0.7 copy-done.4
  70.8 7.8 %all-to-all-start = ((bf16[32,32,256]{2,1,0:T(8,128)(2,1)}), bf16[32,32,256]{2,1,0:T(8,128)(2,1)S(1)}, u32[]{:S(2)}, u32[]{:S(2)}) async-start(bf16[32,32,256]{2,1,0:T(8,128)(2,1)} %bitcast), calls=%async_computation | async-start | bytes 1048576 | tf_op jit(solution)/shard_map/all_to_all | solution.py:482
  78.7 3.4 %collective-permute-start.12 = (bf16[512,256]{1,0:T(8,128)(2,1)}, bf16[512,256]{1,0:T(8,128)(2,1)S(1)}, u32[]{:S(2)}, u32[]{:S(2)}) collective-permute-start(bf16[512,256]{1,0:T(8,128)(2,1)} %get-tuple-element.27), channel_id=1, source_target_pairs={{0,4},{1,5},{2,6},{3,7},{4,0},{5,1},{6,2},{7,3},{8,12},{9,13},{10,... | collective-permute-start | bytes 786440 | tf_op jit(solution)/shard_map/ppermute | solution.py:335
  82.1 1.6 %copy-done.6 = bf16[256,4096]{1,0:T(8,128)(2,1)S(1)} copy-done((bf16[256,4096]{1,0:T(8,128)(2,1)S(1)}, bf16[256,4096]{1,0:T(8,128)(2,1)}, u32[]{:S(2)}) %copy-start.6) | copy-done | bytes 2097176
  83.7 7.8 %source_grads.1 = (bf16[512,256]{1,0:T(8,128)(2,1)S(1)}, bf16[512,256]{1,0:T(8,128)(2,1)}, bf16[512,256]{1,0:T(8,128)(2,1)}, bf16[512,256]{1,0:T(8,128)(2,1)}) custom-call(s32[4]{0:T(128)S(1)} %copy-done.3, bf16[256,4096]{1,0:T(8,128)(2,1)S(1)} %copy-done.6, s32[4,1,1024]{2,1,0:T(1,128)S(1)} %reshape.44.refs_4_.src_ref, f32[4,256,256]{2,1,0:T(8,128)S(1)} %copy-done), custom_call_target="tpu_custom_call" | custom-call | flops 4000000000 | bytes 28000000 | tf_op jit(solution)/shard_map/source_grads/pallas_call | solution.py:300
  91.5 0.3 collective-permute-start.10
  91.8 1.2 collective-permute-start.8
  93.0 2.1 %all-to-all-done.refs_0_ = bf16[32,32,256]{2,1,0:T(8,128)(2,1)S(1)} async-done(((bf16[32,32,256]{2,1,0:T(8,128)(2,1)}), bf16[32,32,256]{2,1,0:T(8,128)(2,1)S(1)}, u32[]{:S(2)}, u32[]{:S(2)}) %all-to-all-start) | async-done | bytes 524320 | tf_op jit(solution)/shard_map/all_to_all | solution.py:482
  95.1 0.6 collective-permute-start.9
  95.8 0.7 copy-done.1
  96.5 0.9 copy-done.2
  97.4 0.9 copy-done.5
  98.5 2.4 %collective-permute-start.14 = (bf16[512,256]{1,0:T(8,128)(2,1)S(1)}, bf16[512,256]{1,0:T(8,128)(2,1)S(1)}, u32[]{:S(2)}, u32[]{:S(2)}) collective-permute-start(bf16[512,256]{1,0:T(8,128)(2,1)S(1)} %add_up.5.refs_5_), channel_id=1, source_target_pairs={{0,8},{8,16},{16,24},{24,32},{32,40},{40,48},{48,56},{56,64},{64,7... | collective-permute-start | bytes 786440 | tf_op jit(solution)/shard_map/ppermute | solution.py:327
  100.9 7.3 %collective-permute-start.15 = (f32[32,256]{1,0:T(8,128)S(1)}, f32[32,256]{1,0:T(8,128)S(1)}, u32[]{:S(2)}, u32[]{:S(2)}) collective-permute-start(f32[32,256]{1,0:T(8,128)S(1)} %add_up.4.refs_4_), channel_id=1, source_target_pairs={{0,1},{1,0},{2,3},{3,2},{4,5},{5,4},{6,7},{7,6},{8,9},{9,8},{10,11... | collective-permute-start | bytes 98312 | tf_op jit(solution)/shard_map/ppermute | solution.py:331
  108.2 1.3 collective-permute-done.15
  109.5 0.5 collective-permute-start.16
  110.1 3.0 %collective-permute-start.17 = (f32[32,256]{1,0:T(8,128)S(1)}, f32[32,256]{1,0:T(8,128)S(1)}, u32[]{:S(2)}, u32[]{:S(2)}) collective-permute-start(f32[32,256]{1,0:T(8,128)S(1)} %add.57.refs_0_), channel_id=1, source_target_pairs={{0,4},{1,5},{2,6},{3,7},{4,0},{5,1},{6,2},{7,3},{8,12},{9,13},{10,... | collective-permute-start | bytes 98312 | tf_op jit(solution)/shard_map/ppermute | solution.py:335
  113.1 0.2 add_up.6.refs_4_.refs_0_
  113.2 0.9 collective-permute-done.16.refs_1_
  114.1 0.9 collective-permute-done.17.refs_2_
  115.0 1.1 collective-permute-done.18.refs_3_
  116.5 0.8 broadcast_in_dim.2
  117.3 8.6 %all-to-all-start.1 = ((f16[16,40,256]{2,1,0:T(8,128)(2,1)}), f16[16,40,256]{2,1,0:T(8,128)(2,1)S(1)}, u32[]{:S(2)}, u32[]{:S(2)}) async-start(f16[16,40,256]{2,1,0:T(8,128)(2,1)} %broadcast_in_dim.2), calls=%async_computation.1 | async-start | bytes 655360 | tf_op jit(solution)/shard_map/all_to_all | solution.py:425
  125.9 3.4 %collective-permute-start.19 = (bf16[256,256]{1,0:T(8,128)(2,1)S(1)}, bf16[256,256]{1,0:T(8,128)(2,1)S(1)}, u32[]{:S(2)}, u32[]{:S(2)}) collective-permute-start(bf16[256,256]{1,0:T(8,128)(2,1)S(1)} %get-tuple-element.31), channel_id=1, source_target_pairs={{0,1},{1,0},{2,3},{3,2},{4,5},{5,4},{6,7},{7,6},{8,9},{9,8},{10,11... | collective-permute-start | bytes 393224 | tf_op jit(solution)/shard_map/ppermute | solution.py:331
  129.3 7.2 %collective-permute-done.19 = bf16[256,256]{1,0:T(8,128)(2,1)S(1)} collective-permute-done((bf16[256,256]{1,0:T(8,128)(2,1)S(1)}, bf16[256,256]{1,0:T(8,128)(2,1)S(1)}, u32[]{:S(2)}, u32[]{:S(2)}) %collective-permute-start.19) | collective-permute-done | bytes 131104 | tf_op jit(solution)/shard_map/ppermute | solution.py:331
  136.7 1.7 %all-to-all-done.1 = f16[16,40,256]{2,1,0:T(8,128)(2,1)S(1)} async-done(((f16[16,40,256]{2,1,0:T(8,128)(2,1)}), f16[16,40,256]{2,1,0:T(8,128)(2,1)S(1)}, u32[]{:S(2)}, u32[]{:S(2)}) %all-to-all-start.1) | async-done | bytes 327712 | tf_op jit(solution)/shard_map/all_to_all | solution.py:425
  138.3 2.2 %collective-permute-start.20 = (f16[16,40,256]{2,1,0:T(8,128)(2,1)S(1)}, f16[16,40,256]{2,1,0:T(8,128)(2,1)S(1)}, u32[]{:S(2)}, u32[]{:S(2)}) collective-permute-start(f16[16,40,256]{2,1,0:T(8,128)(2,1)S(1)} %all-to-all-done.1), channel_id=1, source_target_pairs={{0,8},{8,0},{16,24},{24,16},{32,40},{40,32},{48,56},{56,48},{64,72... | collective-permute-start | bytes 983048 | tf_op jit(solution)/shard_map/ppermute | solution.py:426
  140.5 0.6 fusion.22
  141.1 0.8 divide_subtract_fusion
  142.2 0.2 copy.16
  142.6 1.1 bitcast_subtract_fusion
  143.7 0.7 mul.55
  (59 shorter events, 1.6 us)
Async XLA Ops:
  1.6 10.5 %collective-permute-start = (bf16[256,256]{1,0:T(8,128)(2,1)S(1)}, bf16[256,256]{1,0:T(8,128)(2,1)S(1)}, u32[]{:S(2)}, u32[]{:S(2)}) collective-permute-start(bf16[256,256]{1,0:T(8,128)(2,1)S(1)} %convert_element_type.15), channel_id=1, source_target_pairs={{0,1},{1,0},{2,3},{3,2},{4,5},{5,4},{6,7},{7,6},{8,9},{9,8},{10,11... | collective-permute-start | bytes 393224 | tf_op jit(solution)/shard_map/ppermute | solution.py:331
  12.1 11.3 %collective-permute-start.2 = (bf16[512,256]{1,0:T(8,128)(2,1)S(1)}, bf16[512,256]{1,0:T(8,128)(2,1)S(1)}, u32[]{:S(2)}, u32[]{:S(2)}) collective-permute-start(bf16[512,256]{1,0:T(8,128)(2,1)S(1)} %pad_maximum_fusion.refs_0_), channel_id=1, source_target_pairs={{0,6},{1,7},{2,0},{3,1},{4,2},{5,3},{6,4},{7,5},{8,14},{9,15},{10,... | collective-permute-start | bytes 786440 | tf_op jit(solution)/shard_map/ppermute | solution.py:335
  15.2 12.1 %collective-permute-start.4 = (bf16[512,256]{1,0:T(8,128)(2,1)S(1)}, bf16[512,256]{1,0:T(8,128)(2,1)S(1)}, u32[]{:S(2)}, u32[]{:S(2)}) collective-permute-start(bf16[512,256]{1,0:T(8,128)(2,1)S(1)} %pad_maximum_fusion.refs_0_), channel_id=1, source_target_pairs={{0,4},{1,5},{2,6},{3,7},{4,0},{5,1},{6,2},{7,3},{8,12},{9,13},{10,... | collective-permute-start | bytes 786440 | tf_op jit(solution)/shard_map/ppermute | solution.py:335
  15.7 14.8 %collective-permute-start.6 = (bf16[512,256]{1,0:T(8,128)(2,1)S(1)}, bf16[512,256]{1,0:T(8,128)(2,1)S(1)}, u32[]{:S(2)}, u32[]{:S(2)}) collective-permute-start(bf16[512,256]{1,0:T(8,128)(2,1)S(1)} %pad_maximum_fusion.refs_0_), channel_id=1, source_target_pairs={{0,2},{1,3},{2,4},{3,5},{4,6},{5,7},{6,0},{7,1},{8,10},{9,11},{10,... | collective-permute-start | bytes 786440 | tf_op jit(solution)/shard_map/ppermute | solution.py:335
  17.9 14.9 %copy-start = (f32[4,256,256]{2,1,0:T(8,128)S(1)}, f32[4,256,256]{2,1,0:T(8,128)}, u32[]{:S(2)}) copy-start(f32[4,256,256]{2,1,0:T(8,128)} %mat_ref.1) | copy-start | bytes 3145732
  17.9 14.9 %copy-start.3 = (s32[4]{0:T(128)S(1)}, s32[4]{0:T(128)}, u32[]{:S(2)}) copy-start(s32[4]{0:T(128)} %rel_ref.5) | copy-start | bytes 52
  21.1 18.9 %collective-permute-start.1 = (bf16[512,256]{1,0:T(8,128)(2,1)S(1)}, bf16[512,256]{1,0:T(8,128)(2,1)S(1)}, u32[]{:S(2)}, u32[]{:S(2)}) collective-permute-start(bf16[512,256]{1,0:T(8,128)(2,1)S(1)} %pad_maximum_fusion.refs_0_), channel_id=1, source_target_pairs={{0,248},{8,0},{16,8},{24,16},{32,24},{40,32},{48,40},{56,48},{64,5... | collective-permute-start | bytes 786440 | tf_op jit(solution)/shard_map/ppermute | solution.py:327
  23.4 16.6 %collective-permute-start.3 = (bf16[512,256]{1,0:T(8,128)(2,1)S(1)}, bf16[512,256]{1,0:T(8,128)(2,1)S(1)}, u32[]{:S(2)}, u32[]{:S(2)}) collective-permute-start(bf16[512,256]{1,0:T(8,128)(2,1)S(1)} %collective-permute-done.2.refs_1_), channel_id=1, source_target_pairs={{0,248},{8,0},{16,8},{24,16},{32,24},{40,32},{48,40},{56,48},{64,5... | collective-permute-start | bytes 786440 | tf_op jit(solution)/shard_map/ppermute | solution.py:327
  27.4 12.7 %collective-permute-start.5 = (bf16[512,256]{1,0:T(8,128)(2,1)S(1)}, bf16[512,256]{1,0:T(8,128)(2,1)S(1)}, u32[]{:S(2)}, u32[]{:S(2)}) collective-permute-start(bf16[512,256]{1,0:T(8,128)(2,1)S(1)} %collective-permute-done.4.refs_2_), channel_id=1, source_target_pairs={{0,248},{8,0},{16,8},{24,16},{32,24},{40,32},{48,40},{56,48},{64,5... | collective-permute-start | bytes 786440 | tf_op jit(solution)/shard_map/ppermute | solution.py:327
  30.6 9.5 %collective-permute-start.7 = (bf16[512,256]{1,0:T(8,128)(2,1)S(1)}, bf16[512,256]{1,0:T(8,128)(2,1)S(1)}, u32[]{:S(2)}, u32[]{:S(2)}) collective-permute-start(bf16[512,256]{1,0:T(8,128)(2,1)S(1)} %collective-permute-done.6.refs_3_), channel_id=1, source_target_pairs={{0,248},{8,0},{16,8},{24,16},{32,24},{40,32},{48,40},{56,48},{64,5... | collective-permute-start | bytes 786440 | tf_op jit(solution)/shard_map/ppermute | solution.py:327
  70.1 0.7 copy-start.4
  70.8 24.2 %all-to-all-start = ((bf16[32,32,256]{2,1,0:T(8,128)(2,1)}), bf16[32,32,256]{2,1,0:T(8,128)(2,1)S(1)}, u32[]{:S(2)}, u32[]{:S(2)}) async-start(bf16[32,32,256]{2,1,0:T(8,128)(2,1)} %bitcast), calls=%async_computation | async-start | bytes 1048576 | tf_op jit(solution)/shard_map/all_to_all | solution.py:482
  78.6 16.5 %collective-permute-start.11 = (bf16[512,256]{1,0:T(8,128)(2,1)}, bf16[512,256]{1,0:T(8,128)(2,1)S(1)}, u32[]{:S(2)}, u32[]{:S(2)}) collective-permute-start(bf16[512,256]{1,0:T(8,128)(2,1)} %get-tuple-element.26), channel_id=1, source_target_pairs={{0,2},{1,3},{2,4},{3,5},{4,6},{5,7},{6,0},{7,1},{8,10},{9,11},{10,... | collective-permute-start | bytes 786440 | tf_op jit(solution)/shard_map/ppermute | solution.py:335
  78.7 17.0 %collective-permute-start.12 = (bf16[512,256]{1,0:T(8,128)(2,1)}, bf16[512,256]{1,0:T(8,128)(2,1)S(1)}, u32[]{:S(2)}, u32[]{:S(2)}) collective-permute-start(bf16[512,256]{1,0:T(8,128)(2,1)} %get-tuple-element.27), channel_id=1, source_target_pairs={{0,4},{1,5},{2,6},{3,7},{4,0},{5,1},{6,2},{7,3},{8,12},{9,13},{10,... | collective-permute-start | bytes 786440 | tf_op jit(solution)/shard_map/ppermute | solution.py:335
  82.1 13.6 %collective-permute-start.13 = (bf16[512,256]{1,0:T(8,128)(2,1)}, bf16[512,256]{1,0:T(8,128)(2,1)S(1)}, u32[]{:S(2)}, u32[]{:S(2)}) collective-permute-start(bf16[512,256]{1,0:T(8,128)(2,1)} %get-tuple-element.28), channel_id=1, source_target_pairs={{0,6},{1,7},{2,0},{3,1},{4,2},{5,3},{6,4},{7,5},{8,14},{9,15},{10,... | collective-permute-start | bytes 786440 | tf_op jit(solution)/shard_map/ppermute | solution.py:335
  82.1 1.6 %copy-start.6 = (bf16[256,4096]{1,0:T(8,128)(2,1)S(1)}, bf16[256,4096]{1,0:T(8,128)(2,1)}, u32[]{:S(2)}) copy-start(bf16[256,4096]{1,0:T(8,128)(2,1)} %get-tuple-element.20.gq_ref) | copy-start | bytes 6291460
  91.5 18.6 %collective-permute-start.10 = (bf16[512,256]{1,0:T(8,128)(2,1)}, bf16[512,256]{1,0:T(8,128)(2,1)S(1)}, u32[]{:S(2)}, u32[]{:S(2)}) collective-permute-start(bf16[512,256]{1,0:T(8,128)(2,1)} %get-tuple-element.24), channel_id=1, source_target_pairs={{0,6},{1,7},{2,0},{3,1},{4,2},{5,3},{6,4},{7,5},{8,14},{9,15},{10,... | collective-permute-start | bytes 786440 | tf_op jit(solution)/shard_map/ppermute | solution.py:335
  91.8 21.3 %collective-permute-start.8 = (bf16[512,256]{1,0:T(8,128)(2,1)}, bf16[512,256]{1,0:T(8,128)(2,1)S(1)}, u32[]{:S(2)}, u32[]{:S(2)}) collective-permute-start(bf16[512,256]{1,0:T(8,128)(2,1)} %get-tuple-element.22), channel_id=1, source_target_pairs={{0,2},{1,3},{2,4},{3,5},{4,6},{5,7},{6,0},{7,1},{8,10},{9,11},{10,... | collective-permute-start | bytes 786440 | tf_op jit(solution)/shard_map/ppermute | solution.py:335
  95.0 13.1 %copy-start.8 = (f32[4,256]{1,0:T(4,128)S(1)}, f32[4,256]{1,0:T(4,128)}, u32[]{:S(2)}) copy-start(f32[4,256]{1,0:T(4,128)} %param.12) | copy-start | bytes 12292
  95.1 17.9 %collective-permute-start.9 = (bf16[512,256]{1,0:T(8,128)(2,1)}, bf16[512,256]{1,0:T(8,128)(2,1)S(1)}, u32[]{:S(2)}, u32[]{:S(2)}) collective-permute-start(bf16[512,256]{1,0:T(8,128)(2,1)} %get-tuple-element.23), channel_id=1, source_target_pairs={{0,4},{1,5},{2,6},{3,7},{4,0},{5,1},{6,2},{7,3},{8,12},{9,13},{10,... | collective-permute-start | bytes 786440 | tf_op jit(solution)/shard_map/ppermute | solution.py:335
  95.8 0.7 copy-start.1
  96.5 0.9 copy-start.2
  97.4 0.9 copy-start.5
  98.5 14.6 %collective-permute-start.14 = (bf16[512,256]{1,0:T(8,128)(2,1)S(1)}, bf16[512,256]{1,0:T(8,128)(2,1)S(1)}, u32[]{:S(2)}, u32[]{:S(2)}) collective-permute-start(bf16[512,256]{1,0:T(8,128)(2,1)S(1)} %add_up.5.refs_5_), channel_id=1, source_target_pairs={{0,8},{8,16},{16,24},{24,32},{32,40},{40,48},{48,56},{56,64},{64,7... | collective-permute-start | bytes 786440 | tf_op jit(solution)/shard_map/ppermute | solution.py:327
  100.9 8.6 %collective-permute-start.15 = (f32[32,256]{1,0:T(8,128)S(1)}, f32[32,256]{1,0:T(8,128)S(1)}, u32[]{:S(2)}, u32[]{:S(2)}) collective-permute-start(f32[32,256]{1,0:T(8,128)S(1)} %add_up.4.refs_4_), channel_id=1, source_target_pairs={{0,1},{1,0},{2,3},{3,2},{4,5},{5,4},{6,7},{7,6},{8,9},{9,8},{10,11... | collective-permute-start | bytes 98312 | tf_op jit(solution)/shard_map/ppermute | solution.py:331
  109.5 4.6 %collective-permute-start.16 = (f32[32,256]{1,0:T(8,128)S(1)}, f32[32,256]{1,0:T(8,128)S(1)}, u32[]{:S(2)}, u32[]{:S(2)}) collective-permute-start(f32[32,256]{1,0:T(8,128)S(1)} %add.57.refs_0_), channel_id=1, source_target_pairs={{0,2},{1,3},{2,4},{3,5},{4,6},{5,7},{6,0},{7,1},{8,10},{9,11},{10,... | collective-permute-start | bytes 98312 | tf_op jit(solution)/shard_map/ppermute | solution.py:335
  110.1 5.0 %collective-permute-start.17 = (f32[32,256]{1,0:T(8,128)S(1)}, f32[32,256]{1,0:T(8,128)S(1)}, u32[]{:S(2)}, u32[]{:S(2)}) collective-permute-start(f32[32,256]{1,0:T(8,128)S(1)} %add.57.refs_0_), channel_id=1, source_target_pairs={{0,4},{1,5},{2,6},{3,7},{4,0},{5,1},{6,2},{7,3},{8,12},{9,13},{10,... | collective-permute-start | bytes 98312 | tf_op jit(solution)/shard_map/ppermute | solution.py:335
  113.0 3.1 %collective-permute-start.18 = (f32[32,256]{1,0:T(8,128)S(1)}, f32[32,256]{1,0:T(8,128)S(1)}, u32[]{:S(2)}, u32[]{:S(2)}) collective-permute-start(f32[32,256]{1,0:T(8,128)S(1)} %add.57.refs_0_), channel_id=1, source_target_pairs={{0,6},{1,7},{2,0},{3,1},{4,2},{5,3},{6,4},{7,5},{8,14},{9,15},{10,... | collective-permute-start | bytes 98312 | tf_op jit(solution)/shard_map/ppermute | solution.py:335
  117.3 23.2 %copy-start.9 = (f32[256]{0:T(256)S(1)}, f32[256]{0:T(256)}, u32[]{:S(2)}) copy-start(f32[256]{0:T(256)} %param.10) | copy-start | bytes 3076
  117.3 23.8 %copy-start.7 = (f32[256,256]{1,0:T(8,128)S(1)}, f32[256,256]{1,0:T(8,128)}, u32[]{:S(2)}) copy-start(f32[256,256]{1,0:T(8,128)} %param.9) | copy-start | bytes 786436
  117.3 21.1 %all-to-all-start.1 = ((f16[16,40,256]{2,1,0:T(8,128)(2,1)}), f16[16,40,256]{2,1,0:T(8,128)(2,1)S(1)}, u32[]{:S(2)}, u32[]{:S(2)}) async-start(f16[16,40,256]{2,1,0:T(8,128)(2,1)} %broadcast_in_dim.2), calls=%async_computation.1 | async-start | bytes 655360 | tf_op jit(solution)/shard_map/all_to_all | solution.py:425
  125.9 10.7 %collective-permute-start.19 = (bf16[256,256]{1,0:T(8,128)(2,1)S(1)}, bf16[256,256]{1,0:T(8,128)(2,1)S(1)}, u32[]{:S(2)}, u32[]{:S(2)}) collective-permute-start(bf16[256,256]{1,0:T(8,128)(2,1)S(1)} %get-tuple-element.31), channel_id=1, source_target_pairs={{0,1},{1,0},{2,3},{3,2},{4,5},{5,4},{6,7},{7,6},{8,9},{9,8},{10,11... | collective-permute-start | bytes 393224 | tf_op jit(solution)/shard_map/ppermute | solution.py:331
  138.3 3.6 %collective-permute-start.20 = (f16[16,40,256]{2,1,0:T(8,128)(2,1)S(1)}, f16[16,40,256]{2,1,0:T(8,128)(2,1)S(1)}, u32[]{:S(2)}, u32[]{:S(2)}) collective-permute-start(f16[16,40,256]{2,1,0:T(8,128)(2,1)S(1)} %all-to-all-done.1), channel_id=1, source_target_pairs={{0,8},{8,0},{16,24},{24,16},{32,40},{40,32},{48,56},{56,48},{64,72... | collective-permute-start | bytes 983048 | tf_op jit(solution)/shard_map/ppermute | solution.py:426

commit v12 on v11

--- a/solution.py
+++ b/solution.py
@@ -311,7 +311,7 @@
             scratch_shapes=[pltpu.VMEM((ROWS, D), f32)],
         ),
         out_shape=send_shapes(),
-        compiler_params=params(16),
+        compiler_params=params(48),
         cost_estimate=cost(8),
         name="source_grads",
     )(rel_id, gq, src_rows, relation)
@@ -343,10 +343,13 @@
     return [blocks[0]] + [shift_x(blocks[k], k) for k in (1, 2, 3)]
 
 
-def add_up(blocks, after, dtype, copies=None):
+def whole_of(shape):
+    return pl.BlockSpec(shape, lambda: (0,) * len(shape))
+
+
+def add_up(blocks, after, dtype):
     stacked = len(blocks) == 1
     shape = blocks[0].shape[1:] if stacked else blocks[0].shape
-    whole = pl.BlockSpec(memory_space=pltpu.VMEM)
 
     def kernel(*refs):
         out = refs[-1]
@@ -361,17 +364,13 @@
                 part = ref[...].astype(f32)
                 total = part if total is None else total + part
             total = total.astype(dtype)
-        if copies is None:
-            out[...] = total
-        else:
-            for i in range(copies):
-                out[i] = total
+        out[...] = total
 
     return pl.pallas_call(
         kernel,
-        in_specs=[whole] * len(blocks) + [pl.BlockSpec(memory_space=pl.ANY)],
-        out_specs=whole,
-        out_shape=jax.ShapeDtypeStruct(shape if copies is None else (copies,) + shape, dtype),
+        in_specs=[whole_of(block.shape) for block in blocks] + [pl.BlockSpec(memory_space=pl.ANY)],
+        out_specs=whole_of(shape),
+        out_shape=jax.ShapeDtypeStruct(shape, dtype),
         compiler_params=pltpu.CompilerParams(vmem_limit_bytes=16 * MB),
         cost_estimate=cost(1),
         name="add_up",
@@ -380,7 +379,6 @@
 
 def split_sum(blocks, after):
     half = blocks[0].shape[0] // 2
-    whole = pl.BlockSpec(memory_space=pltpu.VMEM)
 
     def kernel(*refs):
         for out, at in ((refs[-2], slice(0, half)), (refs[-1], slice(half, 2 * half))):
@@ -392,8 +390,8 @@
 
     return pl.pallas_call(
         kernel,
-        in_specs=[whole] * len(blocks) + [pl.BlockSpec(memory_space=pl.ANY)],
-        out_specs=[whole] * 2,
+        in_specs=[whole_of(block.shape) for block in blocks] + [pl.BlockSpec(memory_space=pl.ANY)],
+        out_specs=[whole_of((half, D))] * 2,
         out_shape=[jax.ShapeDtypeStruct((half, D), f32), jax.ShapeDtypeStruct((half, D), bf16)],
         compiler_params=pltpu.CompilerParams(vmem_limit_bytes=16 * MB),
         cost_estimate=cost(1),

time: 147 us -> 147 us (level)
  no operation moved by 1% of the time
where the time goes in v12:
time: 147 us; the launch traced here: 144 us
  starting transfers between devices  63 us (43%)
  Pallas kernels  48.6 us (33%)
  waiting for transfers between devices  18.6 us (13%)
  local copies, waits for them, and re-layouts  6.71 us (5%)
  other arithmetic  5.9 us (4%)
  between operations  1.55 us (1%)
    pallas_call x1, Pallas kernels, score_side(): pl.pallas_call(score_kernel, grid_spec=pltpu.PrefetchScalarGridSpec(num_s...  30.1 us
    ppermute x3, starting transfers between devices, swap_z(): return lax.ppermute(block, 'rep', [(i, i ^ 1) for i in range(8)])  18.5 us
    ppermute x12, starting transfers between devices, shift_x(): return lax.ppermute(block, 'rep', [(i, (i + 2 * by) % 8) for i in range(8)])  13.3 us
    ppermute x5, starting transfers between devices, shift_dom(): lax.ppermute(block, 'dom', [(i, (i + by) % size) for i in range(size)])  12.5 us
    ppermute x3, waiting for transfers between devices, swap_z(): return lax.ppermute(block, 'rep', [(i, i ^ 1) for i in range(8)])  10.4 us
    all_to_all x1, starting transfers between devices, operator_update(): half = lax.all_to_all(shares, 'dom', 0, 0, axis_index_groups=cores)  8.56 us
    all_to_all x1, starting transfers between devices, on_device(): got = lax.all_to_all(rel_grad.reshape(32, -1, D), 'dom', 0, 0)  7.84 us
    pallas_call x1, Pallas kernels, source_side(): pl.pallas_call(source_kernel, grid_spec=pltpu.PrefetchScalarGridSpec(num_...  7.76 us
  transfers between devices with their start and end apart: 23, of which 9 were waited for; matrix products, arithmetic and copies ran while one was open for 2% of the time, Pallas kernels for 13%

profile of v12, /device:TPU:1, one launch (start us, length us, event | category | flops | bytes accessed | tf_op | source)
XLA Modules:
  0.0 144.3 jit_solution(16994584750874007333)
XLA Ops:
  0.6 1.0 convert_element_type.15
  1.6 7.8 %collective-permute-start = (bf16[256,256]{1,0:T(8,128)(2,1)S(1)}, bf16[256,256]{1,0:T(8,128)(2,1)S(1)}, u32[]{:S(2)}, u32[]{:S(2)}) collective-permute-start(bf16[256,256]{1,0:T(8,128)(2,1)S(1)} %convert_element_type.15), channel_id=1, source_target_pairs={{0,1},{1,0},{2,3},{3,2},{4,5},{5,4},{6,7},{7,6},{8,9},{9,8},{10,11... | collective-permute-start | bytes 393224 | tf_op jit(solution)/shard_map/ppermute | solution.py:331
  9.4 0.8 fusion.1
  10.3 1.8 %collective-permute-done = bf16[256,256]{1,0:T(8,128)(2,1)S(1)} collective-permute-done((bf16[256,256]{1,0:T(8,128)(2,1)S(1)}, bf16[256,256]{1,0:T(8,128)(2,1)S(1)}, u32[]{:S(2)}, u32[]{:S(2)}) %collective-permute-start) | collective-permute-done | bytes 131104 | tf_op jit(solution)/shard_map/ppermute | solution.py:331
  12.1 3.1 %collective-permute-start.2 = (bf16[512,256]{1,0:T(8,128)(2,1)S(1)}, bf16[512,256]{1,0:T(8,128)(2,1)S(1)}, u32[]{:S(2)}, u32[]{:S(2)}) collective-permute-start(bf16[512,256]{1,0:T(8,128)(2,1)S(1)} %pad_maximum_fusion.refs_0_), channel_id=1, source_target_pairs={{0,6},{1,7},{2,0},{3,1},{4,2},{5,3},{6,4},{7,5},{8,14},{9,15},{10,... | collective-permute-start | bytes 786440 | tf_op jit(solution)/shard_map/ppermute | solution.py:335
  15.2 0.5 collective-permute-start.4
  15.7 0.6 collective-permute-start.6
  16.4 0.7 fusion.5
  17.9 3.2 %neg_weights.1.refs_7_ = f32[4,8,2048]{2,1,0:T(8,128)S(1)} custom-call(s32[4,1,1024]{2,1,0:T(1,128)S(1)} %reshape.47.neg_ref), custom_call_target="tpu_custom_call" | custom-call | flops 1500000000 | bytes 10500000 | tf_op jit(solution)/shard_map/neg_weights/pallas_call | solution.py:78
  21.1 2.2 %collective-permute-start.1 = (bf16[512,256]{1,0:T(8,128)(2,1)S(1)}, bf16[512,256]{1,0:T(8,128)(2,1)S(1)}, u32[]{:S(2)}, u32[]{:S(2)}) collective-permute-start(bf16[512,256]{1,0:T(8,128)(2,1)S(1)} %pad_maximum_fusion.refs_0_), channel_id=1, source_target_pairs={{0,248},{8,0},{16,8},{24,16},{32,24},{40,32},{48,40},{56,48},{64,5... | collective-permute-start | bytes 786440 | tf_op jit(solution)/shard_map/ppermute | solution.py:327
  23.4 4.0 %collective-permute-start.3 = (bf16[512,256]{1,0:T(8,128)(2,1)S(1)}, bf16[512,256]{1,0:T(8,128)(2,1)S(1)}, u32[]{:S(2)}, u32[]{:S(2)}) collective-permute-start(bf16[512,256]{1,0:T(8,128)(2,1)S(1)} %collective-permute-done.2.refs_1_), channel_id=1, source_target_pairs={{0,248},{8,0},{16,8},{24,16},{32,24},{40,32},{48,40},{56,48},{64,5... | collective-permute-start | bytes 786440 | tf_op jit(solution)/shard_map/ppermute | solution.py:327
  27.4 1.7 %collective-permute-start.5 = (bf16[512,256]{1,0:T(8,128)(2,1)S(1)}, bf16[512,256]{1,0:T(8,128)(2,1)S(1)}, u32[]{:S(2)}, u32[]{:S(2)}) collective-permute-start(bf16[512,256]{1,0:T(8,128)(2,1)S(1)} %collective-permute-done.4.refs_2_), channel_id=1, source_target_pairs={{0,248},{8,0},{16,8},{24,16},{32,24},{40,32},{48,40},{56,48},{64,5... | collective-permute-start | bytes 786440 | tf_op jit(solution)/shard_map/ppermute | solution.py:327
  29.0 1.5 %collective-permute-done.6.refs_3_ = bf16[512,256]{1,0:T(8,128)(2,1)S(1)} collective-permute-done((bf16[512,256]{1,0:T(8,128)(2,1)S(1)}, bf16[512,256]{1,0:T(8,128)(2,1)S(1)}, u32[]{:S(2)}, u32[]{:S(2)}) %collective-permute-start.6) | collective-permute-done | bytes 262176 | tf_op jit(solution)/shard_map/ppermute | solution.py:335
  30.6 2.2 %collective-permute-start.7 = (bf16[512,256]{1,0:T(8,128)(2,1)S(1)}, bf16[512,256]{1,0:T(8,128)(2,1)S(1)}, u32[]{:S(2)}, u32[]{:S(2)}) collective-permute-start(bf16[512,256]{1,0:T(8,128)(2,1)S(1)} %collective-permute-done.6.refs_3_), channel_id=1, source_target_pairs={{0,248},{8,0},{16,8},{24,16},{32,24},{40,32},{48,40},{56,48},{64,5... | collective-permute-start | bytes 786440 | tf_op jit(solution)/shard_map/ppermute | solution.py:327
  32.8 7.2 %queries.1 = (bf16[4096,256]{1,0:T(8,128)(2,1)S(1)}, bf16[256,4096]{1,0:T(8,128)(2,1)S(1)}) custom-call(s32[4]{0:T(128)S(1)} %copy-done.3, bf16[512,256]{1,0:T(8,128)(2,1)S(1)} %pad_maximum_fusion.refs_0_, bf16[512,256]{1,0:T(8,128)(2,1)S(1)} %collective-permute-done.2.refs_1_, bf16[512,256]{1,0:T(8,128)(2,1)S(1)} %collective-permute-done.4.refs_2_, ...), custom_call_target="tpu_custom_call" | custom-call | flops 4499999744 | bytes 31500000 | tf_op jit(solution)/shard_map/queries/pallas_call | solution.py:113
  40.1 30.1 %scores.1 = (bf16[256,4096]{1,0:T(8,128)(2,1)}, bf16[512,256]{1,0:T(8,128)(2,1)S(1)}, bf16[512,256]{1,0:T(8,128)(2,1)}, bf16[512,256]{1,0:T(8,128)(2,1)}, bf16[5...) custom-call(s32[4]{0:T(128)S(1)} %copy-done.3, s32[1]{0:T(128)S(6)} %copy.18.cnt_ref, ...), custom_call_target="tpu_custom_call" | custom-call | flops 14000000000 | bytes 98000000 | tf_op jit(solution)/shard_map/scores/pallas_call | solution.py:239
  70.1 0.7 copy-done.4
  70.8 7.8 %all-to-all-start = ((bf16[32,32,256]{2,1,0:T(8,128)(2,1)}), bf16[32,32,256]{2,1,0:T(8,128)(2,1)S(1)}, u32[]{:S(2)}, u32[]{:S(2)}) async-start(bf16[32,32,256]{2,1,0:T(8,128)(2,1)} %bitcast), calls=%async_computation | async-start | bytes 1048576 | tf_op jit(solution)/shard_map/all_to_all | solution.py:480
  78.7 3.4 %collective-permute-start.12 = (bf16[512,256]{1,0:T(8,128)(2,1)}, bf16[512,256]{1,0:T(8,128)(2,1)S(1)}, u32[]{:S(2)}, u32[]{:S(2)}) collective-permute-start(bf16[512,256]{1,0:T(8,128)(2,1)} %get-tuple-element.27), channel_id=1, source_target_pairs={{0,4},{1,5},{2,6},{3,7},{4,0},{5,1},{6,2},{7,3},{8,12},{9,13},{10,... | collective-permute-start | bytes 786440 | tf_op jit(solution)/shard_map/ppermute | solution.py:335
  82.1 1.6 %copy-done.6 = bf16[256,4096]{1,0:T(8,128)(2,1)S(1)} copy-done((bf16[256,4096]{1,0:T(8,128)(2,1)S(1)}, bf16[256,4096]{1,0:T(8,128)(2,1)}, u32[]{:S(2)}) %copy-start.6) | copy-done | bytes 2097176
  83.7 7.8 %source_grads.1 = (bf16[512,256]{1,0:T(8,128)(2,1)S(1)}, bf16[512,256]{1,0:T(8,128)(2,1)}, bf16[512,256]{1,0:T(8,128)(2,1)}, bf16[512,256]{1,0:T(8,128)(2,1)}) custom-call(s32[4]{0:T(128)S(1)} %copy-done.3, bf16[256,4096]{1,0:T(8,128)(2,1)S(1)} %copy-done.6, s32[4,1,1024]{2,1,0:T(1,128)S(1)} %reshape.44.refs_4_.src_ref, f32[4,256,256]{2,1,0:T(8,128)S(1)} %copy-done), custom_call_target="tpu_custom_call" | custom-call | flops 4000000000 | bytes 28000000 | tf_op jit(solution)/shard_map/source_grads/pallas_call | solution.py:300
  91.5 0.3 collective-permute-start.10
  91.8 1.2 collective-permute-start.8
  93.0 2.1 %all-to-all-done.refs_0_ = bf16[32,32,256]{2,1,0:T(8,128)(2,1)S(1)} async-done(((bf16[32,32,256]{2,1,0:T(8,128)(2,1)}), bf16[32,32,256]{2,1,0:T(8,128)(2,1)S(1)}, u32[]{:S(2)}, u32[]{:S(2)}) %all-to-all-start) | async-done | bytes 524320 | tf_op jit(solution)/shard_map/all_to_all | solution.py:480
  95.1 0.6 collective-permute-start.9
  95.8 0.7 copy-done.1
  96.5 0.9 copy-done.2
  97.4 0.9 copy-done.5
  98.5 2.4 %collective-permute-start.14 = (bf16[512,256]{1,0:T(8,128)(2,1)S(1)}, bf16[512,256]{1,0:T(8,128)(2,1)S(1)}, u32[]{:S(2)}, u32[]{:S(2)}) collective-permute-start(bf16[512,256]{1,0:T(8,128)(2,1)S(1)} %add_up.5.refs_5_), channel_id=1, source_target_pairs={{0,8},{8,16},{16,24},{24,32},{32,40},{40,48},{48,56},{56,64},{64,7... | collective-permute-start | bytes 786440 | tf_op jit(solution)/shard_map/ppermute | solution.py:327
  100.9 7.3 %collective-permute-start.15 = (f32[32,256]{1,0:T(8,128)S(1)}, f32[32,256]{1,0:T(8,128)S(1)}, u32[]{:S(2)}, u32[]{:S(2)}) collective-permute-start(f32[32,256]{1,0:T(8,128)S(1)} %add_up.4.refs_4_), channel_id=1, source_target_pairs={{0,1},{1,0},{2,3},{3,2},{4,5},{5,4},{6,7},{7,6},{8,9},{9,8},{10,11... | collective-permute-start | bytes 98312 | tf_op jit(solution)/shard_map/ppermute | solution.py:331
  108.2 1.3 collective-permute-done.15
  109.5 0.5 collective-permute-start.16
  110.1 3.0 %collective-permute-start.17 = (f32[32,256]{1,0:T(8,128)S(1)}, f32[32,256]{1,0:T(8,128)S(1)}, u32[]{:S(2)}, u32[]{:S(2)}) collective-permute-start(f32[32,256]{1,0:T(8,128)S(1)} %add.57.refs_0_), channel_id=1, source_target_pairs={{0,4},{1,5},{2,6},{3,7},{4,0},{5,1},{6,2},{7,3},{8,12},{9,13},{10,... | collective-permute-start | bytes 98312 | tf_op jit(solution)/shard_map/ppermute | solution.py:335
  113.1 0.2 add_up.6.refs_4_.refs_0_
  113.2 0.9 collective-permute-done.16.refs_1_
  114.1 0.9 collective-permute-done.17.refs_2_
  115.0 1.1 collective-permute-done.18.refs_3_
  116.5 0.8 broadcast_in_dim.2
  117.3 8.6 %all-to-all-start.1 = ((f16[16,40,256]{2,1,0:T(8,128)(2,1)}), f16[16,40,256]{2,1,0:T(8,128)(2,1)S(1)}, u32[]{:S(2)}, u32[]{:S(2)}) async-start(f16[16,40,256]{2,1,0:T(8,128)(2,1)} %broadcast_in_dim.2), calls=%async_computation.1 | async-start | bytes 655360 | tf_op jit(solution)/shard_map/all_to_all | solution.py:423
  125.9 3.4 %collective-permute-start.19 = (bf16[256,256]{1,0:T(8,128)(2,1)S(1)}, bf16[256,256]{1,0:T(8,128)(2,1)S(1)}, u32[]{:S(2)}, u32[]{:S(2)}) collective-permute-start(bf16[256,256]{1,0:T(8,128)(2,1)S(1)} %get-tuple-element.31), channel_id=1, source_target_pairs={{0,1},{1,0},{2,3},{3,2},{4,5},{5,4},{6,7},{7,6},{8,9},{9,8},{10,11... | collective-permute-start | bytes 393224 | tf_op jit(solution)/shard_map/ppermute | solution.py:331
  129.3 7.2 %collective-permute-done.19 = bf16[256,256]{1,0:T(8,128)(2,1)S(1)} collective-permute-done((bf16[256,256]{1,0:T(8,128)(2,1)S(1)}, bf16[256,256]{1,0:T(8,128)(2,1)S(1)}, u32[]{:S(2)}, u32[]{:S(2)}) %collective-permute-start.19) | collective-permute-done | bytes 131104 | tf_op jit(solution)/shard_map/ppermute | solution.py:331
  136.7 1.7 %all-to-all-done.1 = f16[16,40,256]{2,1,0:T(8,128)(2,1)S(1)} async-done(((f16[16,40,256]{2,1,0:T(8,128)(2,1)}), f16[16,40,256]{2,1,0:T(8,128)(2,1)S(1)}, u32[]{:S(2)}, u32[]{:S(2)}) %all-to-all-start.1) | async-done | bytes 327712 | tf_op jit(solution)/shard_map/all_to_all | solution.py:423
  138.3 2.2 %collective-permute-start.20 = (f16[16,40,256]{2,1,0:T(8,128)(2,1)S(1)}, f16[16,40,256]{2,1,0:T(8,128)(2,1)S(1)}, u32[]{:S(2)}, u32[]{:S(2)}) collective-permute-start(f16[16,40,256]{2,1,0:T(8,128)(2,1)S(1)} %all-to-all-done.1), channel_id=1, source_target_pairs={{0,8},{8,0},{16,24},{24,16},{32,40},{40,32},{48,56},{56,48},{64,72... | collective-permute-start | bytes 983048 | tf_op jit(solution)/shard_map/ppermute | solution.py:424
  140.5 0.6 fusion.22
  141.1 0.8 divide_subtract_fusion
  142.2 0.2 copy.16
  142.6 1.1 bitcast_subtract_fusion
  143.7 0.7 mul.55
  (59 shorter events, 1.6 us)
Async XLA Ops:
  1.6 10.5 %collective-permute-start = (bf16[256,256]{1,0:T(8,128)(2,1)S(1)}, bf16[256,256]{1,0:T(8,128)(2,1)S(1)}, u32[]{:S(2)}, u32[]{:S(2)}) collective-permute-start(bf16[256,256]{1,0:T(8,128)(2,1)S(1)} %convert_element_type.15), channel_id=1, source_target_pairs={{0,1},{1,0},{2,3},{3,2},{4,5},{5,4},{6,7},{7,6},{8,9},{9,8},{10,11... | collective-permute-start | bytes 393224 | tf_op jit(solution)/shard_map/ppermute | solution.py:331
  12.1 11.3 %collective-permute-start.2 = (bf16[512,256]{1,0:T(8,128)(2,1)S(1)}, bf16[512,256]{1,0:T(8,128)(2,1)S(1)}, u32[]{:S(2)}, u32[]{:S(2)}) collective-permute-start(bf16[512,256]{1,0:T(8,128)(2,1)S(1)} %pad_maximum_fusion.refs_0_), channel_id=1, source_target_pairs={{0,6},{1,7},{2,0},{3,1},{4,2},{5,3},{6,4},{7,5},{8,14},{9,15},{10,... | collective-permute-start | bytes 786440 | tf_op jit(solution)/shard_map/ppermute | solution.py:335
  15.2 12.1 %collective-permute-start.4 = (bf16[512,256]{1,0:T(8,128)(2,1)S(1)}, bf16[512,256]{1,0:T(8,128)(2,1)S(1)}, u32[]{:S(2)}, u32[]{:S(2)}) collective-permute-start(bf16[512,256]{1,0:T(8,128)(2,1)S(1)} %pad_maximum_fusion.refs_0_), channel_id=1, source_target_pairs={{0,4},{1,5},{2,6},{3,7},{4,0},{5,1},{6,2},{7,3},{8,12},{9,13},{10,... | collective-permute-start | bytes 786440 | tf_op jit(solution)/shard_map/ppermute | solution.py:335
  15.7 14.8 %collective-permute-start.6 = (bf16[512,256]{1,0:T(8,128)(2,1)S(1)}, bf16[512,256]{1,0:T(8,128)(2,1)S(1)}, u32[]{:S(2)}, u32[]{:S(2)}) collective-permute-start(bf16[512,256]{1,0:T(8,128)(2,1)S(1)} %pad_maximum_fusion.refs_0_), channel_id=1, source_target_pairs={{0,2},{1,3},{2,4},{3,5},{4,6},{5,7},{6,0},{7,1},{8,10},{9,11},{10,... | collective-permute-start | bytes 786440 | tf_op jit(solution)/shard_map/ppermute | solution.py:335
  17.9 14.9 %copy-start = (f32[4,256,256]{2,1,0:T(8,128)S(1)}, f32[4,256,256]{2,1,0:T(8,128)}, u32[]{:S(2)}) copy-start(f32[4,256,256]{2,1,0:T(8,128)} %mat_ref.1) | copy-start | bytes 3145732
  17.9 14.9 %copy-start.3 = (s32[4]{0:T(128)S(1)}, s32[4]{0:T(128)}, u32[]{:S(2)}) copy-start(s32[4]{0:T(128)} %rel_ref.5) | copy-start | bytes 52
  21.1 18.9 %collective-permute-start.1 = (bf16[512,256]{1,0:T(8,128)(2,1)S(1)}, bf16[512,256]{1,0:T(8,128)(2,1)S(1)}, u32[]{:S(2)}, u32[]{:S(2)}) collective-permute-start(bf16[512,256]{1,0:T(8,128)(2,1)S(1)} %pad_maximum_fusion.refs_0_), channel_id=1, source_target_pairs={{0,248},{8,0},{16,8},{24,16},{32,24},{40,32},{48,40},{56,48},{64,5... | collective-permute-start | bytes 786440 | tf_op jit(solution)/shard_map/ppermute | solution.py:327
  23.4 16.6 %collective-permute-start.3 = (bf16[512,256]{1,0:T(8,128)(2,1)S(1)}, bf16[512,256]{1,0:T(8,128)(2,1)S(1)}, u32[]{:S(2)}, u32[]{:S(2)}) collective-permute-start(bf16[512,256]{1,0:T(8,128)(2,1)S(1)} %collective-permute-done.2.refs_1_), channel_id=1, source_target_pairs={{0,248},{8,0},{16,8},{24,16},{32,24},{40,32},{48,40},{56,48},{64,5... | collective-permute-start | bytes 786440 | tf_op jit(solution)/shard_map/ppermute | solution.py:327
  27.4 12.7 %collective-permute-start.5 = (bf16[512,256]{1,0:T(8,128)(2,1)S(1)}, bf16[512,256]{1,0:T(8,128)(2,1)S(1)}, u32[]{:S(2)}, u32[]{:S(2)}) collective-permute-start(bf16[512,256]{1,0:T(8,128)(2,1)S(1)} %collective-permute-done.4.refs_2_), channel_id=1, source_target_pairs={{0,248},{8,0},{16,8},{24,16},{32,24},{40,32},{48,40},{56,48},{64,5... | collective-permute-start | bytes 786440 | tf_op jit(solution)/shard_map/ppermute | solution.py:327
  30.6 9.5 %collective-permute-start.7 = (bf16[512,256]{1,0:T(8,128)(2,1)S(1)}, bf16[512,256]{1,0:T(8,128)(2,1)S(1)}, u32[]{:S(2)}, u32[]{:S(2)}) collective-permute-start(bf16[512,256]{1,0:T(8,128)(2,1)S(1)} %collective-permute-done.6.refs_3_), channel_id=1, source_target_pairs={{0,248},{8,0},{16,8},{24,16},{32,24},{40,32},{48,40},{56,48},{64,5... | collective-permute-start | bytes 786440 | tf_op jit(solution)/shard_map/ppermute | solution.py:327
  70.1 0.7 copy-start.4
  70.8 24.2 %all-to-all-start = ((bf16[32,32,256]{2,1,0:T(8,128)(2,1)}), bf16[32,32,256]{2,1,0:T(8,128)(2,1)S(1)}, u32[]{:S(2)}, u32[]{:S(2)}) async-start(bf16[32,32,256]{2,1,0:T(8,128)(2,1)} %bitcast), calls=%async_computation | async-start | bytes 1048576 | tf_op jit(solution)/shard_map/all_to_all | solution.py:480
  78.6 16.5 %collective-permute-start.11 = (bf16[512,256]{1,0:T(8,128)(2,1)}, bf16[512,256]{1,0:T(8,128)(2,1)S(1)}, u32[]{:S(2)}, u32[]{:S(2)}) collective-permute-start(bf16[512,256]{1,0:T(8,128)(2,1)} %get-tuple-element.26), channel_id=1, source_target_pairs={{0,2},{1,3},{2,4},{3,5},{4,6},{5,7},{6,0},{7,1},{8,10},{9,11},{10,... | collective-permute-start | bytes 786440 | tf_op jit(solution)/shard_map/ppermute | solution.py:335
  78.7 17.0 %collective-permute-start.12 = (bf16[512,256]{1,0:T(8,128)(2,1)}, bf16[512,256]{1,0:T(8,128)(2,1)S(1)}, u32[]{:S(2)}, u32[]{:S(2)}) collective-permute-start(bf16[512,256]{1,0:T(8,128)(2,1)} %get-tuple-element.27), channel_id=1, source_target_pairs={{0,4},{1,5},{2,6},{3,7},{4,0},{5,1},{6,2},{7,3},{8,12},{9,13},{10,... | collective-permute-start | bytes 786440 | tf_op jit(solution)/shard_map/ppermute | solution.py:335
  82.1 13.6 %collective-permute-start.13 = (bf16[512,256]{1,0:T(8,128)(2,1)}, bf16[512,256]{1,0:T(8,128)(2,1)S(1)}, u32[]{:S(2)}, u32[]{:S(2)}) collective-permute-start(bf16[512,256]{1,0:T(8,128)(2,1)} %get-tuple-element.28), channel_id=1, source_target_pairs={{0,6},{1,7},{2,0},{3,1},{4,2},{5,3},{6,4},{7,5},{8,14},{9,15},{10,... | collective-permute-start | bytes 786440 | tf_op jit(solution)/shard_map/ppermute | solution.py:335
  82.1 1.6 %copy-start.6 = (bf16[256,4096]{1,0:T(8,128)(2,1)S(1)}, bf16[256,4096]{1,0:T(8,128)(2,1)}, u32[]{:S(2)}) copy-start(bf16[256,4096]{1,0:T(8,128)(2,1)} %get-tuple-element.20.gq_ref) | copy-start | bytes 6291460
  91.5 18.6 %collective-permute-start.10 = (bf16[512,256]{1,0:T(8,128)(2,1)}, bf16[512,256]{1,0:T(8,128)(2,1)S(1)}, u32[]{:S(2)}, u32[]{:S(2)}) collective-permute-start(bf16[512,256]{1,0:T(8,128)(2,1)} %get-tuple-element.24), channel_id=1, source_target_pairs={{0,6},{1,7},{2,0},{3,1},{4,2},{5,3},{6,4},{7,5},{8,14},{9,15},{10,... | collective-permute-start | bytes 786440 | tf_op jit(solution)/shard_map/ppermute | solution.py:335
  91.8 21.3 %collective-permute-start.8 = (bf16[512,256]{1,0:T(8,128)(2,1)}, bf16[512,256]{1,0:T(8,128)(2,1)S(1)}, u32[]{:S(2)}, u32[]{:S(2)}) collective-permute-start(bf16[512,256]{1,0:T(8,128)(2,1)} %get-tuple-element.22), channel_id=1, source_target_pairs={{0,2},{1,3},{2,4},{3,5},{4,6},{5,7},{6,0},{7,1},{8,10},{9,11},{10,... | collective-permute-start | bytes 786440 | tf_op jit(solution)/shard_map/ppermute | solution.py:335
  95.0 13.1 %copy-start.8 = (f32[4,256]{1,0:T(4,128)S(1)}, f32[4,256]{1,0:T(4,128)}, u32[]{:S(2)}) copy-start(f32[4,256]{1,0:T(4,128)} %param.12) | copy-start | bytes 12292
  95.1 17.9 %collective-permute-start.9 = (bf16[512,256]{1,0:T(8,128)(2,1)}, bf16[512,256]{1,0:T(8,128)(2,1)S(1)}, u32[]{:S(2)}, u32[]{:S(2)}) collective-permute-start(bf16[512,256]{1,0:T(8,128)(2,1)} %get-tuple-element.23), channel_id=1, source_target_pairs={{0,4},{1,5},{2,6},{3,7},{4,0},{5,1},{6,2},{7,3},{8,12},{9,13},{10,... | collective-permute-start | bytes 786440 | tf_op jit(solution)/shard_map/ppermute | solution.py:335
  95.8 0.7 copy-start.1
  96.5 0.9 copy-start.2
  97.4 0.9 copy-start.5
  98.5 14.6 %collective-permute-start.14 = (bf16[512,256]{1,0:T(8,128)(2,1)S(1)}, bf16[512,256]{1,0:T(8,128)(2,1)S(1)}, u32[]{:S(2)}, u32[]{:S(2)}) collective-permute-start(bf16[512,256]{1,0:T(8,128)(2,1)S(1)} %add_up.5.refs_5_), channel_id=1, source_target_pairs={{0,8},{8,16},{16,24},{24,32},{32,40},{40,48},{48,56},{56,64},{64,7... | collective-permute-start | bytes 786440 | tf_op jit(solution)/shard_map/ppermute | solution.py:327
  100.9 8.6 %collective-permute-start.15 = (f32[32,256]{1,0:T(8,128)S(1)}, f32[32,256]{1,0:T(8,128)S(1)}, u32[]{:S(2)}, u32[]{:S(2)}) collective-permute-start(f32[32,256]{1,0:T(8,128)S(1)} %add_up.4.refs_4_), channel_id=1, source_target_pairs={{0,1},{1,0},{2,3},{3,2},{4,5},{5,4},{6,7},{7,6},{8,9},{9,8},{10,11... | collective-permute-start | bytes 98312 | tf_op jit(solution)/shard_map/ppermute | solution.py:331
  109.5 4.6 %collective-permute-start.16 = (f32[32,256]{1,0:T(8,128)S(1)}, f32[32,256]{1,0:T(8,128)S(1)}, u32[]{:S(2)}, u32[]{:S(2)}) collective-permute-start(f32[32,256]{1,0:T(8,128)S(1)} %add.57.refs_0_), channel_id=1, source_target_pairs={{0,2},{1,3},{2,4},{3,5},{4,6},{5,7},{6,0},{7,1},{8,10},{9,11},{10,... | collective-permute-start | bytes 98312 | tf_op jit(solution)/shard_map/ppermute | solution.py:335
  110.1 5.0 %collective-permute-start.17 = (f32[32,256]{1,0:T(8,128)S(1)}, f32[32,256]{1,0:T(8,128)S(1)}, u32[]{:S(2)}, u32[]{:S(2)}) collective-permute-start(f32[32,256]{1,0:T(8,128)S(1)} %add.57.refs_0_), channel_id=1, source_target_pairs={{0,4},{1,5},{2,6},{3,7},{4,0},{5,1},{6,2},{7,3},{8,12},{9,13},{10,... | collective-permute-start | bytes 98312 | tf_op jit(solution)/shard_map/ppermute | solution.py:335
  113.0 3.1 %collective-permute-start.18 = (f32[32,256]{1,0:T(8,128)S(1)}, f32[32,256]{1,0:T(8,128)S(1)}, u32[]{:S(2)}, u32[]{:S(2)}) collective-permute-start(f32[32,256]{1,0:T(8,128)S(1)} %add.57.refs_0_), channel_id=1, source_target_pairs={{0,6},{1,7},{2,0},{3,1},{4,2},{5,3},{6,4},{7,5},{8,14},{9,15},{10,... | collective-permute-start | bytes 98312 | tf_op jit(solution)/shard_map/ppermute | solution.py:335
  117.3 23.2 %copy-start.9 = (f32[256]{0:T(256)S(1)}, f32[256]{0:T(256)}, u32[]{:S(2)}) copy-start(f32[256]{0:T(256)} %param.10) | copy-start | bytes 3076
  117.3 23.8 %copy-start.7 = (f32[256,256]{1,0:T(8,128)S(1)}, f32[256,256]{1,0:T(8,128)}, u32[]{:S(2)}) copy-start(f32[256,256]{1,0:T(8,128)} %param.9) | copy-start | bytes 786436
  117.3 21.1 %all-to-all-start.1 = ((f16[16,40,256]{2,1,0:T(8,128)(2,1)}), f16[16,40,256]{2,1,0:T(8,128)(2,1)S(1)}, u32[]{:S(2)}, u32[]{:S(2)}) async-start(f16[16,40,256]{2,1,0:T(8,128)(2,1)} %broadcast_in_dim.2), calls=%async_computation.1 | async-start | bytes 655360 | tf_op jit(solution)/shard_map/all_to_all | solution.py:423
  125.9 10.7 %collective-permute-start.19 = (bf16[256,256]{1,0:T(8,128)(2,1)S(1)}, bf16[256,256]{1,0:T(8,128)(2,1)S(1)}, u32[]{:S(2)}, u32[]{:S(2)}) collective-permute-start(bf16[256,256]{1,0:T(8,128)(2,1)S(1)} %get-tuple-element.31), channel_id=1, source_target_pairs={{0,1},{1,0},{2,3},{3,2},{4,5},{5,4},{6,7},{7,6},{8,9},{9,8},{10,11... | collective-permute-start | bytes 393224 | tf_op jit(solution)/shard_map/ppermute | solution.py:331
  138.3 3.6 %collective-permute-start.20 = (f16[16,40,256]{2,1,0:T(8,128)(2,1)S(1)}, f16[16,40,256]{2,1,0:T(8,128)(2,1)S(1)}, u32[]{:S(2)}, u32[]{:S(2)}) collective-permute-start(f16[16,40,256]{2,1,0:T(8,128)(2,1)S(1)} %all-to-all-done.1), channel_id=1, source_target_pairs={{0,8},{8,0},{16,24},{24,16},{32,40},{40,32},{48,56},{56,48},{64,72... | collective-permute-start | bytes 983048 | tf_op jit(solution)/shard_map/ppermute | solution.py:424

commit v13 on v11

--- a/solution.py
+++ b/solution.py
@@ -53,7 +53,7 @@
 
 
 def send_shapes():
-    return [jax.ShapeDtypeStruct((PART, D), bf16)] + [pltpu.HBM((PART, D), bf16)] * (PARTS - 1)
+    return [pltpu.HBM((PART, D), bf16)] * PARTS
 
 
 def block_of(parts, b):

time: 147 us -> 147 us (level)
    unnamed x21 -> x23, local copies, waits for them, and re-layouts: 4.91 us -> 5.17 us
where the time goes in v13:
time: 147 us; the launch traced here: 145 us
  starting transfers between devices  63.1 us (43%)
  Pallas kernels  48.8 us (33%)
  waiting for transfers between devices  18.4 us (13%)
  local copies, waits for them, and re-layouts  6.97 us (5%)
  other arithmetic  5.9 us (4%)
  between operations  1.57 us (1%)
    pallas_call x1, Pallas kernels, score_side(): pl.pallas_call(score_kernel, grid_spec=pltpu.PrefetchScalarGridSpec(num_s...  30.1 us
    ppermute x3, starting transfers between devices, swap_z(): return lax.ppermute(block, 'rep', [(i, i ^ 1) for i in range(8)])  18.5 us
    ppermute x12, starting transfers between devices, shift_x(): return lax.ppermute(block, 'rep', [(i, (i + 2 * by) % 8) for i in range(8)])  13.3 us
    ppermute x5, starting transfers between devices, shift_dom(): lax.ppermute(block, 'dom', [(i, (i + by) % size) for i in range(size)])  12.6 us
    ppermute x3, waiting for transfers between devices, swap_z(): return lax.ppermute(block, 'rep', [(i, i ^ 1) for i in range(8)])  10.3 us
    all_to_all x1, starting transfers between devices, operator_update(): half = lax.all_to_all(shares, 'dom', 0, 0, axis_index_groups=cores)  8.55 us
    pallas_call x1, Pallas kernels, source_side(): pl.pallas_call(source_kernel, grid_spec=pltpu.PrefetchScalarGridSpec(num_...  7.85 us
    all_to_all x1, starting transfers between devices, on_device(): got = lax.all_to_all(rel_grad.reshape(32, -1, D), 'dom', 0, 0)  7.85 us
  transfers between devices with their start and end apart: 23, of which 9 were waited for; matrix products, arithmetic and copies ran while one was open for 2% of the time, Pallas kernels for 13%

profile of v13, /device:TPU:1, one launch (start us, length us, event | category | flops | bytes accessed | tf_op | source)
XLA Modules:
  0.0 144.8 jit_solution(16932323456327641855)
XLA Ops:
  0.6 1.0 convert_element_type.15
  1.6 7.8 %collective-permute-start = (bf16[256,256]{1,0:T(8,128)(2,1)S(1)}, bf16[256,256]{1,0:T(8,128)(2,1)S(1)}, u32[]{:S(2)}, u32[]{:S(2)}) collective-permute-start(bf16[256,256]{1,0:T(8,128)(2,1)S(1)} %convert_element_type.15), channel_id=1, source_target_pairs={{0,1},{1,0},{2,3},{3,2},{4,5},{5,4},{6,7},{7,6},{8,9},{9,8},{10,11... | collective-permute-start | bytes 393224 | tf_op jit(solution)/shard_map/ppermute | solution.py:331
  9.4 0.8 fusion.1
  10.3 1.8 %collective-permute-done = bf16[256,256]{1,0:T(8,128)(2,1)S(1)} collective-permute-done((bf16[256,256]{1,0:T(8,128)(2,1)S(1)}, bf16[256,256]{1,0:T(8,128)(2,1)S(1)}, u32[]{:S(2)}, u32[]{:S(2)}) %collective-permute-start) | collective-permute-done | bytes 131104 | tf_op jit(solution)/shard_map/ppermute | solution.py:331
  12.1 3.1 %collective-permute-start.2 = (bf16[512,256]{1,0:T(8,128)(2,1)S(1)}, bf16[512,256]{1,0:T(8,128)(2,1)S(1)}, u32[]{:S(2)}, u32[]{:S(2)}) collective-permute-start(bf16[512,256]{1,0:T(8,128)(2,1)S(1)} %pad_maximum_fusion.refs_0_), channel_id=1, source_target_pairs={{0,6},{1,7},{2,0},{3,1},{4,2},{5,3},{6,4},{7,5},{8,14},{9,15},{10,... | collective-permute-start | bytes 786440 | tf_op jit(solution)/shard_map/ppermute | solution.py:335
  15.2 0.5 collective-permute-start.4
  15.7 0.6 collective-permute-start.6
  16.4 0.7 fusion.5
  17.9 3.2 %neg_weights.1.refs_7_ = f32[4,8,2048]{2,1,0:T(8,128)S(1)} custom-call(s32[4,1,1024]{2,1,0:T(1,128)S(1)} %reshape.47.neg_ref), custom_call_target="tpu_custom_call" | custom-call | flops 1500000000 | bytes 10500000 | tf_op jit(solution)/shard_map/neg_weights/pallas_call | solution.py:78
  21.1 2.2 %collective-permute-start.1 = (bf16[512,256]{1,0:T(8,128)(2,1)S(1)}, bf16[512,256]{1,0:T(8,128)(2,1)S(1)}, u32[]{:S(2)}, u32[]{:S(2)}) collective-permute-start(bf16[512,256]{1,0:T(8,128)(2,1)S(1)} %pad_maximum_fusion.refs_0_), channel_id=1, source_target_pairs={{0,248},{8,0},{16,8},{24,16},{32,24},{40,32},{48,40},{56,48},{64,5... | collective-permute-start | bytes 786440 | tf_op jit(solution)/shard_map/ppermute | solution.py:327
  23.4 4.0 %collective-permute-start.3 = (bf16[512,256]{1,0:T(8,128)(2,1)S(1)}, bf16[512,256]{1,0:T(8,128)(2,1)S(1)}, u32[]{:S(2)}, u32[]{:S(2)}) collective-permute-start(bf16[512,256]{1,0:T(8,128)(2,1)S(1)} %collective-permute-done.2.refs_1_), channel_id=1, source_target_pairs={{0,248},{8,0},{16,8},{24,16},{32,24},{40,32},{48,40},{56,48},{64,5... | collective-permute-start | bytes 786440 | tf_op jit(solution)/shard_map/ppermute | solution.py:327
  27.4 1.7 %collective-permute-start.5 = (bf16[512,256]{1,0:T(8,128)(2,1)S(1)}, bf16[512,256]{1,0:T(8,128)(2,1)S(1)}, u32[]{:S(2)}, u32[]{:S(2)}) collective-permute-start(bf16[512,256]{1,0:T(8,128)(2,1)S(1)} %collective-permute-done.4.refs_2_), channel_id=1, source_target_pairs={{0,248},{8,0},{16,8},{24,16},{32,24},{40,32},{48,40},{56,48},{64,5... | collective-permute-start | bytes 786440 | tf_op jit(solution)/shard_map/ppermute | solution.py:327
  29.0 1.5 %collective-permute-done.6.refs_3_ = bf16[512,256]{1,0:T(8,128)(2,1)S(1)} collective-permute-done((bf16[512,256]{1,0:T(8,128)(2,1)S(1)}, bf16[512,256]{1,0:T(8,128)(2,1)S(1)}, u32[]{:S(2)}, u32[]{:S(2)}) %collective-permute-start.6) | collective-permute-done | bytes 262176 | tf_op jit(solution)/shard_map/ppermute | solution.py:335
  30.6 2.2 %collective-permute-start.7 = (bf16[512,256]{1,0:T(8,128)(2,1)S(1)}, bf16[512,256]{1,0:T(8,128)(2,1)S(1)}, u32[]{:S(2)}, u32[]{:S(2)}) collective-permute-start(bf16[512,256]{1,0:T(8,128)(2,1)S(1)} %collective-permute-done.6.refs_3_), channel_id=1, source_target_pairs={{0,248},{8,0},{16,8},{24,16},{32,24},{40,32},{48,40},{56,48},{64,5... | collective-permute-start | bytes 786440 | tf_op jit(solution)/shard_map/ppermute | solution.py:327
  32.8 7.2 %queries.1 = (bf16[4096,256]{1,0:T(8,128)(2,1)S(1)}, bf16[256,4096]{1,0:T(8,128)(2,1)S(1)}) custom-call(s32[4]{0:T(128)S(1)} %copy-done.5, bf16[512,256]{1,0:T(8,128)(2,1)S(1)} %pad_maximum_fusion.refs_0_, bf16[512,256]{1,0:T(8,128)(2,1)S(1)} %collective-permute-done.2.refs_1_, bf16[512,256]{1,0:T(8,128)(2,1)S(1)} %collective-permute-done.4.refs_2_, ...), custom_call_target="tpu_custom_call" | custom-call | flops 4499999744 | bytes 31500000 | tf_op jit(solution)/shard_map/queries/pallas_call | solution.py:113
  40.1 30.1 %scores.1 = (bf16[256,4096]{1,0:T(8,128)(2,1)}, bf16[512,256]{1,0:T(8,128)(2,1)}, bf16[512,256]{1,0:T(8,128)(2,1)}, bf16[512,256]{1,0:T(8,128)(2,1)}, bf16[512,2...) custom-call(s32[4]{0:T(128)S(1)} %copy-done.5, s32[1]{0:T(128)S(6)} %copy.18.cnt_ref, ...), custom_call_target="tpu_custom_call" | custom-call | flops 14000000000 | bytes 98000000 | tf_op jit(solution)/shard_map/scores/pallas_call | solution.py:239
  70.2 7.8 %all-to-all-start = ((bf16[32,32,256]{2,1,0:T(8,128)(2,1)}), bf16[32,32,256]{2,1,0:T(8,128)(2,1)S(1)}, u32[]{:S(2)}, u32[]{:S(2)}) async-start(bf16[32,32,256]{2,1,0:T(8,128)(2,1)} %bitcast), calls=%async_computation | async-start | bytes 1048576 | tf_op jit(solution)/shard_map/all_to_all | solution.py:482
  78.1 3.4 %collective-permute-start.12 = (bf16[512,256]{1,0:T(8,128)(2,1)}, bf16[512,256]{1,0:T(8,128)(2,1)S(1)}, u32[]{:S(2)}, u32[]{:S(2)}) collective-permute-start(bf16[512,256]{1,0:T(8,128)(2,1)} %get-tuple-element.27), channel_id=1, source_target_pairs={{0,4},{1,5},{2,6},{3,7},{4,0},{5,1},{6,2},{7,3},{8,12},{9,13},{10,... | collective-permute-start | bytes 786440 | tf_op jit(solution)/shard_map/ppermute | solution.py:335
  81.5 1.6 %copy-done.7 = bf16[256,4096]{1,0:T(8,128)(2,1)S(1)} copy-done((bf16[256,4096]{1,0:T(8,128)(2,1)S(1)}, bf16[256,4096]{1,0:T(8,128)(2,1)}, u32[]{:S(2)}) %copy-start.7) | copy-done | bytes 2097176
  83.1 7.8 %source_grads.1 = (bf16[512,256]{1,0:T(8,128)(2,1)}, bf16[512,256]{1,0:T(8,128)(2,1)}, bf16[512,256]{1,0:T(8,128)(2,1)}, bf16[512,256]{1,0:T(8,128)(2,1)}) custom-call(s32[4]{0:T(128)S(1)} %copy-done.5, bf16[256,4096]{1,0:T(8,128)(2,1)S(1)} %copy-done.7, s32[4,1,1024]{2,1,0:T(1,128)S(1)} %reshape.44.refs_4_.src_ref, f32[4,256,256]{2,1,0:T(8,128)S(1)} %copy-done), custom_call_target="tpu_custom_call" | custom-call | flops 4000000000 | bytes 28000000 | tf_op jit(solution)/shard_map/source_grads/pallas_call | solution.py:300
  91.0 0.3 collective-permute-start.10
  91.3 1.2 collective-permute-start.8
  92.5 2.0 %all-to-all-done.refs_0_ = bf16[32,32,256]{2,1,0:T(8,128)(2,1)S(1)} async-done(((bf16[32,32,256]{2,1,0:T(8,128)(2,1)}), bf16[32,32,256]{2,1,0:T(8,128)(2,1)S(1)}, u32[]{:S(2)}, u32[]{:S(2)}) %all-to-all-start) | async-done | bytes 524320 | tf_op jit(solution)/shard_map/all_to_all | solution.py:482
  94.5 0.9 copy-done.1
  95.5 0.6 collective-permute-start.9
  96.1 0.7 copy-done.3
  96.8 0.9 copy-done.4
  97.8 0.9 copy-done.6
  98.9 2.5 %collective-permute-start.14 = (bf16[512,256]{1,0:T(8,128)(2,1)S(1)}, bf16[512,256]{1,0:T(8,128)(2,1)S(1)}, u32[]{:S(2)}, u32[]{:S(2)}) collective-permute-start(bf16[512,256]{1,0:T(8,128)(2,1)S(1)} %add_up.5.refs_5_), channel_id=1, source_target_pairs={{0,8},{8,16},{16,24},{24,32},{32,40},{40,48},{48,56},{56,64},{64,7... | collective-permute-start | bytes 786440 | tf_op jit(solution)/shard_map/ppermute | solution.py:327
  101.4 7.3 %collective-permute-start.15 = (f32[32,256]{1,0:T(8,128)S(1)}, f32[32,256]{1,0:T(8,128)S(1)}, u32[]{:S(2)}, u32[]{:S(2)}) collective-permute-start(f32[32,256]{1,0:T(8,128)S(1)} %add_up.4.refs_4_), channel_id=1, source_target_pairs={{0,1},{1,0},{2,3},{3,2},{4,5},{5,4},{6,7},{7,6},{8,9},{9,8},{10,11... | collective-permute-start | bytes 98312 | tf_op jit(solution)/shard_map/ppermute | solution.py:331
  108.6 1.3 collective-permute-done.15
  110.0 0.5 collective-permute-start.16
  110.5 3.0 %collective-permute-start.17 = (f32[32,256]{1,0:T(8,128)S(1)}, f32[32,256]{1,0:T(8,128)S(1)}, u32[]{:S(2)}, u32[]{:S(2)}) collective-permute-start(f32[32,256]{1,0:T(8,128)S(1)} %add.57.refs_0_), channel_id=1, source_target_pairs={{0,4},{1,5},{2,6},{3,7},{4,0},{5,1},{6,2},{7,3},{8,12},{9,13},{10,... | collective-permute-start | bytes 98312 | tf_op jit(solution)/shard_map/ppermute | solution.py:335
  113.5 0.2 add_up.6.refs_4_.refs_0_
  113.7 0.9 collective-permute-done.16.refs_1_
  114.6 0.9 collective-permute-done.17.refs_2_
  115.5 1.1 collective-permute-done.18.refs_3_
  117.0 0.8 broadcast_in_dim.2
  117.7 8.5 %all-to-all-start.1 = ((f16[16,40,256]{2,1,0:T(8,128)(2,1)}), f16[16,40,256]{2,1,0:T(8,128)(2,1)S(1)}, u32[]{:S(2)}, u32[]{:S(2)}) async-start(f16[16,40,256]{2,1,0:T(8,128)(2,1)} %broadcast_in_dim.2), calls=%async_computation.1 | async-start | bytes 655360 | tf_op jit(solution)/shard_map/all_to_all | solution.py:425
  126.3 3.5 %collective-permute-start.19 = (bf16[256,256]{1,0:T(8,128)(2,1)S(1)}, bf16[256,256]{1,0:T(8,128)(2,1)S(1)}, u32[]{:S(2)}, u32[]{:S(2)}) collective-permute-start(bf16[256,256]{1,0:T(8,128)(2,1)S(1)} %get-tuple-element.31), channel_id=1, source_target_pairs={{0,1},{1,0},{2,3},{3,2},{4,5},{5,4},{6,7},{7,6},{8,9},{9,8},{10,11... | collective-permute-start | bytes 393224 | tf_op jit(solution)/shard_map/ppermute | solution.py:331
  129.8 7.2 %collective-permute-done.19 = bf16[256,256]{1,0:T(8,128)(2,1)S(1)} collective-permute-done((bf16[256,256]{1,0:T(8,128)(2,1)S(1)}, bf16[256,256]{1,0:T(8,128)(2,1)S(1)}, u32[]{:S(2)}, u32[]{:S(2)}) %collective-permute-start.19) | collective-permute-done | bytes 131104 | tf_op jit(solution)/shard_map/ppermute | solution.py:331
  137.1 1.7 %all-to-all-done.1 = f16[16,40,256]{2,1,0:T(8,128)(2,1)S(1)} async-done(((f16[16,40,256]{2,1,0:T(8,128)(2,1)}), f16[16,40,256]{2,1,0:T(8,128)(2,1)S(1)}, u32[]{:S(2)}, u32[]{:S(2)}) %all-to-all-start.1) | async-done | bytes 327712 | tf_op jit(solution)/shard_map/all_to_all | solution.py:425
  138.7 2.2 %collective-permute-start.20 = (f16[16,40,256]{2,1,0:T(8,128)(2,1)S(1)}, f16[16,40,256]{2,1,0:T(8,128)(2,1)S(1)}, u32[]{:S(2)}, u32[]{:S(2)}) collective-permute-start(f16[16,40,256]{2,1,0:T(8,128)(2,1)S(1)} %all-to-all-done.1), channel_id=1, source_target_pairs={{0,8},{8,0},{16,24},{24,16},{32,40},{40,32},{48,56},{56,48},{64,72... | collective-permute-start | bytes 983048 | tf_op jit(solution)/shard_map/ppermute | solution.py:426
  141.0 0.6 fusion.22
  141.5 0.8 divide_subtract_fusion
  142.6 0.2 copy.16
  143.0 1.1 bitcast_subtract_fusion
  144.1 0.7 mul.55
  (61 shorter events, 1.6 us)
Async XLA Ops:
  1.6 10.5 %collective-permute-start = (bf16[256,256]{1,0:T(8,128)(2,1)S(1)}, bf16[256,256]{1,0:T(8,128)(2,1)S(1)}, u32[]{:S(2)}, u32[]{:S(2)}) collective-permute-start(bf16[256,256]{1,0:T(8,128)(2,1)S(1)} %convert_element_type.15), channel_id=1, source_target_pairs={{0,1},{1,0},{2,3},{3,2},{4,5},{5,4},{6,7},{7,6},{8,9},{9,8},{10,11... | collective-permute-start | bytes 393224 | tf_op jit(solution)/shard_map/ppermute | solution.py:331
  12.1 11.3 %collective-permute-start.2 = (bf16[512,256]{1,0:T(8,128)(2,1)S(1)}, bf16[512,256]{1,0:T(8,128)(2,1)S(1)}, u32[]{:S(2)}, u32[]{:S(2)}) collective-permute-start(bf16[512,256]{1,0:T(8,128)(2,1)S(1)} %pad_maximum_fusion.refs_0_), channel_id=1, source_target_pairs={{0,6},{1,7},{2,0},{3,1},{4,2},{5,3},{6,4},{7,5},{8,14},{9,15},{10,... | collective-permute-start | bytes 786440 | tf_op jit(solution)/shard_map/ppermute | solution.py:335
  15.2 12.1 %collective-permute-start.4 = (bf16[512,256]{1,0:T(8,128)(2,1)S(1)}, bf16[512,256]{1,0:T(8,128)(2,1)S(1)}, u32[]{:S(2)}, u32[]{:S(2)}) collective-permute-start(bf16[512,256]{1,0:T(8,128)(2,1)S(1)} %pad_maximum_fusion.refs_0_), channel_id=1, source_target_pairs={{0,4},{1,5},{2,6},{3,7},{4,0},{5,1},{6,2},{7,3},{8,12},{9,13},{10,... | collective-permute-start | bytes 786440 | tf_op jit(solution)/shard_map/ppermute | solution.py:335
  15.7 14.8 %collective-permute-start.6 = (bf16[512,256]{1,0:T(8,128)(2,1)S(1)}, bf16[512,256]{1,0:T(8,128)(2,1)S(1)}, u32[]{:S(2)}, u32[]{:S(2)}) collective-permute-start(bf16[512,256]{1,0:T(8,128)(2,1)S(1)} %pad_maximum_fusion.refs_0_), channel_id=1, source_target_pairs={{0,2},{1,3},{2,4},{3,5},{4,6},{5,7},{6,0},{7,1},{8,10},{9,11},{10,... | collective-permute-start | bytes 786440 | tf_op jit(solution)/shard_map/ppermute | solution.py:335
  17.9 14.9 %copy-start = (f32[4,256,256]{2,1,0:T(8,128)S(1)}, f32[4,256,256]{2,1,0:T(8,128)}, u32[]{:S(2)}) copy-start(f32[4,256,256]{2,1,0:T(8,128)} %mat_ref.1) | copy-start | bytes 3145732
  17.9 14.9 %copy-start.5 = (s32[4]{0:T(128)S(1)}, s32[4]{0:T(128)}, u32[]{:S(2)}) copy-start(s32[4]{0:T(128)} %rel_ref.5) | copy-start | bytes 52
  21.1 18.9 %collective-permute-start.1 = (bf16[512,256]{1,0:T(8,128)(2,1)S(1)}, bf16[512,256]{1,0:T(8,128)(2,1)S(1)}, u32[]{:S(2)}, u32[]{:S(2)}) collective-permute-start(bf16[512,256]{1,0:T(8,128)(2,1)S(1)} %pad_maximum_fusion.refs_0_), channel_id=1, source_target_pairs={{0,248},{8,0},{16,8},{24,16},{32,24},{40,32},{48,40},{56,48},{64,5... | collective-permute-start | bytes 786440 | tf_op jit(solution)/shard_map/ppermute | solution.py:327
  23.4 16.6 %collective-permute-start.3 = (bf16[512,256]{1,0:T(8,128)(2,1)S(1)}, bf16[512,256]{1,0:T(8,128)(2,1)S(1)}, u32[]{:S(2)}, u32[]{:S(2)}) collective-permute-start(bf16[512,256]{1,0:T(8,128)(2,1)S(1)} %collective-permute-done.2.refs_1_), channel_id=1, source_target_pairs={{0,248},{8,0},{16,8},{24,16},{32,24},{40,32},{48,40},{56,48},{64,5... | collective-permute-start | bytes 786440 | tf_op jit(solution)/shard_map/ppermute | solution.py:327
  27.4 12.7 %collective-permute-start.5 = (bf16[512,256]{1,0:T(8,128)(2,1)S(1)}, bf16[512,256]{1,0:T(8,128)(2,1)S(1)}, u32[]{:S(2)}, u32[]{:S(2)}) collective-permute-start(bf16[512,256]{1,0:T(8,128)(2,1)S(1)} %collective-permute-done.4.refs_2_), channel_id=1, source_target_pairs={{0,248},{8,0},{16,8},{24,16},{32,24},{40,32},{48,40},{56,48},{64,5... | collective-permute-start | bytes 786440 | tf_op jit(solution)/shard_map/ppermute | solution.py:327
  30.6 9.5 %collective-permute-start.7 = (bf16[512,256]{1,0:T(8,128)(2,1)S(1)}, bf16[512,256]{1,0:T(8,128)(2,1)S(1)}, u32[]{:S(2)}, u32[]{:S(2)}) collective-permute-start(bf16[512,256]{1,0:T(8,128)(2,1)S(1)} %collective-permute-done.6.refs_3_), channel_id=1, source_target_pairs={{0,248},{8,0},{16,8},{24,16},{32,24},{40,32},{48,40},{56,48},{64,5... | collective-permute-start | bytes 786440 | tf_op jit(solution)/shard_map/ppermute | solution.py:327
  70.2 24.3 %all-to-all-start = ((bf16[32,32,256]{2,1,0:T(8,128)(2,1)}), bf16[32,32,256]{2,1,0:T(8,128)(2,1)S(1)}, u32[]{:S(2)}, u32[]{:S(2)}) async-start(bf16[32,32,256]{2,1,0:T(8,128)(2,1)} %bitcast), calls=%async_computation | async-start | bytes 1048576 | tf_op jit(solution)/shard_map/all_to_all | solution.py:482
  78.1 17.5 %collective-permute-start.11 = (bf16[512,256]{1,0:T(8,128)(2,1)}, bf16[512,256]{1,0:T(8,128)(2,1)S(1)}, u32[]{:S(2)}, u32[]{:S(2)}) collective-permute-start(bf16[512,256]{1,0:T(8,128)(2,1)} %get-tuple-element.26), channel_id=1, source_target_pairs={{0,2},{1,3},{2,4},{3,5},{4,6},{5,7},{6,0},{7,1},{8,10},{9,11},{10,... | collective-permute-start | bytes 786440 | tf_op jit(solution)/shard_map/ppermute | solution.py:335
  78.1 18.0 %collective-permute-start.12 = (bf16[512,256]{1,0:T(8,128)(2,1)}, bf16[512,256]{1,0:T(8,128)(2,1)S(1)}, u32[]{:S(2)}, u32[]{:S(2)}) collective-permute-start(bf16[512,256]{1,0:T(8,128)(2,1)} %get-tuple-element.27), channel_id=1, source_target_pairs={{0,4},{1,5},{2,6},{3,7},{4,0},{5,1},{6,2},{7,3},{8,12},{9,13},{10,... | collective-permute-start | bytes 786440 | tf_op jit(solution)/shard_map/ppermute | solution.py:335
  81.5 14.6 %collective-permute-start.13 = (bf16[512,256]{1,0:T(8,128)(2,1)}, bf16[512,256]{1,0:T(8,128)(2,1)S(1)}, u32[]{:S(2)}, u32[]{:S(2)}) collective-permute-start(bf16[512,256]{1,0:T(8,128)(2,1)} %get-tuple-element.28), channel_id=1, source_target_pairs={{0,6},{1,7},{2,0},{3,1},{4,2},{5,3},{6,4},{7,5},{8,14},{9,15},{10,... | collective-permute-start | bytes 786440 | tf_op jit(solution)/shard_map/ppermute | solution.py:335
  81.5 1.6 %copy-start.7 = (bf16[256,4096]{1,0:T(8,128)(2,1)S(1)}, bf16[256,4096]{1,0:T(8,128)(2,1)}, u32[]{:S(2)}) copy-start(bf16[256,4096]{1,0:T(8,128)(2,1)} %get-tuple-element.20.gq_ref) | copy-start | bytes 6291460
  91.0 19.5 %collective-permute-start.10 = (bf16[512,256]{1,0:T(8,128)(2,1)}, bf16[512,256]{1,0:T(8,128)(2,1)S(1)}, u32[]{:S(2)}, u32[]{:S(2)}) collective-permute-start(bf16[512,256]{1,0:T(8,128)(2,1)} %get-tuple-element.24), channel_id=1, source_target_pairs={{0,6},{1,7},{2,0},{3,1},{4,2},{5,3},{6,4},{7,5},{8,14},{9,15},{10,... | collective-permute-start | bytes 786440 | tf_op jit(solution)/shard_map/ppermute | solution.py:335
  91.3 22.2 %collective-permute-start.8 = (bf16[512,256]{1,0:T(8,128)(2,1)}, bf16[512,256]{1,0:T(8,128)(2,1)S(1)}, u32[]{:S(2)}, u32[]{:S(2)}) collective-permute-start(bf16[512,256]{1,0:T(8,128)(2,1)} %get-tuple-element.22), channel_id=1, source_target_pairs={{0,2},{1,3},{2,4},{3,5},{4,6},{5,7},{6,0},{7,1},{8,10},{9,11},{10,... | collective-permute-start | bytes 786440 | tf_op jit(solution)/shard_map/ppermute | solution.py:335
  94.5 1.0 copy-start.1
  95.4 13.2 %copy-start.9 = (f32[4,256]{1,0:T(4,128)S(1)}, f32[4,256]{1,0:T(4,128)}, u32[]{:S(2)}) copy-start(f32[4,256]{1,0:T(4,128)} %param.12) | copy-start | bytes 12292
  95.5 18.0 %copy-start.2 = (bf16[512,256]{1,0:T(8,128)(2,1)S(1)}, bf16[512,256]{1,0:T(8,128)(2,1)}, u32[]{:S(2)}) copy-start(bf16[512,256]{1,0:T(8,128)(2,1)} %get-tuple-element.21.refs_1_.refs_0_) | copy-start | bytes 786436
  95.5 18.0 %collective-permute-start.9 = (bf16[512,256]{1,0:T(8,128)(2,1)}, bf16[512,256]{1,0:T(8,128)(2,1)S(1)}, u32[]{:S(2)}, u32[]{:S(2)}) collective-permute-start(bf16[512,256]{1,0:T(8,128)(2,1)} %get-tuple-element.23), channel_id=1, source_target_pairs={{0,4},{1,5},{2,6},{3,7},{4,0},{5,1},{6,2},{7,3},{8,12},{9,13},{10,... | collective-permute-start | bytes 786440 | tf_op jit(solution)/shard_map/ppermute | solution.py:335
  96.1 0.7 copy-start.3
  96.8 0.9 copy-start.4
  97.8 0.9 copy-start.6
  98.9 14.7 %collective-permute-start.14 = (bf16[512,256]{1,0:T(8,128)(2,1)S(1)}, bf16[512,256]{1,0:T(8,128)(2,1)S(1)}, u32[]{:S(2)}, u32[]{:S(2)}) collective-permute-start(bf16[512,256]{1,0:T(8,128)(2,1)S(1)} %add_up.5.refs_5_), channel_id=1, source_target_pairs={{0,8},{8,16},{16,24},{24,32},{32,40},{40,48},{48,56},{56,64},{64,7... | collective-permute-start | bytes 786440 | tf_op jit(solution)/shard_map/ppermute | solution.py:327
  101.4 8.6 %collective-permute-start.15 = (f32[32,256]{1,0:T(8,128)S(1)}, f32[32,256]{1,0:T(8,128)S(1)}, u32[]{:S(2)}, u32[]{:S(2)}) collective-permute-start(f32[32,256]{1,0:T(8,128)S(1)} %add_up.4.refs_4_), channel_id=1, source_target_pairs={{0,1},{1,0},{2,3},{3,2},{4,5},{5,4},{6,7},{7,6},{8,9},{9,8},{10,11... | collective-permute-start | bytes 98312 | tf_op jit(solution)/shard_map/ppermute | solution.py:331
  110.0 4.6 %collective-permute-start.16 = (f32[32,256]{1,0:T(8,128)S(1)}, f32[32,256]{1,0:T(8,128)S(1)}, u32[]{:S(2)}, u32[]{:S(2)}) collective-permute-start(f32[32,256]{1,0:T(8,128)S(1)} %add.57.refs_0_), channel_id=1, source_target_pairs={{0,2},{1,3},{2,4},{3,5},{4,6},{5,7},{6,0},{7,1},{8,10},{9,11},{10,... | collective-permute-start | bytes 98312 | tf_op jit(solution)/shard_map/ppermute | solution.py:335
  110.5 5.0 %collective-permute-start.17 = (f32[32,256]{1,0:T(8,128)S(1)}, f32[32,256]{1,0:T(8,128)S(1)}, u32[]{:S(2)}, u32[]{:S(2)}) collective-permute-start(f32[32,256]{1,0:T(8,128)S(1)} %add.57.refs_0_), channel_id=1, source_target_pairs={{0,4},{1,5},{2,6},{3,7},{4,0},{5,1},{6,2},{7,3},{8,12},{9,13},{10,... | collective-permute-start | bytes 98312 | tf_op jit(solution)/shard_map/ppermute | solution.py:335
  113.5 3.1 %collective-permute-start.18 = (f32[32,256]{1,0:T(8,128)S(1)}, f32[32,256]{1,0:T(8,128)S(1)}, u32[]{:S(2)}, u32[]{:S(2)}) collective-permute-start(f32[32,256]{1,0:T(8,128)S(1)} %add.57.refs_0_), channel_id=1, source_target_pairs={{0,6},{1,7},{2,0},{3,1},{4,2},{5,3},{6,4},{7,5},{8,14},{9,15},{10,... | collective-permute-start | bytes 98312 | tf_op jit(solution)/shard_map/ppermute | solution.py:335
  117.7 23.2 %copy-start.10 = (f32[256]{0:T(256)S(1)}, f32[256]{0:T(256)}, u32[]{:S(2)}) copy-start(f32[256]{0:T(256)} %param.10) | copy-start | bytes 3076
  117.7 23.8 %copy-start.8 = (f32[256,256]{1,0:T(8,128)S(1)}, f32[256,256]{1,0:T(8,128)}, u32[]{:S(2)}) copy-start(f32[256,256]{1,0:T(8,128)} %param.9) | copy-start | bytes 786436
  117.7 21.0 %all-to-all-start.1 = ((f16[16,40,256]{2,1,0:T(8,128)(2,1)}), f16[16,40,256]{2,1,0:T(8,128)(2,1)S(1)}, u32[]{:S(2)}, u32[]{:S(2)}) async-start(f16[16,40,256]{2,1,0:T(8,128)(2,1)} %broadcast_in_dim.2), calls=%async_computation.1 | async-start | bytes 655360 | tf_op jit(solution)/shard_map/all_to_all | solution.py:425
  126.3 10.6 %collective-permute-start.19 = (bf16[256,256]{1,0:T(8,128)(2,1)S(1)}, bf16[256,256]{1,0:T(8,128)(2,1)S(1)}, u32[]{:S(2)}, u32[]{:S(2)}) collective-permute-start(bf16[256,256]{1,0:T(8,128)(2,1)S(1)} %get-tuple-element.31), channel_id=1, source_target_pairs={{0,1},{1,0},{2,3},{3,2},{4,5},{5,4},{6,7},{7,6},{8,9},{9,8},{10,11... | collective-permute-start | bytes 393224 | tf_op jit(solution)/shard_map/ppermute | solution.py:331
  138.7 3.6 %collective-permute-start.20 = (f16[16,40,256]{2,1,0:T(8,128)(2,1)S(1)}, f16[16,40,256]{2,1,0:T(8,128)(2,1)S(1)}, u32[]{:S(2)}, u32[]{:S(2)}) collective-permute-start(f16[16,40,256]{2,1,0:T(8,128)(2,1)S(1)} %all-to-all-done.1), channel_id=1, source_target_pairs={{0,8},{8,0},{16,24},{24,16},{32,40},{40,32},{48,56},{56,48},{64,72... | collective-permute-start | bytes 983048 | tf_op jit(solution)/shard_map/ppermute | solution.py:426

commit v14 on v11

--- a/solution.py
+++ b/solution.py
@@ -491,7 +491,7 @@
     shares = operator_step(total, relation_accum)
     relation_new, relation_accum_new = operator_update(shares, relation, relation_accum)
     keep, give = split_sum([src_sum], total)
-    grads = keep + swap_z(give).astype(f32)
+    grads = add_up([keep, swap_z(give)], relation_new, f32)
     entity_new, entity_accum_new = rowwise(entity, entity_accum, grads)
     return (entity_new, entity_accum_new, relation_new, relation_accum_new)
 

time: 147 us -> 151 us (1.027); the launches traced: 144 us -> 150 us
  blocking collectives: 0 us -> 19.9 us
  starting transfers between devices: 63 us -> 53.5 us
  waiting for transfers between devices: 18.6 us -> 15.5 us
    all_to_all x0 -> x1, blocking collectives: none -> 19.9 us  [operator_update(): half = lax.all_to_all(shares, 'dom', 0, 0, axis_index_groups=cores)]
    all_to_all x1 -> x0, starting transfers between devices: 8.56 us -> none  [operator_update(): half = lax.all_to_all(shares, 'dom', 0, 0, axis_index_groups=cores)]
    all_to_all x1 -> x0, waiting for transfers between devices: 1.68 us -> none  [operator_update(): half = lax.all_to_all(shares, 'dom', 0, 0, axis_index_groups=cores)]
    unnamed x21 -> x23, local copies, waits for them, and re-layouts: 4.91 us -> 4.92 us
  transfers between devices with their start and end apart: 23 -> 22, of which waited for: 9 -> 8; matrix products, arithmetic and copies ran while one was open for 2% -> 2% of each run, Pallas kernels for 13% -> 12%
where the time goes in v14:
time: 151 us; the launch traced here: 150 us
  starting transfers between devices  53.5 us (35%)
  Pallas kernels  48.7 us (32%)
  blocking collectives  19.9 us (13%)
  waiting for transfers between devices  15.5 us (10%)
  local copies, waits for them, and re-layouts  5.85 us (4%)
  other arithmetic  5.11 us (3%)
  between operations  1.59 us (1%)
    pallas_call x1, Pallas kernels, score_side(): pl.pallas_call(score_kernel, grid_spec=pltpu.PrefetchScalarGridSpec(num_s...  30.1 us
    all_to_all x1, blocking collectives, operator_update(): half = lax.all_to_all(shares, 'dom', 0, 0, axis_index_groups=cores)  19.9 us
    ppermute x3, starting transfers between devices, swap_z(): return lax.ppermute(block, 'rep', [(i, i ^ 1) for i in range(8)])  18.7 us
    ppermute x12, starting transfers between devices, shift_x(): return lax.ppermute(block, 'rep', [(i, (i + 2 * by) % 8) for i in range(8)])  13.3 us
    ppermute x5, starting transfers between devices, shift_dom(): lax.ppermute(block, 'dom', [(i, (i + by) % size) for i in range(size)])  12.6 us
    ppermute x3, waiting for transfers between devices, swap_z(): return lax.ppermute(block, 'rep', [(i, i ^ 1) for i in range(8)])  8.99 us
    all_to_all x1, starting transfers between devices, on_device(): got = lax.all_to_all(rel_grad.reshape(32, -1, D), 'dom', 0, 0)  7.85 us
    pallas_call x1, Pallas kernels, source_side(): pl.pallas_call(source_kernel, grid_spec=pltpu.PrefetchScalarGridSpec(num_...  7.78 us
  transfers between devices with their start and end apart: 22, of which 8 were waited for; matrix products, arithmetic and copies ran while one was open for 2% of the time, Pallas kernels for 12%

profile of v14, /device:TPU:1, one launch (start us, length us, event | category | flops | bytes accessed | tf_op | source)
XLA Modules:
  0.0 150.2 jit_solution(16670582166601818264)
XLA Ops:
  0.6 1.0 convert_element_type.12
  1.6 7.8 %collective-permute-start = (bf16[256,256]{1,0:T(8,128)(2,1)S(1)}, bf16[256,256]{1,0:T(8,128)(2,1)S(1)}, u32[]{:S(2)}, u32[]{:S(2)}) collective-permute-start(bf16[256,256]{1,0:T(8,128)(2,1)S(1)} %convert_element_type.12), channel_id=1, source_target_pairs={{0,1},{1,0},{2,3},{3,2},{4,5},{5,4},{6,7},{7,6},{8,9},{9,8},{10,11... | collective-permute-start | bytes 393224 | tf_op jit(solution)/shard_map/ppermute | solution.py:331
  9.4 0.8 fusion.1
  10.3 1.8 %collective-permute-done = bf16[256,256]{1,0:T(8,128)(2,1)S(1)} collective-permute-done((bf16[256,256]{1,0:T(8,128)(2,1)S(1)}, bf16[256,256]{1,0:T(8,128)(2,1)S(1)}, u32[]{:S(2)}, u32[]{:S(2)}) %collective-permute-start) | collective-permute-done | bytes 131104 | tf_op jit(solution)/shard_map/ppermute | solution.py:331
  12.1 3.1 %collective-permute-start.2 = (bf16[512,256]{1,0:T(8,128)(2,1)S(1)}, bf16[512,256]{1,0:T(8,128)(2,1)S(1)}, u32[]{:S(2)}, u32[]{:S(2)}) collective-permute-start(bf16[512,256]{1,0:T(8,128)(2,1)S(1)} %pad_maximum_fusion.1.refs_0_), channel_id=1, source_target_pairs={{0,6},{1,7},{2,0},{3,1},{4,2},{5,3},{6,4},{7,5},{8,14},{9,15},{10,... | collective-permute-start | bytes 786440 | tf_op jit(solution)/shard_map/ppermute | solution.py:335
  15.2 0.5 collective-permute-start.4
  15.7 0.6 collective-permute-start.6
  16.4 0.7 fusion.5
  17.9 3.2 %neg_weights.1.refs_7_ = f32[4,8,2048]{2,1,0:T(8,128)S(1)} custom-call(s32[4,1,1024]{2,1,0:T(1,128)S(1)} %reshape.47.neg_ref), custom_call_target="tpu_custom_call" | custom-call | flops 1500000000 | bytes 10500000 | tf_op jit(solution)/shard_map/neg_weights/pallas_call | solution.py:78
  21.1 2.2 %collective-permute-start.1 = (bf16[512,256]{1,0:T(8,128)(2,1)S(1)}, bf16[512,256]{1,0:T(8,128)(2,1)S(1)}, u32[]{:S(2)}, u32[]{:S(2)}) collective-permute-start(bf16[512,256]{1,0:T(8,128)(2,1)S(1)} %pad_maximum_fusion.1.refs_0_), channel_id=1, source_target_pairs={{0,248},{8,0},{16,8},{24,16},{32,24},{40,32},{48,40},{56,48},{64,5... | collective-permute-start | bytes 786440 | tf_op jit(solution)/shard_map/ppermute | solution.py:327
  23.4 4.0 %collective-permute-start.3 = (bf16[512,256]{1,0:T(8,128)(2,1)S(1)}, bf16[512,256]{1,0:T(8,128)(2,1)S(1)}, u32[]{:S(2)}, u32[]{:S(2)}) collective-permute-start(bf16[512,256]{1,0:T(8,128)(2,1)S(1)} %collective-permute-done.2.refs_1_), channel_id=1, source_target_pairs={{0,248},{8,0},{16,8},{24,16},{32,24},{40,32},{48,40},{56,48},{64,5... | collective-permute-start | bytes 786440 | tf_op jit(solution)/shard_map/ppermute | solution.py:327
  27.4 1.7 %collective-permute-start.5 = (bf16[512,256]{1,0:T(8,128)(2,1)S(1)}, bf16[512,256]{1,0:T(8,128)(2,1)S(1)}, u32[]{:S(2)}, u32[]{:S(2)}) collective-permute-start(bf16[512,256]{1,0:T(8,128)(2,1)S(1)} %collective-permute-done.4.refs_2_), channel_id=1, source_target_pairs={{0,248},{8,0},{16,8},{24,16},{32,24},{40,32},{48,40},{56,48},{64,5... | collective-permute-start | bytes 786440 | tf_op jit(solution)/shard_map/ppermute | solution.py:327
  29.0 1.5 %collective-permute-done.6.refs_3_ = bf16[512,256]{1,0:T(8,128)(2,1)S(1)} collective-permute-done((bf16[512,256]{1,0:T(8,128)(2,1)S(1)}, bf16[512,256]{1,0:T(8,128)(2,1)S(1)}, u32[]{:S(2)}, u32[]{:S(2)}) %collective-permute-start.6) | collective-permute-done | bytes 262176 | tf_op jit(solution)/shard_map/ppermute | solution.py:335
  30.6 2.2 %collective-permute-start.7 = (bf16[512,256]{1,0:T(8,128)(2,1)S(1)}, bf16[512,256]{1,0:T(8,128)(2,1)S(1)}, u32[]{:S(2)}, u32[]{:S(2)}) collective-permute-start(bf16[512,256]{1,0:T(8,128)(2,1)S(1)} %collective-permute-done.6.refs_3_), channel_id=1, source_target_pairs={{0,248},{8,0},{16,8},{24,16},{32,24},{40,32},{48,40},{56,48},{64,5... | collective-permute-start | bytes 786440 | tf_op jit(solution)/shard_map/ppermute | solution.py:327
  32.8 7.2 %queries.1 = (bf16[4096,256]{1,0:T(8,128)(2,1)S(1)}, bf16[256,4096]{1,0:T(8,128)(2,1)S(1)}) custom-call(s32[4]{0:T(128)S(1)} %copy-done.4, bf16[512,256]{1,0:T(8,128)(2,1)S(1)} %pad_maximum_fusion.1.refs_0_, bf16[512,256]{1,0:T(8,128)(2,1)S(1)} %collective-permute-done.2.refs_1_, bf16[512,256]{1,0:T(8,128)(2,1)S(1)} %collective-permute-done.4.refs_2_, ...), custom_call_target="tpu_custom_call" | custom-call | flops 4499999744 | bytes 31500000 | tf_op jit(solution)/shard_map/queries/pallas_call | solution.py:113
  40.1 30.1 %scores.1 = (bf16[256,4096]{1,0:T(8,128)(2,1)}, bf16[512,256]{1,0:T(8,128)(2,1)S(1)}, bf16[512,256]{1,0:T(8,128)(2,1)}, bf16[512,256]{1,0:T(8,128)(2,1)}, bf16[5...) custom-call(s32[4]{0:T(128)S(1)} %copy-done.4, s32[1]{0:T(128)S(6)} %copy.15.cnt_ref, ...), custom_call_target="tpu_custom_call" | custom-call | flops 14000000000 | bytes 98000000 | tf_op jit(solution)/shard_map/scores/pallas_call | solution.py:239
  70.2 0.7 copy-done.5
  70.9 7.8 %all-to-all-start = ((bf16[32,32,256]{2,1,0:T(8,128)(2,1)}), bf16[32,32,256]{2,1,0:T(8,128)(2,1)S(1)}, u32[]{:S(2)}, u32[]{:S(2)}) async-start(bf16[32,32,256]{2,1,0:T(8,128)(2,1)} %bitcast), calls=%async_computation | async-start | bytes 1048576 | tf_op jit(solution)/shard_map/all_to_all | solution.py:482
  78.8 3.4 %collective-permute-start.12 = (bf16[512,256]{1,0:T(8,128)(2,1)}, bf16[512,256]{1,0:T(8,128)(2,1)S(1)}, u32[]{:S(2)}, u32[]{:S(2)}) collective-permute-start(bf16[512,256]{1,0:T(8,128)(2,1)} %get-tuple-element.27), channel_id=1, source_target_pairs={{0,4},{1,5},{2,6},{3,7},{4,0},{5,1},{6,2},{7,3},{8,12},{9,13},{10,... | collective-permute-start | bytes 786440 | tf_op jit(solution)/shard_map/ppermute | solution.py:335
  82.2 1.6 %copy-done.7 = bf16[256,4096]{1,0:T(8,128)(2,1)S(1)} copy-done((bf16[256,4096]{1,0:T(8,128)(2,1)S(1)}, bf16[256,4096]{1,0:T(8,128)(2,1)}, u32[]{:S(2)}) %copy-start.7) | copy-done | bytes 2097176
  83.8 7.8 %source_grads.1 = (bf16[512,256]{1,0:T(8,128)(2,1)S(1)}, bf16[512,256]{1,0:T(8,128)(2,1)}, bf16[512,256]{1,0:T(8,128)(2,1)}, bf16[512,256]{1,0:T(8,128)(2,1)}) custom-call(s32[4]{0:T(128)S(1)} %copy-done.4, bf16[256,4096]{1,0:T(8,128)(2,1)S(1)} %copy-done.7, s32[4,1,1024]{2,1,0:T(1,128)S(1)} %reshape.44.refs_4_.src_ref, f32[4,256,256]{2,1,0:T(8,128)S(1)} %copy-done), custom_call_target="tpu_custom_call" | custom-call | flops 4000000000 | bytes 28000000 | tf_op jit(solution)/shard_map/source_grads/pallas_call | solution.py:300
  91.6 0.3 collective-permute-start.10
  91.9 1.2 collective-permute-start.8
  93.1 2.1 %all-to-all-done.refs_0_ = bf16[32,32,256]{2,1,0:T(8,128)(2,1)S(1)} async-done(((bf16[32,32,256]{2,1,0:T(8,128)(2,1)}), bf16[32,32,256]{2,1,0:T(8,128)(2,1)S(1)}, u32[]{:S(2)}, u32[]{:S(2)}) %all-to-all-start) | async-done | bytes 524320 | tf_op jit(solution)/shard_map/all_to_all | solution.py:482
  95.2 0.6 collective-permute-start.9
  95.8 0.7 copy-done.2
  96.5 0.9 copy-done.3
  97.5 0.9 copy-done.6
  98.6 2.4 %collective-permute-start.14 = (bf16[512,256]{1,0:T(8,128)(2,1)S(1)}, bf16[512,256]{1,0:T(8,128)(2,1)S(1)}, u32[]{:S(2)}, u32[]{:S(2)}) collective-permute-start(bf16[512,256]{1,0:T(8,128)(2,1)S(1)} %add_up.6.refs_5_), channel_id=1, source_target_pairs={{0,8},{8,16},{16,24},{24,32},{32,40},{40,48},{48,56},{56,64},{64,7... | collective-permute-start | bytes 786440 | tf_op jit(solution)/shard_map/ppermute | solution.py:327
  101.0 7.3 %collective-permute-start.15 = (f32[32,256]{1,0:T(8,128)S(1)}, f32[32,256]{1,0:T(8,128)S(1)}, u32[]{:S(2)}, u32[]{:S(2)}) collective-permute-start(f32[32,256]{1,0:T(8,128)S(1)} %add_up.5.refs_4_), channel_id=1, source_target_pairs={{0,1},{1,0},{2,3},{3,2},{4,5},{5,4},{6,7},{7,6},{8,9},{9,8},{10,11... | collective-permute-start | bytes 98312 | tf_op jit(solution)/shard_map/ppermute | solution.py:331
  108.3 1.3 collective-permute-done.15
  109.6 0.5 collective-permute-start.16
  110.2 3.0 %collective-permute-start.17 = (f32[32,256]{1,0:T(8,128)S(1)}, f32[32,256]{1,0:T(8,128)S(1)}, u32[]{:S(2)}, u32[]{:S(2)}) collective-permute-start(f32[32,256]{1,0:T(8,128)S(1)} %add.54.refs_0_), channel_id=1, source_target_pairs={{0,4},{1,5},{2,6},{3,7},{4,0},{5,1},{6,2},{7,3},{8,12},{9,13},{10,... | collective-permute-start | bytes 98312 | tf_op jit(solution)/shard_map/ppermute | solution.py:335
  113.2 0.2 add_up.7.refs_4_.refs_0_
  113.3 0.9 collective-permute-done.16.refs_1_
  114.2 0.9 collective-permute-done.17.refs_2_
  115.1 1.1 collective-permute-done.18.refs_3_
  116.6 19.9 %all_to_all.10 = f16[16,40,256]{2,1,0:T(8,128)(2,1)S(1)} all-to-all(f16[16,40,256]{2,1,0:T(8,128)(2,1)S(1)} %broadcast_in_dim.2), channel_id=1, replica_groups={{0,16,32,48,64,80,96,112,128,144,160,176,192,208,224,240},{8,24,40,56,7..., dimensions={0} | all-to-all | bytes 655360 | tf_op jit(solution)/shard_map/all_to_all | solution.py:425
  136.5 1.1 collective-permute-start.20
  137.6 3.6 %collective-permute-start.19 = (bf16[256,256]{1,0:T(8,128)(2,1)S(1)}, bf16[256,256]{1,0:T(8,128)(2,1)S(1)}, u32[]{:S(2)}, u32[]{:S(2)}) collective-permute-start(bf16[256,256]{1,0:T(8,128)(2,1)S(1)} %get-tuple-element.31), channel_id=1, source_target_pairs={{0,1},{1,0},{2,3},{3,2},{4,5},{5,4},{6,7},{7,6},{8,9},{9,8},{10,11... | collective-permute-start | bytes 393224 | tf_op jit(solution)/shard_map/ppermute | solution.py:331
  141.2 0.2 select_bitcast_fusion.1
  141.4 0.2 pad_maximum_fusion
  141.6 0.1 bitcast_convert_fusion
  141.8 0.1 bitcast_subtract_fusion.refs_2_
  142.1 5.8 %collective-permute-done.19.refs_1_ = bf16[256,256]{1,0:T(8,128)(2,1)S(1)} collective-permute-done((bf16[256,256]{1,0:T(8,128)(2,1)S(1)}, bf16[256,256]{1,0:T(8,128)(2,1)S(1)}, u32[]{:S(2)}, u32[]{:S(2)}) %collective-permute-start.19) | collective-permute-done | bytes 131104 | tf_op jit(solution)/shard_map/ppermute | solution.py:331
  148.1 0.6 fusion.21
  148.7 0.8 divide_subtract_fusion
  149.5 0.7 mul.55
  (61 shorter events, 1.4 us)
Async XLA Ops:
  1.6 10.5 %collective-permute-start = (bf16[256,256]{1,0:T(8,128)(2,1)S(1)}, bf16[256,256]{1,0:T(8,128)(2,1)S(1)}, u32[]{:S(2)}, u32[]{:S(2)}) collective-permute-start(bf16[256,256]{1,0:T(8,128)(2,1)S(1)} %convert_element_type.12), channel_id=1, source_target_pairs={{0,1},{1,0},{2,3},{3,2},{4,5},{5,4},{6,7},{7,6},{8,9},{9,8},{10,11... | collective-permute-start | bytes 393224 | tf_op jit(solution)/shard_map/ppermute | solution.py:331
  12.1 11.3 %collective-permute-start.2 = (bf16[512,256]{1,0:T(8,128)(2,1)S(1)}, bf16[512,256]{1,0:T(8,128)(2,1)S(1)}, u32[]{:S(2)}, u32[]{:S(2)}) collective-permute-start(bf16[512,256]{1,0:T(8,128)(2,1)S(1)} %pad_maximum_fusion.1.refs_0_), channel_id=1, source_target_pairs={{0,6},{1,7},{2,0},{3,1},{4,2},{5,3},{6,4},{7,5},{8,14},{9,15},{10,... | collective-permute-start | bytes 786440 | tf_op jit(solution)/shard_map/ppermute | solution.py:335
  15.2 12.1 %collective-permute-start.4 = (bf16[512,256]{1,0:T(8,128)(2,1)S(1)}, bf16[512,256]{1,0:T(8,128)(2,1)S(1)}, u32[]{:S(2)}, u32[]{:S(2)}) collective-permute-start(bf16[512,256]{1,0:T(8,128)(2,1)S(1)} %pad_maximum_fusion.1.refs_0_), channel_id=1, source_target_pairs={{0,4},{1,5},{2,6},{3,7},{4,0},{5,1},{6,2},{7,3},{8,12},{9,13},{10,... | collective-permute-start | bytes 786440 | tf_op jit(solution)/shard_map/ppermute | solution.py:335
  15.7 14.8 %collective-permute-start.6 = (bf16[512,256]{1,0:T(8,128)(2,1)S(1)}, bf16[512,256]{1,0:T(8,128)(2,1)S(1)}, u32[]{:S(2)}, u32[]{:S(2)}) collective-permute-start(bf16[512,256]{1,0:T(8,128)(2,1)S(1)} %pad_maximum_fusion.1.refs_0_), channel_id=1, source_target_pairs={{0,2},{1,3},{2,4},{3,5},{4,6},{5,7},{6,0},{7,1},{8,10},{9,11},{10,... | collective-permute-start | bytes 786440 | tf_op jit(solution)/shard_map/ppermute | solution.py:335
  17.9 14.9 %copy-start = (f32[4,256,256]{2,1,0:T(8,128)S(1)}, f32[4,256,256]{2,1,0:T(8,128)}, u32[]{:S(2)}) copy-start(f32[4,256,256]{2,1,0:T(8,128)} %mat_ref.1) | copy-start | bytes 3145732
  17.9 14.9 %copy-start.4 = (s32[4]{0:T(128)S(1)}, s32[4]{0:T(128)}, u32[]{:S(2)}) copy-start(s32[4]{0:T(128)} %rel_ref.5) | copy-start | bytes 52
  21.1 18.9 %collective-permute-start.1 = (bf16[512,256]{1,0:T(8,128)(2,1)S(1)}, bf16[512,256]{1,0:T(8,128)(2,1)S(1)}, u32[]{:S(2)}, u32[]{:S(2)}) collective-permute-start(bf16[512,256]{1,0:T(8,128)(2,1)S(1)} %pad_maximum_fusion.1.refs_0_), channel_id=1, source_target_pairs={{0,248},{8,0},{16,8},{24,16},{32,24},{40,32},{48,40},{56,48},{64,5... | collective-permute-start | bytes 786440 | tf_op jit(solution)/shard_map/ppermute | solution.py:327
  23.4 16.6 %collective-permute-start.3 = (bf16[512,256]{1,0:T(8,128)(2,1)S(1)}, bf16[512,256]{1,0:T(8,128)(2,1)S(1)}, u32[]{:S(2)}, u32[]{:S(2)}) collective-permute-start(bf16[512,256]{1,0:T(8,128)(2,1)S(1)} %collective-permute-done.2.refs_1_), channel_id=1, source_target_pairs={{0,248},{8,0},{16,8},{24,16},{32,24},{40,32},{48,40},{56,48},{64,5... | collective-permute-start | bytes 786440 | tf_op jit(solution)/shard_map/ppermute | solution.py:327
  27.4 12.7 %collective-permute-start.5 = (bf16[512,256]{1,0:T(8,128)(2,1)S(1)}, bf16[512,256]{1,0:T(8,128)(2,1)S(1)}, u32[]{:S(2)}, u32[]{:S(2)}) collective-permute-start(bf16[512,256]{1,0:T(8,128)(2,1)S(1)} %collective-permute-done.4.refs_2_), channel_id=1, source_target_pairs={{0,248},{8,0},{16,8},{24,16},{32,24},{40,32},{48,40},{56,48},{64,5... | collective-permute-start | bytes 786440 | tf_op jit(solution)/shard_map/ppermute | solution.py:327
  30.6 9.5 %collective-permute-start.7 = (bf16[512,256]{1,0:T(8,128)(2,1)S(1)}, bf16[512,256]{1,0:T(8,128)(2,1)S(1)}, u32[]{:S(2)}, u32[]{:S(2)}) collective-permute-start(bf16[512,256]{1,0:T(8,128)(2,1)S(1)} %collective-permute-done.6.refs_3_), channel_id=1, source_target_pairs={{0,248},{8,0},{16,8},{24,16},{32,24},{40,32},{48,40},{56,48},{64,5... | collective-permute-start | bytes 786440 | tf_op jit(solution)/shard_map/ppermute | solution.py:327
  70.2 0.7 copy-start.5
  70.9 24.3 %all-to-all-start = ((bf16[32,32,256]{2,1,0:T(8,128)(2,1)}), bf16[32,32,256]{2,1,0:T(8,128)(2,1)S(1)}, u32[]{:S(2)}, u32[]{:S(2)}) async-start(bf16[32,32,256]{2,1,0:T(8,128)(2,1)} %bitcast), calls=%async_computation | async-start | bytes 1048576 | tf_op jit(solution)/shard_map/all_to_all | solution.py:482
  78.7 16.5 %collective-permute-start.11 = (bf16[512,256]{1,0:T(8,128)(2,1)}, bf16[512,256]{1,0:T(8,128)(2,1)S(1)}, u32[]{:S(2)}, u32[]{:S(2)}) collective-permute-start(bf16[512,256]{1,0:T(8,128)(2,1)} %get-tuple-element.26), channel_id=1, source_target_pairs={{0,2},{1,3},{2,4},{3,5},{4,6},{5,7},{6,0},{7,1},{8,10},{9,11},{10,... | collective-permute-start | bytes 786440 | tf_op jit(solution)/shard_map/ppermute | solution.py:335
  78.8 17.0 %collective-permute-start.12 = (bf16[512,256]{1,0:T(8,128)(2,1)}, bf16[512,256]{1,0:T(8,128)(2,1)S(1)}, u32[]{:S(2)}, u32[]{:S(2)}) collective-permute-start(bf16[512,256]{1,0:T(8,128)(2,1)} %get-tuple-element.27), channel_id=1, source_target_pairs={{0,4},{1,5},{2,6},{3,7},{4,0},{5,1},{6,2},{7,3},{8,12},{9,13},{10,... | collective-permute-start | bytes 786440 | tf_op jit(solution)/shard_map/ppermute | solution.py:335
  82.2 13.6 %collective-permute-start.13 = (bf16[512,256]{1,0:T(8,128)(2,1)}, bf16[512,256]{1,0:T(8,128)(2,1)S(1)}, u32[]{:S(2)}, u32[]{:S(2)}) collective-permute-start(bf16[512,256]{1,0:T(8,128)(2,1)} %get-tuple-element.28), channel_id=1, source_target_pairs={{0,6},{1,7},{2,0},{3,1},{4,2},{5,3},{6,4},{7,5},{8,14},{9,15},{10,... | collective-permute-start | bytes 786440 | tf_op jit(solution)/shard_map/ppermute | solution.py:335
  82.2 1.6 %copy-start.7 = (bf16[256,4096]{1,0:T(8,128)(2,1)S(1)}, bf16[256,4096]{1,0:T(8,128)(2,1)}, u32[]{:S(2)}) copy-start(bf16[256,4096]{1,0:T(8,128)(2,1)} %get-tuple-element.20.gq_ref) | copy-start | bytes 6291460
  91.6 18.6 %collective-permute-start.10 = (bf16[512,256]{1,0:T(8,128)(2,1)}, bf16[512,256]{1,0:T(8,128)(2,1)S(1)}, u32[]{:S(2)}, u32[]{:S(2)}) collective-permute-start(bf16[512,256]{1,0:T(8,128)(2,1)} %get-tuple-element.24), channel_id=1, source_target_pairs={{0,6},{1,7},{2,0},{3,1},{4,2},{5,3},{6,4},{7,5},{8,14},{9,15},{10,... | collective-permute-start | bytes 786440 | tf_op jit(solution)/shard_map/ppermute | solution.py:335
  91.9 21.3 %collective-permute-start.8 = (bf16[512,256]{1,0:T(8,128)(2,1)}, bf16[512,256]{1,0:T(8,128)(2,1)S(1)}, u32[]{:S(2)}, u32[]{:S(2)}) collective-permute-start(bf16[512,256]{1,0:T(8,128)(2,1)} %get-tuple-element.22), channel_id=1, source_target_pairs={{0,2},{1,3},{2,4},{3,5},{4,6},{5,7},{6,0},{7,1},{8,10},{9,11},{10,... | collective-permute-start | bytes 786440 | tf_op jit(solution)/shard_map/ppermute | solution.py:335
  95.1 13.2 %copy-start.9 = (f32[4,256]{1,0:T(4,128)S(1)}, f32[4,256]{1,0:T(4,128)}, u32[]{:S(2)}) copy-start(f32[4,256]{1,0:T(4,128)} %param.12) | copy-start | bytes 12292
  95.2 17.9 %collective-permute-start.9 = (bf16[512,256]{1,0:T(8,128)(2,1)}, bf16[512,256]{1,0:T(8,128)(2,1)S(1)}, u32[]{:S(2)}, u32[]{:S(2)}) collective-permute-start(bf16[512,256]{1,0:T(8,128)(2,1)} %get-tuple-element.23), channel_id=1, source_target_pairs={{0,4},{1,5},{2,6},{3,7},{4,0},{5,1},{6,2},{7,3},{8,12},{9,13},{10,... | collective-permute-start | bytes 786440 | tf_op jit(solution)/shard_map/ppermute | solution.py:335
  95.8 0.7 copy-start.2
  96.5 0.9 copy-start.3
  97.5 0.9 copy-start.6
  98.6 14.6 %collective-permute-start.14 = (bf16[512,256]{1,0:T(8,128)(2,1)S(1)}, bf16[512,256]{1,0:T(8,128)(2,1)S(1)}, u32[]{:S(2)}, u32[]{:S(2)}) collective-permute-start(bf16[512,256]{1,0:T(8,128)(2,1)S(1)} %add_up.6.refs_5_), channel_id=1, source_target_pairs={{0,8},{8,16},{16,24},{24,32},{32,40},{40,48},{48,56},{56,64},{64,7... | collective-permute-start | bytes 786440 | tf_op jit(solution)/shard_map/ppermute | solution.py:327
  101.0 8.6 %collective-permute-start.15 = (f32[32,256]{1,0:T(8,128)S(1)}, f32[32,256]{1,0:T(8,128)S(1)}, u32[]{:S(2)}, u32[]{:S(2)}) collective-permute-start(f32[32,256]{1,0:T(8,128)S(1)} %add_up.5.refs_4_), channel_id=1, source_target_pairs={{0,1},{1,0},{2,3},{3,2},{4,5},{5,4},{6,7},{7,6},{8,9},{9,8},{10,11... | collective-permute-start | bytes 98312 | tf_op jit(solution)/shard_map/ppermute | solution.py:331
  109.6 4.6 %collective-permute-start.16 = (f32[32,256]{1,0:T(8,128)S(1)}, f32[32,256]{1,0:T(8,128)S(1)}, u32[]{:S(2)}, u32[]{:S(2)}) collective-permute-start(f32[32,256]{1,0:T(8,128)S(1)} %add.54.refs_0_), channel_id=1, source_target_pairs={{0,2},{1,3},{2,4},{3,5},{4,6},{5,7},{6,0},{7,1},{8,10},{9,11},{10,... | collective-permute-start | bytes 98312 | tf_op jit(solution)/shard_map/ppermute | solution.py:335
  110.2 5.0 %collective-permute-start.17 = (f32[32,256]{1,0:T(8,128)S(1)}, f32[32,256]{1,0:T(8,128)S(1)}, u32[]{:S(2)}, u32[]{:S(2)}) collective-permute-start(f32[32,256]{1,0:T(8,128)S(1)} %add.54.refs_0_), channel_id=1, source_target_pairs={{0,4},{1,5},{2,6},{3,7},{4,0},{5,1},{6,2},{7,3},{8,12},{9,13},{10,... | collective-permute-start | bytes 98312 | tf_op jit(solution)/shard_map/ppermute | solution.py:335
  113.2 3.1 %collective-permute-start.18 = (f32[32,256]{1,0:T(8,128)S(1)}, f32[32,256]{1,0:T(8,128)S(1)}, u32[]{:S(2)}, u32[]{:S(2)}) collective-permute-start(f32[32,256]{1,0:T(8,128)S(1)} %add.54.refs_0_), channel_id=1, source_target_pairs={{0,6},{1,7},{2,0},{3,1},{4,2},{5,3},{6,4},{7,5},{8,14},{9,15},{10,... | collective-permute-start | bytes 98312 | tf_op jit(solution)/shard_map/ppermute | solution.py:335
  136.5 4.7 %collective-permute-start.20 = (f16[16,40,256]{2,1,0:T(8,128)(2,1)S(1)}, f16[16,40,256]{2,1,0:T(8,128)(2,1)S(1)}, u32[]{:S(2)}, u32[]{:S(2)}) collective-permute-start(f16[16,40,256]{2,1,0:T(8,128)(2,1)S(1)} %all_to_all.10), channel_id=1, source_target_pairs={{0,8},{8,0},{16,24},{24,16},{32,40},{40,32},{48,56},{56,48},{64,72... | collective-permute-start | bytes 983048 | tf_op jit(solution)/shard_map/ppermute | solution.py:426
  137.6 10.4 %collective-permute-start.19 = (bf16[256,256]{1,0:T(8,128)(2,1)S(1)}, bf16[256,256]{1,0:T(8,128)(2,1)S(1)}, u32[]{:S(2)}, u32[]{:S(2)}) collective-permute-start(bf16[256,256]{1,0:T(8,128)(2,1)S(1)} %get-tuple-element.31), channel_id=1, source_target_pairs={{0,1},{1,0},{2,3},{3,2},{4,5},{5,4},{6,7},{7,6},{8,9},{9,8},{10,11... | collective-permute-start | bytes 393224 | tf_op jit(solution)/shard_map/ppermute | solution.py:331
  142.0 7.5 %copy-start.1 = (f32[4,256,256]{2,1,0:T(8,128)}, f32[4,256,256]{2,1,0:T(8,128)S(1)}, u32[]{:S(2)}) copy-start(f32[4,256,256]{2,1,0:T(8,128)S(1)} %bitcast_subtract_fusion.refs_2_) | copy-start | bytes 3145732
  142.0 6.1 %copy-start.10 = (f32[256]{0:T(256)S(1)}, f32[256]{0:T(256)}, u32[]{:S(2)}) copy-start(f32[256]{0:T(256)} %param.10) | copy-start | bytes 3076
  142.0 6.7 %copy-start.8 = (f32[256,256]{1,0:T(8,128)S(1)}, f32[256,256]{1,0:T(8,128)}, u32[]{:S(2)}) copy-start(f32[256,256]{1,0:T(8,128)} %param.9) | copy-start | bytes 786436
